TPU v7x, 512 devices: a whole 4x8x8 slice. The times are simulated.
512 devices in a mesh: tm: 32 (over x, y), panel: 16 (over z, core).
Axes of the slice: x: 4, y: 8, z: 8, core: 2. Of those that a mesh axis runs over, the one named last changes fastest.
Arguments:
- transition: float32 [16384, 512], P(('tm', 'panel'))
- offset: float32 [16384], P(('tm', 'panel')), may hold values from -6 to 6
- covariance: float32 [16384, 512], P(('tm', 'panel')), as said below
- info_vector: float32 [16384], P(('tm', 'panel')), may hold values from -6 to 6
- information: float32 [16384, 512], P(('tm', 'panel')), as said below
- inverses: float32 [3, 16384, 512], P(None, ('tm', 'panel'))
Outputs:
- scan_transition: float32 [16384, 512], P(('tm', 'panel'))
- scan_offset: float32 [16384], P(('tm', 'panel'))
- scan_covariance: float32 [16384, 512], P(('tm', 'panel'))
- scan_info_vector: float32 [16384], P(('tm', 'panel'))
- scan_information: float32 [16384, 512], P(('tm', 'panel'))
Inputs may be any that keep to these rules, and one draw needn't show every extreme that they name: `covariance`: each block's 512 x 512 matrix is symmetric. `information`: each block's 512 x 512 matrix is symmetric.
All inputs are finite; a program needn't handle non-finite values.
Results may differ from a plain program's by a relative error of at most 0.0003.
Values sent between devices are 32-bit elements; how exact they have to be, the bound alone decides.
No kernel may reach another device: no remote copies, remote signals or barrier semaphores. Data moves between devices by JAX's collectives and lax.ppermute only.
A program may use at most 64 MiB of HBM per device.

v0:
```python
import jax
import jax.numpy as jnp
from jax import lax
from jax.sharding import PartitionSpec as P

HIGH = lax.Precision.HIGHEST


def passed_along(shard, axis, by):
    peers = lax.axis_size(axis)
    pairs = [(i, i + by) for i in range(peers) if 0 <= i + by < peers]
    return lax.ppermute(shard, axis, pairs)


def precise(left, right):
    return jnp.dot(left, right, precision=HIGH, preferred_element_type=jnp.float32)


def along_rows(left, right):
    return lax.dot_general(
        left, right, (((0,), (0,)), ((), ())), precision=HIGH, preferred_element_type=jnp.float32
    )


def against_rows(left, right):
    return lax.dot_general(
        left, right, (((1,), (1,)), ((), ())), precision=HIGH, preferred_element_type=jnp.float32
    )


def combine_level(state, inverse_local, level, position):
    own_transition, own_covariance, own_information, own_offset, own_vector = state
    distance = 2**level
    premix = precise(own_transition, lax.all_gather(inverse_local, "panel", axis=0, tiled=True))
    vector_whole = lax.all_gather(own_vector, "panel", axis=0, tiled=True)
    prior_transition, prior_covariance, prior_information, prior_offset, prior_vector = (
        passed_along(
            (own_transition, own_covariance, own_information, own_offset, own_vector),
            "tm",
            distance,
        )
    )
    transition_piece = lax.all_gather(prior_transition, "panel", axis=0, tiled=True)
    covariance_piece = lax.all_gather(prior_covariance, "panel", axis=0, tiled=True)
    offset_piece = lax.all_gather(prior_offset, "panel", axis=0, tiled=True)
    new_transition = precise(premix, transition_piece)
    carried = precise(premix, covariance_piece)
    gram = precise(inverse_local, transition_piece)
    kernel = precise(own_information, transition_piece)
    mixed_offset = precise(premix, offset_piece)
    weighted_offset = precise(own_information, offset_piece)
    new_covariance = (
        against_rows(carried, lax.all_gather(own_transition, "panel", axis=0, tiled=True))
        + own_covariance
    )
    new_offset = mixed_offset + precise(carried, vector_whole) + own_offset
    residual = own_vector - weighted_offset
    information_part, vector_part = (
        lax.psum_scatter(along_rows(gram, kernel), "panel", scatter_dimension=0, tiled=True),
        lax.psum_scatter(along_rows(gram, residual), "panel", scatter_dimension=0, tiled=True),
    )
    new_information = information_part + prior_information
    new_vector = vector_part + prior_vector
    active = position >= distance
    merged = (new_transition, new_covariance, new_information, new_offset, new_vector)
    return tuple((jnp.where(active, fresh, stale) for fresh, stale in zip(merged, state)))


def local(transition, offset, covariance, info_vector, information, inverses):
    levels = inverses.shape[0]
    position = lax.axis_index("tm")
    state = (transition, covariance, information, offset, info_vector)
    for level in range(levels):
        state = combine_level(state, inverses[level], level, position)
    return (state[0], state[3], state[1], state[4], state[2])


def solution(mesh):
    placed = (
        P(("tm", "panel"), None),
        P(("tm", "panel")),
        P(("tm", "panel"), None),
        P(("tm", "panel")),
        P(("tm", "panel"), None),
        P(None, ("tm", "panel"), None),
    )
    return jax.shard_map(
        local,
        mesh=mesh,
        in_specs=placed,
        out_specs=(
            P(("tm", "panel"), None),
            P(("tm", "panel")),
            P(("tm", "panel"), None),
            P(("tm", "panel")),
            P(("tm", "panel"), None),
        ),
        check_vma=False,
    )
```

profile of v0, /device:TPU:7, one launch (start us, length us, event | category | flops | bytes accessed | tf_op | source)
XLA Modules:
  0.0 714.9 jit_solution(504865055504002178)
XLA Ops:
  9.6 3.2 collective-permute-start
  12.8 3.9 collective-permute-done
  19.4 5.2 collective-permute-done.4
  26.4 31.3 %all-gather.34.cloned.1.call-done = f32[1,512,512]{2,1,0:T(8,128)} async-done(((f32[1,32,512]{2,1,0:T(8,128)}), f32[1,512,512]{2,1,0:T(8,128)}) %all-gather.34.cloned.1.call-update) | async-done | bytes 1048592 | tf_op jit(solution)/shard_map/all_gather | solution.py:34
  59.7 40.2 %all-gather.16.cloned.1.call-done = f32[512,512]{1,0:T(8,128)} async-done(((f32[32,512]{1,0:T(8,128)}), f32[512,512]{1,0:T(8,128)}) %all-gather.16.cloned.1.call-update) | async-done | bytes 1048592 | tf_op jit(solution)/shard_map/all_gather | solution.py:43
  99.9 2.0 convolution_select_fusion.2
  101.9 4.0 collective-permute-start.1
  106.0 5.4 collective-permute-done.1
  115.7 26.5 %all-gather.22.cloned.1.call-done = f32[512,512]{1,0:T(8,128)} async-done(((f32[32,512]{1,0:T(8,128)}), f32[512,512]{1,0:T(8,128)}) %all-gather.22.cloned.1.call-update) | async-done | bytes 1048592 | tf_op jit(solution)/shard_map/all_gather | solution.py:44
  144.1 40.1 %all-gather.24.cloned.1.call-done = f32[512,512]{1,0:T(8,128)} async-done(((f32[32,512]{1,0:T(8,128)}), f32[512,512]{1,0:T(8,128)}) %all-gather.24.cloned.1.call-update) | async-done | bytes 1048592 | tf_op jit(solution)/shard_map/all_gather | solution.py:53
  184.2 2.3 fusion.2
  186.5 4.0 collective-permute-start.6
  190.5 5.4 collective-permute-done.6
  198.0 28.9 %all-gather.36.cloned.1.call-done = f32[1,512,512]{2,1,0:T(8,128)} async-done(((f32[1,32,512]{2,1,0:T(8,128)}), f32[1,512,512]{2,1,0:T(8,128)}) %all-gather.36.cloned.1.call-update) | async-done | bytes 1048592 | tf_op jit(solution)/shard_map/all_gather | solution.py:34
  228.8 40.1 %all-gather.18.cloned.1.call-done = f32[512,512]{1,0:T(8,128)} async-done(((f32[32,512]{1,0:T(8,128)}), f32[512,512]{1,0:T(8,128)}) %all-gather.18.cloned.1.call-update) | async-done | bytes 1048592 | tf_op jit(solution)/shard_map/all_gather | solution.py:43
  268.9 2.0 convolution_select_fusion.1
  271.0 7.1 collective-permute-start.2
  278.1 2.8 collective-permute-done.2
  281.6 3.1 collective-permute-start.10
  285.5 3.2 collective-permute-done.10
  288.7 38.6 %reduce-scatter.4.cloned.1.call-done = f32[32,512]{1,0:T(8,128)} async-done(((f32[512,512]{1,0:T(8,128)}), f32[32,512]{1,0:T(8,128)}) %reduce-scatter.4.cloned.1.call-update) | async-done | bytes 65552 | tf_op jit(solution)/shard_map/reduce_scatter | solution.py:59
  328.8 2.0 fusion.48
  330.9 42.0 %all-gather.26.cloned.1.call-done = f32[512,512]{1,0:T(8,128)} async-done(((f32[32,512]{1,0:T(8,128)}), f32[512,512]{1,0:T(8,128)}) %all-gather.26.cloned.1.call-update) | async-done | bytes 1048592 | tf_op jit(solution)/shard_map/all_gather | solution.py:44
  374.9 41.1 %all-gather.28.cloned.1.call-done = f32[512,512]{1,0:T(8,128)} async-done(((f32[32,512]{1,0:T(8,128)}), f32[512,512]{1,0:T(8,128)}) %all-gather.28.cloned.1.call-update) | async-done | bytes 1048592 | tf_op jit(solution)/shard_map/all_gather | solution.py:53
  415.9 2.3 fusion.1
  418.2 7.1 collective-permute-start.9
  425.3 2.8 collective-permute-done.9
  428.8 3.1 collective-permute-start.3
  432.0 5.3 collective-permute-start.7
  440.4 24.3 %all-reduce = f32[512]{0:T(512)S(1)} all-reduce(f32[512]{0:T(512)S(1)} %dynamic-update-slice), channel_id=1, replica_groups=mesh['tm'=32,'panel'=16] {'panel'}, use_global_device_ids=true, to_apply=%add | all-reduce | flops 512 | bytes 4096
  465.0 24.2 %all-reduce.12 = (f32[512]{0:T(512)S(1)}, f32[512]{0:T(512)S(1)}) all-reduce(f32[512]{0:T(512)S(1)} %dynamic-update-slice.1, f32[512]{0:T(512)S(1)} %bitcast.157), channel_id=1, replica_groups=mesh['tm'=32,'panel'=16] {'panel'}, use_global_device_ids=true, to_apply=%add.1 | all-reduce | flops 1024 | bytes 8192
  489.6 2.3 collective-permute-start.5
  492.1 4.3 collective-permute-start.11
  497.1 24.4 %all-reduce.11 = (f32[512]{0:T(512)S(1)}, f32[512]{0:T(512)S(1)}) all-reduce(f32[512]{0:T(512)S(1)} %get-tuple-element.15, f32[512]{0:T(512)S(1)} %dynamic-update-slice.2), channel_id=1, replica_groups=mesh['tm'=32,'panel'=16] {'panel'}, use_global_device_ids=true, to_apply=%add.3 | all-reduce | flops 1024 | bytes 8192
  521.8 3.2 collective-permute-start.8
  527.0 4.0 collective-permute-done.8
  533.2 2.1 fusion.26
  535.3 3.9 collective-permute-done.12
  539.1 21.7 %reduce-scatter.6.cloned.1.call-done = f32[32,512]{1,0:T(8,128)} async-done(((f32[512,512]{1,0:T(8,128)}), f32[32,512]{1,0:T(8,128)}) %reduce-scatter.6.cloned.1.call-update) | async-done | bytes 65552 | tf_op jit(solution)/shard_map/reduce_scatter | solution.py:59
  562.4 2.0 fusion.50
  564.6 26.6 %all-reduce.10 = (f32[512]{0:T(512)S(1)}, f32[512]{0:T(512)S(1)}) all-reduce(f32[512]{0:T(512)S(1)} %bitcast.158, f32[512]{0:T(512)S(1)} %dynamic-update-slice.4), channel_id=7, replica_groups=mesh['tm'=32,'panel'=16] {'panel'}, use_global_device_ids=true, to_apply=%region_2.3.clone | all-reduce | flops 1024 | bytes 8192
  591.3 7.1 collective-permute-start.13
  598.4 8.2 %all-gather.30.cloned.1.call-done = f32[512,512]{1,0:T(8,128)} async-done(((f32[32,512]{1,0:T(8,128)}), f32[512,512]{1,0:T(8,128)}) %all-gather.30.cloned.1.call-update) | async-done | bytes 1048592 | tf_op jit(solution)/shard_map/all_gather | solution.py:44
  609.9 38.8 %all-gather.32.cloned.1.call-done = f32[512,512]{1,0:T(8,128)} async-done(((f32[32,512]{1,0:T(8,128)}), f32[512,512]{1,0:T(8,128)}) %all-gather.32.cloned.1.call-update) | async-done | bytes 1048592 | tf_op jit(solution)/shard_map/all_gather | solution.py:53
  648.6 2.9 fusion
  651.5 7.1 collective-permute-start.14
  659.0 23.4 %all-reduce.9 = (f32[512]{0:T(512)S(1)}, f32[512]{0:T(512)S(1)}) all-reduce(f32[512]{0:T(512)S(1)} %get-tuple-element.13, f32[512]{0:T(512)S(1)} %bitcast.156), channel_id=1, replica_groups=mesh['tm'=32,'panel'=16] {'panel'}, use_global_device_ids=true, to_apply=%add.5 | all-reduce | flops 1024 | bytes 8192
  683.9 23.0 %reduce-scatter.8.cloned.1.call-done = f32[32,512]{1,0:T(8,128)} async-done(((f32[512,512]{1,0:T(8,128)}), f32[32,512]{1,0:T(8,128)}) %reduce-scatter.8.cloned.1.call-update) | async-done | bytes 65552 | tf_op jit(solution)/shard_map/reduce_scatter | solution.py:59
  (125 shorter events, 40.7 us)
Async XLA Ops:
  7.2 50.6 %all-gather.34.cloned.1.call-start = ((), (), s32[]{:S(2)}) async-start(), calls=%async_computation.15 | async-start | bytes 1114112 | tf_op jit(solution)/shard_map/all_gather | solution.py:34
  8.8 0.8 copy-start.8
  8.8 8.6 %copy-start.11 = (f32[32,512]{1,0:T(8,128)S(1)}, f32[32,512]{1,0:T(8,128)}, u32[]{:S(2)}) copy-start(f32[32,512]{1,0:T(8,128)} %param.8) | copy-start | bytes 196612
  8.8 91.1 %all-gather.16.cloned.1.call-start = ((), (), s32[]{:S(2)}) async-start(), calls=%async_computation.3 | async-start | bytes 1114112 | tf_op jit(solution)/shard_map/all_gather | solution.py:43
  9.6 7.1 collective-permute-start
  16.7 0.6 copy-start.17
  17.4 124.7 %all-gather.22.cloned.1.call-start = ((), (), s32[]{:S(2)}) async-start(), calls=%async_computation.6 | async-start | bytes 1114112 | tf_op jit(solution)/shard_map/all_gather | solution.py:44
  17.5 7.1 collective-permute-start.4
  25.2 32.5 %copy-start.9 = (f32[32,512]{1,0:T(8,128)S(1)}, f32[32,512]{1,0:T(8,128)}, u32[]{:S(2)}) copy-start(f32[32,512]{1,0:T(8,128)} %param.6) | copy-start | bytes 196612
  25.2 159.0 %all-gather.24.cloned.1.call-start = ((), (), s32[]{:S(2)}) async-start(), calls=%async_computation.7 | async-start | bytes 1114112 | tf_op jit(solution)/shard_map/all_gather | solution.py:53
  25.8 201.1 %all-gather.36.cloned.1.call-start = ((), (), s32[]{:S(2)}) async-start(), calls=%async_computation.16 | async-start | bytes 1114112 | tf_op jit(solution)/shard_map/all_gather | solution.py:34
  26.4 242.6 %all-gather.18.cloned.1.call-start = ((), (), s32[]{:S(2)}) async-start(), calls=%async_computation.4 | async-start | bytes 1114112 | tf_op jit(solution)/shard_map/all_gather | solution.py:43
  59.7 52.4 %copy-start.7 = (f32[3,32,512]{2,1,0:T(8,128)S(1)}, f32[3,32,512]{2,1,0:T(8,128)}, u32[]{:S(2)}) copy-start(f32[3,32,512]{2,1,0:T(8,128)} %param.11) | copy-start | bytes 589828
  99.9 12.2 %copy-start.2 = (f32[512,512]{1,0:T(8,128)S(1)}, f32[512,512]{1,0:T(8,128)}, u32[]{:S(2)}) copy-start(f32[512,512]{1,0:T(8,128)} %all-gather.16.cloned.1.call-done) | copy-start | bytes 3145732
  101.9 10.9 %copy-start.5 = (f32[32,512]{1,0:T(8,128)}, f32[32,512]{1,0:T(8,128)S(1)}, u32[]{:S(2)}) copy-start(f32[32,512]{1,0:T(8,128)S(1)} %convolution_select_fusion.2) | copy-start | bytes 196612
  101.9 9.5 %collective-permute-start.1 = (f32[32,512]{1,0:T(8,128)S(1)}, f32[32,512]{1,0:T(8,128)S(1)}, u32[]{:S(2)}, u32[]{:S(2)}) collective-permute-start(f32[32,512]{1,0:T(8,128)S(1)} %convolution_select_fusion.2), channel_id=1, source_target_pairs={{0,32},{16,48},{32,64},{48,80},{64,96},{80,112},{96,128},{112,144}... | collective-permute-start | bytes 196616 | tf_op jit(solution)/shard_map/ppermute | solution.py:12
  112.1 0.8 copy-start.10
  112.1 215.2 %reduce-scatter.4.cloned.1.call-start = ((), (), s32[]{:S(2)}) async-start(), calls=%async_computation.11 | async-start | bytes 1114112 | tf_op jit(solution)/shard_map/reduce_scatter | solution.py:59
  115.6 257.3 %all-gather.26.cloned.1.call-start = ((), (), s32[]{:S(2)}) async-start(), calls=%async_computation.8 | async-start | bytes 1114112 | tf_op jit(solution)/shard_map/all_gather | solution.py:44
  186.5 9.5 %collective-permute-start.6 = (f32[32,512]{1,0:T(8,128)S(1)}, f32[32,512]{1,0:T(8,128)S(1)}, u32[]{:S(2)}, u32[]{:S(2)}) collective-permute-start(f32[32,512]{1,0:T(8,128)S(1)} %fusion.2), channel_id=1, source_target_pairs={{0,32},{16,48},{32,64},{48,80},{64,96},{80,112},{96,128},{112,144}... | collective-permute-start | bytes 196616 | tf_op jit(solution)/shard_map/ppermute | solution.py:12
  196.6 30.3 %copy-start.6 = (f32[32,512]{1,0:T(8,128)S(1)}, f32[32,512]{1,0:T(8,128)}, u32[]{:S(2)}) copy-start(f32[32,512]{1,0:T(8,128)} %copy-done.5) | copy-start | bytes 196612
  196.6 219.3 %all-gather.28.cloned.1.call-start = ((), (), s32[]{:S(2)}) async-start(), calls=%async_computation.9 | async-start | bytes 1114112 | tf_op jit(solution)/shard_map/all_gather | solution.py:53
  197.3 327.7 %all-gather.38.cloned.1.call-start = ((), (), s32[]{:S(2)}) async-start(), calls=%async_computation.17 | async-start | bytes 1114112 | tf_op jit(solution)/shard_map/all_gather | solution.py:34
  197.9 335.3 %all-gather.20.cloned.1.call-start = ((), (), s32[]{:S(2)}) async-start(), calls=%async_computation.5 | async-start | bytes 1114112 | tf_op jit(solution)/shard_map/all_gather | solution.py:43
  268.9 15.8 %copy-start.1 = (f32[512,512]{1,0:T(8,128)S(1)}, f32[512,512]{1,0:T(8,128)}, u32[]{:S(2)}) copy-start(f32[512,512]{1,0:T(8,128)} %all-gather.18.cloned.1.call-done) | copy-start | bytes 3145732
  271.0 14.5 %copy-start.3 = (f32[32,512]{1,0:T(8,128)}, f32[32,512]{1,0:T(8,128)S(1)}, u32[]{:S(2)}) copy-start(f32[32,512]{1,0:T(8,128)S(1)} %convolution_select_fusion.1) | copy-start | bytes 196612
  271.0 9.9 %collective-permute-start.2 = (f32[32,512]{1,0:T(8,128)S(1)}, f32[32,512]{1,0:T(8,128)S(1)}, u32[]{:S(2)}, u32[]{:S(2)}) collective-permute-start(f32[32,512]{1,0:T(8,128)S(1)} %convolution_select_fusion.1), channel_id=1, source_target_pairs={{0,64},{16,80},{32,96},{48,112},{64,128},{80,144},{96,160},{112,17... | collective-permute-start | bytes 196616 | tf_op jit(solution)/shard_map/ppermute | solution.py:12
  280.9 0.6 copy-start.12
  281.5 279.3 %reduce-scatter.6.cloned.1.call-start = ((), (), s32[]{:S(2)}) async-start(), calls=%async_computation.13 | async-start | bytes 1114112 | tf_op jit(solution)/shard_map/reduce_scatter | solution.py:59
  281.6 7.1 collective-permute-start.10
  330.9 275.7 %all-gather.30.cloned.1.call-start = ((), (), s32[]{:S(2)}) async-start(), calls=%async_computation.10 | async-start | bytes 1114112 | tf_op jit(solution)/shard_map/all_gather | solution.py:44
  418.2 9.9 %collective-permute-start.9 = (f32[32,512]{1,0:T(8,128)S(1)}, f32[32,512]{1,0:T(8,128)S(1)}, u32[]{:S(2)}, u32[]{:S(2)}) collective-permute-start(f32[32,512]{1,0:T(8,128)S(1)} %fusion.1), channel_id=1, source_target_pairs={{0,64},{16,80},{32,96},{48,112},{64,128},{80,144},{96,160},{112,17... | collective-permute-start | bytes 196616 | tf_op jit(solution)/shard_map/ppermute | solution.py:12
  428.1 0.6 copy-start.13
  428.1 0.7 copy-start.19
  428.1 3.8 copy-start.18
  428.8 219.9 %all-gather.32.cloned.1.call-start = ((), (), s32[]{:S(2)}) async-start(), calls=%async_computation.12 | async-start | bytes 1114112 | tf_op jit(solution)/shard_map/all_gather | solution.py:53
  428.8 11.3 %collective-permute-start.3 = (f32[32]{0:T(128)S(1)}, f32[32]{0:T(128)S(1)}, u32[]{:S(2)}, u32[]{:S(2)}) collective-permute-start(f32[32]{0:T(128)S(1)} %copy-done.19), channel_id=1, source_target_pairs={{0,16},{16,32},{32,48},{48,64},{64,80},{80,96},{96,112},{112,128},... | collective-permute-start | bytes 392 | tf_op jit(solution)/shard_map/ppermute | solution.py:12
  432.0 59.9 %collective-permute-start.7 = (f32[32]{0:T(128)S(1)}, f32[32]{0:T(128)S(1)}, u32[]{:S(2)}, u32[]{:S(2)}) collective-permute-start(f32[32]{0:T(128)S(1)} %copy-done.18), channel_id=1, source_target_pairs={{0,16},{16,32},{32,48},{48,64},{64,80},{80,96},{96,112},{112,128},... | collective-permute-start | bytes 392 | tf_op jit(solution)/shard_map/ppermute | solution.py:12
  437.3 0.7 copy-start.20
  489.4 217.4 %reduce-scatter.8.cloned.1.call-start = ((), (), s32[]{:S(2)}) async-start(), calls=%async_computation.14 | async-start | bytes 1114112 | tf_op jit(solution)/shard_map/reduce_scatter | solution.py:59
  489.6 7.3 %collective-permute-start.5 = (f32[32]{0:T(128)S(1)}, f32[32]{0:T(128)S(1)}, u32[]{:S(2)}, u32[]{:S(2)}) collective-permute-start(f32[32]{0:T(128)S(1)} %fusion.5), channel_id=1, source_target_pairs={{0,32},{16,48},{32,64},{48,80},{64,96},{80,112},{96,128},{112,144}... | collective-permute-start | bytes 392 | tf_op jit(solution)/shard_map/ppermute | solution.py:12
  492.1 99.1 %collective-permute-start.11 = (f32[32]{0:T(128)S(1)}, f32[32]{0:T(128)S(1)}, u32[]{:S(2)}, u32[]{:S(2)}) collective-permute-start(f32[32]{0:T(128)S(1)} %get-tuple-element.16), channel_id=1, source_target_pairs={{0,32},{16,48},{32,64},{48,80},{64,96},{80,112},{96,128},{112,144}... | collective-permute-start | bytes 392 | tf_op jit(solution)/shard_map/ppermute | solution.py:12
  521.5 3.5 copy-start.4
  521.8 9.1 %collective-permute-start.8 = (f32[32]{0:T(128)S(1)}, f32[32]{0:T(128)S(1)}, u32[]{:S(2)}, u32[]{:S(2)}) collective-permute-start(f32[32]{0:T(128)S(1)} %fusion.8), channel_id=1, source_target_pairs={{0,64},{16,80},{32,96},{48,112},{64,128},{80,144},{96,160},{112,17... | collective-permute-start | bytes 392 | tf_op jit(solution)/shard_map/ppermute | solution.py:12
  531.1 8.0 %collective-permute-start.12 = (f32[32,512]{1,0:T(8,128)S(1)}, f32[32,512]{1,0:T(8,128)S(1)}, u32[]{:S(2)}, u32[]{:S(2)}) collective-permute-start(f32[32,512]{1,0:T(8,128)S(1)} %add_select_fusion.2), channel_id=1, source_target_pairs={{0,32},{16,48},{32,64},{48,80},{64,96},{80,112},{96,128},{112,144}... | collective-permute-start | bytes 196616 | tf_op jit(solution)/shard_map/ppermute | solution.py:12
  533.2 28.5 %copy-start = (f32[512,512]{1,0:T(8,128)S(1)}, f32[512,512]{1,0:T(8,128)}, u32[]{:S(2)}) copy-start(f32[512,512]{1,0:T(8,128)} %all-gather.20.cloned.1.call-done) | copy-start | bytes 3145732
  591.3 91.9 %collective-permute-start.13 = (f32[32]{0:T(128)S(1)}, f32[32]{0:T(128)S(1)}, u32[]{:S(2)}, u32[]{:S(2)}) collective-permute-start(f32[32]{0:T(128)S(1)} %get-tuple-element.14), channel_id=1, source_target_pairs={{0,64},{16,80},{32,96},{48,112},{64,128},{80,144},{96,160},{112,17... | collective-permute-start | bytes 392 | tf_op jit(solution)/shard_map/ppermute | solution.py:12
  651.5 32.3 %collective-permute-start.14 = (f32[32,512]{1,0:T(8,128)S(1)}, f32[32,512]{1,0:T(8,128)S(1)}, u32[]{:S(2)}, u32[]{:S(2)}) collective-permute-start(f32[32,512]{1,0:T(8,128)S(1)} %add_select_fusion.1), channel_id=1, source_target_pairs={{0,64},{16,80},{32,96},{48,112},{64,128},{80,144},{96,160},{112,17... | collective-permute-start | bytes 196616 | tf_op jit(solution)/shard_map/ppermute | solution.py:12
  (3 other events, 1.9 us)
Sparse Core Ops, SparseCore 0:
  10.7 46.9 all-gather.33
  59.8 40.0 all-gather.15
  102.0 40.0 all-gather.21
  144.1 40.0 all-gather.23
  186.8 40.0 all-gather.35
  228.8 40.0 all-gather.17
  271.7 55.4 reduce-scatter.3
  329.6 43.2 all-gather.25
  375.8 40.0 all-gather.27
  418.7 40.1 all-gather.37
  461.8 39.9 all-gather.19
  504.7 56.0 reduce-scatter.5
  563.5 43.0 all-gather.29
  608.6 40.0 all-gather.31
  651.3 55.5 reduce-scatter.7
where the time goes:
time: 719 us; the launch traced here: 715 us
  waiting for transfers between devices  460 us (64%)
  blocking collectives  123 us (17%)
  starting transfers between devices  65.4 us (9%)
  matrix products  38.4 us (5%)
  between operations  15.7 us (2%)
  local copies, waits for them, and re-layouts  8.3 us (1%)
    unnamed x5, blocking collectives  123 us
    all_gather x3, waiting for transfers between devices, combine_level(): lax.all_gather(own_transition, 'panel', axis=0, tiled=True)  120 us
    reduce_scatter x3, waiting for transfers between devices, combine_level(): lax.psum_scatter(along_rows(gram, kernel), 'panel', scatter_dimension=0,...  83.3 us
    all_gather x3, waiting for transfers between devices, combine_level(): lax.all_gather(prior_transition, 'panel', axis=0, tiled=True)  80.4 us
    all_gather x3, waiting for transfers between devices, combine_level(): lax.all_gather(prior_covariance, 'panel', axis=0, tiled=True)  76.6 us
    ppermute x15, starting transfers between devices, passed_along(): return lax.ppermute(shard, axis, pairs)  64.8 us
    all_gather x3, waiting for transfers between devices, combine_level(): lax.all_gather(inverse_local, 'panel', axis=0, tiled=True)  60.2 us
    ppermute x15, waiting for transfers between devices, passed_along(): return lax.ppermute(shard, axis, pairs)  37.1 us
  transfers between devices with their start and end apart: 30, of which 23 were waited for; matrix products, arithmetic and copies ran while one was open for 6% of the time, Pallas kernels for 0%

commit v1 on v0

v1 whole, which is shorter than its diff:
```python
import jax
import jax.numpy as jnp
from jax import lax
from jax.sharding import PartitionSpec as P

HIGH = lax.Precision.HIGH


def passed_along(shard, by):
    peers = lax.axis_size("tm")
    return lax.ppermute(shard, "tm", [(i, i + by) for i in range(peers - by)])


def dot(left, right, over=((1,), (0,))):
    return lax.dot_general(left, right, (over, ((), ())), precision=HIGH, preferred_element_type=jnp.float32)


def gathered(shards):
    rows, width = shards[0].shape
    whole = lax.all_gather(jnp.stack(shards), "panel", axis=0, tiled=False)
    return [whole[:, i].reshape(-1, width) for i in range(len(shards))]


def local(transition, offset, covariance, info_vector, information, inverses):
    levels, rows, width = inverses.shape
    position = lax.axis_index("tm")
    mine = lax.axis_index("panel")

    def own_rows(whole):
        return lax.dynamic_slice_in_dim(whole, mine * rows, rows, 0)

    vectors = jnp.zeros((8, width), jnp.float32).at[0, :rows].set(offset).at[1, :rows].set(info_vector)
    own = jnp.concatenate([transition, covariance, information, vectors])
    prior = passed_along(own, 1)
    span = own.shape[0]
    whole = lax.all_gather(
        jnp.concatenate([own, prior, inverses.reshape(levels * rows, width)]), "panel", axis=0, tiled=False
    )

    def part(start, count=rows):
        return whole[:, start : start + count].reshape(-1, width)

    def vector(start):
        return whole[:, start, :rows].reshape(1, width)

    a2, j2 = part(0), part(2 * rows)
    b2, e2 = vector(3 * rows), vector(3 * rows + 1)
    c2 = covariance
    a1, c1, j1 = part(span), part(span + rows), part(span + 2 * rows)
    b1, e1 = vector(span + 3 * rows), vector(span + 3 * rows + 1)
    mixers = [part(2 * span + level * rows) for level in range(levels)]
    for level in range(levels):
        distance = 2**level
        if level:
            sent = jnp.concatenate([own_rows(a2), c2, own_rows(j2)]), jnp.concatenate([b2, e2])
            (prior, earlier) = passed_along(sent, distance)
            whole = lax.all_gather(prior, "panel", axis=0, tiled=False)
            a1, c1, j1 = part(0), part(rows), part(2 * rows)
            b1, e1 = earlier[:1], earlier[1:]
        active = position >= distance
        m = mixers[level]
        premix = dot(a2, m)
        gram = dot(m, a1)
        a = dot(premix, a1)
        carried = dot(own_rows(premix), c1)
        c = dot(carried, a2, ((1,), (1,))) + c2
        j = dot(gram, dot(j2, a1), ((0,), (0,))) + j1
        mixed = b1 + dot(e2, c1, ((1,), (1,)))
        b = dot(mixed, premix, ((1,), (1,))) + b2
        e = dot(e2 - dot(b1, j2, ((1,), (1,))), gram) + e1
        a2, c2, j2, b2, e2 = (
            jnp.where(active, fresh, stale) for fresh, stale in zip((a, c, j, b, e), (a2, c2, j2, b2, e2))
        )

    def own_part(row):
        return lax.dynamic_slice_in_dim(row[0], mine * rows, rows, 0)

    return own_rows(a2), own_part(b2), c2, own_part(e2), own_rows(j2)


def solution(mesh):
    matrix = P(("tm", "panel"), None)
    vector = P(("tm", "panel"))
    return jax.shard_map(
        local,
        mesh=mesh,
        in_specs=(matrix, vector, matrix, vector, matrix, P(None, ("tm", "panel"), None)),
        out_specs=(matrix, vector, matrix, vector, matrix),
        check_vma=False,
    )
```

time: 719 us -> 253 us (0.35)
  waiting for transfers between devices: 460 us -> 151 us
  blocking collectives: 123 us -> 0 us
  starting transfers between devices: 65.4 us -> 27.5 us
  local copies, waits for them, and re-layouts: 8.3 us -> 20.8 us
    all_gather x12 -> x3, waiting for transfers between devices: 337 us -> 128 us  [the longest x1 71.8 us: local(): lax.all_gather(jnp.concatenate([own, prior, inverses.reshape(levels * row...]
    unnamed x5 -> x0, blocking collectives: 123 us -> none
    reduce_scatter x3 -> x0, waiting for transfers between devices: 83.3 us -> none  [combine_level(): lax.psum_scatter(along_rows(gram, kernel), 'panel', scatter_dimension=0,...]
    ppermute x15 -> x5, starting transfers between devices: 64.8 us -> 27.2 us  [passed_along(): return lax.ppermute(shard, 'tm', [(i, i + by) for i in range(peers - by)])]
    ppermute x15 -> x5, waiting for transfers between devices: 37.1 us -> 23.2 us  [passed_along(): return lax.ppermute(shard, 'tm', [(i, i + by) for i in range(peers - by)])]
    slice x1 -> x5, local copies, waits for them, and re-layouts: 1.58 us -> 11.5 us  [the longest x3 10.5 us: part(): return whole[:, start:start + count].reshape(-1, width)]
  transfers between devices with their start and end apart: 30 -> 8, of which waited for: 23 -> 8; matrix products, arithmetic and copies ran while one was open for 6% -> 8% of each run, Pallas kernels for 0% -> 0%
where the time goes in v1:
time: 253 us; the launch traced here: 251 us
  waiting for transfers between devices  151 us (60%)
  matrix products  35 us (14%)
  starting transfers between devices  27.5 us (11%)
  local copies, waits for them, and re-layouts  20.8 us (8%)
  between operations  14.2 us (6%)
    all_gather x1, waiting for transfers between devices, local(): lax.all_gather(jnp.concatenate([own, prior, inverses.reshape(levels * row...  71.8 us
    all_gather x2, waiting for transfers between devices, local(): whole = lax.all_gather(prior, 'panel', axis=0, tiled=False)  56.1 us
    dot_general x33, matrix products, dot(): lax.dot_general(left, right, (over, ((), ())), precision=HIGH, preferred_...  35 us
    ppermute x5, starting transfers between devices, passed_along(): return lax.ppermute(shard, 'tm', [(i, i + by) for i in range(peers - by)])  27.2 us
    ppermute x5, waiting for transfers between devices, passed_along(): return lax.ppermute(shard, 'tm', [(i, i + by) for i in range(peers - by)])  23.2 us
    slice x3, local copies, waits for them, and re-layouts, part(): return whole[:, start:start + count].reshape(-1, width)  10.5 us
    unnamed x39, local copies, waits for them, and re-layouts  5.81 us
  transfers between devices with their start and end apart: 8, of which 8 were waited for; matrix products, arithmetic and copies ran while one was open for 8% of the time, Pallas kernels for 0%

profile of v1, /device:TPU:7, one launch (start us, length us, event | category | flops | bytes accessed | tf_op | source)
XLA Modules:
  0.0 250.9 jit_solution(454126032135132663)
XLA Ops:
  7.9 0.8 scatter.9
  8.6 0.9 pad_maximum_fusion
  9.6 3.2 %collective-permute-start = (f32[104,512]{1,0:T(8,128)S(1)}, f32[104,512]{1,0:T(8,128)S(1)}, u32[]{:S(2)}, u32[]{:S(2)}) collective-permute-start(f32[104,512]{1,0:T(8,128)S(1)} %pad_maximum_fusion), channel_id=1, source_target_pairs={{0,16},{16,32},{32,48},{48,64},{64,80},{80,96},{96,112},{112,128},... | collective-permute-start | bytes 638984 | tf_op jit(solution)/shard_map/ppermute | solution.py:11
  12.8 0.8 constant_dynamic-update-slice_fusion.5
  13.6 0.8 constant_dynamic-update-slice_fusion.4
  14.5 0.8 constant_dynamic-update-slice_fusion.3
  15.3 4.4 %collective-permute-done = f32[104,512]{1,0:T(8,128)S(1)} collective-permute-done((f32[104,512]{1,0:T(8,128)S(1)}, f32[104,512]{1,0:T(8,128)S(1)}, u32[]{:S(2)}, u32[]{:S(2)}) %collective-permute-start) | collective-permute-done | bytes 213024 | tf_op jit(solution)/shard_map/ppermute | solution.py:11
  19.7 0.9 constant_dynamic-update-slice_fusion
  20.7 0.9 copy-done.13
  21.6 71.8 %all-gather.7.cloned.1.call-done = f32[4864,512]{1,0:T(8,128)} async-done(((f32[304,512]{1,0:T(8,128)}), f32[4864,512]{1,0:T(8,128)}) %all-gather.7.cloned.1.call-update) | async-done | bytes 9961488 | tf_op jit(solution)/shard_map/all_gather | solution.py:36
  93.4 6.0 %fusion.26 = (f32[16,32,512]{2,1,0:T(8,128)}, f32[16,32,512]{2,1,0:T(8,128)S(1)}, f32[16,32,512]{2,1,0:T(8,128)S(1)}, f32[16,32,512]{2,1,0:T(8,128)S(1)}, f32[16...) fusion(f32[16,304,512]{2,1,0:T(8,128)} %bitcast.154), kind=kLoop, calls=%fused_computation.67 | loop fusion | bytes 16777216 | tf_op jit(solution)/shard_map/slice | solution.py:41
  99.4 1.0 fusion.31
  100.5 1.0 fusion.29
  101.5 1.0 fusion.32
  102.6 1.1 convolution_select_fusion.1
  103.7 1.2 fusion
  106.0 4.0 %collective-permute-start.1 = (f32[96,512]{1,0:T(8,128)S(1)}, f32[96,512]{1,0:T(8,128)S(1)}, u32[]{:S(2)}, u32[]{:S(2)}) collective-permute-start(f32[96,512]{1,0:T(8,128)S(1)} %pad_maximum_fusion.1), channel_id=1, source_target_pairs={{0,32},{16,48},{32,64},{48,80},{64,96},{80,112},{96,128},{112,144}... | collective-permute-start | bytes 589832 | tf_op jit(solution)/shard_map/ppermute | solution.py:11
  110.0 9.3 %collective-permute-done.1 = f32[96,512]{1,0:T(8,128)S(1)} collective-permute-done((f32[96,512]{1,0:T(8,128)S(1)}, f32[96,512]{1,0:T(8,128)S(1)}, u32[]{:S(2)}, u32[]{:S(2)}) %collective-permute-start.1) | collective-permute-done | bytes 196640 | tf_op jit(solution)/shard_map/ppermute | solution.py:11
  119.3 0.7 copy-done.16
  120.3 3.2 %fusion.30 = f32[512,512]{1,0:T(8,128)} fusion(f32[512,512]{1,0:T(8,128)S(1)} %convolution_select_fusion.1, f32[512,512]{1,0:T(8,128)} %bitcast.144), kind=kOutput, calls=%fused_computation.71 | convolution fusion | flops 805306368 | bytes 3145728 | tf_op jit(solution)/shard_map/dot_general | solution.py:15
  123.5 41.1 %all-gather.9.cloned.1.call-done = f32[1536,512]{1,0:T(8,128)} async-done(((f32[96,512]{1,0:T(8,128)}), f32[1536,512]{1,0:T(8,128)}) %all-gather.9.cloned.1.call-update) | async-done | bytes 3145744 | tf_op jit(solution)/shard_map/all_gather | solution.py:57
  164.5 2.3 fusion.28
  166.8 1.0 fusion.34
  167.9 1.0 fusion.35
  168.9 1.0 convolution_select_fusion
  171.1 1.1 fusion.7
  172.2 1.0 copy-done.2
  173.2 7.2 %collective-permute-start.2 = (f32[96,512]{1,0:T(8,128)S(1)}, f32[96,512]{1,0:T(8,128)S(1)}, u32[]{:S(2)}, u32[]{:S(2)}) collective-permute-start(f32[96,512]{1,0:T(8,128)S(1)} %pad_maximum_fusion.2), channel_id=1, source_target_pairs={{0,64},{16,80},{32,96},{48,112},{64,128},{80,144},{96,160},{112,17... | collective-permute-start | bytes 589832 | tf_op jit(solution)/shard_map/ppermute | solution.py:11
  180.4 7.7 %collective-permute-done.2 = f32[96,512]{1,0:T(8,128)S(1)} collective-permute-done((f32[96,512]{1,0:T(8,128)S(1)}, f32[96,512]{1,0:T(8,128)S(1)}, u32[]{:S(2)}, u32[]{:S(2)}) %collective-permute-start.2) | collective-permute-done | bytes 196640 | tf_op jit(solution)/shard_map/ppermute | solution.py:11
  188.8 1.0 slice_reduce_fusion
  190.9 1.8 fusion.37
  192.6 1.7 fusion.40
  194.9 7.0 %collective-permute-start.3 = (f32[2,512]{1,0:T(2,128)S(1)}, f32[2,512]{1,0:T(2,128)S(1)}, u32[]{:S(2)}, u32[]{:S(2)}) collective-permute-start(f32[2,512]{1,0:T(2,128)S(1)} %pad_maximum_fusion.3), channel_id=1, source_target_pairs={{0,32},{16,48},{32,64},{48,80},{64,96},{80,112},{96,128},{112,144}... | collective-permute-start | bytes 12296 | tf_op jit(solution)/shard_map/ppermute | solution.py:11
  201.8 0.7 collective-permute-done.3
  203.1 1.8 fusion.6
  204.9 1.8 fusion.41
  206.7 1.6 broadcast_select_fusion
  208.3 5.8 %collective-permute-start.4 = (f32[2,512]{1,0:T(2,128)S(1)}, f32[2,512]{1,0:T(2,128)S(1)}, u32[]{:S(2)}, u32[]{:S(2)}) collective-permute-start(f32[2,512]{1,0:T(2,128)S(1)} %pad_maximum_fusion.4), channel_id=1, source_target_pairs={{0,64},{16,80},{32,96},{48,112},{64,128},{80,144},{96,160},{112,17... | collective-permute-start | bytes 12296 | tf_op jit(solution)/shard_map/ppermute | solution.py:11
  214.1 2.3 fusion.33
  216.3 1.1 collective-permute-done.4
  218.0 15.0 %all-gather.11.cloned.1.call-done = f32[1536,512]{1,0:T(8,128)} async-done(((f32[96,512]{1,0:T(8,128)}), f32[1536,512]{1,0:T(8,128)}) %all-gather.11.cloned.1.call-update) | async-done | bytes 3145744 | tf_op jit(solution)/shard_map/all_gather | solution.py:57
  233.0 2.3 fusion.27
  235.3 1.0 fusion.43
  236.3 1.0 fusion.45
  237.4 1.0 fusion.36
  239.9 1.2 fusion.1
  242.1 1.1 fusion.46
  243.7 0.7 fusion.8
  (75 shorter events, 9.5 us)
Async XLA Ops:
  7.2 86.3 %all-gather.7.cloned.1.call-start = ((), (), s32[]{:S(2)}) async-start(), calls=%async_computation | async-start | bytes 10584064 | tf_op jit(solution)/shard_map/all_gather | solution.py:36
  9.6 10.1 %collective-permute-start = (f32[104,512]{1,0:T(8,128)S(1)}, f32[104,512]{1,0:T(8,128)S(1)}, u32[]{:S(2)}, u32[]{:S(2)}) collective-permute-start(f32[104,512]{1,0:T(8,128)S(1)} %pad_maximum_fusion), channel_id=1, source_target_pairs={{0,16},{16,32},{32,48},{48,64},{64,80},{80,96},{96,112},{112,128},... | collective-permute-start | bytes 638984 | tf_op jit(solution)/shard_map/ppermute | solution.py:11
  20.7 0.9 copy-start.13
  21.6 143.0 %all-gather.9.cloned.1.call-start = ((), (), s32[]{:S(2)}) async-start(), calls=%async_computation.1 | async-start | bytes 3342336 | tf_op jit(solution)/shard_map/all_gather | solution.py:57
  99.4 5.5 %copy-start.9 = (f32[16,32,512]{2,1,0:T(8,128)}, f32[16,32,512]{2,1,0:T(8,128)S(1)}, u32[]{:S(2)}) copy-start(f32[16,32,512]{2,1,0:T(8,128)S(1)} %get-tuple-element.38) | copy-start | bytes 3145732
  100.5 3.2 %copy-start.10 = (f32[512,512]{1,0:T(8,128)}, f32[512,512]{1,0:T(8,128)S(1)}, u32[]{:S(2)}) copy-start(f32[512,512]{1,0:T(8,128)S(1)} %fusion.31) | copy-start | bytes 3145732
  101.5 3.4 %copy-start.4 = (f32[512,512]{1,0:T(8,128)}, f32[512,512]{1,0:T(8,128)S(1)}, u32[]{:S(2)}) copy-start(f32[512,512]{1,0:T(8,128)S(1)} %fusion.29) | copy-start | bytes 3145732
  103.7 1.7 copy-start.14
  106.0 13.3 %collective-permute-start.1 = (f32[96,512]{1,0:T(8,128)S(1)}, f32[96,512]{1,0:T(8,128)S(1)}, u32[]{:S(2)}, u32[]{:S(2)}) collective-permute-start(f32[96,512]{1,0:T(8,128)S(1)} %pad_maximum_fusion.1), channel_id=1, source_target_pairs={{0,32},{16,48},{32,64},{48,80},{64,96},{80,112},{96,128},{112,144}... | collective-permute-start | bytes 589832 | tf_op jit(solution)/shard_map/ppermute | solution.py:11
  119.3 0.7 copy-start.16
  120.0 113.0 %all-gather.11.cloned.1.call-start = ((), (), s32[]{:S(2)}) async-start(), calls=%async_computation.2 | async-start | bytes 3342336 | tf_op jit(solution)/shard_map/all_gather | solution.py:57
  164.5 2.3 copy-start.8
  166.8 3.2 %copy-start.12 = (f32[16,32,512]{2,1,0:T(8,128)}, f32[16,32,512]{2,1,0:T(8,128)S(1)}, u32[]{:S(2)}) copy-start(f32[16,32,512]{2,1,0:T(8,128)S(1)} %get-tuple-element.46) | copy-start | bytes 3145732
  166.8 2.1 copy-start.6
  167.9 3.2 %copy-start.11 = (f32[512,512]{1,0:T(8,128)}, f32[512,512]{1,0:T(8,128)S(1)}, u32[]{:S(2)}) copy-start(f32[512,512]{1,0:T(8,128)S(1)} %fusion.34) | copy-start | bytes 3145732
  170.0 1.0 copy-start
  172.2 1.0 copy-start.2
  173.2 21.1 %copy-start.5 = (f32[512,512]{1,0:T(8,128)S(1)}, f32[512,512]{1,0:T(8,128)}, u32[]{:S(2)}) copy-start(f32[512,512]{1,0:T(8,128)} %copy-done.4) | copy-start | bytes 3145732
  173.2 14.9 %collective-permute-start.2 = (f32[96,512]{1,0:T(8,128)S(1)}, f32[96,512]{1,0:T(8,128)S(1)}, u32[]{:S(2)}, u32[]{:S(2)}) collective-permute-start(f32[96,512]{1,0:T(8,128)S(1)} %pad_maximum_fusion.2), channel_id=1, source_target_pairs={{0,64},{16,80},{32,96},{48,112},{64,128},{80,144},{96,160},{112,17... | collective-permute-start | bytes 589832 | tf_op jit(solution)/shard_map/ppermute | solution.py:11
  188.1 0.7 copy-start.15
  192.6 21.5 %copy-start.1 = (f32[512,512]{1,0:T(8,128)S(1)}, f32[512,512]{1,0:T(8,128)}, u32[]{:S(2)}) copy-start(f32[512,512]{1,0:T(8,128)} %copy-done) | copy-start | bytes 3145732
  194.9 7.7 %collective-permute-start.3 = (f32[2,512]{1,0:T(2,128)S(1)}, f32[2,512]{1,0:T(2,128)S(1)}, u32[]{:S(2)}, u32[]{:S(2)}) collective-permute-start(f32[2,512]{1,0:T(2,128)S(1)} %pad_maximum_fusion.3), channel_id=1, source_target_pairs={{0,32},{16,48},{32,64},{48,80},{64,96},{80,112},{96,128},{112,144}... | collective-permute-start | bytes 12296 | tf_op jit(solution)/shard_map/ppermute | solution.py:11
  203.1 14.4 %copy-start.3 = (f32[512,512]{1,0:T(8,128)S(1)}, f32[512,512]{1,0:T(8,128)}, u32[]{:S(2)}) copy-start(f32[512,512]{1,0:T(8,128)} %copy-done.2) | copy-start | bytes 3145732
  208.3 9.2 %collective-permute-start.4 = (f32[2,512]{1,0:T(2,128)S(1)}, f32[2,512]{1,0:T(2,128)S(1)}, u32[]{:S(2)}, u32[]{:S(2)}) collective-permute-start(f32[2,512]{1,0:T(2,128)S(1)} %pad_maximum_fusion.4), channel_id=1, source_target_pairs={{0,64},{16,80},{32,96},{48,112},{64,128},{80,144},{96,160},{112,17... | collective-permute-start | bytes 12296 | tf_op jit(solution)/shard_map/ppermute | solution.py:11
  233.0 2.3 copy-start.7
Sparse Core Ops, SparseCore 0:
  21.7 71.7 all-gather.6
  120.1 44.3 all-gather.8
  189.0 44.0 all-gather.10

commit v2 on v1

v2 whole, which is shorter than its diff:
```python
import functools

import jax
import jax.numpy as jnp
from jax import lax
from jax.experimental import pallas as pl
from jax.experimental.pallas import tpu as pltpu
from jax.sharding import PartitionSpec as P

HIGH = lax.Precision.HIGH


def passed_along(shard, by):
    peers = lax.axis_size("tm")
    return lax.ppermute(shard, "tm", [(i, i + by) for i in range(peers - by)])


def dot(left, right):
    return jnp.dot(left, right, precision=HIGH, preferred_element_type=jnp.float32)


def dot_nt(left, right):
    return lax.dot_general(left, right, (((1,), (1,)), ((), ())), precision=HIGH, preferred_element_type=jnp.float32)


def rowwise(matrix, vector):
    return jnp.sum(matrix * vector[None, :], axis=1)


def gathered(shard):
    return lax.all_gather(shard, "panel", axis=0, tiled=False)


def whole_vectors(slices):
    count, rows = slices.shape
    padded = jnp.pad(slices, ((0, 8 - count), (0, 128 - rows)))
    whole = gathered(padded)[:, :count, :rows]
    return whole.transpose(1, 0, 2).reshape(count, -1)


def pack_kernel(count, rows, peers, slices_ref, packed_ref):
    for peer in range(peers):
        for i in range(count):
            block = slices_ref[i * rows : (i + 1) * rows, peer * rows : (peer + 1) * rows]
            packed_ref[peer, :, i * rows : (i + 1) * rows] = block


def pack_vectors_kernel(count, rows, peers, slices_ref, extra_ref, packed_ref):
    pack_kernel(count, rows, peers, slices_ref, packed_ref)
    for peer in range(peers):
        packed_ref[peer, :, count * rows :] = extra_ref[...]


def turn_kernel(received_ref, columns_ref):
    columns_ref[...] = received_ref[...].T


IN_VMEM = pl.BlockSpec(memory_space=pltpu.VMEM)


def turned(slices, extra):
    peers = lax.axis_size("panel")
    rows, width = slices[0].shape
    count = len(slices)
    lanes = count * rows + (0 if extra is None else extra.shape[1])
    operands = (jnp.concatenate(slices),) + (() if extra is None else (extra,))
    body = pack_kernel if extra is None else pack_vectors_kernel
    packed = pl.pallas_call(
        functools.partial(body, count, rows, peers),
        out_shape=jax.ShapeDtypeStruct((peers, rows, lanes), jnp.float32),
        in_specs=[IN_VMEM] * len(operands),
        out_specs=IN_VMEM,
    )(*operands)
    there = lax.all_to_all(packed, "panel", split_axis=0, concat_axis=0, tiled=True)
    return pl.pallas_call(
        turn_kernel,
        out_shape=jax.ShapeDtypeStruct((lanes, width), jnp.float32),
        in_specs=[IN_VMEM],
        out_specs=IN_VMEM,
    )(there.reshape(width, lanes))


def local(transition, offset, covariance, info_vector, information, inverses):
    rows, width = transition.shape
    time = lax.axis_index("tm")
    mine = lax.axis_index("panel")
    row = lax.broadcasted_iota(jnp.int32, (rows, width), 0) + mine * rows
    eye = (row == lax.broadcasted_iota(jnp.int32, (rows, width), 1)).astype(jnp.float32)

    def present(shard, since):
        return jnp.where(time >= since, shard, eye)

    a0, c0, j0 = transition, covariance, information
    m0, m1, m2 = present(inverses[0], 1), present(inverses[1], 2), present(inverses[2], 4)
    v0 = jnp.stack([offset, info_vector])

    def sent(parts, by):
        vectors = jnp.pad(v0, ((0, 6), (0, width - rows)))
        got = passed_along(jnp.concatenate([*parts, vectors]), by)
        count = len(parts)
        return [got[i * rows : (i + 1) * rows] for i in range(count)] + [got[count * rows : count * rows + 2, :rows]]

    a1, v1 = sent([a0], 1)
    a2, m0p, v2 = sent([a0, m0], 2)
    a3, v3 = sent([a0], 3)
    a1, a2, m0p, a3 = present(a1, 1), present(a2, 2), present(m0p, 2), present(a3, 3)
    whole = gathered(jnp.concatenate([a0, a1, a2, a3, m0, m0p, m1]))

    pair = jnp.concatenate([c0, j0])
    pair, _ = lax.optimization_barrier((pair, a3))
    (c1, j1), (c2, j2), (c3, j3) = (jnp.split(passed_along(pair, by), 2) for by in (1, 2, 3))
    b0, e0, b1, e1, b2, e2, b3, e3 = whole_vectors(jnp.concatenate([v0, v1, v2, v3]))
    u1, u2, u3, u4 = whole_vectors(jnp.stack([rowwise(c1, e0), rowwise(j0, b1), rowwise(c3, e2), rowwise(j2, b3)]))

    a0w, a1w, a2w, a3w, m0w, m0pw, m1w = (
        whole[:, i * rows : (i + 1) * rows].reshape(width, width) for i in range(7)
    )
    drows = dot(dot(dot(dot(dot(dot(a0, m0w), a1w), m1w), a2w), m0pw), a3w)
    earlier = present(passed_along(drows, 4), 4)
    second = gathered(jnp.concatenate([earlier, m2]))

    p0 = dot(a0w, m0w)
    bw = dot(p0, a1w)
    p0p = dot(a2w, m0pw)
    bp = dot(p0p, a3w)

    e_t = dot(dot((e0 - u2)[None], m0w), a1w)[0] + e1
    e_p = dot(dot((e2 - u4)[None], m0pw), a3w)[0] + e3
    b_t = dot_nt((b1 + u1)[None], p0)[0] + b0
    b_p = dot_nt((b3 + u3)[None], p0p)[0] + b2
    w1 = rowwise(c3, dot(e_t[None], a2w)[0])
    w2 = rowwise(c2, e_t)
    w3 = rowwise(j0, dot_nt(b_p[None], a1w)[0])
    w4 = rowwise(j1, b_p)

    right = dot_nt(jnp.concatenate([dot_nt(c3, a2w), c2]), bw)
    x3, x2 = right[:rows], right[rows:]
    x1 = dot_nt(c1, a0w)
    right = dot(jnp.concatenate([dot(j0, a1w), j1]), bp)
    y0, y1 = right[:rows], right[rows:]
    y2 = dot(j2, a3w)
    columns = turned([x1, x2, x3, y0, y1, y2], jnp.pad(jnp.stack([w1, w2, w3, w4], axis=1), ((0, 0), (0, 2 * rows - 4))))
    x1, x2, x3, y0, y1, y2 = (columns[i * rows : (i + 1) * rows] for i in range(6))
    w1, w2, w3, w4 = columns[6 * rows : 6 * rows + 4]

    p1 = dot(bw, m1w)
    dw = dot(p1, bp)
    inner = dot_nt(jnp.concatenate([x3, w1[None]]), p0p) + jnp.concatenate([x2, (b_p + w2)[None]])
    outer = dot_nt(inner, p1) + jnp.concatenate([dot_nt(x1, p0) + c0, b_t[None]])
    inner = dot(dot(jnp.concatenate([y0, -w3[None]]), m0w), a1w) + jnp.concatenate([y1, (e_t - w4)[None]])
    outer_j = dot(dot(inner, m1w), bp) + jnp.concatenate([dot(dot(y2, m0pw), a3w) + j3, e_p[None]])
    own_c, own_b = outer[:rows], outer[rows]
    own_j, own_e = outer_j[:rows], outer_j[rows]

    state = jnp.concatenate([own_c, own_j, own_b[None], own_e[None], jnp.zeros((6, width), jnp.float32)])
    prior = passed_along(state, 4)
    prior_c, prior_j, prior_b, prior_e = prior[:rows], prior[rows : 2 * rows], prior[2 * rows], prior[2 * rows + 1]

    ew, m2w = second[:, :rows].reshape(width, width), second[:, rows:].reshape(width, width)
    left = dot_nt(dot_nt(prior_c, m2w), dw)
    left_j = dot(dot(jnp.concatenate([own_j, own_e[None]]), m2w), ew)
    back = turned([left, own_c, left_j[:rows], prior_j], None)
    v, c_rows, z, j_rows = (back[i * rows : (i + 1) * rows] for i in range(4))

    def own_part(vector):
        return lax.dynamic_slice_in_dim(vector, mine * rows, rows, 0)

    new_a = dot(dot(drows, m2w), ew)
    new_c = dot_nt(v, dw) + c_rows
    new_j = dot(z, ew) + j_rows
    new_b = rowwise(drows, dot_nt(prior_b[None], m2w)[0]) + rowwise(v, own_e) + own_part(own_b)
    new_e = own_part(left_j[rows] + prior_e) - rowwise(z, prior_b)
    return new_a, new_b, new_c, new_e, new_j


def solution(mesh):
    matrix = P(("tm", "panel"), None)
    vector = P(("tm", "panel"))
    return jax.shard_map(
        local,
        mesh=mesh,
        in_specs=(matrix, vector, matrix, vector, matrix, P(None, ("tm", "panel"), None)),
        out_specs=(matrix, vector, matrix, vector, matrix),
        check_vma=False,
    )
```

time: 253 us -> 220 us (0.87)
  waiting for transfers between devices: 151 us -> 38.8 us
  blocking collectives: 0 us -> 40.7 us
  other arithmetic: 2.29 us -> 18.1 us
  starting transfers between devices: 27.5 us -> 41.3 us
  Pallas kernels: 0 us -> 7.95 us
  matrix products: 35 us -> 40.9 us
  local copies, waits for them, and re-layouts: 20.8 us -> 15.3 us
    all_gather x3 -> x2, waiting for transfers between devices: 128 us -> 2.28 us  [gathered(): return lax.all_gather(shard, 'panel', axis=0, tiled=False)]
    all_gather x0 -> x2, blocking collectives: none -> 40.7 us  [gathered(): return lax.all_gather(shard, 'panel', axis=0, tiled=False)]
    all_to_all x0 -> x2, waiting for transfers between devices: none -> 18.2 us  [turned(): lax.all_to_all(packed, 'panel', split_axis=0, concat_axis=0, tiled=True)]
    all_to_all x0 -> x2, starting transfers between devices: none -> 8.46 us  [turned(): lax.all_to_all(packed, 'panel', split_axis=0, concat_axis=0, tiled=True)]
    pallas_call x0 -> x4, Pallas kernels: none -> 7.95 us  [the longest x2 4.14 us: turned(): pl.pallas_call(functools.partial(body, count, rows, peers), out_shape=jax...]
    dot_general x33 -> x44, matrix products: 35 us -> 40.9 us  [the longest x31 26.4 us: dot(): jnp.dot(left, right, precision=HIGH, preferred_element_type=jnp.float32)]
    ppermute x5 -> x8, starting transfers between devices: 27.2 us -> 32.8 us  [passed_along(): return lax.ppermute(shard, 'tm', [(i, i + by) for i in range(peers - by)])]
    ppermute x5 -> x8, waiting for transfers between devices: 23.2 us -> 18.4 us  [passed_along(): return lax.ppermute(shard, 'tm', [(i, i + by) for i in range(peers - by)])]
  transfers between devices with their start and end apart: 8 -> 12, of which waited for: 8 -> 7; matrix products, arithmetic and copies ran while one was open for 8% -> 18% of each run, Pallas kernels for 0% -> 2%
where the time goes in v2:
time: 220 us; the launch traced here: 218 us
  starting transfers between devices  41.3 us (19%)
  matrix products  40.9 us (19%)
  blocking collectives  40.7 us (19%)
  waiting for transfers between devices  38.8 us (18%)
  other arithmetic  18.1 us (8%)
  local copies, waits for them, and re-layouts  15.3 us (7%)
  between operations  14.7 us (7%)
  Pallas kernels  7.95 us (4%)
    all_gather x2, blocking collectives, gathered(): return lax.all_gather(shard, 'panel', axis=0, tiled=False)  40.7 us
    ppermute x8, starting transfers between devices, passed_along(): return lax.ppermute(shard, 'tm', [(i, i + by) for i in range(peers - by)])  32.8 us
    dot_general x31, matrix products, dot(): jnp.dot(left, right, precision=HIGH, preferred_element_type=jnp.float32)  26.4 us
    ppermute x8, waiting for transfers between devices, passed_along(): return lax.ppermute(shard, 'tm', [(i, i + by) for i in range(peers - by)])  18.4 us
    all_to_all x2, waiting for transfers between devices, turned(): lax.all_to_all(packed, 'panel', split_axis=0, concat_axis=0, tiled=True)  18.2 us
    dot_general x13, matrix products, dot_nt(): lax.dot_general(left, right, (((1,), (1,)), ((), ())), precision=HIGH, pr...  14.5 us
    all_to_all x2, starting transfers between devices, turned(): lax.all_to_all(packed, 'panel', split_axis=0, concat_axis=0, tiled=True)  8.46 us
    slice x1, local copies, waits for them, and re-layouts, local(): whole[:, i * rows:(i + 1) * rows].reshape(width, width)  4.57 us
  transfers between devices with their start and end apart: 12, of which 7 were waited for; matrix products, arithmetic and copies ran while one was open for 18% of the time, Pallas kernels for 2%

profile of v2, /device:TPU:7, one launch (start us, length us, event | category | flops | bytes accessed | tf_op | source)
XLA Modules:
  0.0 217.9 jit_solution(2740046266010471398)
XLA Ops:
  8.7 3.2 %collective-permute-start = (f32[40,512]{1,0:T(8,128)S(1)}, f32[40,512]{1,0:T(8,128)S(1)}, u32[]{:S(2)}, u32[]{:S(2)}) collective-permute-start(f32[40,512]{1,0:T(8,128)S(1)} %pad_maximum_fusion.4), channel_id=1, source_target_pairs={{0,16},{16,32},{32,48},{48,64},{64,80},{80,96},{96,112},{112,128},... | collective-permute-start | bytes 245768 | tf_op jit(solution)/shard_map/ppermute | solution.py:15
  12.8 3.2 %collective-permute-done = f32[40,512]{1,0:T(8,128)S(1)} collective-permute-done((f32[40,512]{1,0:T(8,128)S(1)}, f32[40,512]{1,0:T(8,128)S(1)}, u32[]{:S(2)}, u32[]{:S(2)}) %collective-permute-start) | collective-permute-done | bytes 81952 | tf_op jit(solution)/shard_map/ppermute | solution.py:15
  16.0 1.6 convert_select_fusion
  18.5 2.1 collective-permute-start.1
  20.6 5.5 %collective-permute-start.2 = (f32[40,512]{1,0:T(8,128)S(1)}, f32[40,512]{1,0:T(8,128)S(1)}, u32[]{:S(2)}, u32[]{:S(2)}) collective-permute-start(f32[40,512]{1,0:T(8,128)S(1)} %pad_maximum_fusion.4), channel_id=1, source_target_pairs={{0,48},{16,64},{32,80},{48,96},{64,112},{80,128},{96,144},{112,160... | collective-permute-start | bytes 245768 | tf_op jit(solution)/shard_map/ppermute | solution.py:15
  26.1 3.7 %collective-permute-done.1 = f32[72,512]{1,0:T(8,128)S(1)} collective-permute-done((f32[72,512]{1,0:T(8,128)S(1)}, f32[72,512]{1,0:T(8,128)S(1)}, u32[]{:S(2)}, u32[]{:S(2)}) %collective-permute-start.1) | collective-permute-done | bytes 147488 | tf_op jit(solution)/shard_map/ppermute | solution.py:15
  30.0 3.2 %collective-permute-done.2 = f32[40,512]{1,0:T(8,128)S(1)} collective-permute-done((f32[40,512]{1,0:T(8,128)S(1)}, f32[40,512]{1,0:T(8,128)S(1)}, u32[]{:S(2)}, u32[]{:S(2)}) %collective-permute-start.2) | collective-permute-done | bytes 81952 | tf_op jit(solution)/shard_map/ppermute | solution.py:15
  35.9 7.6 %collective-permute-start.6 = (f32[64,512]{1,0:T(8,128)S(1)}, f32[64,512]{1,0:T(8,128)S(1)}, u32[]{:S(2)}, u32[]{:S(2)}) collective-permute-start(f32[64,512]{1,0:T(8,128)S(1)} %pad_maximum_fusion.3), channel_id=1, source_target_pairs={{0,32},{16,48},{32,64},{48,80},{64,96},{80,112},{96,128},{112,144}... | collective-permute-start | bytes 393224 | tf_op jit(solution)/shard_map/ppermute | solution.py:15
  43.5 3.2 %collective-permute-start.5 = (f32[64,512]{1,0:T(8,128)S(1)}, f32[64,512]{1,0:T(8,128)S(1)}, u32[]{:S(2)}, u32[]{:S(2)}) collective-permute-start(f32[64,512]{1,0:T(8,128)S(1)} %pad_maximum_fusion.3), channel_id=1, source_target_pairs={{0,48},{16,64},{32,80},{48,96},{64,112},{80,128},{96,144},{112,160... | collective-permute-start | bytes 393224 | tf_op jit(solution)/shard_map/ppermute | solution.py:15
  46.7 1.9 collective-permute-start.4
  49.3 26.0 %all-gather.2 = f32[128,128]{1,0:T(8,128)S(1)} all-gather(f32[8,128]{1,0:T(8,128)S(1)} %pad.19), channel_id=4, replica_groups=mesh['tm'=32,'panel'=16] {'panel'}, dimensions={0}, use_global_device_ids=true | all-gather | bytes 69632 | tf_op jit(solution)/shard_map/all_gather | solution.py:31
  77.1 14.8 %all-gather.3 = f32[128,128]{1,0:T(8,128)S(1)} all-gather(f32[8,128]{1,0:T(8,128)S(1)} %select_maximum_fusion.1), channel_id=5, replica_groups=mesh['tm'=32,'panel'=16] {'panel'}, dimensions={0}, use_global_device_ids=true | all-gather | bytes 69632 | tf_op jit(solution)/shard_map/all_gather | solution.py:31
  94.4 2.3 %all-gather.7.cloned.1.call-done = f32[3584,512]{1,0:T(8,128)} async-done(((f32[224,512]{1,0:T(8,128)}), f32[3584,512]{1,0:T(8,128)}) %all-gather.7.cloned.1.call-update) | async-done | bytes 7340048 | tf_op jit(solution)/shard_map/all_gather | solution.py:31
  96.7 4.6 %fusion.43 = (f32[16,32,512]{2,1,0:T(8,128)S(1)}, f32[16,32,512]{2,1,0:T(8,128)S(1)}, f32[16,32,512]{2,1,0:T(8,128)S(1)}, f32[16,32,512]{2,1,0:T(8,128)S(1)}, f3...) fusion(f32[16,224,512]{2,1,0:T(8,128)} %bitcast.181), kind=kLoop, calls=%fused_computation.117 | loop fusion | bytes 14680064 | tf_op jit(solution)/shard_map/slice | solution.py:116
  101.7 1.0 fusion.47
  103.8 1.0 fusion.57
  107.3 1.0 fusion.58
  109.4 7.1 %collective-permute-start.3 = (f32[32,512]{1,0:T(8,128)S(1)}, f32[32,512]{1,0:T(8,128)}, u32[]{:S(2)}, u32[]{:S(2)}) collective-permute-start(f32[32,512]{1,0:T(8,128)S(1)} %fusion.52), channel_id=1, source_target_pairs={{0,64},{16,80},{32,96},{48,112},{64,128},{80,144},{96,160},{112,17... | collective-permute-start | bytes 196616 | tf_op jit(solution)/shard_map/ppermute | solution.py:15
  116.5 1.0 fusion.55
  117.6 1.0 fusion.56
  121.2 1.2 convolution_dynamic-update-slice_fusion.1.slices_ref
  124.0 2.2 %shard_map.101 = f32[16,32,256]{2,1,0:T(8,128)} custom-call(f32[192,512]{1,0:T(8,128)} %copy-done.14, f32[32,64]{1,0:T(8,128)} %pad.21.extra_ref), custom_call_target="tpu_custom_call" | custom-call | tf_op jit(solution)/shard_map/pallas_call | solution.py:68
  126.2 4.5 %all-to-all-start = ((f32[16,32,256]{2,1,0:T(8,128)}), f32[16,32,256]{2,1,0:T(8,128)}, u32[]{:S(2)}, u32[]{:S(2)}) async-start(f32[16,32,256]{2,1,0:T(8,128)} %shard_map.101), calls=%async_computation | async-start | bytes 1048576 | tf_op jit(solution)/shard_map/all_to_all | solution.py:74
  131.7 1.5 pad_maximum_fusion.2
  134.2 1.7 fusion.64
  136.7 3.6 %fusion.63 = f32[512,512]{1,0:T(8,128)} fusion(f32[512,512]{1,0:T(8,128)} %copy-done.8, f32[512,512]{1,0:T(8,128)} %bitcast.174), kind=kOutput, calls=%fused_computation.137 | convolution fusion | flops 805306368 | bytes 3145728 | tf_op jit(solution)/shard_map/dot_general | solution.py:19
  140.3 7.9 %all-to-all-done = f32[16,32,256]{2,1,0:T(8,128)} async-done(((f32[16,32,256]{2,1,0:T(8,128)}), f32[16,32,256]{2,1,0:T(8,128)}, u32[]{:S(2)}, u32[]{:S(2)}) %all-to-all-start) | async-done | bytes 524320 | tf_op jit(solution)/shard_map/all_to_all | solution.py:74
  148.1 2.0 shard_map.102
  152.1 1.8 convolution_add_fusion.2
  153.9 1.8 convolution_add_fusion.5
  155.8 1.8 convolution_add_fusion.1
  158.0 1.8 fusion.20
  160.6 1.2 slice_add_fusion
  162.4 2.1 collective-permute-start.7
  164.6 3.2 %fusion.67 = f32[512,512]{1,0:T(8,128)} fusion(f32[512,512]{1,0:T(8,128)} %fusion.63, f32[512,512]{1,0:T(8,128)S(1)} %copy-done.5), kind=kOutput, calls=%fused_computation.141 | convolution fusion | flops 805306368 | bytes 3145728 | tf_op jit(solution)/shard_map/dot_general | solution.py:19
  167.8 8.2 %collective-permute-done.7 = f32[72,512]{1,0:T(8,128)S(1)} collective-permute-done((f32[72,512]{1,0:T(8,128)S(1)}, f32[72,512]{1,0:T(8,128)S(1)}, u32[]{:S(2)}, u32[]{:S(2)}) %collective-permute-start.7) | collective-permute-done | bytes 147488 | tf_op jit(solution)/shard_map/ppermute | solution.py:15
  177.2 1.8 fusion.44
  179.9 1.2 fusion.31
  183.6 1.9 shard_map.103
  185.5 4.0 %all-to-all-start.1 = ((f32[16,32,128]{2,1,0:T(8,128)}), f32[16,32,128]{2,1,0:T(8,128)S(1)}, u32[]{:S(2)}, u32[]{:S(2)}) async-start(f32[16,32,128]{2,1,0:T(8,128)} %shard_map.103), calls=%async_computation.1 | async-start | bytes 524288 | tf_op jit(solution)/shard_map/all_to_all | solution.py:74
  189.9 1.0 fusion.54
  190.9 10.3 %all-to-all-done.1 = f32[16,32,128]{2,1,0:T(8,128)S(1)} async-done(((f32[16,32,128]{2,1,0:T(8,128)}), f32[16,32,128]{2,1,0:T(8,128)S(1)}, u32[]{:S(2)}, u32[]{:S(2)}) %all-to-all-start.1) | async-done | bytes 262176 | tf_op jit(solution)/shard_map/all_to_all | solution.py:74
  201.9 1.8 shard_map.104
  203.7 2.1 convolution_add_fusion.4
  205.8 1.9 convolution_add_fusion.3
  207.7 1.0 multiply_reduce_fusion
  208.6 1.2 fusion.34
  209.9 1.2 fusion.37
  (146 shorter events, 32.0 us)
Async XLA Ops:
  7.2 89.5 %all-gather.7.cloned.1.call-start = ((), (), s32[]{:S(2)}) async-start(), calls=%async_computation.2 | async-start | bytes 7798784 | tf_op jit(solution)/shard_map/all_gather | solution.py:31
  8.7 7.3 %collective-permute-start = (f32[40,512]{1,0:T(8,128)S(1)}, f32[40,512]{1,0:T(8,128)S(1)}, u32[]{:S(2)}, u32[]{:S(2)}) collective-permute-start(f32[40,512]{1,0:T(8,128)S(1)} %pad_maximum_fusion.4), channel_id=1, source_target_pairs={{0,16},{16,32},{32,48},{48,64},{64,80},{80,96},{96,112},{112,128},... | collective-permute-start | bytes 245768 | tf_op jit(solution)/shard_map/ppermute | solution.py:15
  18.5 11.4 %collective-permute-start.1 = (f32[72,512]{1,0:T(8,128)S(1)}, f32[72,512]{1,0:T(8,128)S(1)}, u32[]{:S(2)}, u32[]{:S(2)}) collective-permute-start(f32[72,512]{1,0:T(8,128)S(1)} %pad_maximum_fusion.1), channel_id=1, source_target_pairs={{0,32},{16,48},{32,64},{48,80},{64,96},{80,112},{96,128},{112,144}... | collective-permute-start | bytes 442376 | tf_op jit(solution)/shard_map/ppermute | solution.py:15
  20.6 12.6 %collective-permute-start.2 = (f32[40,512]{1,0:T(8,128)S(1)}, f32[40,512]{1,0:T(8,128)S(1)}, u32[]{:S(2)}, u32[]{:S(2)}) collective-permute-start(f32[40,512]{1,0:T(8,128)S(1)} %pad_maximum_fusion.4), channel_id=1, source_target_pairs={{0,48},{16,64},{32,80},{48,96},{64,112},{80,128},{96,144},{112,160... | collective-permute-start | bytes 245768 | tf_op jit(solution)/shard_map/ppermute | solution.py:15
  34.2 0.8 copy-start.13
  35.9 40.8 %collective-permute-start.6 = (f32[64,512]{1,0:T(8,128)S(1)}, f32[64,512]{1,0:T(8,128)S(1)}, u32[]{:S(2)}, u32[]{:S(2)}) collective-permute-start(f32[64,512]{1,0:T(8,128)S(1)} %pad_maximum_fusion.3), channel_id=1, source_target_pairs={{0,32},{16,48},{32,64},{48,80},{64,96},{80,112},{96,128},{112,144}... | collective-permute-start | bytes 393224 | tf_op jit(solution)/shard_map/ppermute | solution.py:15
  43.5 33.3 %collective-permute-start.5 = (f32[64,512]{1,0:T(8,128)S(1)}, f32[64,512]{1,0:T(8,128)S(1)}, u32[]{:S(2)}, u32[]{:S(2)}) collective-permute-start(f32[64,512]{1,0:T(8,128)S(1)} %pad_maximum_fusion.3), channel_id=1, source_target_pairs={{0,48},{16,64},{32,80},{48,96},{64,112},{80,128},{96,144},{112,160... | collective-permute-start | bytes 393224 | tf_op jit(solution)/shard_map/ppermute | solution.py:15
  46.7 30.2 %collective-permute-start.4 = (f32[64,512]{1,0:T(8,128)S(1)}, f32[64,512]{1,0:T(8,128)S(1)}, u32[]{:S(2)}, u32[]{:S(2)}) collective-permute-start(f32[64,512]{1,0:T(8,128)S(1)} %pad_maximum_fusion.3), channel_id=1, source_target_pairs={{0,16},{16,32},{32,48},{48,64},{64,80},{80,96},{96,112},{112,128},... | collective-permute-start | bytes 393224 | tf_op jit(solution)/shard_map/ppermute | solution.py:15
  76.7 42.5 %copy-start.16 = (f32[64,512]{1,0:T(8,128)}, f32[64,512]{1,0:T(8,128)S(1)}, u32[]{:S(2)}) copy-start(f32[64,512]{1,0:T(8,128)S(1)} %collective-permute-done.6) | copy-start | bytes 393220
  76.8 44.3 %copy-start.15 = (f32[64,512]{1,0:T(8,128)}, f32[64,512]{1,0:T(8,128)S(1)}, u32[]{:S(2)}) copy-start(f32[64,512]{1,0:T(8,128)S(1)} %collective-permute-done.5) | copy-start | bytes 393220
  76.9 19.7 %copy-start.17 = (f32[64,512]{1,0:T(8,128)}, f32[64,512]{1,0:T(8,128)S(1)}, u32[]{:S(2)}) copy-start(f32[64,512]{1,0:T(8,128)S(1)} %collective-permute-done.4) | copy-start | bytes 393220
  96.7 4.6 %copy-start.11 = (f32[32,512]{1,0:T(8,128)S(1)}, f32[32,512]{1,0:T(8,128)}, u32[]{:S(2)}) copy-start(f32[32,512]{1,0:T(8,128)} %param.10) | copy-start | bytes 196612
  96.7 5.0 %copy-start.12 = (f32[32,512]{1,0:T(8,128)S(1)}, f32[32,512]{1,0:T(8,128)}, u32[]{:S(2)}) copy-start(f32[32,512]{1,0:T(8,128)} %param.6) | copy-start | bytes 196612
  101.3 5.5 %copy-start = (f32[16,32,512]{2,1,0:T(8,128)}, f32[16,32,512]{2,1,0:T(8,128)S(1)}, u32[]{:S(2)}) copy-start(f32[16,32,512]{2,1,0:T(8,128)S(1)} %get-tuple-element.25) | copy-start | bytes 3145732
  101.3 5.5 %copy-start.1 = (f32[16,32,512]{2,1,0:T(8,128)}, f32[16,32,512]{2,1,0:T(8,128)S(1)}, u32[]{:S(2)}) copy-start(f32[16,32,512]{2,1,0:T(8,128)S(1)} %get-tuple-element.27) | copy-start | bytes 3145732
  104.8 12.8 %copy-start.6 = (f32[512,512]{1,0:T(8,128)}, f32[512,512]{1,0:T(8,128)S(1)}, u32[]{:S(2)}) copy-start(f32[512,512]{1,0:T(8,128)S(1)} %fusion.57) | copy-start | bytes 3145732
  107.3 12.6 %copy-start.18 = (f32[64,512]{1,0:T(8,128)S(1)}, f32[64,512]{1,0:T(8,128)}, u32[]{:S(2)}) copy-start(f32[64,512]{1,0:T(8,128)} %copy-done.17) | copy-start | bytes 393220
  108.3 14.1 %copy-start.3 = (f32[512,512]{1,0:T(8,128)}, f32[512,512]{1,0:T(8,128)S(1)}, u32[]{:S(2)}) copy-start(f32[512,512]{1,0:T(8,128)S(1)} %fusion.58) | copy-start | bytes 3145732
  109.4 21.3 %collective-permute-start.3 = (f32[32,512]{1,0:T(8,128)S(1)}, f32[32,512]{1,0:T(8,128)}, u32[]{:S(2)}, u32[]{:S(2)}) collective-permute-start(f32[32,512]{1,0:T(8,128)S(1)} %fusion.52), channel_id=1, source_target_pairs={{0,64},{16,80},{32,96},{48,112},{64,128},{80,144},{96,160},{112,17... | collective-permute-start | bytes 196616 | tf_op jit(solution)/shard_map/ppermute | solution.py:15
  117.6 4.9 %copy-start.7 = (f32[512,512]{1,0:T(8,128)}, f32[512,512]{1,0:T(8,128)S(1)}, u32[]{:S(2)}) copy-start(f32[512,512]{1,0:T(8,128)S(1)} %fusion.55) | copy-start | bytes 3145732
  118.6 3.9 %copy-start.8 = (f32[512,512]{1,0:T(8,128)}, f32[512,512]{1,0:T(8,128)S(1)}, u32[]{:S(2)}) copy-start(f32[512,512]{1,0:T(8,128)S(1)} %fusion.56) | copy-start | bytes 3145732
  119.9 34.0 %copy-start.19 = (f32[32,512]{1,0:T(8,128)S(1)}, f32[32,512]{1,0:T(8,128)}, u32[]{:S(2)}) copy-start(f32[32,512]{1,0:T(8,128)} %param.8) | copy-start | bytes 196612
  122.5 0.8 copy-start.14
  126.2 22.0 %all-to-all-start = ((f32[16,32,256]{2,1,0:T(8,128)}), f32[16,32,256]{2,1,0:T(8,128)}, u32[]{:S(2)}, u32[]{:S(2)}) async-start(f32[16,32,256]{2,1,0:T(8,128)} %shard_map.101), calls=%async_computation | async-start | bytes 1048576 | tf_op jit(solution)/shard_map/all_to_all | solution.py:74
  130.7 46.5 %all-gather.9.cloned.1.call-start = ((), (), s32[]{:S(2)}) async-start(), calls=%async_computation.3 | async-start | bytes 2228224 | tf_op jit(solution)/shard_map/all_gather | solution.py:31
  150.2 10.0 %copy-start.2 = (f32[16,32,512]{2,1,0:T(8,128)S(1)}, f32[16,32,512]{2,1,0:T(8,128)}, u32[]{:S(2)}) copy-start(f32[16,32,512]{2,1,0:T(8,128)} %copy-done.1) | copy-start | bytes 3145732
  150.2 11.7 %copy-start.4 = (f32[512,512]{1,0:T(8,128)S(1)}, f32[512,512]{1,0:T(8,128)}, u32[]{:S(2)}) copy-start(f32[512,512]{1,0:T(8,128)} %copy-done.3) | copy-start | bytes 3145732
  158.0 6.5 %copy-start.5 = (f32[512,512]{1,0:T(8,128)S(1)}, f32[512,512]{1,0:T(8,128)}, u32[]{:S(2)}) copy-start(f32[512,512]{1,0:T(8,128)} %copy-done.3) | copy-start | bytes 3145732
  162.4 13.6 %collective-permute-start.7 = (f32[72,512]{1,0:T(8,128)S(1)}, f32[72,512]{1,0:T(8,128)S(1)}, u32[]{:S(2)}, u32[]{:S(2)}) collective-permute-start(f32[72,512]{1,0:T(8,128)S(1)} %concatenate.69), channel_id=1, source_target_pairs={{0,64},{16,80},{32,96},{48,112},{64,128},{80,144},{96,160},{112,17... | collective-permute-start | bytes 442376 | tf_op jit(solution)/shard_map/ppermute | solution.py:15
  167.8 14.5 %copy-start.9 = (f32[512,512]{1,0:T(8,128)S(1)}, f32[512,512]{1,0:T(8,128)}, u32[]{:S(2)}) copy-start(f32[512,512]{1,0:T(8,128)} %fusion.67) | copy-start | bytes 3145732
  176.0 0.7 copy-start.20
  177.2 5.7 %slice-start = ((f32[72,512]{1,0:T(8,128)}), f32[32,512]{1,0:T(8,128)S(1)}, s32[]{:S(2)}) async-start(f32[72,512]{1,0:T(8,128)} %copy-done.20), calls=%async_computation.4 | async-start | bytes 131072 | tf_op jit(solution)/shard_map/slice | solution.py:157
  177.2 4.5 %copy-start.21 = (f32[72,512]{1,0:T(8,128)S(1)}, f32[72,512]{1,0:T(8,128)}, u32[]{:S(2)}) copy-start(f32[72,512]{1,0:T(8,128)} %copy-done.20) | copy-start | bytes 442372
  185.5 15.7 %all-to-all-start.1 = ((f32[16,32,128]{2,1,0:T(8,128)}), f32[16,32,128]{2,1,0:T(8,128)S(1)}, u32[]{:S(2)}, u32[]{:S(2)}) async-start(f32[16,32,128]{2,1,0:T(8,128)} %shard_map.103), calls=%async_computation.1 | async-start | bytes 524288 | tf_op jit(solution)/shard_map/all_to_all | solution.py:74
  201.2 0.7 copy-start.10
Sparse Core Ops, SparseCore 0:
  35.1 61.5 all-gather.6
  133.7 39.9 all-gather.8

commit v3 on v1

v3 whole, which is shorter than its diff:
```python
import functools

import jax
import jax.numpy as jnp
from jax import lax
from jax.experimental import pallas as pl
from jax.experimental.pallas import tpu as pltpu
from jax.sharding import PartitionSpec as P

F32, BF16 = jnp.float32, jnp.bfloat16
IN_VMEM = pl.BlockSpec(memory_space=pltpu.VMEM)
IN_PLACE = pl.BlockSpec(memory_space=pl.ANY)


def split(x):
    high = x.astype(BF16)
    return high, (x - high.astype(F32)).astype(BF16)


def product(left, right, over):
    def one(x, y):
        return lax.dot_general(x, y, (over, ((), ())), preferred_element_type=F32)

    count = left[0].shape[0]
    if count <= 128:
        both = one(jnp.concatenate(left), right[0])
        return both[:count] + (both[count:] + one(left[0], right[1]))
    return one(left[0], right[0]) + (one(left[1], right[0]) + one(left[0], right[1]))


def dot(left, right):
    return product(left, right, ((1,), (0,)))


def dot_nt(left, right):
    return product(left, right, ((1,), (1,)))


def stacked(*parts):
    return jnp.concatenate(parts)


def sixteen(*rows):
    room = jnp.zeros((16 - len(rows), rows[0].shape[1]), F32)
    return jnp.concatenate([*rows, room])


def rowwise(matrix, row):
    return jnp.sum(matrix * row, axis=1, keepdims=True)


def in_lanes(columns, rows, lanes):
    lane = lax.broadcasted_iota(jnp.int32, (rows, lanes), 1)
    total = jnp.zeros((rows, lanes), F32)
    for i, column in enumerate(columns):
        total = jnp.where(lane == i, column, total)
    return total


def pack(slices, packed_ref, rows):
    for i, whole in enumerate(slices):
        for peer in range(packed_ref.shape[0]):
            packed_ref[peer, :, i * rows : (i + 1) * rows] = whole[:, peer * rows : (peer + 1) * rows]


class Fetch:
    def __init__(self, sources, buffers, sems):
        self.copies = [pltpu.make_async_copy(s, b, sems.at[i]) for i, (s, b) in enumerate(zip(sources, buffers))]
        self.buffers = buffers
        for copy in self.copies:
            copy.start()

    def __call__(self, i):
        self.copies[i].wait()
        value = self.buffers[i][...]
        return value


def fetch_parts(stack_ref, order, rows, buf, sems):
    sources = [stack_ref.at[:, pl.ds(i * rows, rows), :] for i in order]
    fetch = Fetch(sources, [buf.at[k] for k in range(len(order))], sems)
    width = stack_ref.shape[2]
    return lambda k: split(fetch(k).reshape(width, width))


def keep(pair, ref):
    ref[0], ref[1] = pair


def drows_kernel(rows, whole_ref, a0_ref, drows_ref, buf, sems):
    order = (4, 1, 6, 2, 5, 3)
    part = fetch_parts(whole_ref, order, rows, buf, sems)
    total = a0_ref[...]
    for k in range(len(order)):
        total = dot(split(total), part(k))
    drows_ref[...] = total


def first_kernel(rows, whole_ref, own_ref, vec_ref, u_ref, packed_ref, p0_ref, bw_ref, p0p_ref, bp_ref, vout_ref, buf, sems):
    part = fetch_parts(whole_ref, (0, 4, 1, 2, 5, 3), rows, buf, sems)
    width = whole_ref.shape[2]
    c1, c2, c3, j0, j1, j2 = (own_ref[i * rows : (i + 1) * rows] for i in range(6))
    b0, e0, b1, e1, b2, e2, b3, e3 = (vec_ref[i : i + 1] for i in range(8))
    u1, u2, u3, u4 = (u_ref[i : i + 1] for i in range(4))

    a0, m0 = part(0), part(1)
    both = dot(split(sixteen(e0 - u2)), m0)
    p0 = split(dot(a0, m0))
    keep(p0, p0_ref)
    a1 = part(2)
    bw = split(dot(p0, a1))
    keep(bw, bw_ref)
    both = dot(split(stacked(j0, both)), a1)
    y0, e_t = both[:rows], both[rows : rows + 1] + e1
    a2, m0p = part(3), part(4)
    p0p = split(dot(a2, m0p))
    keep(p0p, p0p_ref)
    a3 = part(5)
    bp = split(dot(p0p, a3))
    keep(bp, bp_ref)
    both = dot(split(stacked(j2, dot(split(sixteen(e2 - u4)), m0p))), a3)
    y2, e_p = both[:rows], both[rows : rows + 1] + e3
    b_t = dot_nt(split(sixteen(b1 + u1)), p0)[:1] + b0
    b_p = dot_nt(split(sixteen(b3 + u3)), p0p)[:1] + b2
    w1 = rowwise(c3, dot(split(sixteen(e_t)), a2)[:1])
    w2 = rowwise(c2, e_t)
    w3 = rowwise(j0, dot_nt(split(sixteen(b_p)), a1)[:1])
    w4 = rowwise(j1, b_p)
    x1 = dot_nt(split(c1), a0)
    right = dot_nt(split(stacked(dot_nt(split(c3), a2), c2)), bw)
    x3, x2 = right[:rows], right[rows:]
    right = dot(split(stacked(y0, j1)), bp)
    y0, y1 = right[:rows], right[rows:]
    pack((x1, x2, x3, y0, y1, y2), packed_ref, rows)
    extra = in_lanes((w1, w2, w3, w4), rows, 2 * rows)
    for peer in range(packed_ref.shape[0]):
        packed_ref[peer, :, 6 * rows :] = extra
    vout_ref[...] = jnp.concatenate([b_t, e_t, b_p, e_p, jnp.zeros((4, width), F32)])


def middle_kernel(rows, whole_ref, bw_ref, bp_ref, p1_ref, d_ref, g0_ref, g0p_ref, g1_ref, buf, sems):
    part = fetch_parts(whole_ref, (6, 4, 1, 5, 3), rows, buf, sems)
    bw, bp = (bw_ref[0], bw_ref[1]), (bp_ref[0], bp_ref[1])
    m1 = part(0)
    p1 = split(dot(bw, m1))
    keep(p1, p1_ref)
    keep(split(dot(p1, bp)), d_ref)
    keep(split(dot(m1, bp)), g1_ref)
    keep(split(dot(part(1), part(2))), g0_ref)
    keep(split(dot(part(3), part(4))), g0p_ref)


def second_kernel(
    rows, received_ref, own_ref, vec_ref, p0_ref, p0p_ref, p1_ref, g0_ref, g0p_ref, g1_ref, c_ref, j_ref, buf, sems
):
    sources = (p0p_ref, p0_ref, g0_ref, g0p_ref, p1_ref, g1_ref)
    fetch = Fetch(sources, [buf.at[k] for k in range(6)], sems)

    def pair(k):
        both = fetch(k)
        return both[0], both[1]

    columns = received_ref[...].T
    x1, x2, x3, y0, y1, y2 = (columns[i * rows : (i + 1) * rows] for i in range(6))
    w1, w2, w3, w4 = (columns[6 * rows + i : 6 * rows + i + 1] for i in range(4))
    b_t, e_t, b_p, e_p = (vec_ref[i : i + 1] for i in range(4))
    c0, j3 = own_ref[:rows], own_ref[rows:]
    inner = dot_nt(split(stacked(x3, sixteen(w1))), pair(0)) + stacked(x2, sixteen(b_p + w2))
    other = dot_nt(split(x1), pair(1)) + c0
    inner_j = dot(split(stacked(y0, sixteen(-w3))), pair(2)) + stacked(y1, sixteen(e_t - w4))
    other_j = dot(split(y2), pair(3)) + j3
    outer = dot_nt(split(inner), pair(4))
    outer_j = dot(split(inner_j), pair(5))
    c_ref[...] = outer[:rows] + other
    j_ref[:rows] = outer_j[:rows] + other_j
    j_ref[rows:] = sixteen(outer[rows : rows + 1] + b_t, outer_j[rows : rows + 1] + e_p)


def third_kernel(rows, second_ref, j_ref, drows_ref, d_ref, z_ref, p2_ref, p2rows_ref, new_a_ref, ew_ref, buf, sems):
    part = fetch_parts(second_ref, (1, 0), rows, buf, sems)
    m2 = part(0)
    e_row = j_ref[rows + 1 : rows + 2]
    both = dot(split(stacked(j_ref[:rows], drows_ref[...], sixteen(e_row))), m2)
    p2rows_ref[...] = both[rows : 2 * rows]
    ew = part(1)
    keep(ew, ew_ref)
    both = dot(split(both), ew)
    z_ref[:rows] = both[:rows]
    z_ref[rows:] = both[2 * rows :]
    new_a_ref[...] = both[rows : 2 * rows]
    keep(split(dot((d_ref[0], d_ref[1]), m2)), p2_ref)


def fourth_kernel(rows, prior_ref, prior_j_ref, c_ref, z_ref, p2_ref, packed_ref):
    v = dot_nt(split(prior_ref[...]), (p2_ref[0], p2_ref[1]))
    pack((v, c_ref[...], z_ref[:rows], prior_j_ref[:rows]), packed_ref, rows)


def last_kernel(
    rows, received_ref, d_ref, ew_ref, p2rows_ref, j_ref, prior_j_ref, part_ref, new_c_ref, new_j_ref, vectors_ref
):
    back = received_ref[...].T
    v, c_rows, z, j_rows = (back[i * rows : (i + 1) * rows] for i in range(4))
    new_c_ref[...] = dot_nt(split(v), (d_ref[0], d_ref[1])) + c_rows
    new_j_ref[...] = dot(split(z), (ew_ref[0], ew_ref[1])) + j_rows
    e_own, b_prior = j_ref[rows + 1 : rows + 2], prior_j_ref[rows : rows + 1]
    new_b = rowwise(p2rows_ref[...], b_prior) + rowwise(v, e_own)
    new_e = -rowwise(z, b_prior)
    vectors_ref[...] = in_lanes((new_b, new_e), rows, 128) + part_ref[...]


def call(kernel, rows, operands, outs, placed=None, scratch=(), flops=0):
    nbytes = sum(x.size * x.dtype.itemsize for x in operands)
    specs = [IN_VMEM if placed is None or i not in placed else IN_PLACE for i in range(len(operands))]
    return pl.pallas_call(
        functools.partial(kernel, rows),
        out_shape=[jax.ShapeDtypeStruct(shape, dtype) for shape, dtype in outs],
        in_specs=specs,
        out_specs=[IN_VMEM] * len(outs),
        scratch_shapes=scratch,
        compiler_params=pltpu.CompilerParams(vmem_limit_bytes=48 * 2**20),
        cost_estimate=pl.CostEstimate(flops=flops, bytes_accessed=nbytes, transcendentals=0),
    )(*operands)


def passed_along(shard, by):
    peers = lax.axis_size("tm")
    return lax.ppermute(shard, "tm", [(i, i + by) for i in range(peers - by)])


def gathered(shard):
    return lax.all_gather(shard, "panel", axis=0, tiled=False)


def exchanged(packed):
    return lax.all_to_all(packed, "panel", split_axis=0, concat_axis=0, tiled=True).reshape(-1, packed.shape[2])


def whole_vectors(slices):
    count, rows = slices.shape
    whole = gathered(jnp.pad(slices, ((0, 8 - count), (0, 128 - rows))))[:, :, :rows]
    return whole.transpose(1, 0, 2).reshape(8, -1)


def local(transition, offset, covariance, info_vector, information, inverses):
    rows, width = transition.shape
    peers = lax.axis_size("panel")
    time = lax.axis_index("tm")
    mine = lax.axis_index("panel")
    row = lax.broadcasted_iota(jnp.int32, (rows, width), 0) + mine * rows
    eye = (row == lax.broadcasted_iota(jnp.int32, (rows, width), 1)).astype(F32)

    def present(shard, since):
        return jnp.where(time >= since, shard, eye)

    a0, c0, j0 = transition, covariance, information
    m0, m1, m2 = present(inverses[0], 1), present(inverses[1], 2), present(inverses[2], 4)

    sent = passed_along(a0, 1), passed_along(jnp.concatenate([a0, m0]), 2), passed_along(a0, 3)
    a1, late, a3 = lax.optimization_barrier(sent)
    a1, a2, m0p, a3 = present(a1, 1), present(late[:rows], 2), present(late[rows:], 2), present(a3, 3)
    ready = jnp.concatenate([a0, a1, a2, a3, m0, m0p, m1])
    whole = gathered(ready)

    v0 = jnp.stack([offset, info_vector])
    own = jnp.concatenate([c0, j0, jnp.pad(v0, ((0, 6), (0, width - rows)))])
    own, _ = lax.optimization_barrier((own, ready))
    got = lax.optimization_barrier(tuple(passed_along(own, by) for by in (1, 2, 3)))
    (c1, c2, c3), (j1, j2, j3) = ([g[i * rows : (i + 1) * rows] for g in got] for i in range(2))
    vectors = whole_vectors(jnp.concatenate([v0] + [g[2 * rows : 2 * rows + 2, :rows] for g in got]))
    b0, e0, b1, e1, b2, e2, b3, e3 = vectors

    def along(matrix, vector):
        return jnp.sum(matrix * vector[None, :], axis=1)

    u = whole_vectors(jnp.stack([along(c1, e0), along(j0, b1), along(c3, e2), along(j2, b3)]))

    square, pair = (width, width), ((2, width, width), BF16)
    mults = 6 * width**3

    def stage(parts):
        return [pltpu.VMEM((parts, peers, rows, width), F32), pltpu.SemaphoreType.DMA((parts,))]

    (drows,) = call(drows_kernel, rows, (whole, a0), [((rows, width), F32)], {0}, stage(6), flops=mults)
    earlier = present(passed_along(drows, 4), 4)
    second = gathered(jnp.concatenate([earlier, m2]))

    packed, p0, bw, p0p, bp, vec = call(
        first_kernel,
        rows,
        (whole, jnp.concatenate([c1, c2, c3, j0, j1, j2]), vectors, u),
        [((peers, rows, 8 * rows), F32), pair, pair, pair, pair, ((8, width), F32)],
        {0},
        stage(6),
        flops=6 * mults,
    )
    received = exchanged(packed)
    p1, d, g0, g0p, g1 = call(middle_kernel, rows, (whole, bw, bp), [pair] * 5, {0}, stage(5), flops=5 * mults)
    state_c, state_j = call(
        second_kernel,
        rows,
        (received, jnp.concatenate([c0, j3]), vec, p0, p0p, p1, g0, g0p, g1),
        [((rows, width), F32), ((rows + 16, width), F32)],
        set(range(3, 9)),
        [pltpu.VMEM((6, 2, *square), BF16), pltpu.SemaphoreType.DMA((6,))],
        flops=mults,
    )

    prior_c = passed_along(state_c, 4)
    prior_j = passed_along(state_j, 4)
    z, p2, p2rows, new_a, ew = call(
        third_kernel,
        rows,
        (second, state_j, drows, d),
        [((rows + 16, width), F32), pair, ((rows, width), F32), ((rows, width), F32), pair],
        {0},
        stage(2),
        flops=2 * mults,
    )
    (packed,) = call(
        fourth_kernel, rows, (prior_c, prior_j, state_c, z, p2), [((peers, rows, 4 * rows), F32)], flops=mults
    )
    back = exchanged(packed)

    def own_part(vector):
        return lax.dynamic_slice_in_dim(vector, mine * rows, rows, 0)

    parts = jnp.stack([own_part(state_j[rows]), own_part(z[rows] + prior_j[rows + 1])], axis=1)
    parts = jnp.pad(parts, ((0, 0), (0, 126)))
    new_c, new_j, both = call(
        last_kernel,
        rows,
        (back, d, ew, p2rows, state_j, prior_j, parts),
        [((rows, width), F32), ((rows, width), F32), ((rows, 128), F32)],
        flops=mults,
    )
    return new_a, both[:, 0], new_c, both[:, 1], new_j


def solution(mesh):
    matrix = P(("tm", "panel"), None)
    vector = P(("tm", "panel"))
    return jax.shard_map(
        local,
        mesh=mesh,
        in_specs=(matrix, vector, matrix, vector, matrix, P(None, ("tm", "panel"), None)),
        out_specs=(matrix, vector, matrix, vector, matrix),
        check_vma=False,
    )
```

time: 253 us -> 251 us (level)
  waiting for transfers between devices: 151 us -> 101 us
  matrix products: 35 us -> 0 us
  blocking collectives: 0 us -> 31.4 us
  Pallas kernels: 0 us -> 27.4 us
  starting transfers between devices: 27.5 us -> 46.7 us
  other arithmetic: 2.29 us -> 5.31 us
    all_gather x3 -> x2, waiting for transfers between devices: 128 us -> 59.8 us  [gathered(): return lax.all_gather(shard, 'panel', axis=0, tiled=False)]
    dot_general x33 -> x0, matrix products: 35 us -> none  [dot(): lax.dot_general(left, right, (over, ((), ())), precision=HIGH, preferred_...]
    all_gather x0 -> x2, blocking collectives: none -> 31.4 us  [gathered(): return lax.all_gather(shard, 'panel', axis=0, tiled=False)]
    pallas_call x0 -> x7, Pallas kernels: none -> 27.4 us  [call(): pl.pallas_call(functools.partial(kernel, rows), out_shape=[jax.ShapeDtype...]
    all_to_all x0 -> x2, waiting for transfers between devices: none -> 15.9 us  [exchanged(): lax.all_to_all(packed, 'panel', split_axis=0, concat_axis=0, tiled=True)]
    unnamed x39 -> x46, local copies, waits for them, and re-layouts: 5.81 us -> 19.3 us
    slice x5 -> x7, local copies, waits for them, and re-layouts: 11.5 us -> 0.71 us  [the longest x1 0.7 us: local(): return (new_a, both[:, 0], new_c, both[:, 1], new_j)]
    all_to_all x0 -> x2, starting transfers between devices: none -> 10 us  [exchanged(): lax.all_to_all(packed, 'panel', split_axis=0, concat_axis=0, tiled=True)]
  transfers between devices with their start and end apart: 8 -> 13, of which waited for: 8 -> 8; matrix products, arithmetic and copies ran while one was open for 8% -> 1% of each run, Pallas kernels for 0% -> 9%
where the time goes in v3:
time: 251 us; the launch traced here: 247 us
  waiting for transfers between devices  101 us (40%)
  starting transfers between devices  46.7 us (19%)
  blocking collectives  31.4 us (13%)
  Pallas kernels  27.4 us (11%)
  local copies, waits for them, and re-layouts  20.8 us (8%)
  between operations  14.4 us (6%)
  other arithmetic  5.31 us (2%)
    all_gather x2, waiting for transfers between devices, gathered(): return lax.all_gather(shard, 'panel', axis=0, tiled=False)  59.8 us
    ppermute x9, starting transfers between devices, passed_along(): return lax.ppermute(shard, 'tm', [(i, i + by) for i in range(peers - by)])  36.6 us
    all_gather x2, blocking collectives, gathered(): return lax.all_gather(shard, 'panel', axis=0, tiled=False)  31.4 us
    pallas_call x7, Pallas kernels, call(): pl.pallas_call(functools.partial(kernel, rows), out_shape=[jax.ShapeDtype...  27.4 us
    ppermute x9, waiting for transfers between devices, passed_along(): return lax.ppermute(shard, 'tm', [(i, i + by) for i in range(peers - by)])  24.8 us
    unnamed x46, local copies, waits for them, and re-layouts  19.3 us
    all_to_all x2, waiting for transfers between devices, exchanged(): lax.all_to_all(packed, 'panel', split_axis=0, concat_axis=0, tiled=True)  15.9 us
    all_to_all x2, starting transfers between devices, exchanged(): lax.all_to_all(packed, 'panel', split_axis=0, concat_axis=0, tiled=True)  10 us
  transfers between devices with their start and end apart: 13, of which 8 were waited for; matrix products, arithmetic and copies ran while one was open for 1% of the time, Pallas kernels for 9%

profile of v3, /device:TPU:7, one launch (start us, length us, event | category | flops | bytes accessed | tf_op | source)
XLA Modules:
  0.0 246.5 jit_solution(16634555440898781273)
XLA Ops:
  7.3 0.9 convert_select_fusion.7
  8.2 0.8 pad_maximum_fusion.1
  9.0 4.2 %collective-permute-start.1 = (f32[64,512]{1,0:T(8,128)S(1)}, f32[64,512]{1,0:T(8,128)S(1)}, u32[]{:S(2)}, u32[]{:S(2)}) collective-permute-start(f32[64,512]{1,0:T(8,128)S(1)} %pad_maximum_fusion.1), channel_id=1, source_target_pairs={{0,32},{16,48},{32,64},{48,80},{64,96},{80,112},{96,128},{112,144}... | collective-permute-start | bytes 393224 | tf_op jit(solution)/shard_map/ppermute | solution.py:228
  13.3 3.2 %collective-permute-start = (f32[32,512]{1,0:T(8,128)}, f32[32,512]{1,0:T(8,128)S(1)}, u32[]{:S(2)}, u32[]{:S(2)}) collective-permute-start(f32[32,512]{1,0:T(8,128)} %a0_ref.1), channel_id=1, source_target_pairs={{0,16},{16,32},{32,48},{48,64},{64,80},{80,96},{96,112},{112,128},... | collective-permute-start | bytes 196616 | tf_op jit(solution)/shard_map/ppermute | solution.py:228
  16.5 4.6 %collective-permute-start.2 = (f32[32,512]{1,0:T(8,128)}, f32[32,512]{1,0:T(8,128)S(1)}, u32[]{:S(2)}, u32[]{:S(2)}) collective-permute-start(f32[32,512]{1,0:T(8,128)} %a0_ref.1), channel_id=1, source_target_pairs={{0,48},{16,64},{32,80},{48,96},{64,112},{80,128},{96,144},{112,160... | collective-permute-start | bytes 196616 | tf_op jit(solution)/shard_map/ppermute | solution.py:228
  21.1 0.8 constant_dynamic-update-slice_fusion.1
  22.0 1.6 collective-permute-done
  23.6 2.8 %collective-permute-done.2 = f32[32,512]{1,0:T(8,128)S(1)} collective-permute-done((f32[32,512]{1,0:T(8,128)}, f32[32,512]{1,0:T(8,128)S(1)}, u32[]{:S(2)}, u32[]{:S(2)}) %collective-permute-start.2) | collective-permute-done | bytes 65568 | tf_op jit(solution)/shard_map/ppermute | solution.py:228
  26.7 0.9 constant_dynamic-update-slice_fusion
  27.6 1.0 fusion.4
  29.4 59.8 %all-gather.7.cloned.1.call-done = f32[3584,512]{1,0:T(8,128)} async-done(((f32[224,512]{1,0:T(8,128)}), f32[3584,512]{1,0:T(8,128)}) %all-gather.7.cloned.1.call-update) | async-done | bytes 7340048 | tf_op jit(solution)/shard_map/all_gather | solution.py:232
  90.1 3.1 %shard_map.101.drows_ref = f32[32,512]{1,0:T(8,128)S(1)} custom-call(f32[16,224,512]{2,1,0:T(8,128)} %bitcast.33, f32[32,512]{1,0:T(8,128)S(1)} %copy-done.7), custom_call_target="tpu_custom_call" | custom-call | flops 805306368 | bytes 7405568 | tf_op jit(solution)/shard_map/pallas_call | solution.py:215
  93.2 7.1 %collective-permute-start.3 = (f32[32,512]{1,0:T(8,128)S(1)}, f32[32,512]{1,0:T(8,128)S(1)}, u32[]{:S(2)}, u32[]{:S(2)}) collective-permute-start(f32[32,512]{1,0:T(8,128)S(1)} %shard_map.101.drows_ref), channel_id=1, source_target_pairs={{0,64},{16,80},{32,96},{48,112},{64,128},{80,144},{96,160},{112,17... | collective-permute-start | bytes 196616 | tf_op jit(solution)/shard_map/ppermute | solution.py:228
  100.3 2.8 %collective-permute-done.3 = f32[32,512]{1,0:T(8,128)S(1)} collective-permute-done((f32[32,512]{1,0:T(8,128)S(1)}, f32[32,512]{1,0:T(8,128)S(1)}, u32[]{:S(2)}, u32[]{:S(2)}) %collective-permute-start.3) | collective-permute-done | bytes 65568 | tf_op jit(solution)/shard_map/ppermute | solution.py:228
  104.0 3.1 %collective-permute-start.4 = (f32[72,512]{1,0:T(8,128)S(1)}, f32[72,512]{1,0:T(8,128)S(1)}, u32[]{:S(2)}, u32[]{:S(2)}) collective-permute-start(f32[72,512]{1,0:T(8,128)S(1)} %pad_maximum_fusion), channel_id=1, source_target_pairs={{0,16},{16,32},{32,48},{48,64},{64,80},{80,96},{96,112},{112,128},... | collective-permute-start | bytes 442376 | tf_op jit(solution)/shard_map/ppermute | solution.py:228
  107.1 5.0 %collective-permute-start.5 = (f32[72,512]{1,0:T(8,128)S(1)}, f32[72,512]{1,0:T(8,128)S(1)}, u32[]{:S(2)}, u32[]{:S(2)}) collective-permute-start(f32[72,512]{1,0:T(8,128)S(1)} %pad_maximum_fusion), channel_id=1, source_target_pairs={{0,32},{16,48},{32,64},{48,80},{64,96},{80,112},{96,128},{112,144}... | collective-permute-start | bytes 442376 | tf_op jit(solution)/shard_map/ppermute | solution.py:228
  112.1 4.3 %collective-permute-start.6 = (f32[72,512]{1,0:T(8,128)S(1)}, f32[72,512]{1,0:T(8,128)S(1)}, u32[]{:S(2)}, u32[]{:S(2)}) collective-permute-start(f32[72,512]{1,0:T(8,128)S(1)} %pad_maximum_fusion), channel_id=1, source_target_pairs={{0,48},{16,64},{32,80},{48,96},{64,112},{80,128},{96,144},{112,160... | collective-permute-start | bytes 442376 | tf_op jit(solution)/shard_map/ppermute | solution.py:228
  116.5 14.9 %collective-permute-done.6 = f32[72,512]{1,0:T(8,128)S(1)} collective-permute-done((f32[72,512]{1,0:T(8,128)S(1)}, f32[72,512]{1,0:T(8,128)S(1)}, u32[]{:S(2)}, u32[]{:S(2)}) %collective-permute-start.6) | collective-permute-done | bytes 147488 | tf_op jit(solution)/shard_map/ppermute | solution.py:228
  131.4 16.4 %all-gather.2 = f32[128,128]{1,0:T(8,128)S(1)} all-gather(f32[8,128]{1,0:T(8,128)S(1)} %pad.17), channel_id=4, replica_groups=mesh['tm'=32,'panel'=16] {'panel'}, dimensions={0}, use_global_device_ids=true | all-gather | bytes 69632 | tf_op jit(solution)/shard_map/all_gather | solution.py:232
  148.8 15.0 %all-gather.3 = f32[128,128]{1,0:T(8,128)S(1)} all-gather(f32[8,128]{1,0:T(8,128)S(1)} %select_maximum_fusion.1), channel_id=5, replica_groups=mesh['tm'=32,'panel'=16] {'panel'}, dimensions={0}, use_global_device_ids=true | all-gather | bytes 69632 | tf_op jit(solution)/shard_map/all_gather | solution.py:232
  164.0 9.7 %shard_map.102 = (f32[16,32,256]{2,1,0:T(8,128)}, bf16[2,512,512]{2,1,0:T(8,128)(2,1)S(1)}, bf16[2,512,512]{2,1,0:T(8,128)(2,1)S(1)}, bf16[2,512,512]{2,1,0:T(8,...) custom-call(f32[16,224,512]{2,1,0:T(8,128)} %bitcast.34, ...), custom_call_target="tpu_custom_call" | custom-call | flops 4831838208 | bytes 7766016 | tf_op jit(solution)/shard_map/pallas_call | solution.py:215
  173.7 1.0 copy-done.14
  174.7 1.0 copy-done.15
  175.6 5.3 %all-to-all-start = ((f32[16,32,256]{2,1,0:T(8,128)}), f32[16,32,256]{2,1,0:T(8,128)S(1)}, u32[]{:S(2)}, u32[]{:S(2)}) async-start(f32[16,32,256]{2,1,0:T(8,128)} %get-tuple-element.40), calls=%async_computation | async-start | bytes 1048576 | tf_op jit(solution)/shard_map/all_to_all | solution.py:236
  181.0 7.9 %shard_map.103 = (bf16[2,512,512]{2,1,0:T(8,128)(2,1)S(1)}, bf16[2,512,512]{2,1,0:T(8,128)(2,1)S(1)}, bf16[2,512,512]{2,1,0:T(8,128)(2,1)S(1)}, bf16[2,512,512]{2,1,0:T(8,128)(2,1)S(1)}, bf16[2,512,512]{2,1,0:T(8,128)(2,1)S(1)}) custom-call(f32[16,224,512]{2,1,0:T(8,128)} %bitcast.35, bf16[2,512,512]{2,1,0:T(8,128)(2,1)} %copy-done.14, ...), custom_call_target="tpu_custom_call" | custom-call | flops 4026531840 | bytes 9437184 | tf_op jit(solution)/shard_map/pallas_call | solution.py:215
  188.9 1.0 copy-done
  189.8 1.0 copy-done.2
  190.8 1.0 copy-done.4
  191.8 1.0 copy-done.6
  192.8 1.0 copy-done.9
  193.8 4.5 %all-to-all-done = f32[16,32,256]{2,1,0:T(8,128)S(1)} async-done(((f32[16,32,256]{2,1,0:T(8,128)}), f32[16,32,256]{2,1,0:T(8,128)S(1)}, u32[]{:S(2)}, u32[]{:S(2)}) %all-to-all-start) | async-done | bytes 524320 | tf_op jit(solution)/shard_map/all_to_all | solution.py:236
  198.3 1.2 copy-done.1
  199.5 1.2 copy-done.3
  200.8 1.2 copy-done.5
  202.0 2.5 %shard_map.104 = (f32[32,512]{1,0:T(8,128)S(1)}, f32[48,512]{1,0:T(8,128)S(1)}) custom-call(f32[512,256]{1,0:T(8,128)S(1)} %bitcast.30, f32[64,512]{1,0:T(8,128)S(1)} %pad_maximum_fusion.3.own_ref, f32[8,512]{1,0:T(8,128)S(1)} %get-tuple-element.41.vec_ref, bf16[2,512,512]{2,1,0:T(8,128)(2,1)S(1)} %get-tuple-element.42.p0_ref, ...), custom_call_target="tpu_custom_call" | custom-call | flops 805306368 | bytes 6963200 | tf_op jit(solution)/shard_map/pallas_call | solution.py:215
  204.5 3.0 %collective-permute-start.8 = (f32[48,512]{1,0:T(8,128)S(1)}, f32[48,512]{1,0:T(8,128)S(1)}, u32[]{:S(2)}, u32[]{:S(2)}) collective-permute-start(f32[48,512]{1,0:T(8,128)S(1)} %get-tuple-element.50.j_ref), channel_id=1, source_target_pairs={{0,64},{16,80},{32,96},{48,112},{64,128},{80,144},{96,160},{112,17... | collective-permute-start | bytes 294920 | tf_op jit(solution)/shard_map/ppermute | solution.py:228
  207.5 1.9 collective-permute-start.7
  209.5 1.6 copy-done.8
  211.1 1.2 copy-done.10
  212.3 1.7 shard_map.105
  214.0 1.0 copy-done.12
  215.0 2.7 %collective-permute-done.7.prior_ref = f32[32,512]{1,0:T(8,128)S(1)} collective-permute-done((f32[32,512]{1,0:T(8,128)S(1)}, f32[32,512]{1,0:T(8,128)S(1)}, u32[]{:S(2)}, u32[]{:S(2)}) %collective-permute-start.7) | collective-permute-done | bytes 65568 | tf_op jit(solution)/shard_map/ppermute | solution.py:228
  217.7 1.3 shard_map.106
  218.9 4.7 %all-to-all-start.1 = ((f32[16,32,128]{2,1,0:T(8,128)}), f32[16,32,128]{2,1,0:T(8,128)S(1)}, u32[]{:S(2)}, u32[]{:S(2)}) async-start(f32[16,32,128]{2,1,0:T(8,128)} %shard_map.106), calls=%async_computation.1 | async-start | bytes 524288 | tf_op jit(solution)/shard_map/all_to_all | solution.py:236
  223.9 11.4 %all-to-all-done.1 = f32[16,32,128]{2,1,0:T(8,128)S(1)} async-done(((f32[16,32,128]{2,1,0:T(8,128)}), f32[16,32,128]{2,1,0:T(8,128)S(1)}, u32[]{:S(2)}, u32[]{:S(2)}) %all-to-all-start.1) | async-done | bytes 262176 | tf_op jit(solution)/shard_map/all_to_all | solution.py:236
  235.3 1.2 copy-done.11
  236.5 1.2 copy-done.13
  237.8 1.2 shard_map.107
  (77 shorter events, 5.1 us)
Async XLA Ops:
  7.2 96.7 %copy-start.20 = (f32[32]{0:T(128)S(1)}, f32[32]{0:T(128)}, u32[]{:S(2)}) copy-start(f32[32]{0:T(128)} %param.7) | copy-start | bytes 388
  7.2 96.7 %copy-start.19 = (f32[32]{0:T(128)S(1)}, f32[32]{0:T(128)}, u32[]{:S(2)}) copy-start(f32[32]{0:T(128)} %param.9) | copy-start | bytes 388
  7.2 96.7 %copy-start.17 = (f32[32,512]{1,0:T(8,128)S(1)}, f32[32,512]{1,0:T(8,128)}, u32[]{:S(2)}) copy-start(f32[32,512]{1,0:T(8,128)} %param.10) | copy-start | bytes 196612
  7.2 96.7 %copy-start.18 = (f32[32,512]{1,0:T(8,128)S(1)}, f32[32,512]{1,0:T(8,128)}, u32[]{:S(2)}) copy-start(f32[32,512]{1,0:T(8,128)} %param.8) | copy-start | bytes 196612
  7.2 82.0 %all-gather.7.cloned.1.call-start = ((), (), s32[]{:S(2)}) async-start(), calls=%async_computation.2 | async-start | bytes 7798784 | tf_op jit(solution)/shard_map/all_gather | solution.py:232
  9.0 17.4 %collective-permute-start.1 = (f32[64,512]{1,0:T(8,128)S(1)}, f32[64,512]{1,0:T(8,128)S(1)}, u32[]{:S(2)}, u32[]{:S(2)}) collective-permute-start(f32[64,512]{1,0:T(8,128)S(1)} %pad_maximum_fusion.1), channel_id=1, source_target_pairs={{0,32},{16,48},{32,64},{48,80},{64,96},{80,112},{96,128},{112,144}... | collective-permute-start | bytes 393224 | tf_op jit(solution)/shard_map/ppermute | solution.py:228
  13.3 10.3 %collective-permute-start = (f32[32,512]{1,0:T(8,128)}, f32[32,512]{1,0:T(8,128)S(1)}, u32[]{:S(2)}, u32[]{:S(2)}) collective-permute-start(f32[32,512]{1,0:T(8,128)} %a0_ref.1), channel_id=1, source_target_pairs={{0,16},{16,32},{32,48},{48,64},{64,80},{80,96},{96,112},{112,128},... | collective-permute-start | bytes 196616 | tf_op jit(solution)/shard_map/ppermute | solution.py:228
  16.5 9.9 %collective-permute-start.2 = (f32[32,512]{1,0:T(8,128)}, f32[32,512]{1,0:T(8,128)S(1)}, u32[]{:S(2)}, u32[]{:S(2)}) collective-permute-start(f32[32,512]{1,0:T(8,128)} %a0_ref.1), channel_id=1, source_target_pairs={{0,48},{16,64},{32,80},{48,96},{64,112},{80,128},{96,144},{112,160... | collective-permute-start | bytes 196616 | tf_op jit(solution)/shard_map/ppermute | solution.py:228
  28.6 0.8 copy-start.16
  29.4 180.1 %all-gather.9.cloned.1.call-start = ((), (), s32[]{:S(2)}) async-start(), calls=%async_computation.3 | async-start | bytes 2228224 | tf_op jit(solution)/shard_map/all_gather | solution.py:232
  89.2 0.8 copy-start.7
  93.2 9.9 %collective-permute-start.3 = (f32[32,512]{1,0:T(8,128)S(1)}, f32[32,512]{1,0:T(8,128)S(1)}, u32[]{:S(2)}, u32[]{:S(2)}) collective-permute-start(f32[32,512]{1,0:T(8,128)S(1)} %shard_map.101.drows_ref), channel_id=1, source_target_pairs={{0,64},{16,80},{32,96},{48,112},{64,128},{80,144},{96,160},{112,17... | collective-permute-start | bytes 196616 | tf_op jit(solution)/shard_map/ppermute | solution.py:228
  104.0 12.5 %collective-permute-start.4 = (f32[72,512]{1,0:T(8,128)S(1)}, f32[72,512]{1,0:T(8,128)S(1)}, u32[]{:S(2)}, u32[]{:S(2)}) collective-permute-start(f32[72,512]{1,0:T(8,128)S(1)} %pad_maximum_fusion), channel_id=1, source_target_pairs={{0,16},{16,32},{32,48},{48,64},{64,80},{80,96},{96,112},{112,128},... | collective-permute-start | bytes 442376 | tf_op jit(solution)/shard_map/ppermute | solution.py:228
  107.1 9.4 %collective-permute-start.5 = (f32[72,512]{1,0:T(8,128)S(1)}, f32[72,512]{1,0:T(8,128)S(1)}, u32[]{:S(2)}, u32[]{:S(2)}) collective-permute-start(f32[72,512]{1,0:T(8,128)S(1)} %pad_maximum_fusion), channel_id=1, source_target_pairs={{0,32},{16,48},{32,64},{48,80},{64,96},{80,112},{96,128},{112,144}... | collective-permute-start | bytes 442376 | tf_op jit(solution)/shard_map/ppermute | solution.py:228
  112.1 19.2 %collective-permute-start.6 = (f32[72,512]{1,0:T(8,128)S(1)}, f32[72,512]{1,0:T(8,128)S(1)}, u32[]{:S(2)}, u32[]{:S(2)}) collective-permute-start(f32[72,512]{1,0:T(8,128)S(1)} %pad_maximum_fusion), channel_id=1, source_target_pairs={{0,48},{16,64},{32,80},{48,96},{64,112},{80,128},{96,144},{112,160... | collective-permute-start | bytes 442376 | tf_op jit(solution)/shard_map/ppermute | solution.py:228
  173.7 1.0 copy-start.14
  174.7 1.0 copy-start.15
  175.6 22.7 %all-to-all-start = ((f32[16,32,256]{2,1,0:T(8,128)}), f32[16,32,256]{2,1,0:T(8,128)S(1)}, u32[]{:S(2)}, u32[]{:S(2)}) async-start(f32[16,32,256]{2,1,0:T(8,128)} %get-tuple-element.40), calls=%async_computation | async-start | bytes 1048576 | tf_op jit(solution)/shard_map/all_to_all | solution.py:236
  188.9 1.0 copy-start
  189.8 1.0 copy-start.2
  190.8 1.0 copy-start.4
  191.8 1.0 copy-start.6
  192.8 1.0 copy-start.9
  198.3 1.2 copy-start.1
  199.5 1.2 copy-start.3
  200.8 1.2 copy-start.5
  204.5 13.1 %collective-permute-start.8 = (f32[48,512]{1,0:T(8,128)S(1)}, f32[48,512]{1,0:T(8,128)S(1)}, u32[]{:S(2)}, u32[]{:S(2)}) collective-permute-start(f32[48,512]{1,0:T(8,128)S(1)} %get-tuple-element.50.j_ref), channel_id=1, source_target_pairs={{0,64},{16,80},{32,96},{48,112},{64,128},{80,144},{96,160},{112,17... | collective-permute-start | bytes 294920 | tf_op jit(solution)/shard_map/ppermute | solution.py:228
  207.5 10.1 %collective-permute-start.7 = (f32[32,512]{1,0:T(8,128)S(1)}, f32[32,512]{1,0:T(8,128)S(1)}, u32[]{:S(2)}, u32[]{:S(2)}) collective-permute-start(f32[32,512]{1,0:T(8,128)S(1)} %get-tuple-element.53.c_ref), channel_id=1, source_target_pairs={{0,64},{16,80},{32,96},{48,112},{64,128},{80,144},{96,160},{112,17... | collective-permute-start | bytes 196616 | tf_op jit(solution)/shard_map/ppermute | solution.py:228
  209.5 1.6 copy-start.8
  211.1 1.2 copy-start.10
  214.0 1.0 copy-start.12
  218.9 16.4 %all-to-all-start.1 = ((f32[16,32,128]{2,1,0:T(8,128)}), f32[16,32,128]{2,1,0:T(8,128)S(1)}, u32[]{:S(2)}, u32[]{:S(2)}) async-start(f32[16,32,128]{2,1,0:T(8,128)} %shard_map.106), calls=%async_computation.1 | async-start | bytes 524288 | tf_op jit(solution)/shard_map/all_to_all | solution.py:236
  235.3 1.2 copy-start.11
  236.5 1.2 copy-start.13
Sparse Core Ops, SparseCore 0:
  29.5 59.6 all-gather.6
  104.0 41.8 all-gather.8

commit v4 on v3

--- a/solution.py
+++ b/solution.py
@@ -10,6 +10,7 @@
 F32, BF16 = jnp.float32, jnp.bfloat16
 IN_VMEM = pl.BlockSpec(memory_space=pltpu.VMEM)
 IN_PLACE = pl.BlockSpec(memory_space=pl.ANY)
+IN_HBM = pl.BlockSpec(memory_space=pltpu.HBM)
 
 
 def split(x):
@@ -87,10 +88,11 @@
     ref[0], ref[1] = pair
 
 
-def drows_kernel(rows, whole_ref, a0_ref, drows_ref, buf, sems):
+def drows_kernel(rows, whole_ref, a0_ref, drows_ref, buf, sems, start, start_sems):
     order = (4, 1, 6, 2, 5, 3)
+    first = Fetch([a0_ref], [start], start_sems)
     part = fetch_parts(whole_ref, order, rows, buf, sems)
-    total = a0_ref[...]
+    total = first(0)
     for k in range(len(order)):
         total = dot(split(total), part(k))
     drows_ref[...] = total
@@ -151,7 +153,7 @@
 
 
 def second_kernel(
-    rows, received_ref, own_ref, vec_ref, p0_ref, p0p_ref, p1_ref, g0_ref, g0p_ref, g1_ref, c_ref, j_ref, buf, sems
+    rows, received_ref, own_ref, vec_ref, p0_ref, p0p_ref, p1_ref, g0_ref, g0p_ref, g1_ref, state_ref, buf, sems
 ):
     sources = (p0p_ref, p0_ref, g0_ref, g0p_ref, p1_ref, g1_ref)
     fetch = Fetch(sources, [buf.at[k] for k in range(6)], sems)
@@ -171,16 +173,16 @@
     other_j = dot(split(y2), pair(3)) + j3
     outer = dot_nt(split(inner), pair(4))
     outer_j = dot(split(inner_j), pair(5))
-    c_ref[...] = outer[:rows] + other
-    j_ref[:rows] = outer_j[:rows] + other_j
-    j_ref[rows:] = sixteen(outer[rows : rows + 1] + b_t, outer_j[rows : rows + 1] + e_p)
-
-
-def third_kernel(rows, second_ref, j_ref, drows_ref, d_ref, z_ref, p2_ref, p2rows_ref, new_a_ref, ew_ref, buf, sems):
+    state_ref[:rows] = outer[:rows] + other
+    state_ref[rows : 2 * rows] = outer_j[:rows] + other_j
+    state_ref[2 * rows :] = sixteen(outer[rows : rows + 1] + b_t, outer_j[rows : rows + 1] + e_p)[:8]
+
+
+def third_kernel(rows, second_ref, state_ref, drows_ref, d_ref, z_ref, p2_ref, p2rows_ref, new_a_ref, ew_ref, buf, sems):
     part = fetch_parts(second_ref, (1, 0), rows, buf, sems)
     m2 = part(0)
-    e_row = j_ref[rows + 1 : rows + 2]
-    both = dot(split(stacked(j_ref[:rows], drows_ref[...], sixteen(e_row))), m2)
+    e_row = state_ref[2 * rows + 1 : 2 * rows + 2]
+    both = dot(split(stacked(state_ref[rows : 2 * rows], drows_ref[...], sixteen(e_row))), m2)
     p2rows_ref[...] = both[rows : 2 * rows]
     ew = part(1)
     keep(ew, ew_ref)
@@ -191,34 +193,34 @@
     keep(split(dot((d_ref[0], d_ref[1]), m2)), p2_ref)
 
 
-def fourth_kernel(rows, prior_ref, prior_j_ref, c_ref, z_ref, p2_ref, packed_ref):
-    v = dot_nt(split(prior_ref[...]), (p2_ref[0], p2_ref[1]))
-    pack((v, c_ref[...], z_ref[:rows], prior_j_ref[:rows]), packed_ref, rows)
+def fourth_kernel(rows, prior_ref, state_ref, z_ref, p2_ref, packed_ref):
+    v = dot_nt(split(prior_ref[:rows]), (p2_ref[0], p2_ref[1]))
+    pack((v, state_ref[:rows], z_ref[:rows], prior_ref[rows : 2 * rows]), packed_ref, rows)
 
 
 def last_kernel(
-    rows, received_ref, d_ref, ew_ref, p2rows_ref, j_ref, prior_j_ref, part_ref, new_c_ref, new_j_ref, vectors_ref
+    rows, received_ref, d_ref, ew_ref, p2rows_ref, state_ref, prior_ref, part_ref, new_c_ref, new_j_ref, vectors_ref
 ):
     back = received_ref[...].T
     v, c_rows, z, j_rows = (back[i * rows : (i + 1) * rows] for i in range(4))
     new_c_ref[...] = dot_nt(split(v), (d_ref[0], d_ref[1])) + c_rows
     new_j_ref[...] = dot(split(z), (ew_ref[0], ew_ref[1])) + j_rows
-    e_own, b_prior = j_ref[rows + 1 : rows + 2], prior_j_ref[rows : rows + 1]
+    e_own, b_prior = state_ref[2 * rows + 1 : 2 * rows + 2], prior_ref[2 * rows : 2 * rows + 1]
     new_b = rowwise(p2rows_ref[...], b_prior) + rowwise(v, e_own)
     new_e = -rowwise(z, b_prior)
     vectors_ref[...] = in_lanes((new_b, new_e), rows, 128) + part_ref[...]
 
 
-def call(kernel, rows, operands, outs, placed=None, scratch=(), flops=0):
+def call(kernel, rows, operands, outs, placed=None, scratch=(), flops=0, grant=8):
     nbytes = sum(x.size * x.dtype.itemsize for x in operands)
-    specs = [IN_VMEM if placed is None or i not in placed else IN_PLACE for i in range(len(operands))]
+    specs = [(placed or {}).get(i, IN_VMEM) for i in range(len(operands))]
     return pl.pallas_call(
         functools.partial(kernel, rows),
         out_shape=[jax.ShapeDtypeStruct(shape, dtype) for shape, dtype in outs],
         in_specs=specs,
         out_specs=[IN_VMEM] * len(outs),
         scratch_shapes=scratch,
-        compiler_params=pltpu.CompilerParams(vmem_limit_bytes=48 * 2**20),
+        compiler_params=pltpu.CompilerParams(vmem_limit_bytes=grant * 2**20),
         cost_estimate=pl.CostEstimate(flops=flops, bytes_accessed=nbytes, transcendentals=0),
     )(*operands)
 
@@ -275,13 +277,24 @@
 
     u = whole_vectors(jnp.stack([along(c1, e0), along(j0, b1), along(c3, e2), along(j2, b3)]))
 
+    whole, vectors, u = lax.optimization_barrier((whole, vectors, u))
+
     square, pair = (width, width), ((2, width, width), BF16)
     mults = 6 * width**3
 
     def stage(parts):
         return [pltpu.VMEM((parts, peers, rows, width), F32), pltpu.SemaphoreType.DMA((parts,))]
 
-    (drows,) = call(drows_kernel, rows, (whole, a0), [((rows, width), F32)], {0}, stage(6), flops=mults)
+    (drows,) = call(
+        drows_kernel,
+        rows,
+        (whole, a0),
+        [((rows, width), F32)],
+        {0: IN_HBM, 1: IN_PLACE},
+        stage(6) + [pltpu.VMEM((rows, width), F32), pltpu.SemaphoreType.DMA((1,))],
+        flops=mults,
+        grant=56,
+    )
     earlier = present(passed_along(drows, 4), 4)
     second = gathered(jnp.concatenate([earlier, m2]))
 
@@ -290,47 +303,49 @@
         rows,
         (whole, jnp.concatenate([c1, c2, c3, j0, j1, j2]), vectors, u),
         [((peers, rows, 8 * rows), F32), pair, pair, pair, pair, ((8, width), F32)],
-        {0},
+        {0: IN_HBM},
         stage(6),
         flops=6 * mults,
+        grant=24,
     )
     received = exchanged(packed)
-    p1, d, g0, g0p, g1 = call(middle_kernel, rows, (whole, bw, bp), [pair] * 5, {0}, stage(5), flops=5 * mults)
-    state_c, state_j = call(
+    p1, d, g0, g0p, g1 = call(middle_kernel, rows, (whole, bw, bp), [pair] * 5, {0: IN_HBM}, stage(5), flops=5 * mults, grant=24)
+    (state,) = call(
         second_kernel,
         rows,
         (received, jnp.concatenate([c0, j3]), vec, p0, p0p, p1, g0, g0p, g1),
-        [((rows, width), F32), ((rows + 16, width), F32)],
-        set(range(3, 9)),
+        [((2 * rows + 8, width), F32)],
+        dict.fromkeys(range(3, 9), IN_PLACE),
         [pltpu.VMEM((6, 2, *square), BF16), pltpu.SemaphoreType.DMA((6,))],
         flops=mults,
-    )
-
-    prior_c = passed_along(state_c, 4)
-    prior_j = passed_along(state_j, 4)
+        grant=12,
+    )
+
+    prior = passed_along(state, 4)
     z, p2, p2rows, new_a, ew = call(
         third_kernel,
         rows,
-        (second, state_j, drows, d),
+        (second, state, drows, d),
         [((rows + 16, width), F32), pair, ((rows, width), F32), ((rows, width), F32), pair],
-        {0},
+        {0: IN_HBM},
         stage(2),
         flops=2 * mults,
+        grant=12,
     )
     (packed,) = call(
-        fourth_kernel, rows, (prior_c, prior_j, state_c, z, p2), [((peers, rows, 4 * rows), F32)], flops=mults
+        fourth_kernel, rows, (prior, state, z, p2), [((peers, rows, 4 * rows), F32)], flops=mults
     )
     back = exchanged(packed)
 
     def own_part(vector):
         return lax.dynamic_slice_in_dim(vector, mine * rows, rows, 0)
 
-    parts = jnp.stack([own_part(state_j[rows]), own_part(z[rows] + prior_j[rows + 1])], axis=1)
+    parts = jnp.stack([own_part(state[2 * rows]), own_part(z[rows] + prior[2 * rows + 1])], axis=1)
     parts = jnp.pad(parts, ((0, 0), (0, 126)))
     new_c, new_j, both = call(
         last_kernel,
         rows,
-        (back, d, ew, p2rows, state_j, prior_j, parts),
+        (back, d, ew, p2rows, state, prior, parts),
         [((rows, width), F32), ((rows, width), F32), ((rows, 128), F32)],
         flops=mults,
     )

time: 251 us -> 207 us (0.82); the launches traced: 247 us -> 206 us
  waiting for transfers between devices: 101 us -> 46.8 us
  blocking collectives: 31.4 us -> 43.7 us
  local copies, waits for them, and re-layouts: 20.8 us -> 28.4 us
  starting transfers between devices: 46.7 us -> 39.2 us
    all_gather x2, waiting for transfers between devices: 59.8 us -> 0.04 us  [gathered(): return lax.all_gather(shard, 'panel', axis=0, tiled=False)]
    all_gather x2, blocking collectives: 31.4 us -> 43.7 us  [gathered(): return lax.all_gather(shard, 'panel', axis=0, tiled=False)]
    ppermute x9 -> x8, starting transfers between devices: 36.6 us -> 28.4 us  [passed_along(): return lax.ppermute(shard, 'tm', [(i, i + by) for i in range(peers - by)])]
    unnamed x46, local copies, waits for them, and re-layouts: 19.3 us -> 26.2 us
    ppermute x9 -> x8, waiting for transfers between devices: 24.8 us -> 30.6 us  [passed_along(): return lax.ppermute(shard, 'tm', [(i, i + by) for i in range(peers - by)])]
  transfers between devices with their start and end apart: 13 -> 12, of which waited for: 8 -> 8; matrix products, arithmetic and copies ran while one was open for 1% -> 3% of each run, Pallas kernels for 9% -> 9%
where the time goes in v4:
time: 207 us; the launch traced here: 206 us
  waiting for transfers between devices  46.8 us (23%)
  blocking collectives  43.7 us (21%)
  starting transfers between devices  39.2 us (19%)
  local copies, waits for them, and re-layouts  28.4 us (14%)
  Pallas kernels  26.1 us (13%)
  between operations  14.3 us (7%)
  other arithmetic  7.69 us (4%)
    all_gather x2, blocking collectives, gathered(): return lax.all_gather(shard, 'panel', axis=0, tiled=False)  43.7 us
    ppermute x8, waiting for transfers between devices, passed_along(): return lax.ppermute(shard, 'tm', [(i, i + by) for i in range(peers - by)])  30.6 us
    ppermute x8, starting transfers between devices, passed_along(): return lax.ppermute(shard, 'tm', [(i, i + by) for i in range(peers - by)])  28.4 us
    unnamed x46, local copies, waits for them, and re-layouts  26.2 us
    pallas_call x7, Pallas kernels, call(): pl.pallas_call(functools.partial(kernel, rows), out_shape=[jax.ShapeDtype...  26.1 us
    all_to_all x2, waiting for transfers between devices, exchanged(): lax.all_to_all(packed, 'panel', split_axis=0, concat_axis=0, tiled=True)  16.1 us
    all_to_all x2, starting transfers between devices, exchanged(): lax.all_to_all(packed, 'panel', split_axis=0, concat_axis=0, tiled=True)  10.7 us
  transfers between devices with their start and end apart: 12, of which 8 were waited for; matrix products, arithmetic and copies ran while one was open for 3% of the time, Pallas kernels for 9%

profile of v4, /device:TPU:7, one launch (start us, length us, event | category | flops | bytes accessed | tf_op | source)
XLA Modules:
  0.0 206.2 jit_solution(13803390032949361537)
XLA Ops:
  7.2 0.9 convert_select_fusion.7
  9.0 4.2 %collective-permute-start.1 = (f32[64,512]{1,0:T(8,128)S(1)}, f32[64,512]{1,0:T(8,128)S(1)}, u32[]{:S(2)}, u32[]{:S(2)}) collective-permute-start(f32[64,512]{1,0:T(8,128)S(1)} %pad_maximum_fusion.1), channel_id=1, source_target_pairs={{0,32},{16,48},{32,64},{48,80},{64,96},{80,112},{96,128},{112,144}... | collective-permute-start | bytes 393224 | tf_op jit(solution)/shard_map/ppermute | solution.py:230
  13.2 3.2 %collective-permute-start = (f32[32,512]{1,0:T(8,128)}, f32[32,512]{1,0:T(8,128)S(1)}, u32[]{:S(2)}, u32[]{:S(2)}) collective-permute-start(f32[32,512]{1,0:T(8,128)} %a0_ref.1), channel_id=1, source_target_pairs={{0,16},{16,32},{32,48},{48,64},{64,80},{80,96},{96,112},{112,128},... | collective-permute-start | bytes 196616 | tf_op jit(solution)/shard_map/ppermute | solution.py:230
  16.4 4.6 %collective-permute-start.2 = (f32[32,512]{1,0:T(8,128)}, f32[32,512]{1,0:T(8,128)S(1)}, u32[]{:S(2)}, u32[]{:S(2)}) collective-permute-start(f32[32,512]{1,0:T(8,128)} %a0_ref.1), channel_id=1, source_target_pairs={{0,48},{16,64},{32,80},{48,96},{64,112},{80,128},{96,144},{112,160... | collective-permute-start | bytes 196616 | tf_op jit(solution)/shard_map/ppermute | solution.py:230
  22.0 1.6 collective-permute-done
  23.5 2.8 %collective-permute-done.2 = f32[32,512]{1,0:T(8,128)S(1)} collective-permute-done((f32[32,512]{1,0:T(8,128)}, f32[32,512]{1,0:T(8,128)S(1)}, u32[]{:S(2)}, u32[]{:S(2)}) %collective-permute-start.2) | collective-permute-done | bytes 65568 | tf_op jit(solution)/shard_map/ppermute | solution.py:230
  27.6 1.0 fusion.4
  31.0 5.7 %collective-permute-start.3 = (f32[72,512]{1,0:T(8,128)S(1)}, f32[72,512]{1,0:T(8,128)S(1)}, u32[]{:S(2)}, u32[]{:S(2)}) collective-permute-start(f32[72,512]{1,0:T(8,128)S(1)} %pad_maximum_fusion), channel_id=1, source_target_pairs={{0,16},{16,32},{32,48},{48,64},{64,80},{80,96},{96,112},{112,128},... | collective-permute-start | bytes 442376 | tf_op jit(solution)/shard_map/ppermute | solution.py:230
  36.7 1.9 collective-permute-start.4
  38.6 3.9 %collective-permute-start.5 = (f32[72,512]{1,0:T(8,128)S(1)}, f32[72,512]{1,0:T(8,128)S(1)}, u32[]{:S(2)}, u32[]{:S(2)}) collective-permute-start(f32[72,512]{1,0:T(8,128)S(1)} %pad_maximum_fusion), channel_id=1, source_target_pairs={{0,48},{16,64},{32,80},{48,96},{64,112},{80,128},{96,144},{112,160... | collective-permute-start | bytes 442376 | tf_op jit(solution)/shard_map/ppermute | solution.py:230
  42.6 9.1 %collective-permute-done.4 = f32[72,512]{1,0:T(8,128)S(1)} collective-permute-done((f32[72,512]{1,0:T(8,128)S(1)}, f32[72,512]{1,0:T(8,128)S(1)}, u32[]{:S(2)}, u32[]{:S(2)}) %collective-permute-start.4) | collective-permute-done | bytes 147488 | tf_op jit(solution)/shard_map/ppermute | solution.py:230
  51.7 1.3 collective-permute-done.5
  53.7 29.1 %all-gather.1 = f32[128,128]{1,0:T(8,128)S(1)} all-gather(f32[8,128]{1,0:T(8,128)S(1)} %pad.17), channel_id=3, replica_groups=mesh['tm'=32,'panel'=16] {'panel'}, dimensions={0}, use_global_device_ids=true | all-gather | bytes 69632 | tf_op jit(solution)/shard_map/all_gather | solution.py:234
  83.4 1.0 constant_dynamic-update-slice_fusion.2
  84.6 14.6 %all-gather.2 = f32[128,128]{1,0:T(8,128)S(1)} all-gather(f32[8,128]{1,0:T(8,128)S(1)} %select_maximum_fusion.1), channel_id=4, replica_groups=mesh['tm'=32,'panel'=16] {'panel'}, dimensions={0}, use_global_device_ids=true | all-gather | bytes 69632 | tf_op jit(solution)/shard_map/all_gather | solution.py:234
  99.5 4.9 %shard_map.101.drows_ref = f32[32,512]{1,0:T(8,128)} custom-call(f32[16,224,512]{2,1,0:T(8,128)} %bitcast.30, f32[32,512]{1,0:T(8,128)} %a0_ref.1), custom_call_target="tpu_custom_call" | custom-call | flops 805306368 | bytes 7405568 | tf_op jit(solution)/shard_map/pallas_call | solution.py:217
  104.4 2.8 %collective-permute-start.6 = (f32[32,512]{1,0:T(8,128)}, f32[32,512]{1,0:T(8,128)S(1)}, u32[]{:S(2)}, u32[]{:S(2)}) collective-permute-start(f32[32,512]{1,0:T(8,128)} %shard_map.101.drows_ref), channel_id=1, source_target_pairs={{0,64},{16,80},{32,96},{48,112},{64,128},{80,144},{96,160},{112,17... | collective-permute-start | bytes 196616 | tf_op jit(solution)/shard_map/ppermute | solution.py:230
  107.2 7.8 %collective-permute-done.6 = f32[32,512]{1,0:T(8,128)S(1)} collective-permute-done((f32[32,512]{1,0:T(8,128)}, f32[32,512]{1,0:T(8,128)S(1)}, u32[]{:S(2)}, u32[]{:S(2)}) %collective-permute-start.6) | collective-permute-done | bytes 65568 | tf_op jit(solution)/shard_map/ppermute | solution.py:230
  115.8 3.1 %copy-done = f32[3584,512]{1,0:T(8,128)S(1)} copy-done((f32[3584,512]{1,0:T(8,128)S(1)}, f32[3584,512]{1,0:T(8,128)}, u32[]{:S(2)}) %copy-start) | copy-done | bytes 7340056
  118.8 8.8 %shard_map.102 = (f32[16,32,256]{2,1,0:T(8,128)}, bf16[2,512,512]{2,1,0:T(8,128)(2,1)S(1)}, bf16[2,512,512]{2,1,0:T(8,128)(2,1)S(1)}, bf16[2,512,512]{2,1,0:T(8,...) custom-call(f32[16,224,512]{2,1,0:T(8,128)S(1)} %bitcast.31, ...), custom_call_target="tpu_custom_call" | custom-call | flops 4831838208 | bytes 7766016 | tf_op jit(solution)/shard_map/pallas_call | solution.py:217
  127.6 1.0 copy-done.15
  128.6 1.0 copy-done.17
  129.6 5.7 %all-to-all-start = ((f32[16,32,256]{2,1,0:T(8,128)}), f32[16,32,256]{2,1,0:T(8,128)S(1)}, u32[]{:S(2)}, u32[]{:S(2)}) async-start(f32[16,32,256]{2,1,0:T(8,128)} %get-tuple-element.44), calls=%async_computation | async-start | bytes 1048576 | tf_op jit(solution)/shard_map/all_to_all | solution.py:238
  135.4 3.2 %copy-done.1 = f32[3584,512]{1,0:T(8,128)S(1)} copy-done((f32[3584,512]{1,0:T(8,128)S(1)}, f32[3584,512]{1,0:T(8,128)}, u32[]{:S(2)}) %copy-start.1) | copy-done | bytes 7340056
  138.5 1.2 copy-done.16
  139.7 1.2 copy-done.18
  141.0 5.6 %shard_map.103 = (bf16[2,512,512]{2,1,0:T(8,128)(2,1)S(1)}, bf16[2,512,512]{2,1,0:T(8,128)(2,1)S(1)}, bf16[2,512,512]{2,1,0:T(8,128)(2,1)S(1)}, bf16[2,512,512]{2,1,0:T(8,128)(2,1)S(1)}, bf16[2,512,512]{2,1,0:T(8,128)(2,1)S(1)}) custom-call(f32[16,224,512]{2,1,0:T(8,128)S(1)} %bitcast.32, bf16[2,512,512]{2,1,0:T(8,128)(2,1)S(1)} %copy-done.16, ...), custom_call_target="tpu_custom_call" | custom-call | flops 4026531840 | bytes 9437184 | tf_op jit(solution)/shard_map/pallas_call | solution.py:217
  146.6 1.0 copy-done.2
  147.6 1.0 copy-done.4
  148.5 1.0 copy-done.6
  149.5 1.0 copy-done.8
  150.5 1.0 copy-done.12
  151.5 4.7 %all-to-all-done = f32[16,32,256]{2,1,0:T(8,128)S(1)} async-done(((f32[16,32,256]{2,1,0:T(8,128)}), f32[16,32,256]{2,1,0:T(8,128)S(1)}, u32[]{:S(2)}, u32[]{:S(2)}) %all-to-all-start) | async-done | bytes 524320 | tf_op jit(solution)/shard_map/all_to_all | solution.py:238
  156.2 1.2 copy-done.3
  157.4 1.2 copy-done.5
  158.6 1.2 copy-done.7
  159.9 1.2 copy-done.9
  161.1 2.6 %shard_map.104.state_ref = f32[72,512]{1,0:T(8,128)S(1)} custom-call(f32[512,256]{1,0:T(8,128)S(1)} %bitcast.33, f32[64,512]{1,0:T(8,128)S(1)} %pad_maximum_fusion.3.own_ref, f32[8,512]{1,0:T(8,128)S(1)} %get-tuple-element.45.vec_ref, bf16[2,512,512]{2,1,0:T(8,128)(2,1)S(1)} %get-tuple-element.46.p0_ref, bf16[2,512,512]{2,1,0:T(8,128)(2,1)S(1)} %get-tuple-element.47.p0p_ref, ...), custom_call_target="tpu_custom_call" | custom-call | flops 805306368 | bytes 6963200 | tf_op jit(solution)/shard_map/pallas_call | solution.py:217
  163.7 1.9 collective-permute-start.7
  165.7 1.6 copy-done.11
  167.3 1.2 copy-done.13
  168.5 1.7 shard_map.105
  170.2 8.0 %collective-permute-done.7.prior_ref = f32[72,512]{1,0:T(8,128)S(1)} collective-permute-done((f32[72,512]{1,0:T(8,128)S(1)}, f32[72,512]{1,0:T(8,128)S(1)}, u32[]{:S(2)}, u32[]{:S(2)}) %collective-permute-start.7) | collective-permute-done | bytes 147488 | tf_op jit(solution)/shard_map/ppermute | solution.py:230
  178.2 1.3 shard_map.106
  179.5 5.0 %all-to-all-start.1 = ((f32[16,32,128]{2,1,0:T(8,128)}), f32[16,32,128]{2,1,0:T(8,128)S(1)}, u32[]{:S(2)}, u32[]{:S(2)}) async-start(f32[16,32,128]{2,1,0:T(8,128)} %shard_map.106), calls=%async_computation.1 | async-start | bytes 524288 | tf_op jit(solution)/shard_map/all_to_all | solution.py:238
  184.8 11.4 %all-to-all-done.1 = f32[16,32,128]{2,1,0:T(8,128)S(1)} async-done(((f32[16,32,128]{2,1,0:T(8,128)}), f32[16,32,128]{2,1,0:T(8,128)S(1)}, u32[]{:S(2)}, u32[]{:S(2)}) %all-to-all-start.1) | async-done | bytes 262176 | tf_op jit(solution)/shard_map/all_to_all | solution.py:238
  196.2 1.2 copy-done.14
  197.4 1.2 shard_map.107
  (75 shorter events, 8.9 us)
Async XLA Ops:
  7.2 92.3 %all-gather.7.cloned.1.call-start = ((), (), s32[]{:S(2)}) async-start(), calls=%async_computation.2 | async-start | bytes 7798784 | tf_op jit(solution)/shard_map/all_gather | solution.py:234
  9.0 17.4 %collective-permute-start.1 = (f32[64,512]{1,0:T(8,128)S(1)}, f32[64,512]{1,0:T(8,128)S(1)}, u32[]{:S(2)}, u32[]{:S(2)}) collective-permute-start(f32[64,512]{1,0:T(8,128)S(1)} %pad_maximum_fusion.1), channel_id=1, source_target_pairs={{0,32},{16,48},{32,64},{48,80},{64,96},{80,112},{96,128},{112,144}... | collective-permute-start | bytes 393224 | tf_op jit(solution)/shard_map/ppermute | solution.py:230
  13.2 10.3 %collective-permute-start = (f32[32,512]{1,0:T(8,128)}, f32[32,512]{1,0:T(8,128)S(1)}, u32[]{:S(2)}, u32[]{:S(2)}) collective-permute-start(f32[32,512]{1,0:T(8,128)} %a0_ref.1), channel_id=1, source_target_pairs={{0,16},{16,32},{32,48},{48,64},{64,80},{80,96},{96,112},{112,128},... | collective-permute-start | bytes 196616 | tf_op jit(solution)/shard_map/ppermute | solution.py:230
  16.4 9.9 %collective-permute-start.2 = (f32[32,512]{1,0:T(8,128)}, f32[32,512]{1,0:T(8,128)S(1)}, u32[]{:S(2)}, u32[]{:S(2)}) collective-permute-start(f32[32,512]{1,0:T(8,128)} %a0_ref.1), channel_id=1, source_target_pairs={{0,48},{16,64},{32,80},{48,96},{64,112},{80,128},{96,144},{112,160... | collective-permute-start | bytes 196616 | tf_op jit(solution)/shard_map/ppermute | solution.py:230
  28.6 0.8 copy-start.19
  29.4 136.3 %all-gather.9.cloned.1.call-start = ((), (), s32[]{:S(2)}) async-start(), calls=%async_computation.3 | async-start | bytes 2228224 | tf_op jit(solution)/shard_map/all_gather | solution.py:234
  31.0 11.6 %collective-permute-start.3 = (f32[72,512]{1,0:T(8,128)S(1)}, f32[72,512]{1,0:T(8,128)S(1)}, u32[]{:S(2)}, u32[]{:S(2)}) collective-permute-start(f32[72,512]{1,0:T(8,128)S(1)} %pad_maximum_fusion), channel_id=1, source_target_pairs={{0,16},{16,32},{32,48},{48,64},{64,80},{80,96},{96,112},{112,128},... | collective-permute-start | bytes 442376 | tf_op jit(solution)/shard_map/ppermute | solution.py:230
  36.7 15.0 %collective-permute-start.4 = (f32[72,512]{1,0:T(8,128)S(1)}, f32[72,512]{1,0:T(8,128)S(1)}, u32[]{:S(2)}, u32[]{:S(2)}) collective-permute-start(f32[72,512]{1,0:T(8,128)S(1)} %pad_maximum_fusion), channel_id=1, source_target_pairs={{0,32},{16,48},{32,64},{48,80},{64,96},{80,112},{96,128},{112,144}... | collective-permute-start | bytes 442376 | tf_op jit(solution)/shard_map/ppermute | solution.py:230
  38.6 14.4 %collective-permute-start.5 = (f32[72,512]{1,0:T(8,128)S(1)}, f32[72,512]{1,0:T(8,128)S(1)}, u32[]{:S(2)}, u32[]{:S(2)}) collective-permute-start(f32[72,512]{1,0:T(8,128)S(1)} %pad_maximum_fusion), channel_id=1, source_target_pairs={{0,48},{16,64},{32,80},{48,96},{64,112},{80,128},{96,144},{112,160... | collective-permute-start | bytes 442376 | tf_op jit(solution)/shard_map/ppermute | solution.py:230
  104.4 10.6 %collective-permute-start.6 = (f32[32,512]{1,0:T(8,128)}, f32[32,512]{1,0:T(8,128)S(1)}, u32[]{:S(2)}, u32[]{:S(2)}) collective-permute-start(f32[32,512]{1,0:T(8,128)} %shard_map.101.drows_ref), channel_id=1, source_target_pairs={{0,64},{16,80},{32,96},{48,112},{64,128},{80,144},{96,160},{112,17... | collective-permute-start | bytes 196616 | tf_op jit(solution)/shard_map/ppermute | solution.py:230
  115.7 3.1 %copy-start = (f32[3584,512]{1,0:T(8,128)S(1)}, f32[3584,512]{1,0:T(8,128)}, u32[]{:S(2)}) copy-start(f32[3584,512]{1,0:T(8,128)} %all-gather.7.cloned.1.call-done) | copy-start | bytes 22020100
  118.8 16.5 %copy-start.20 = (f32[32,512]{1,0:T(8,128)S(1)}, f32[32,512]{1,0:T(8,128)}, u32[]{:S(2)}) copy-start(f32[32,512]{1,0:T(8,128)} %param.8) | copy-start | bytes 196612
  127.6 1.0 copy-start.15
  128.6 1.0 copy-start.17
  129.6 26.6 %all-to-all-start = ((f32[16,32,256]{2,1,0:T(8,128)}), f32[16,32,256]{2,1,0:T(8,128)S(1)}, u32[]{:S(2)}, u32[]{:S(2)}) async-start(f32[16,32,256]{2,1,0:T(8,128)} %get-tuple-element.44), calls=%async_computation | async-start | bytes 1048576 | tf_op jit(solution)/shard_map/all_to_all | solution.py:238
  135.3 3.2 %copy-start.1 = (f32[3584,512]{1,0:T(8,128)S(1)}, f32[3584,512]{1,0:T(8,128)}, u32[]{:S(2)}) copy-start(f32[3584,512]{1,0:T(8,128)} %all-gather.7.cloned.1.call-done) | copy-start | bytes 22020100
  138.5 1.2 copy-start.16
  139.7 1.2 copy-start.18
  141.0 24.7 %copy-start.10 = (f32[32,512]{1,0:T(8,128)S(1)}, f32[32,512]{1,0:T(8,128)}, u32[]{:S(2)}) copy-start(f32[32,512]{1,0:T(8,128)} %shard_map.101.drows_ref) | copy-start | bytes 196612
  146.6 1.0 copy-start.2
  147.6 1.0 copy-start.4
  148.5 1.0 copy-start.6
  149.5 1.0 copy-start.8
  150.5 1.0 copy-start.12
  156.2 1.2 copy-start.3
  157.4 1.2 copy-start.5
  158.6 1.2 copy-start.7
  159.9 1.2 copy-start.9
  163.7 14.5 %collective-permute-start.7 = (f32[72,512]{1,0:T(8,128)S(1)}, f32[72,512]{1,0:T(8,128)S(1)}, u32[]{:S(2)}, u32[]{:S(2)}) collective-permute-start(f32[72,512]{1,0:T(8,128)S(1)} %shard_map.104.state_ref), channel_id=1, source_target_pairs={{0,64},{16,80},{32,96},{48,112},{64,128},{80,144},{96,160},{112,17... | collective-permute-start | bytes 442376 | tf_op jit(solution)/shard_map/ppermute | solution.py:230
  165.7 1.6 copy-start.11
  167.3 1.2 copy-start.13
  179.5 16.7 %all-to-all-start.1 = ((f32[16,32,128]{2,1,0:T(8,128)}), f32[16,32,128]{2,1,0:T(8,128)S(1)}, u32[]{:S(2)}, u32[]{:S(2)}) async-start(f32[16,32,128]{2,1,0:T(8,128)} %shard_map.106), calls=%async_computation.1 | async-start | bytes 524288 | tf_op jit(solution)/shard_map/all_to_all | solution.py:238
  196.2 1.2 copy-start.14
Sparse Core Ops, SparseCore 0:
  29.5 59.9 all-gather.6
  115.9 44.0 all-gather.8

commit v5 on v3

v5 whole, which is shorter than its diff:
```python
import functools

import jax
import jax.numpy as jnp
from jax import lax
from jax.experimental import pallas as pl
from jax.experimental.pallas import tpu as pltpu
from jax.sharding import PartitionSpec as P

F32, BF16 = jnp.float32, jnp.bfloat16
IN_VMEM = pl.BlockSpec(memory_space=pltpu.VMEM)
IN_PLACE = pl.BlockSpec(memory_space=pl.ANY)


def split(x):
    high = x.astype(BF16)
    return high, (x - high.astype(F32)).astype(BF16)


def product(left, right, over):
    def one(x, y):
        return lax.dot_general(x, y, (over, ((), ())), preferred_element_type=F32)

    count = left[0].shape[0]
    if count <= 128:
        both = one(jnp.concatenate(left), right[0])
        return both[:count] + (both[count:] + one(left[0], right[1]))
    return one(left[0], right[0]) + (one(left[1], right[0]) + one(left[0], right[1]))


def dot(left, right):
    return product(left, right, ((1,), (0,)))


def dot_nt(left, right):
    return product(left, right, ((1,), (1,)))


def stacked(*parts):
    return jnp.concatenate(parts)


def sixteen(*rows):
    room = jnp.zeros((16 - len(rows), rows[0].shape[1]), F32)
    return jnp.concatenate([*rows, room])


def rowwise(matrix, row):
    return jnp.sum(matrix * row, axis=1, keepdims=True)


def in_lanes(columns, rows, lanes):
    lane = lax.broadcasted_iota(jnp.int32, (rows, lanes), 1)
    total = jnp.zeros((rows, lanes), F32)
    for i, column in enumerate(columns):
        total = jnp.where(lane == i, column, total)
    return total


def pack(slices, packed_ref, rows):
    for i, whole in enumerate(slices):
        for peer in range(packed_ref.shape[0]):
            packed_ref[peer, :, i * rows : (i + 1) * rows] = whole[:, peer * rows : (peer + 1) * rows]


class Fetch:
    def __init__(self, sources, buffers, sems):
        self.copies = [pltpu.make_async_copy(s, b, sems.at[i]) for i, (s, b) in enumerate(zip(sources, buffers))]
        self.buffers = buffers
        for copy in self.copies:
            copy.start()

    def __call__(self, i):
        self.copies[i].wait()
        value = self.buffers[i][...]
        return value


def fetch_parts(stack_ref, order, rows, buf, sems):
    sources = [stack_ref.at[:, pl.ds(i * rows, rows), :] for i in order]
    fetch = Fetch(sources, [buf.at[k] for k in range(len(order))], sems)
    width = stack_ref.shape[2]
    return lambda k: split(fetch(k).reshape(width, width))


class Store:
    def __init__(self, refs, buffers, sems):
        self.refs, self.buffers, self.sems = refs, buffers, sems
        self.copies = []

    def __call__(self, pair):
        i = len(self.copies)
        self.buffers[i, 0], self.buffers[i, 1] = pair
        copy = pltpu.make_async_copy(self.buffers.at[i], self.refs[i], self.sems.at[i])
        copy.start()
        self.copies.append(copy)
        return pair

    def finish(self):
        for copy in self.copies:
            copy.wait()


def fetch_pairs(refs, buf, sems):
    fetch = Fetch(refs, [buf.at[k] for k in range(len(refs))], sems)

    def pair(k):
        both = fetch(k)
        return both[0], both[1]

    return pair


def first_kernel(
    rows, whole_ref, own_ref, vec_ref, u_ref, packed_ref, vout_ref, p0_ref, bw_ref, p0p_ref, bp_ref, buf, sems, out, outs
):
    part = fetch_parts(whole_ref, (0, 4, 1, 2, 5, 3), rows, buf, sems)
    store = Store((p0_ref, bw_ref, p0p_ref, bp_ref), out, outs)
    width = whole_ref.shape[2]
    c1, c2, c3, j0, j1, j2 = (own_ref[i * rows : (i + 1) * rows] for i in range(6))
    b0, e0, b1, e1, b2, e2, b3, e3 = (vec_ref[i : i + 1] for i in range(8))
    u1, u2, u3, u4 = (u_ref[i : i + 1] for i in range(4))

    a0, m0 = part(0), part(1)
    p0 = store(split(dot(a0, m0)))
    mixed = dot(split(sixteen(e0 - u2)), m0)
    a1 = part(2)
    bw = store(split(dot(p0, a1)))
    both = dot(split(stacked(j0, mixed)), a1)
    y0, e_t = both[:rows], both[rows : rows + 1] + e1
    a2, m0p = part(3), part(4)
    p0p = store(split(dot(a2, m0p)))
    mixed = dot(split(sixteen(e2 - u4)), m0p)
    a3 = part(5)
    bp = store(split(dot(p0p, a3)))
    both = dot(split(stacked(j2, mixed)), a3)
    y2, e_p = both[:rows], both[rows : rows + 1] + e3
    b_t = dot_nt(split(sixteen(b1 + u1)), p0)[:1] + b0
    b_p = dot_nt(split(sixteen(b3 + u3)), p0p)[:1] + b2
    w1 = rowwise(c3, dot(split(sixteen(e_t)), a2)[:1])
    w2 = rowwise(c2, e_t)
    w3 = rowwise(j0, dot_nt(split(sixteen(b_p)), a1)[:1])
    w4 = rowwise(j1, b_p)
    x1 = dot_nt(split(c1), a0)
    right = dot_nt(split(stacked(dot_nt(split(c3), a2), c2)), bw)
    x3, x2 = right[:rows], right[rows:]
    right = dot(split(stacked(y0, j1)), bp)
    y0, y1 = right[:rows], right[rows:]
    pack((x1, x2, x3, y0, y1, y2), packed_ref, rows)
    extra = in_lanes((w1, w2, w3, w4), rows, 2 * rows)
    for peer in range(packed_ref.shape[0]):
        packed_ref[peer, :, 6 * rows :] = extra
    vout_ref[...] = jnp.concatenate([b_t, e_t, b_p, e_p, jnp.zeros((4, width), F32)])
    store.finish()


def middle_kernel(
    rows, whole_ref, eye_ref, bw_ref, bp_ref, drows_ref, p2rows_ref, p1_ref, d_ref, p2_ref, m2_ref, g1_ref, g0_ref,
    g0p_ref, buf, sems, pairs, pair_sems, out, outs
):
    part = fetch_parts(whole_ref, (6, 7, 4, 1, 5, 3), rows, buf, sems)
    pair = fetch_pairs((bw_ref, bp_ref), pairs, pair_sems)
    store = Store((p1_ref, d_ref, p2_ref, m2_ref, g1_ref, g0_ref, g0p_ref), out, outs)
    m1, bw = part(0), pair(0)
    p1 = store(split(dot(bw, m1)))
    bp = pair(1)
    d = store(split(dot(p1, bp)))
    drows = dot(split(eye_ref[...]), d)
    drows_ref[...] = drows
    m2 = part(1)
    p2rows_ref[...] = dot(split(drows), m2)
    store(split(dot(d, m2)))
    store(m2)
    store(split(dot(m1, bp)))
    store(split(dot(part(2), part(3))))
    store(split(dot(part(4), part(5))))
    store.finish()


def second_kernel(
    rows, received_ref, own_ref, vec_ref, p0p_ref, p0_ref, g0_ref, g0p_ref, p1_ref, g1_ref, m2_ref, plus_ref, minus_ref,
    state_ref, buf, sems
):
    pair = fetch_pairs((p0p_ref, p0_ref, g0_ref, g0p_ref, p1_ref, g1_ref, m2_ref), buf, sems)
    columns = received_ref[...].T
    x1, x2, x3, y0, y1, y2 = (columns[i * rows : (i + 1) * rows] for i in range(6))
    w1, w2, w3, w4 = (columns[6 * rows + i : 6 * rows + i + 1] for i in range(4))
    b_t, e_t, b_p, e_p = (vec_ref[i : i + 1] for i in range(4))
    c0, j3 = own_ref[:rows], own_ref[rows:]
    inner = dot_nt(split(stacked(x3, sixteen(w1))), pair(0)) + stacked(x2, sixteen(b_p + w2))
    other = dot_nt(split(x1), pair(1)) + c0
    inner_j = dot(split(stacked(y0, sixteen(-w3))), pair(2)) + stacked(y1, sixteen(e_t - w4))
    other_j = dot(split(y2), pair(3)) + j3
    outer = dot_nt(split(inner), pair(4)) + stacked(other, sixteen(b_t))
    outer_j = dot(split(inner_j), pair(5)) + stacked(other_j, sixteen(e_p))
    plus_ref[...] = outer[: rows + 8]
    state_ref[...] = outer_j[: rows + 8]
    minus_ref[...] = dot(split(outer_j), pair(6))[: rows + 8]


def third_kernel(
    rows, prior_ref, later_ref, later_p2_ref, plus_ref, state_ref, p2_ref, d_ref, packed_ref, a_ref, row_ref, buf, sems
):
    pair = fetch_pairs((p2_ref, d_ref), buf, sems)
    v = dot_nt(split(prior_ref[:rows]), pair(0))
    both = dot(split(stacked(later_ref[:rows], later_p2_ref[...], sixteen(later_ref[rows : rows + 1]))), pair(1))
    pack((v, plus_ref[:rows], both[:rows], state_ref[:rows]), packed_ref, rows)
    a_ref[...] = both[rows : 2 * rows]
    row_ref[...] = both[2 * rows : 2 * rows + 8]


def last_kernel(
    rows, received_ref, p2rows_ref, prior_ref, plus_ref, state_ref, part_ref, d_ref, new_c_ref, back_ref, j_ref, b_ref,
    buf, sems
):
    pair = fetch_pairs((d_ref,), buf, sems)
    back = received_ref[...].T
    v, c_rows, z, j_rows = (back[i * rows : (i + 1) * rows] for i in range(4))
    d = pair(0)
    back_ref[:rows] = dot(split(z), d) + j_rows
    j_ref[...] = j_rows
    later_e = part_ref[:, 1:2] - rowwise(z, plus_ref[rows : rows + 1])
    row = in_lanes((later_e,), rows, 128).T[:8]
    back_ref[rows:] = jnp.concatenate([row, jnp.zeros((8, back_ref.shape[1] - rows), F32)], axis=1)
    new_c_ref[...] = dot_nt(split(v), d) + c_rows
    new_b = part_ref[:, 0:1] + rowwise(p2rows_ref[...], prior_ref[rows : rows + 1])
    b_ref[...] = in_lanes((new_b + rowwise(v, state_ref[rows : rows + 1]),), rows, 128)


def call(kernel, rows, operands, outs, placed=(), kept=(), scratch=(), flops=0, grant=58):
    nbytes = sum(x.size * x.dtype.itemsize for x in operands)
    specs = [IN_PLACE if i in placed else IN_VMEM for i in range(len(operands))]
    return pl.pallas_call(
        functools.partial(kernel, rows),
        out_shape=[jax.ShapeDtypeStruct(shape, dtype) for shape, dtype in outs],
        in_specs=specs,
        out_specs=[IN_PLACE if i in kept else IN_VMEM for i in range(len(outs))],
        scratch_shapes=scratch,
        compiler_params=pltpu.CompilerParams(vmem_limit_bytes=grant * 2**20),
        cost_estimate=pl.CostEstimate(flops=flops, bytes_accessed=nbytes, transcendentals=0),
    )(*operands)


def passed_along(shard, by):
    peers = lax.axis_size("tm")
    return lax.ppermute(shard, "tm", [(i, i + by) for i in range(peers) if 0 <= i + by < peers])


def gathered(shard):
    return lax.all_gather(shard, "panel", axis=0, tiled=False)


def exchanged(packed):
    return lax.all_to_all(packed, "panel", split_axis=0, concat_axis=0, tiled=True).reshape(-1, packed.shape[2])


def whole_vectors(slices):
    count, rows = slices.shape
    whole = gathered(jnp.pad(slices, ((0, 8 - count), (0, 128 - rows))))[:, :, :rows]
    return whole.transpose(1, 0, 2).reshape(8, -1)


def local(transition, offset, covariance, info_vector, information, inverses):
    rows, width = transition.shape
    peers = lax.axis_size("panel")
    time = lax.axis_index("tm")
    mine = lax.axis_index("panel")
    row = lax.broadcasted_iota(jnp.int32, (rows, width), 0) + mine * rows
    eye = (row == lax.broadcasted_iota(jnp.int32, (rows, width), 1)).astype(F32)

    def present(shard, since):
        return jnp.where(time >= since, shard, eye)

    a0, c0, j0 = transition, covariance, information
    m0, m1, m2 = present(inverses[0], 1), present(inverses[1], 2), present(inverses[2], 4)

    sent = passed_along(a0, 1), passed_along(jnp.concatenate([a0, m0]), 2), passed_along(a0, 3)
    a1, late, a3 = lax.optimization_barrier(sent)
    a1, a2, m0p, a3 = present(a1, 1), present(late[:rows], 2), present(late[rows:], 2), present(a3, 3)
    ready = jnp.concatenate([a0, a1, a2, a3, m0, m0p, m1, m2])
    whole = gathered(ready)

    v0 = jnp.stack([offset, info_vector])
    own = jnp.concatenate([c0, j0, jnp.pad(v0, ((0, 6), (0, width - rows)))])
    own, _ = lax.optimization_barrier((own, ready))
    got = lax.optimization_barrier(tuple(passed_along(own, by) for by in (1, 2, 3)))
    (c1, c2, c3), (j1, j2, j3) = ([g[i * rows : (i + 1) * rows] for g in got] for i in range(2))
    vectors = whole_vectors(jnp.concatenate([v0] + [g[2 * rows : 2 * rows + 2, :rows] for g in got]))
    b0, e0, b1, e1, b2, e2, b3, e3 = vectors

    def along(matrix, vector):
        return jnp.sum(matrix * vector[None, :], axis=1)

    u = whole_vectors(jnp.stack([along(c1, e0), along(j0, b1), along(c3, e2), along(j2, b3)]))

    whole, vectors, u = lax.optimization_barrier((whole, vectors, u))

    square, pair = (width, width), ((2, width, width), BF16)
    mults = 6 * width**3

    def stage(parts):
        return [pltpu.VMEM((parts, peers, rows, width), F32), pltpu.SemaphoreType.DMA((parts,))]

    def pairs(count):
        return [pltpu.VMEM((count, 2, *square), BF16), pltpu.SemaphoreType.DMA((count,))]

    def flat(extra=0):
        return ((rows + extra, width), F32)

    packed, vec, p0, bw, p0p, bp = call(
        first_kernel,
        rows,
        (whole, jnp.concatenate([c1, c2, c3, j0, j1, j2]), vectors, u),
        [((peers, rows, 8 * rows), F32), ((8, width), F32)] + [pair] * 4,
        {0},
        range(2, 6),
        stage(6) + pairs(4),
        flops=6 * mults,
    )
    received = exchanged(packed)
    drows, p2rows, p1, d, p2, m2w, g1, g0, g0p = call(
        middle_kernel,
        rows,
        (whole, eye, bw, bp),
        [flat(), flat()] + [pair] * 7,
        {0, 2, 3},
        range(2, 9),
        stage(6) + pairs(2) + pairs(7),
        flops=6 * mults,
    )
    later_p2 = passed_along(p2rows, -4)
    plus, minus, state = call(
        second_kernel,
        rows,
        (received, jnp.concatenate([c0, j3]), vec, p0p, p0, g0, g0p, p1, g1, m2w),
        [flat(8)] * 3,
        range(3, 10),
        (),
        pairs(7),
        flops=mults,
    )

    prior, later = passed_along(plus, 4), passed_along(minus, -4)
    packed, later_a, row = call(
        third_kernel,
        rows,
        (prior, later, later_p2, plus, state, p2, d),
        [((peers, rows, 4 * rows), F32), flat(), ((8, width), F32)],
        {5, 6},
        (),
        pairs(2),
        flops=mults,
    )
    back = exchanged(packed)
    new_a = passed_along(later_a, 4)

    def own_part(vector):
        return lax.dynamic_slice_in_dim(vector, mine * rows, rows, 0)

    own_e = own_part(state[rows])
    parts = jnp.stack([own_part(plus[rows]), own_part(row[0]) + own_e], axis=1)
    parts = jnp.pad(parts, ((0, 0), (0, 126)))
    new_c, later_j, own_j, new_b = call(
        last_kernel,
        rows,
        (back, p2rows, prior, plus, state, parts, d),
        [flat(), flat(8), flat(), ((rows, 128), F32)],
        {6},
        (),
        pairs(1),
        flops=mults,
    )
    new_j = passed_along(later_j, 4)
    changed = time >= 4
    return (
        jnp.where(changed, new_a, drows),
        new_b[:, 0],
        new_c,
        jnp.where(changed, new_j[rows, :rows], own_e),
        jnp.where(changed, new_j[:rows], own_j),
    )


def solution(mesh):
    matrix = P(("tm", "panel"), None)
    vector = P(("tm", "panel"))
    return jax.shard_map(
        local,
        mesh=mesh,
        in_specs=(matrix, vector, matrix, vector, matrix, P(None, ("tm", "panel"), None)),
        out_specs=(matrix, vector, matrix, vector, matrix),
        check_vma=False,
    )
```

time: 251 us -> 210 us (0.84)
  the two profiles are of different devices: /device:TPU:7 before, /device:TPU:4 now
where the time goes in v5:
time: 210 us; the launch traced here: 208 us
  waiting for transfers between devices  50.1 us (24%)
  starting transfers between devices  48.5 us (23%)
  blocking collectives  38.1 us (18%)
  Pallas kernels  35.5 us (17%)
  between operations  14.3 us (7%)
  other arithmetic  11 us (5%)
  local copies, waits for them, and re-layouts  10.7 us (5%)
    ppermute x11, waiting for transfers between devices, passed_along(): lax.ppermute(shard, 'tm', [(i, i + by) for i in range(peers) if 0 <= i +...  47.9 us
    ppermute x11, starting transfers between devices, passed_along(): lax.ppermute(shard, 'tm', [(i, i + by) for i in range(peers) if 0 <= i +...  40.7 us
    all_gather x2, blocking collectives, gathered(): return lax.all_gather(shard, 'panel', axis=0, tiled=False)  38.1 us
    pallas_call x5, Pallas kernels, call(): pl.pallas_call(functools.partial(kernel, rows), out_shape=[jax.ShapeDtype...  35.5 us
    all_to_all x2, starting transfers between devices, exchanged(): lax.all_to_all(packed, 'panel', split_axis=0, concat_axis=0, tiled=True)  7.77 us
  transfers between devices with their start and end apart: 14, of which 8 were waited for; matrix products, arithmetic and copies ran while one was open for 6% of the time, Pallas kernels for 6%

profile of v5, /device:TPU:4, one launch (start us, length us, event | category | flops | bytes accessed | tf_op | source)
XLA Modules:
  0.0 208.4 jit_solution(10198292654888314362)
XLA Ops:
  7.2 0.9 convert_select_fusion.6
  8.2 0.8 pad_maximum_fusion.1
  9.0 4.5 %collective-permute-start.1 = (f32[64,512]{1,0:T(8,128)S(1)}, f32[64,512]{1,0:T(8,128)S(1)}, u32[]{:S(2)}, u32[]{:S(2)}) collective-permute-start(f32[64,512]{1,0:T(8,128)S(1)} %pad_maximum_fusion.1), channel_id=1, source_target_pairs={{0,32},{16,48},{32,64},{48,80},{64,96},{80,112},{96,128},{112,144}... | collective-permute-start | bytes 393224 | tf_op jit(solution)/shard_map/ppermute | solution.py:246
  13.5 3.5 %collective-permute-start = (f32[32,512]{1,0:T(8,128)}, f32[32,512]{1,0:T(8,128)S(1)}, u32[]{:S(2)}, u32[]{:S(2)}) collective-permute-start(f32[32,512]{1,0:T(8,128)} %param.6), channel_id=1, source_target_pairs={{0,16},{16,32},{32,48},{48,64},{64,80},{80,96},{96,112},{112,128},... | collective-permute-start | bytes 196616 | tf_op jit(solution)/shard_map/ppermute | solution.py:246
  17.0 4.9 %collective-permute-start.2 = (f32[32,512]{1,0:T(8,128)}, f32[32,512]{1,0:T(8,128)S(1)}, u32[]{:S(2)}, u32[]{:S(2)}) collective-permute-start(f32[32,512]{1,0:T(8,128)} %param.6), channel_id=1, source_target_pairs={{0,48},{16,64},{32,80},{48,96},{64,112},{80,128},{96,144},{112,160... | collective-permute-start | bytes 196616 | tf_op jit(solution)/shard_map/ppermute | solution.py:246
  21.9 0.8 constant_dynamic-update-slice_fusion.1
  23.4 5.3 %collective-permute-done.2 = f32[32,512]{1,0:T(8,128)S(1)} collective-permute-done((f32[32,512]{1,0:T(8,128)}, f32[32,512]{1,0:T(8,128)S(1)}, u32[]{:S(2)}, u32[]{:S(2)}) %collective-permute-start.2) | collective-permute-done | bytes 65568 | tf_op jit(solution)/shard_map/ppermute | solution.py:246
  28.8 0.9 constant_dynamic-update-slice_fusion
  29.8 0.9 fusion.4
  30.8 0.9 fusion.5
  31.7 0.8 copy-done.1
  32.5 0.7 select_maximum_fusion
  33.2 0.9 pad_maximum_fusion
  34.1 3.9 %collective-permute-start.3 = (f32[72,512]{1,0:T(8,128)S(1)}, f32[72,512]{1,0:T(8,128)S(1)}, u32[]{:S(2)}, u32[]{:S(2)}) collective-permute-start(f32[72,512]{1,0:T(8,128)S(1)} %pad_maximum_fusion), channel_id=1, source_target_pairs={{0,16},{16,32},{32,48},{48,64},{64,80},{80,96},{96,112},{112,128},... | collective-permute-start | bytes 442376 | tf_op jit(solution)/shard_map/ppermute | solution.py:246
  38.0 3.4 %collective-permute-start.4 = (f32[72,512]{1,0:T(8,128)S(1)}, f32[72,512]{1,0:T(8,128)S(1)}, u32[]{:S(2)}, u32[]{:S(2)}) collective-permute-start(f32[72,512]{1,0:T(8,128)S(1)} %pad_maximum_fusion), channel_id=1, source_target_pairs={{0,32},{16,48},{32,64},{48,80},{64,96},{80,112},{96,128},{112,144}... | collective-permute-start | bytes 442376 | tf_op jit(solution)/shard_map/ppermute | solution.py:246
  41.4 3.7 %collective-permute-start.5 = (f32[72,512]{1,0:T(8,128)S(1)}, f32[72,512]{1,0:T(8,128)S(1)}, u32[]{:S(2)}, u32[]{:S(2)}) collective-permute-start(f32[72,512]{1,0:T(8,128)S(1)} %pad_maximum_fusion), channel_id=1, source_target_pairs={{0,48},{16,64},{32,80},{48,96},{64,112},{80,128},{96,144},{112,160... | collective-permute-start | bytes 442376 | tf_op jit(solution)/shard_map/ppermute | solution.py:246
  45.2 8.8 %collective-permute-done.4 = f32[72,512]{1,0:T(8,128)S(1)} collective-permute-done((f32[72,512]{1,0:T(8,128)S(1)}, f32[72,512]{1,0:T(8,128)S(1)}, u32[]{:S(2)}, u32[]{:S(2)}) %collective-permute-start.4) | collective-permute-done | bytes 147488 | tf_op jit(solution)/shard_map/ppermute | solution.py:246
  54.0 4.8 %collective-permute-done.5 = f32[72,512]{1,0:T(8,128)S(1)} collective-permute-done((f32[72,512]{1,0:T(8,128)S(1)}, f32[72,512]{1,0:T(8,128)S(1)}, u32[]{:S(2)}, u32[]{:S(2)}) %collective-permute-start.5) | collective-permute-done | bytes 147488 | tf_op jit(solution)/shard_map/ppermute | solution.py:246
  58.9 0.7 concatenate.22
  59.6 23.4 %all-gather.1 = f32[128,128]{1,0:T(8,128)S(1)} all-gather(f32[8,128]{1,0:T(8,128)S(1)} %pad.17), channel_id=3, replica_groups=mesh['tm'=32,'panel'=16] {'panel'}, dimensions={0}, use_global_device_ids=true | all-gather | bytes 69632 | tf_op jit(solution)/shard_map/all_gather | solution.py:250
  83.6 1.0 constant_dynamic-update-slice_fusion.2
  84.8 14.7 %all-gather.2 = f32[128,128]{1,0:T(8,128)S(1)} all-gather(f32[8,128]{1,0:T(8,128)S(1)} %select_maximum_fusion.1), channel_id=4, replica_groups=mesh['tm'=32,'panel'=16] {'panel'}, dimensions={0}, use_global_device_ids=true | all-gather | bytes 69632 | tf_op jit(solution)/shard_map/all_gather | solution.py:250
  99.5 0.7 reshape.55.u_ref
  100.2 0.7 reshape.54.vec_ref
  100.9 10.7 %shard_map.101 = (f32[16,32,256]{2,1,0:T(8,128)}, f32[8,512]{1,0:T(8,128)}, bf16[2,512,512]{2,1,0:T(8,128)(2,1)}, bf16[2,512,512]{2,1,0:T(8,128)(2,1)}, bf16[2,5...) custom-call(f32[16,256,512]{2,1,0:T(8,128)} %bitcast.44, f32[192,512]{1,0:T(8,128)} %copy-done.5, ...), custom_call_target="tpu_custom_call" | custom-call | flops 4831838208 | bytes 8814592 | tf_op jit(solution)/shard_map/pallas_call | solution.py:233
  111.6 3.8 %all-to-all-start = ((f32[16,32,256]{2,1,0:T(8,128)}), f32[16,32,256]{2,1,0:T(8,128)S(1)}, u32[]{:S(2)}, u32[]{:S(2)}) async-start(f32[16,32,256]{2,1,0:T(8,128)} %get-tuple-element.50), calls=%async_computation | async-start | bytes 1048576 | tf_op jit(solution)/shard_map/all_to_all | solution.py:254
  115.4 0.7 fusion.6.eye_ref
  116.1 0.7 pad_maximum_fusion.2.own_ref
  116.7 12.1 %shard_map.102 = (f32[32,512]{1,0:T(8,128)}, f32[32,512]{1,0:T(8,128)}, bf16[2,512,512]{2,1,0:T(8,128)(2,1)}, bf16[2,512,512]{2,1,0:T(8,128)(2,1)}, bf16[2,512,5...) custom-call(f32[16,256,512]{2,1,0:T(8,128)} %bitcast.45, ...), custom_call_target="tpu_custom_call" | custom-call | flops 4831838208 | bytes 10551296 | tf_op jit(solution)/shard_map/pallas_call | solution.py:233
  128.8 2.2 %all-to-all-done = f32[16,32,256]{2,1,0:T(8,128)S(1)} async-done(((f32[16,32,256]{2,1,0:T(8,128)}), f32[16,32,256]{2,1,0:T(8,128)S(1)}, u32[]{:S(2)}, u32[]{:S(2)}) %all-to-all-start) | async-done | bytes 524320 | tf_op jit(solution)/shard_map/all_to_all | solution.py:254
  131.1 0.8 copy-done
  131.9 5.3 %shard_map.103 = (f32[40,512]{1,0:T(8,128)}, f32[40,512]{1,0:T(8,128)}, f32[40,512]{1,0:T(8,128)}) custom-call(f32[512,256]{1,0:T(8,128)} %bitcast.31, f32[64,512]{1,0:T(8,128)} %pad_maximum_fusion.2.own_ref, f32[8,512]{1,0:T(8,128)} %get-tuple-element.51.vec_ref, bf16[2,512,512]{2,1,0:T(8,128)(2,1)} %get-tuple-element.52.p0p_ref, ...), custom_call_target="tpu_custom_call" | custom-call | flops 805306368 | bytes 8011776 | tf_op jit(solution)/shard_map/pallas_call | solution.py:233
  137.2 2.9 %collective-permute-start.6 = (f32[40,512]{1,0:T(8,128)}, f32[40,512]{1,0:T(8,128)S(1)}, u32[]{:S(2)}, u32[]{:S(2)}) collective-permute-start(f32[40,512]{1,0:T(8,128)} %get-tuple-element.61.plus_ref), channel_id=1, source_target_pairs={{0,64},{16,80},{32,96},{48,112},{64,128},{80,144},{96,160},{112,17... | collective-permute-start | bytes 245768 | tf_op jit(solution)/shard_map/ppermute | solution.py:246
  140.1 7.8 %collective-permute-start.7 = (f32[40,512]{1,0:T(8,128)}, f32[40,512]{1,0:T(8,128)S(1)}, u32[]{:S(2)}, u32[]{:S(2)}) collective-permute-start(f32[40,512]{1,0:T(8,128)} %get-tuple-element.62), channel_id=1, source_target_pairs={{64,0},{80,16},{96,32},{112,48},{128,64},{144,80},{160,96},{176,11... | collective-permute-start | bytes 245768 | tf_op jit(solution)/shard_map/ppermute | solution.py:246
  147.9 1.9 collective-permute-start.8
  149.8 0.7 slice.86
  150.5 10.1 %collective-permute-done.8.later_p2_ref = f32[32,512]{1,0:T(8,128)S(1)} collective-permute-done((f32[32,512]{1,0:T(8,128)}, f32[32,512]{1,0:T(8,128)S(1)}, u32[]{:S(2)}, u32[]{:S(2)}) %collective-permute-start.8) | collective-permute-done | bytes 65568 | tf_op jit(solution)/shard_map/ppermute | solution.py:246
  161.3 3.8 %shard_map.104 = (f32[16,32,128]{2,1,0:T(8,128)}, f32[32,512]{1,0:T(8,128)}, f32[8,512]{1,0:T(8,128)}) custom-call(f32[40,512]{1,0:T(8,128)} %copy-done.6, f32[40,512]{1,0:T(8,128)} %copy-done.7, f32[32,512]{1,0:T(8,128)} %copy-done.8, f32[40,512]{1,0:T(8,128)} %get-tuple-element.61.plus_ref, f32[40,512]{1,0:T(8,128)} %get-tuple-element.64.state_ref, ...), custom_call_target="tpu_custom_call" | custom-call | flops 805306368 | bytes 2490368 | tf_op jit(solution)/shard_map/pallas_call | solution.py:233
  165.2 4.0 %all-to-all-start.1 = ((f32[16,32,128]{2,1,0:T(8,128)}), f32[16,32,128]{2,1,0:T(8,128)S(1)}, u32[]{:S(2)}, u32[]{:S(2)}) async-start(f32[16,32,128]{2,1,0:T(8,128)} %get-tuple-element.69), calls=%async_computation.1 | async-start | bytes 524288 | tf_op jit(solution)/shard_map/all_to_all | solution.py:254
  169.3 0.7 slice.88
  170.0 0.7 slice.87
  170.7 2.3 %collective-permute-start.9 = (f32[32,512]{1,0:T(8,128)}, f32[32,512]{1,0:T(8,128)S(1)}, u32[]{:S(2)}, u32[]{:S(2)}) collective-permute-start(f32[32,512]{1,0:T(8,128)} %get-tuple-element.67), channel_id=1, source_target_pairs={{0,64},{16,80},{32,96},{48,112},{64,128},{80,144},{96,160},{112,17... | collective-permute-start | bytes 196616 | tf_op jit(solution)/shard_map/ppermute | solution.py:246
  173.8 8.4 %collective-permute-done.9 = f32[32,512]{1,0:T(8,128)S(1)} collective-permute-done((f32[32,512]{1,0:T(8,128)}, f32[32,512]{1,0:T(8,128)S(1)}, u32[]{:S(2)}, u32[]{:S(2)}) %collective-permute-start.9) | collective-permute-done | bytes 65568 | tf_op jit(solution)/shard_map/ppermute | solution.py:246
  182.8 0.7 copy-done.2
  183.5 3.6 %shard_map.105 = (f32[32,512]{1,0:T(8,128)}, f32[40,512]{1,0:T(8,128)}, f32[32,512]{1,0:T(8,128)}, f32[32,128]{1,0:T(8,128)}) custom-call(f32[512,128]{1,0:T(8,128)} %bitcast.33, f32[32,512]{1,0:T(8,128)} %get-tuple-element.63.p2rows_ref, f32[40,512]{1,0:T(8,128)} %copy-done.6, f32[40,512]{1,0:T(8,128)} %get-tuple-element.61.plus_ref, ...), custom_call_target="tpu_custom_call" | custom-call | flops 805306368 | bytes 1638400 | tf_op jit(solution)/shard_map/pallas_call | solution.py:233
  187.1 1.9 collective-permute-start.10
  189.0 1.3 slice_reduce_fusion
  190.4 9.9 %collective-permute-done.10 = f32[40,512]{1,0:T(8,128)S(1)} collective-permute-done((f32[40,512]{1,0:T(8,128)}, f32[40,512]{1,0:T(8,128)S(1)}, u32[]{:S(2)}, u32[]{:S(2)}) %collective-permute-start.10) | collective-permute-done | bytes 81952 | tf_op jit(solution)/shard_map/ppermute | solution.py:246
  (55 shorter events, 5.2 us)
Async XLA Ops:
  7.2 93.7 %all-gather.5.cloned.1.call-start = ((), (), s32[]{:S(2)}) async-start(), calls=%async_computation.2 | async-start | bytes 8912896 | tf_op jit(solution)/shard_map/all_gather | solution.py:250
  9.0 19.6 %collective-permute-start.1 = (f32[64,512]{1,0:T(8,128)S(1)}, f32[64,512]{1,0:T(8,128)S(1)}, u32[]{:S(2)}, u32[]{:S(2)}) collective-permute-start(f32[64,512]{1,0:T(8,128)S(1)} %pad_maximum_fusion.1), channel_id=1, source_target_pairs={{0,32},{16,48},{32,64},{48,80},{64,96},{80,112},{96,128},{112,144}... | collective-permute-start | bytes 393224 | tf_op jit(solution)/shard_map/ppermute | solution.py:246
  13.5 9.8 %collective-permute-start = (f32[32,512]{1,0:T(8,128)}, f32[32,512]{1,0:T(8,128)S(1)}, u32[]{:S(2)}, u32[]{:S(2)}) collective-permute-start(f32[32,512]{1,0:T(8,128)} %param.6), channel_id=1, source_target_pairs={{0,16},{16,32},{32,48},{48,64},{64,80},{80,96},{96,112},{112,128},... | collective-permute-start | bytes 196616 | tf_op jit(solution)/shard_map/ppermute | solution.py:246
  17.0 11.6 %collective-permute-start.2 = (f32[32,512]{1,0:T(8,128)}, f32[32,512]{1,0:T(8,128)S(1)}, u32[]{:S(2)}, u32[]{:S(2)}) collective-permute-start(f32[32,512]{1,0:T(8,128)} %param.6), channel_id=1, source_target_pairs={{0,48},{16,64},{32,80},{48,96},{64,112},{80,128},{96,144},{112,160... | collective-permute-start | bytes 196616 | tf_op jit(solution)/shard_map/ppermute | solution.py:246
  31.7 0.8 copy-start.1
  34.1 11.1 %collective-permute-start.3 = (f32[72,512]{1,0:T(8,128)S(1)}, f32[72,512]{1,0:T(8,128)S(1)}, u32[]{:S(2)}, u32[]{:S(2)}) collective-permute-start(f32[72,512]{1,0:T(8,128)S(1)} %pad_maximum_fusion), channel_id=1, source_target_pairs={{0,16},{16,32},{32,48},{48,64},{64,80},{80,96},{96,112},{112,128},... | collective-permute-start | bytes 442376 | tf_op jit(solution)/shard_map/ppermute | solution.py:246
  38.0 16.0 %collective-permute-start.4 = (f32[72,512]{1,0:T(8,128)S(1)}, f32[72,512]{1,0:T(8,128)S(1)}, u32[]{:S(2)}, u32[]{:S(2)}) collective-permute-start(f32[72,512]{1,0:T(8,128)S(1)} %pad_maximum_fusion), channel_id=1, source_target_pairs={{0,32},{16,48},{32,64},{48,80},{64,96},{80,112},{96,128},{112,144}... | collective-permute-start | bytes 442376 | tf_op jit(solution)/shard_map/ppermute | solution.py:246
  41.4 17.4 %collective-permute-start.5 = (f32[72,512]{1,0:T(8,128)S(1)}, f32[72,512]{1,0:T(8,128)S(1)}, u32[]{:S(2)}, u32[]{:S(2)}) collective-permute-start(f32[72,512]{1,0:T(8,128)S(1)} %pad_maximum_fusion), channel_id=1, source_target_pairs={{0,48},{16,64},{32,80},{48,96},{64,112},{80,128},{96,144},{112,160... | collective-permute-start | bytes 442376 | tf_op jit(solution)/shard_map/ppermute | solution.py:246
  84.8 16.1 %copy-start.5 = (f32[192,512]{1,0:T(8,128)}, f32[192,512]{1,0:T(8,128)S(1)}, u32[]{:S(2)}) copy-start(f32[192,512]{1,0:T(8,128)S(1)} %get-tuple-element.82.own_ref) | copy-start | bytes 1179652
  100.9 15.2 %copy-start.3 = (f32[32,512]{1,0:T(8,128)S(1)}, f32[32,512]{1,0:T(8,128)}, u32[]{:S(2)}) copy-start(f32[32,512]{1,0:T(8,128)} %param.8) | copy-start | bytes 196612
  111.6 19.5 %all-to-all-start = ((f32[16,32,256]{2,1,0:T(8,128)}), f32[16,32,256]{2,1,0:T(8,128)S(1)}, u32[]{:S(2)}, u32[]{:S(2)}) async-start(f32[16,32,256]{2,1,0:T(8,128)} %get-tuple-element.50), calls=%async_computation | async-start | bytes 1048576 | tf_op jit(solution)/shard_map/all_to_all | solution.py:254
  128.8 53.3 %copy-start.4 = (f32[32,512]{1,0:T(8,128)S(1)}, f32[32,512]{1,0:T(8,128)}, u32[]{:S(2)}) copy-start(f32[32,512]{1,0:T(8,128)} %get-tuple-element.68) | copy-start | bytes 196612
  131.1 0.8 copy-start
  137.2 23.4 %collective-permute-start.6 = (f32[40,512]{1,0:T(8,128)}, f32[40,512]{1,0:T(8,128)S(1)}, u32[]{:S(2)}, u32[]{:S(2)}) collective-permute-start(f32[40,512]{1,0:T(8,128)} %get-tuple-element.61.plus_ref), channel_id=1, source_target_pairs={{0,64},{16,80},{32,96},{48,112},{64,128},{80,144},{96,160},{112,17... | collective-permute-start | bytes 245768 | tf_op jit(solution)/shard_map/ppermute | solution.py:246
  140.1 20.6 %collective-permute-start.7 = (f32[40,512]{1,0:T(8,128)}, f32[40,512]{1,0:T(8,128)S(1)}, u32[]{:S(2)}, u32[]{:S(2)}) collective-permute-start(f32[40,512]{1,0:T(8,128)} %get-tuple-element.62), channel_id=1, source_target_pairs={{64,0},{80,16},{96,32},{112,48},{128,64},{144,80},{160,96},{176,11... | collective-permute-start | bytes 245768 | tf_op jit(solution)/shard_map/ppermute | solution.py:246
  147.9 12.8 %collective-permute-start.8 = (f32[32,512]{1,0:T(8,128)}, f32[32,512]{1,0:T(8,128)S(1)}, u32[]{:S(2)}, u32[]{:S(2)}) collective-permute-start(f32[32,512]{1,0:T(8,128)} %get-tuple-element.63.p2rows_ref), channel_id=1, source_target_pairs={{64,0},{80,16},{96,32},{112,48},{128,64},{144,80},{160,96},{176,11... | collective-permute-start | bytes 196616 | tf_op jit(solution)/shard_map/ppermute | solution.py:246
  160.7 0.6 copy-start.8
  160.7 0.6 copy-start.6
  160.7 0.7 copy-start.7
  165.2 17.6 %all-to-all-start.1 = ((f32[16,32,128]{2,1,0:T(8,128)}), f32[16,32,128]{2,1,0:T(8,128)S(1)}, u32[]{:S(2)}, u32[]{:S(2)}) async-start(f32[16,32,128]{2,1,0:T(8,128)} %get-tuple-element.69), calls=%async_computation.1 | async-start | bytes 524288 | tf_op jit(solution)/shard_map/all_to_all | solution.py:254
  170.7 11.4 %collective-permute-start.9 = (f32[32,512]{1,0:T(8,128)}, f32[32,512]{1,0:T(8,128)S(1)}, u32[]{:S(2)}, u32[]{:S(2)}) collective-permute-start(f32[32,512]{1,0:T(8,128)} %get-tuple-element.67), channel_id=1, source_target_pairs={{0,64},{16,80},{32,96},{48,112},{64,128},{80,144},{96,160},{112,17... | collective-permute-start | bytes 196616 | tf_op jit(solution)/shard_map/ppermute | solution.py:246
  182.8 0.7 copy-start.2
  187.1 13.2 %collective-permute-start.10 = (f32[40,512]{1,0:T(8,128)}, f32[40,512]{1,0:T(8,128)S(1)}, u32[]{:S(2)}, u32[]{:S(2)}) collective-permute-start(f32[40,512]{1,0:T(8,128)} %get-tuple-element.73), channel_id=1, source_target_pairs={{0,64},{16,80},{32,96},{48,112},{64,128},{80,144},{96,160},{112,17... | collective-permute-start | bytes 245768 | tf_op jit(solution)/shard_map/ppermute | solution.py:246
Sparse Core Ops, SparseCore 0:
  32.7 62.4 all-gather.4

commit v6 on v5

--- a/solution.py
+++ b/solution.py
@@ -9,6 +9,7 @@
 
 F32, BF16 = jnp.float32, jnp.bfloat16
 IN_VMEM = pl.BlockSpec(memory_space=pltpu.VMEM)
+IN_SMEM = pl.BlockSpec(memory_space=pltpu.SMEM)
 IN_PLACE = pl.BlockSpec(memory_space=pl.ANY)
 
 
@@ -109,6 +110,25 @@
         return both[0], both[1]
 
     return pair
+
+
+def ready_kernel(rows, place_ref, a0_ref, a1_ref, late_ref, a3_ref, inverses_ref, ready_ref):
+    time, mine = place_ref[0], place_ref[1]
+    shape = a0_ref.shape
+    row = lax.broadcasted_iota(jnp.int32, shape, 0) + mine * rows
+    eye = (row == lax.broadcasted_iota(jnp.int32, shape, 1)).astype(F32)
+    parts = (
+        (a0_ref[...], 0),
+        (a1_ref[...], 1),
+        (late_ref[:rows], 2),
+        (a3_ref[...], 3),
+        (inverses_ref[0], 1),
+        (late_ref[rows:], 3),
+        (inverses_ref[1], 2),
+        (inverses_ref[2], 4),
+    )
+    for i, (value, since) in enumerate(parts):
+        ready_ref[i * rows : (i + 1) * rows] = jnp.where(time >= since, value, eye)
 
 
 def first_kernel(
@@ -155,33 +175,49 @@
 
 
 def middle_kernel(
-    rows, whole_ref, eye_ref, bw_ref, bp_ref, drows_ref, p2rows_ref, p1_ref, d_ref, p2_ref, m2_ref, g1_ref, g0_ref,
-    g0p_ref, buf, sems, pairs, pair_sems, out, outs
+    rows, whole_ref, place_ref, bw_ref, bp_ref, drows_ref, p2rows_ref, p1_ref, d_ref, buf, sems, pairs, pair_sems, out, outs
 ):
-    part = fetch_parts(whole_ref, (6, 7, 4, 1, 5, 3), rows, buf, sems)
+    part = fetch_parts(whole_ref, (6, 7), rows, buf, sems)
     pair = fetch_pairs((bw_ref, bp_ref), pairs, pair_sems)
-    store = Store((p1_ref, d_ref, p2_ref, m2_ref, g1_ref, g0_ref, g0p_ref), out, outs)
-    m1, bw = part(0), pair(0)
+    store = Store((p1_ref, d_ref), out, outs)
+    bw, m1 = pair(0), part(0)
     p1 = store(split(dot(bw, m1)))
     bp = pair(1)
     d = store(split(dot(p1, bp)))
-    drows = dot(split(eye_ref[...]), d)
+    shape = drows_ref.shape
+    row = lax.broadcasted_iota(jnp.int32, shape, 0) + place_ref[1] * rows
+    eye = (row == lax.broadcasted_iota(jnp.int32, shape, 1)).astype(F32)
+    drows = dot(split(eye), d)
     drows_ref[...] = drows
-    m2 = part(1)
-    p2rows_ref[...] = dot(split(drows), m2)
-    store(split(dot(d, m2)))
-    store(m2)
-    store(split(dot(m1, bp)))
+    p2rows_ref[...] = dot(split(drows), part(1))
+    store.finish()
+
+
+def grams_kernel(rows, whole_ref, bp_ref, g1_ref, g0_ref, g0p_ref, buf, sems, pairs, pair_sems, out, outs):
+    part = fetch_parts(whole_ref, (4, 1, 5, 3, 6), rows, buf, sems)
+    pair = fetch_pairs((bp_ref,), pairs, pair_sems)
+    store = Store((g0_ref, g0p_ref, g1_ref), out, outs)
+    store(split(dot(part(0), part(1))))
     store(split(dot(part(2), part(3))))
-    store(split(dot(part(4), part(5))))
+    store(split(dot(part(4), pair(0))))
     store.finish()
 
 
+def carry_kernel(rows, whole_ref, d_ref, p2_ref, buf, sems, pairs, pair_sems, out, outs):
+    part = fetch_parts(whole_ref, (7,), rows, buf, sems)
+    pair = fetch_pairs((d_ref,), pairs, pair_sems)
+    store = Store((p2_ref,), out, outs)
+    m2 = part(0)
+    store(split(dot(pair(0), m2)))
+    store.finish()
+
+
 def second_kernel(
-    rows, received_ref, own_ref, vec_ref, p0p_ref, p0_ref, g0_ref, g0p_ref, p1_ref, g1_ref, m2_ref, plus_ref, minus_ref,
-    state_ref, buf, sems
+    rows, received_ref, own_ref, vec_ref, p0p_ref, p0_ref, g0_ref, g0p_ref, p1_ref, g1_ref, whole_ref, plus_ref, minus_ref,
+    state_ref, pairs, pair_sems, buf, sems
 ):
-    pair = fetch_pairs((p0p_ref, p0_ref, g0_ref, g0p_ref, p1_ref, g1_ref, m2_ref), buf, sems)
+    pair = fetch_pairs((p0p_ref, p0_ref, g0_ref, g0p_ref, p1_ref, g1_ref), pairs, pair_sems)
+    part = fetch_parts(whole_ref, (7,), rows, buf, sems)
     columns = received_ref[...].T
     x1, x2, x3, y0, y1, y2 = (columns[i * rows : (i + 1) * rows] for i in range(6))
     w1, w2, w3, w4 = (columns[6 * rows + i : 6 * rows + i + 1] for i in range(4))
@@ -195,7 +231,7 @@
     outer_j = dot(split(inner_j), pair(5)) + stacked(other_j, sixteen(e_p))
     plus_ref[...] = outer[: rows + 8]
     state_ref[...] = outer_j[: rows + 8]
-    minus_ref[...] = dot(split(outer_j), pair(6))[: rows + 8]
+    minus_ref[...] = dot(split(outer_j), part(0))[: rows + 8]
 
 
 def third_kernel(
@@ -227,9 +263,9 @@
     b_ref[...] = in_lanes((new_b + rowwise(v, state_ref[rows : rows + 1]),), rows, 128)
 
 
-def call(kernel, rows, operands, outs, placed=(), kept=(), scratch=(), flops=0, grant=58):
+def call(kernel, rows, operands, outs, placed=(), kept=(), scratch=(), flops=0, grant=58, small=()):
     nbytes = sum(x.size * x.dtype.itemsize for x in operands)
-    specs = [IN_PLACE if i in placed else IN_VMEM for i in range(len(operands))]
+    specs = [IN_SMEM if i in small else IN_PLACE if i in placed else IN_VMEM for i in range(len(operands))]
     return pl.pallas_call(
         functools.partial(kernel, rows),
         out_shape=[jax.ShapeDtypeStruct(shape, dtype) for shape, dtype in outs],
@@ -265,19 +301,12 @@
     peers = lax.axis_size("panel")
     time = lax.axis_index("tm")
     mine = lax.axis_index("panel")
-    row = lax.broadcasted_iota(jnp.int32, (rows, width), 0) + mine * rows
-    eye = (row == lax.broadcasted_iota(jnp.int32, (rows, width), 1)).astype(F32)
-
-    def present(shard, since):
-        return jnp.where(time >= since, shard, eye)
-
+    place = jnp.stack([time, mine]).astype(jnp.int32)
     a0, c0, j0 = transition, covariance, information
-    m0, m1, m2 = present(inverses[0], 1), present(inverses[1], 2), present(inverses[2], 4)
-
-    sent = passed_along(a0, 1), passed_along(jnp.concatenate([a0, m0]), 2), passed_along(a0, 3)
+
+    sent = passed_along(a0, 1), passed_along(jnp.concatenate([a0, inverses[0]]), 2), passed_along(a0, 3)
     a1, late, a3 = lax.optimization_barrier(sent)
-    a1, a2, m0p, a3 = present(a1, 1), present(late[:rows], 2), present(late[rows:], 2), present(a3, 3)
-    ready = jnp.concatenate([a0, a1, a2, a3, m0, m0p, m1, m2])
+    (ready,) = call(ready_kernel, rows, (place, a0, a1, late, a3, inverses), [((8 * rows, width), F32)], small=(0,), grant=4)
     whole = gathered(ready)
 
     v0 = jnp.stack([offset, info_vector])
@@ -318,27 +347,34 @@
         flops=6 * mults,
     )
     received = exchanged(packed)
-    drows, p2rows, p1, d, p2, m2w, g1, g0, g0p = call(
+    drows, p2rows, p1, d = call(
         middle_kernel,
         rows,
-        (whole, eye, bw, bp),
-        [flat(), flat()] + [pair] * 7,
+        (whole, place, bw, bp),
+        [flat(), flat()] + [pair] * 2,
         {0, 2, 3},
-        range(2, 9),
-        stage(6) + pairs(2) + pairs(7),
-        flops=6 * mults,
+        range(2, 4),
+        stage(2) + pairs(2) + pairs(2),
+        flops=2 * mults,
+        small=(1,),
     )
     later_p2 = passed_along(p2rows, -4)
+    g1, g0, g0p = call(
+        grams_kernel, rows, (whole, bp), [pair] * 3, {0, 1}, range(3), stage(5) + pairs(1) + pairs(3), flops=3 * mults
+    )
+    received, later_p2 = lax.optimization_barrier((received, later_p2))
     plus, minus, state = call(
         second_kernel,
         rows,
-        (received, jnp.concatenate([c0, j3]), vec, p0p, p0, g0, g0p, p1, g1, m2w),
+        (received, jnp.concatenate([c0, j3]), vec, p0p, p0, g0, g0p, p1, g1, whole),
         [flat(8)] * 3,
         range(3, 10),
         (),
-        pairs(7),
+        pairs(6) + stage(1),
         flops=mults,
     )
+    d, state = lax.optimization_barrier((d, state))
+    (p2,) = call(carry_kernel, rows, (whole, d), [pair], {0, 1}, {0}, stage(1) + pairs(1) + pairs(1), flops=mults)
 
     prior, later = passed_along(plus, 4), passed_along(minus, -4)
     packed, later_a, row = call(
@@ -350,6 +386,7 @@
         (),
         pairs(2),
         flops=mults,
+        grant=16,
     )
     back = exchanged(packed)
     new_a = passed_along(later_a, 4)
@@ -369,8 +406,10 @@
         (),
         pairs(1),
         flops=mults,
+        grant=16,
     )
     new_j = passed_along(later_j, 4)
+    new_a, later_j = lax.optimization_barrier((new_a, later_j))
     changed = time >= 4
     return (
         jnp.where(changed, new_a, drows),

time: 210 us -> 200 us (0.952)
  the two profiles are of different devices: /device:TPU:4 before, /device:TPU:7 now
where the time goes in v6:
time: 200 us; the launch traced here: 199 us
  starting transfers between devices  53.2 us (27%)
  waiting for transfers between devices  40.3 us (20%)
  blocking collectives  40.3 us (20%)
  Pallas kernels  36.2 us (18%)
  between operations  14.4 us (7%)
  local copies, waits for them, and re-layouts  8.04 us (4%)
  other arithmetic  6.43 us (3%)
    ppermute x11, starting transfers between devices, passed_along(): lax.ppermute(shard, 'tm', [(i, i + by) for i in range(peers) if 0 <= i +...  41.6 us
    all_gather x2, blocking collectives, gathered(): return lax.all_gather(shard, 'panel', axis=0, tiled=False)  40.3 us
    pallas_call x8, Pallas kernels, call(): pl.pallas_call(functools.partial(kernel, rows), out_shape=[jax.ShapeDtype...  36.2 us
    ppermute x11, waiting for transfers between devices, passed_along(): lax.ppermute(shard, 'tm', [(i, i + by) for i in range(peers) if 0 <= i +...  30.6 us
    all_to_all x2, starting transfers between devices, exchanged(): lax.all_to_all(packed, 'panel', split_axis=0, concat_axis=0, tiled=True)  11.6 us
    all_to_all x2, waiting for transfers between devices, exchanged(): lax.all_to_all(packed, 'panel', split_axis=0, concat_axis=0, tiled=True)  9.67 us
  transfers between devices with their start and end apart: 14, of which 8 were waited for; matrix products, arithmetic and copies ran while one was open for 4% of the time, Pallas kernels for 9%

profile of v6, /device:TPU:7, one launch (start us, length us, event | category | flops | bytes accessed | tf_op | source)
XLA Modules:
  0.0 198.8 jit_solution(17203529945510746373)
XLA Ops:
  7.2 0.8 slice_bitcast_fusion.1
  8.1 0.8 pad_maximum_fusion.1
  8.9 4.2 %collective-permute-start.1 = (f32[64,512]{1,0:T(8,128)S(1)}, f32[64,512]{1,0:T(8,128)S(1)}, u32[]{:S(2)}, u32[]{:S(2)}) collective-permute-start(f32[64,512]{1,0:T(8,128)S(1)} %pad_maximum_fusion.1), channel_id=1, source_target_pairs={{0,32},{16,48},{32,64},{48,80},{64,96},{80,112},{96,128},{112,144}... | collective-permute-start | bytes 393224 | tf_op jit(solution)/shard_map/ppermute | solution.py:282
  13.1 3.2 %collective-permute-start = (f32[32,512]{1,0:T(8,128)}, f32[32,512]{1,0:T(8,128)S(1)}, u32[]{:S(2)}, u32[]{:S(2)}) collective-permute-start(f32[32,512]{1,0:T(8,128)} %a0_ref.1), channel_id=1, source_target_pairs={{0,16},{16,32},{32,48},{48,64},{64,80},{80,96},{96,112},{112,128},... | collective-permute-start | bytes 196616 | tf_op jit(solution)/shard_map/ppermute | solution.py:282
  16.3 4.6 %collective-permute-start.2 = (f32[32,512]{1,0:T(8,128)}, f32[32,512]{1,0:T(8,128)S(1)}, u32[]{:S(2)}, u32[]{:S(2)}) collective-permute-start(f32[32,512]{1,0:T(8,128)} %a0_ref.1), channel_id=1, source_target_pairs={{0,48},{16,64},{32,80},{48,96},{64,112},{80,128},{96,144},{112,160... | collective-permute-start | bytes 196616 | tf_op jit(solution)/shard_map/ppermute | solution.py:282
  21.1 2.4 %collective-permute-done.a1_ref = f32[32,512]{1,0:T(8,128)S(1)} collective-permute-done((f32[32,512]{1,0:T(8,128)}, f32[32,512]{1,0:T(8,128)S(1)}, u32[]{:S(2)}, u32[]{:S(2)}) %collective-permute-start) | collective-permute-done | bytes 65568 | tf_op jit(solution)/shard_map/ppermute | solution.py:282
  23.4 2.8 %collective-permute-done.2.a3_ref = f32[32,512]{1,0:T(8,128)S(1)} collective-permute-done((f32[32,512]{1,0:T(8,128)}, f32[32,512]{1,0:T(8,128)S(1)}, u32[]{:S(2)}, u32[]{:S(2)}) %collective-permute-start.2) | collective-permute-done | bytes 65568 | tf_op jit(solution)/shard_map/ppermute | solution.py:282
  26.3 0.9 copy-done.2
  27.2 0.8 copy-done.3
  28.1 1.4 shard_map.101
  29.5 0.7 select_maximum_fusion
  30.2 0.9 pad_maximum_fusion
  31.1 1.9 collective-permute-start.5
  33.0 7.7 %collective-permute-start.4 = (f32[72,512]{1,0:T(8,128)S(1)}, f32[72,512]{1,0:T(8,128)S(1)}, u32[]{:S(2)}, u32[]{:S(2)}) collective-permute-start(f32[72,512]{1,0:T(8,128)S(1)} %pad_maximum_fusion), channel_id=1, source_target_pairs={{0,32},{16,48},{32,64},{48,80},{64,96},{80,112},{96,128},{112,144}... | collective-permute-start | bytes 442376 | tf_op jit(solution)/shard_map/ppermute | solution.py:282
  40.7 1.9 collective-permute-start.3
  42.7 9.8 %collective-permute-done.4 = f32[72,512]{1,0:T(8,128)S(1)} collective-permute-done((f32[72,512]{1,0:T(8,128)S(1)}, f32[72,512]{1,0:T(8,128)S(1)}, u32[]{:S(2)}, u32[]{:S(2)}) %collective-permute-start.4) | collective-permute-done | bytes 147488 | tf_op jit(solution)/shard_map/ppermute | solution.py:282
  52.5 4.1 %collective-permute-done.3 = f32[72,512]{1,0:T(8,128)S(1)} collective-permute-done((f32[72,512]{1,0:T(8,128)S(1)}, f32[72,512]{1,0:T(8,128)S(1)}, u32[]{:S(2)}, u32[]{:S(2)}) %collective-permute-start.3) | collective-permute-done | bytes 147488 | tf_op jit(solution)/shard_map/ppermute | solution.py:282
  56.6 0.7 concatenate.18
  57.3 25.6 %all-gather.1 = f32[128,128]{1,0:T(8,128)S(1)} all-gather(f32[8,128]{1,0:T(8,128)S(1)} %pad.17), channel_id=3, replica_groups=mesh['tm'=32,'panel'=16] {'panel'}, dimensions={0}, use_global_device_ids=true | all-gather | bytes 69632 | tf_op jit(solution)/shard_map/all_gather | solution.py:286
  82.9 0.7 reshape.54.vec_ref
  84.2 1.0 constant_dynamic-update-slice_fusion
  85.4 14.7 %all-gather.2 = f32[128,128]{1,0:T(8,128)S(1)} all-gather(f32[8,128]{1,0:T(8,128)S(1)} %select_maximum_fusion.1), channel_id=4, replica_groups=mesh['tm'=32,'panel'=16] {'panel'}, dimensions={0}, use_global_device_ids=true | all-gather | bytes 69632 | tf_op jit(solution)/shard_map/all_gather | solution.py:286
  100.1 0.7 reshape.55.u_ref
  100.8 10.7 %shard_map.102 = (f32[16,32,256]{2,1,0:T(8,128)}, f32[8,512]{1,0:T(8,128)}, bf16[2,512,512]{2,1,0:T(8,128)(2,1)}, bf16[2,512,512]{2,1,0:T(8,128)(2,1)}, bf16[2,5...) custom-call(f32[16,256,512]{2,1,0:T(8,128)} %bitcast.28, f32[192,512]{1,0:T(8,128)} %copy-done.11, ...), custom_call_target="tpu_custom_call" | custom-call | flops 4831838208 | bytes 8814592 | tf_op jit(solution)/shard_map/pallas_call | solution.py:269
  111.5 3.5 %all-to-all-start = ((f32[16,32,256]{2,1,0:T(8,128)}), f32[16,32,256]{2,1,0:T(8,128)S(1)}, u32[]{:S(2)}, u32[]{:S(2)}) async-start(f32[16,32,256]{2,1,0:T(8,128)} %get-tuple-element.53), calls=%async_computation | async-start | bytes 1048576 | tf_op jit(solution)/shard_map/all_to_all | solution.py:290
  115.0 0.7 pad_maximum_fusion.2.own_ref
  115.7 6.1 %shard_map.103 = (f32[32,512]{1,0:T(8,128)}, f32[32,512]{1,0:T(8,128)}, bf16[2,512,512]{2,1,0:T(8,128)(2,1)}, bf16[2,512,512]{2,1,0:T(8,128)(2,1)}) custom-call(f32[16,256,512]{2,1,0:T(8,128)} %bitcast.29, s32[2]{0:T(128)} %copy-done.4, bf16[2,512,512]{2,1,0:T(8,128)(2,1)} %get-tuple-element.54.bw_ref, bf16[2,512,512]{2,1,0:T(8,128)(2,1)} %get-tuple-element.55.bp_ref), custom_call_target="tpu_custom_call" | custom-call | flops 1610612736 | bytes 10485768 | tf_op jit(solution)/shard_map/pallas_call | solution.py:269
  121.8 4.0 %collective-permute-start.6 = (f32[32,512]{1,0:T(8,128)}, f32[32,512]{1,0:T(8,128)S(1)}, u32[]{:S(2)}, u32[]{:S(2)}) collective-permute-start(f32[32,512]{1,0:T(8,128)} %get-tuple-element.56.p2rows_ref), channel_id=1, source_target_pairs={{64,0},{80,16},{96,32},{112,48},{128,64},{144,80},{160,96},{176,11... | collective-permute-start | bytes 196616 | tf_op jit(solution)/shard_map/ppermute | solution.py:282
  125.8 6.0 %shard_map.104 = (bf16[2,512,512]{2,1,0:T(8,128)(2,1)}, bf16[2,512,512]{2,1,0:T(8,128)(2,1)}, bf16[2,512,512]{2,1,0:T(8,128)(2,1)}) custom-call(f32[16,256,512]{2,1,0:T(8,128)} %bitcast.30, bf16[2,512,512]{2,1,0:T(8,128)(2,1)} %get-tuple-element.55.bp_ref), custom_call_target="tpu_custom_call" | custom-call | flops 2415919104 | bytes 9437184 | tf_op jit(solution)/shard_map/pallas_call | solution.py:269
  131.8 0.5 all-to-all-done
  132.4 0.8 copy-done.8
  133.2 5.3 %shard_map.105 = (f32[40,512]{1,0:T(8,128)}, f32[40,512]{1,0:T(8,128)}, f32[40,512]{1,0:T(8,128)}) custom-call(f32[512,256]{1,0:T(8,128)} %bitcast.33, f32[64,512]{1,0:T(8,128)} %pad_maximum_fusion.2.own_ref, f32[8,512]{1,0:T(8,128)} %get-tuple-element.58.vec_ref, bf16[2,512,512]{2,1,0:T(8,128)(2,1)} %get-tuple-element.59.p0p_ref, ...), custom_call_target="tpu_custom_call" | custom-call | flops 805306368 | bytes 15351808 | tf_op jit(solution)/shard_map/pallas_call | solution.py:269
  138.6 5.3 %collective-permute-start.8 = (f32[40,512]{1,0:T(8,128)}, f32[40,512]{1,0:T(8,128)S(1)}, u32[]{:S(2)}, u32[]{:S(2)}) collective-permute-start(f32[40,512]{1,0:T(8,128)} %get-tuple-element.66), channel_id=1, source_target_pairs={{64,0},{80,16},{96,32},{112,48},{128,64},{144,80},{160,96},{176,11... | collective-permute-start | bytes 245768 | tf_op jit(solution)/shard_map/ppermute | solution.py:282
  143.9 4.0 %collective-permute-start.7 = (f32[40,512]{1,0:T(8,128)}, f32[40,512]{1,0:T(8,128)S(1)}, u32[]{:S(2)}, u32[]{:S(2)}) collective-permute-start(f32[40,512]{1,0:T(8,128)} %get-tuple-element.65.plus_ref), channel_id=1, source_target_pairs={{0,64},{16,80},{32,96},{48,112},{64,128},{80,144},{96,160},{112,17... | collective-permute-start | bytes 245768 | tf_op jit(solution)/shard_map/ppermute | solution.py:282
  147.9 3.5 %shard_map.106.p2_ref = bf16[2,512,512]{2,1,0:T(8,128)(2,1)} custom-call(f32[16,256,512]{2,1,0:T(8,128)} %bitcast.32, bf16[2,512,512]{2,1,0:T(8,128)(2,1)} %get-tuple-element.71.d_ref), custom_call_target="tpu_custom_call" | custom-call | flops 805306368 | bytes 9437184 | tf_op jit(solution)/shard_map/pallas_call | solution.py:269
  151.5 3.9 %collective-permute-done.7.prior_ref = f32[40,512]{1,0:T(8,128)S(1)} collective-permute-done((f32[40,512]{1,0:T(8,128)}, f32[40,512]{1,0:T(8,128)S(1)}, u32[]{:S(2)}, u32[]{:S(2)}) %collective-permute-start.7) | collective-permute-done | bytes 81952 | tf_op jit(solution)/shard_map/ppermute | solution.py:282
  155.4 1.2 copy-done.1
  156.6 1.7 shard_map.107
  158.4 8.0 %all-to-all-start.1 = ((f32[16,32,128]{2,1,0:T(8,128)}), f32[16,32,128]{2,1,0:T(8,128)S(1)}, u32[]{:S(2)}, u32[]{:S(2)}) async-start(f32[16,32,128]{2,1,0:T(8,128)} %get-tuple-element.73), calls=%async_computation.1 | async-start | bytes 524288 | tf_op jit(solution)/shard_map/all_to_all | solution.py:290
  166.7 2.3 %collective-permute-start.9 = (f32[32,512]{1,0:T(8,128)S(1)}, f32[32,512]{1,0:T(8,128)S(1)}, u32[]{:S(2)}, u32[]{:S(2)}) collective-permute-start(f32[32,512]{1,0:T(8,128)S(1)} %get-tuple-element.72), channel_id=1, source_target_pairs={{0,64},{16,80},{32,96},{48,112},{64,128},{80,144},{96,160},{112,17... | collective-permute-start | bytes 196616 | tf_op jit(solution)/shard_map/ppermute | solution.py:282
  169.0 9.1 %all-to-all-done.1 = f32[16,32,128]{2,1,0:T(8,128)S(1)} async-done(((f32[16,32,128]{2,1,0:T(8,128)}), f32[16,32,128]{2,1,0:T(8,128)S(1)}, u32[]{:S(2)}, u32[]{:S(2)}) %all-to-all-start.1) | async-done | bytes 262176 | tf_op jit(solution)/shard_map/all_to_all | solution.py:290
  178.1 1.5 shard_map.108
  179.6 2.3 %collective-permute-start.10 = (f32[40,512]{1,0:T(8,128)S(1)}, f32[40,512]{1,0:T(8,128)S(1)}, u32[]{:S(2)}, u32[]{:S(2)}) collective-permute-start(f32[40,512]{1,0:T(8,128)S(1)} %get-tuple-element.75), channel_id=1, source_target_pairs={{0,64},{16,80},{32,96},{48,112},{64,128},{80,144},{96,160},{112,17... | collective-permute-start | bytes 245768 | tf_op jit(solution)/shard_map/ppermute | solution.py:282
  181.9 0.6 broadcast_select_fusion
  182.5 0.6 slice_reduce_fusion
  183.2 7.5 %collective-permute-done.10 = f32[40,512]{1,0:T(8,128)S(1)} collective-permute-done((f32[40,512]{1,0:T(8,128)S(1)}, f32[40,512]{1,0:T(8,128)S(1)}, u32[]{:S(2)}, u32[]{:S(2)}) %collective-permute-start.10) | collective-permute-done | bytes 81952 | tf_op jit(solution)/shard_map/ppermute | solution.py:282
  190.7 0.6 fusion.3
  191.3 0.6 slice_select_fusion
  (55 shorter events, 1.3 us)
Async XLA Ops:
  7.2 93.6 %all-gather.5.cloned.1.call-start = ((), (), s32[]{:S(2)}) async-start(), calls=%async_computation.2 | async-start | bytes 8912896 | tf_op jit(solution)/shard_map/all_gather | solution.py:286
  8.9 17.4 %collective-permute-start.1 = (f32[64,512]{1,0:T(8,128)S(1)}, f32[64,512]{1,0:T(8,128)S(1)}, u32[]{:S(2)}, u32[]{:S(2)}) collective-permute-start(f32[64,512]{1,0:T(8,128)S(1)} %pad_maximum_fusion.1), channel_id=1, source_target_pairs={{0,32},{16,48},{32,64},{48,80},{64,96},{80,112},{96,128},{112,144}... | collective-permute-start | bytes 393224 | tf_op jit(solution)/shard_map/ppermute | solution.py:282
  13.1 10.3 %collective-permute-start = (f32[32,512]{1,0:T(8,128)}, f32[32,512]{1,0:T(8,128)S(1)}, u32[]{:S(2)}, u32[]{:S(2)}) collective-permute-start(f32[32,512]{1,0:T(8,128)} %a0_ref.1), channel_id=1, source_target_pairs={{0,16},{16,32},{32,48},{48,64},{64,80},{80,96},{96,112},{112,128},... | collective-permute-start | bytes 196616 | tf_op jit(solution)/shard_map/ppermute | solution.py:282
  16.3 9.9 %collective-permute-start.2 = (f32[32,512]{1,0:T(8,128)}, f32[32,512]{1,0:T(8,128)S(1)}, u32[]{:S(2)}, u32[]{:S(2)}) collective-permute-start(f32[32,512]{1,0:T(8,128)} %a0_ref.1), channel_id=1, source_target_pairs={{0,48},{16,64},{32,80},{48,96},{64,112},{80,128},{96,144},{112,160... | collective-permute-start | bytes 196616 | tf_op jit(solution)/shard_map/ppermute | solution.py:282
  21.1 90.4 %copy-start.4 = (s32[2]{0:T(128)}, s32[2]{0:T(128)S(1)}, u32[]{:S(2)}) copy-start(s32[2]{0:T(128)S(1)} %pad_add_fusion.place_ref) | copy-start | bytes 28
  26.3 0.9 copy-start.2
  27.2 0.8 copy-start.3
  31.1 11.6 %collective-permute-start.5 = (f32[72,512]{1,0:T(8,128)S(1)}, f32[72,512]{1,0:T(8,128)S(1)}, u32[]{:S(2)}, u32[]{:S(2)}) collective-permute-start(f32[72,512]{1,0:T(8,128)S(1)} %pad_maximum_fusion), channel_id=1, source_target_pairs={{0,48},{16,64},{32,80},{48,96},{64,112},{80,128},{96,144},{112,160... | collective-permute-start | bytes 442376 | tf_op jit(solution)/shard_map/ppermute | solution.py:282
  33.0 19.5 %collective-permute-start.4 = (f32[72,512]{1,0:T(8,128)S(1)}, f32[72,512]{1,0:T(8,128)S(1)}, u32[]{:S(2)}, u32[]{:S(2)}) collective-permute-start(f32[72,512]{1,0:T(8,128)S(1)} %pad_maximum_fusion), channel_id=1, source_target_pairs={{0,32},{16,48},{32,64},{48,80},{64,96},{80,112},{96,128},{112,144}... | collective-permute-start | bytes 442376 | tf_op jit(solution)/shard_map/ppermute | solution.py:282
  40.7 15.9 %collective-permute-start.3 = (f32[72,512]{1,0:T(8,128)S(1)}, f32[72,512]{1,0:T(8,128)S(1)}, u32[]{:S(2)}, u32[]{:S(2)}) collective-permute-start(f32[72,512]{1,0:T(8,128)S(1)} %pad_maximum_fusion), channel_id=1, source_target_pairs={{0,16},{16,32},{32,48},{48,64},{64,80},{80,96},{96,112},{112,128},... | collective-permute-start | bytes 442376 | tf_op jit(solution)/shard_map/ppermute | solution.py:282
  85.4 15.4 %copy-start.11 = (f32[192,512]{1,0:T(8,128)}, f32[192,512]{1,0:T(8,128)S(1)}, u32[]{:S(2)}) copy-start(f32[192,512]{1,0:T(8,128)S(1)} %get-tuple-element.88.own_ref) | copy-start | bytes 1179652
  100.8 14.2 %copy-start.9 = (f32[32,512]{1,0:T(8,128)S(1)}, f32[32,512]{1,0:T(8,128)}, u32[]{:S(2)}) copy-start(f32[32,512]{1,0:T(8,128)} %param.8) | copy-start | bytes 196612
  111.5 20.9 %all-to-all-start = ((f32[16,32,256]{2,1,0:T(8,128)}), f32[16,32,256]{2,1,0:T(8,128)S(1)}, u32[]{:S(2)}, u32[]{:S(2)}) async-start(f32[16,32,256]{2,1,0:T(8,128)} %get-tuple-element.53), calls=%async_computation | async-start | bytes 1048576 | tf_op jit(solution)/shard_map/all_to_all | solution.py:290
  121.8 10.0 %collective-permute-start.6 = (f32[32,512]{1,0:T(8,128)}, f32[32,512]{1,0:T(8,128)S(1)}, u32[]{:S(2)}, u32[]{:S(2)}) collective-permute-start(f32[32,512]{1,0:T(8,128)} %get-tuple-element.56.p2rows_ref), channel_id=1, source_target_pairs={{64,0},{80,16},{96,32},{112,48},{128,64},{144,80},{160,96},{176,11... | collective-permute-start | bytes 196616 | tf_op jit(solution)/shard_map/ppermute | solution.py:282
  132.4 0.8 copy-start.8
  138.5 16.8 %copy-start = (bf16[2,512,512]{2,1,0:T(8,128)(2,1)S(1)}, bf16[2,512,512]{2,1,0:T(8,128)(2,1)}, u32[]{:S(2)}) copy-start(bf16[2,512,512]{2,1,0:T(8,128)(2,1)} %get-tuple-element.71.d_ref) | copy-start | bytes 3145732
  138.6 16.8 %copy-start.5 = (f32[40,512]{1,0:T(8,128)S(1)}, f32[40,512]{1,0:T(8,128)}, u32[]{:S(2)}) copy-start(f32[40,512]{1,0:T(8,128)} %get-tuple-element.65.plus_ref) | copy-start | bytes 245764
  138.6 16.8 %copy-start.6 = (f32[40,512]{1,0:T(8,128)S(1)}, f32[40,512]{1,0:T(8,128)}, u32[]{:S(2)}) copy-start(f32[40,512]{1,0:T(8,128)} %get-tuple-element.70.state_ref) | copy-start | bytes 245764
  138.6 39.5 %copy-start.7 = (f32[32,512]{1,0:T(8,128)S(1)}, f32[32,512]{1,0:T(8,128)}, u32[]{:S(2)}) copy-start(f32[32,512]{1,0:T(8,128)} %get-tuple-element.56.p2rows_ref) | copy-start | bytes 196612
  138.6 12.9 %collective-permute-start.8 = (f32[40,512]{1,0:T(8,128)}, f32[40,512]{1,0:T(8,128)S(1)}, u32[]{:S(2)}, u32[]{:S(2)}) collective-permute-start(f32[40,512]{1,0:T(8,128)} %get-tuple-element.66), channel_id=1, source_target_pairs={{64,0},{80,16},{96,32},{112,48},{128,64},{144,80},{160,96},{176,11... | collective-permute-start | bytes 245768 | tf_op jit(solution)/shard_map/ppermute | solution.py:282
  143.9 11.5 %collective-permute-start.7 = (f32[40,512]{1,0:T(8,128)}, f32[40,512]{1,0:T(8,128)S(1)}, u32[]{:S(2)}, u32[]{:S(2)}) collective-permute-start(f32[40,512]{1,0:T(8,128)} %get-tuple-element.65.plus_ref), channel_id=1, source_target_pairs={{0,64},{16,80},{32,96},{48,112},{64,128},{80,144},{96,160},{112,17... | collective-permute-start | bytes 245768 | tf_op jit(solution)/shard_map/ppermute | solution.py:282
  147.9 34.0 %copy-start.10 = (f32[32,512]{1,0:T(8,128)S(1)}, f32[32,512]{1,0:T(8,128)}, u32[]{:S(2)}) copy-start(f32[32,512]{1,0:T(8,128)} %get-tuple-element.77) | copy-start | bytes 196612
  155.4 1.2 copy-start.1
  158.4 19.7 %all-to-all-start.1 = ((f32[16,32,128]{2,1,0:T(8,128)}), f32[16,32,128]{2,1,0:T(8,128)S(1)}, u32[]{:S(2)}, u32[]{:S(2)}) async-start(f32[16,32,128]{2,1,0:T(8,128)} %get-tuple-element.73), calls=%async_computation.1 | async-start | bytes 524288 | tf_op jit(solution)/shard_map/all_to_all | solution.py:290
  166.7 15.2 %collective-permute-start.9 = (f32[32,512]{1,0:T(8,128)S(1)}, f32[32,512]{1,0:T(8,128)S(1)}, u32[]{:S(2)}, u32[]{:S(2)}) collective-permute-start(f32[32,512]{1,0:T(8,128)S(1)} %get-tuple-element.72), channel_id=1, source_target_pairs={{0,64},{16,80},{32,96},{48,112},{64,128},{80,144},{96,160},{112,17... | collective-permute-start | bytes 196616 | tf_op jit(solution)/shard_map/ppermute | solution.py:282
  179.6 11.1 %collective-permute-start.10 = (f32[40,512]{1,0:T(8,128)S(1)}, f32[40,512]{1,0:T(8,128)S(1)}, u32[]{:S(2)}, u32[]{:S(2)}) collective-permute-start(f32[40,512]{1,0:T(8,128)S(1)} %get-tuple-element.75), channel_id=1, source_target_pairs={{0,64},{16,80},{32,96},{48,112},{64,128},{80,144},{96,160},{112,17... | collective-permute-start | bytes 245768 | tf_op jit(solution)/shard_map/ppermute | solution.py:282
Sparse Core Ops, SparseCore 0:
  29.6 65.1 all-gather.4

commit v7 on v6

--- a/solution.py
+++ b/solution.py
@@ -77,11 +77,32 @@
         return value
 
 
-def fetch_parts(stack_ref, order, rows, buf, sems):
-    sources = [stack_ref.at[:, pl.ds(i * rows, rows), :] for i in order]
-    fetch = Fetch(sources, [buf.at[k] for k in range(len(order))], sems)
-    width = stack_ref.shape[2]
-    return lambda k: split(fetch(k).reshape(width, width))
+def fetch_parts(stack_ref, order, rows, buf, sems, head_ref=None):
+    width, half = stack_ref.shape[2], rows // 2
+    copies = []
+    for k, i in enumerate(order):
+        if head_ref is not None and i == 7:
+            low, high = pl.ds(0, half), pl.ds(half, half)
+            copies.append(
+                [
+                    pltpu.make_async_copy(head_ref.at[:, pl.ds(8, half), :], buf.at[k, :, low, :], sems.at[k]),
+                    pltpu.make_async_copy(
+                        stack_ref.at[:, pl.ds(i * rows, half), :], buf.at[k, :, high, :], sems.at[len(order)]
+                    ),
+                ]
+            )
+        else:
+            copies.append([pltpu.make_async_copy(stack_ref.at[:, pl.ds(i * rows, rows), :], buf.at[k], sems.at[k])])
+    for group in copies:
+        for copy in group:
+            copy.start()
+
+    def part(k):
+        for copy in copies[k]:
+            copy.wait()
+        return split(buf[k].reshape(width, width))
+
+    return part
 
 
 class Store:
@@ -112,23 +133,27 @@
     return pair
 
 
-def ready_kernel(rows, place_ref, a0_ref, a1_ref, late_ref, a3_ref, inverses_ref, ready_ref):
+def ready_kernel(rows, place_ref, a1_ref, late_ref, a3_ref, a0_ref, inverses_ref, ready_ref, head_ref, own, mixers, sems):
+    fetch = Fetch((a0_ref, inverses_ref), (own, mixers), sems)
     time, mine = place_ref[0], place_ref[1]
-    shape = a0_ref.shape
+    shape, half = a1_ref.shape, rows // 2
     row = lax.broadcasted_iota(jnp.int32, shape, 0) + mine * rows
     eye = (row == lax.broadcasted_iota(jnp.int32, shape, 1)).astype(F32)
-    parts = (
-        (a0_ref[...], 0),
-        (a1_ref[...], 1),
-        (late_ref[:rows], 2),
-        (a3_ref[...], 3),
-        (inverses_ref[0], 1),
-        (late_ref[rows:], 3),
-        (inverses_ref[1], 2),
-        (inverses_ref[2], 4),
-    )
-    for i, (value, since) in enumerate(parts):
+
+    def put(i, value, since):
         ready_ref[i * rows : (i + 1) * rows] = jnp.where(time >= since, value, eye)
+
+    put(1, a1_ref[...], 1)
+    put(2, late_ref[:rows], 2)
+    put(5, late_ref[rows:], 3)
+    put(3, a3_ref[...], 3)
+    ready_ref[:rows] = fetch(0)
+    inverses = fetch(1)
+    put(4, inverses[0], 1)
+    put(6, inverses[1], 2)
+    m2 = jnp.where(time >= 4, inverses[2], eye)
+    head_ref[...] = m2[:half]
+    ready_ref[7 * rows :] = m2[half:]
 
 
 def first_kernel(
@@ -175,11 +200,12 @@
 
 
 def middle_kernel(
-    rows, whole_ref, place_ref, bw_ref, bp_ref, drows_ref, p2rows_ref, p1_ref, d_ref, buf, sems, pairs, pair_sems, out, outs
+    rows, whole_ref, head_ref, place_ref, bw_ref, bp_ref, drows_ref, p2rows_ref, p1_ref, d_ref, m2_ref, buf, sems, pairs,
+    pair_sems, out, outs
 ):
-    part = fetch_parts(whole_ref, (6, 7), rows, buf, sems)
+    part = fetch_parts(whole_ref, (6, 7), rows, buf, sems, head_ref)
     pair = fetch_pairs((bw_ref, bp_ref), pairs, pair_sems)
-    store = Store((p1_ref, d_ref), out, outs)
+    store = Store((p1_ref, d_ref, m2_ref), out, outs)
     bw, m1 = pair(0), part(0)
     p1 = store(split(dot(bw, m1)))
     bp = pair(1)
@@ -189,7 +215,7 @@
     eye = (row == lax.broadcasted_iota(jnp.int32, shape, 1)).astype(F32)
     drows = dot(split(eye), d)
     drows_ref[...] = drows
-    p2rows_ref[...] = dot(split(drows), part(1))
+    p2rows_ref[...] = dot(split(drows), store(part(1)))
     store.finish()
 
 
@@ -203,21 +229,11 @@
     store.finish()
 
 
-def carry_kernel(rows, whole_ref, d_ref, p2_ref, buf, sems, pairs, pair_sems, out, outs):
-    part = fetch_parts(whole_ref, (7,), rows, buf, sems)
-    pair = fetch_pairs((d_ref,), pairs, pair_sems)
-    store = Store((p2_ref,), out, outs)
-    m2 = part(0)
-    store(split(dot(pair(0), m2)))
-    store.finish()
-
-
 def second_kernel(
-    rows, received_ref, own_ref, vec_ref, p0p_ref, p0_ref, g0_ref, g0p_ref, p1_ref, g1_ref, whole_ref, plus_ref, minus_ref,
-    state_ref, pairs, pair_sems, buf, sems
+    rows, received_ref, own_ref, vec_ref, p0p_ref, p0_ref, g0_ref, g0p_ref, p1_ref, g1_ref, m2_ref, plus_ref, minus_ref,
+    state_ref, pairs, pair_sems
 ):
-    pair = fetch_pairs((p0p_ref, p0_ref, g0_ref, g0p_ref, p1_ref, g1_ref), pairs, pair_sems)
-    part = fetch_parts(whole_ref, (7,), rows, buf, sems)
+    pair = fetch_pairs((p0p_ref, p0_ref, g0_ref, g0p_ref, p1_ref, g1_ref, m2_ref), pairs, pair_sems)
     columns = received_ref[...].T
     x1, x2, x3, y0, y1, y2 = (columns[i * rows : (i + 1) * rows] for i in range(6))
     w1, w2, w3, w4 = (columns[6 * rows + i : 6 * rows + i + 1] for i in range(4))
@@ -231,15 +247,17 @@
     outer_j = dot(split(inner_j), pair(5)) + stacked(other_j, sixteen(e_p))
     plus_ref[...] = outer[: rows + 8]
     state_ref[...] = outer_j[: rows + 8]
-    minus_ref[...] = dot(split(outer_j), part(0))[: rows + 8]
+    minus_ref[...] = dot(split(outer_j), pair(6))[: rows + 8]
 
 
 def third_kernel(
-    rows, prior_ref, later_ref, later_p2_ref, plus_ref, state_ref, p2_ref, d_ref, packed_ref, a_ref, row_ref, buf, sems
+    rows, prior_ref, later_ref, later_p2_ref, plus_ref, state_ref, m2_ref, d_ref, packed_ref, a_ref, row_ref, buf, sems
 ):
-    pair = fetch_pairs((p2_ref, d_ref), buf, sems)
+    pair = fetch_pairs((m2_ref, d_ref), buf, sems)
     v = dot_nt(split(prior_ref[:rows]), pair(0))
-    both = dot(split(stacked(later_ref[:rows], later_p2_ref[...], sixteen(later_ref[rows : rows + 1]))), pair(1))
+    d = pair(1)
+    v = dot_nt(split(v), d)
+    both = dot(split(stacked(later_ref[:rows], later_p2_ref[...], sixteen(later_ref[rows : rows + 1]))), d)
     pack((v, plus_ref[:rows], both[:rows], state_ref[:rows]), packed_ref, rows)
     a_ref[...] = both[rows : 2 * rows]
     row_ref[...] = both[2 * rows : 2 * rows + 8]
@@ -290,12 +308,6 @@
     return lax.all_to_all(packed, "panel", split_axis=0, concat_axis=0, tiled=True).reshape(-1, packed.shape[2])
 
 
-def whole_vectors(slices):
-    count, rows = slices.shape
-    whole = gathered(jnp.pad(slices, ((0, 8 - count), (0, 128 - rows))))[:, :, :rows]
-    return whole.transpose(1, 0, 2).reshape(8, -1)
-
-
 def local(transition, offset, covariance, info_vector, information, inverses):
     rows, width = transition.shape
     peers = lax.axis_size("panel")
@@ -306,29 +318,41 @@
 
     sent = passed_along(a0, 1), passed_along(jnp.concatenate([a0, inverses[0]]), 2), passed_along(a0, 3)
     a1, late, a3 = lax.optimization_barrier(sent)
-    (ready,) = call(ready_kernel, rows, (place, a0, a1, late, a3, inverses), [((8 * rows, width), F32)], small=(0,), grant=4)
+    ready, head = call(
+        ready_kernel,
+        rows,
+        (place, a1, late, a3, a0, inverses),
+        [((8 * rows - rows // 2, width), F32), ((rows // 2, width), F32)],
+        {4, 5},
+        (),
+        [pltpu.VMEM(a0.shape, F32), pltpu.VMEM(inverses.shape, F32), pltpu.SemaphoreType.DMA((2,))],
+        small=(0,),
+        grant=4,
+    )
     whole = gathered(ready)
 
     v0 = jnp.stack([offset, info_vector])
     own = jnp.concatenate([c0, j0, jnp.pad(v0, ((0, 6), (0, width - rows)))])
-    own, _ = lax.optimization_barrier((own, ready))
+    own, head = lax.optimization_barrier((own, head))
     got = lax.optimization_barrier(tuple(passed_along(own, by) for by in (1, 2, 3)))
     (c1, c2, c3), (j1, j2, j3) = ([g[i * rows : (i + 1) * rows] for g in got] for i in range(2))
-    vectors = whole_vectors(jnp.concatenate([v0] + [g[2 * rows : 2 * rows + 2, :rows] for g in got]))
-    b0, e0, b1, e1, b2, e2, b3, e3 = vectors
-
-    def along(matrix, vector):
-        return jnp.sum(matrix * vector[None, :], axis=1)
-
-    u = whole_vectors(jnp.stack([along(c1, e0), along(j0, b1), along(c3, e2), along(j2, b3)]))
-
+    slices = jnp.concatenate([v0] + [g[2 * rows : 2 * rows + 2, :rows] for g in got])
+
+    def share(vector, matrix):
+        return jnp.sum(vector[:, None] * matrix, axis=0)
+
+    shares = jnp.stack([share(slices[1], c1), share(slices[2], j0), share(slices[5], c3), share(slices[6], j2)])
+    line = jnp.pad(slices.reshape(1, -1), ((0, 3), (0, width - 8 * rows)))
+    head = gathered(jnp.concatenate([shares, line, head]))
+    vectors = head[:, 4, : 8 * rows].reshape(peers, 8, rows).transpose(1, 0, 2).reshape(8, width)
+    u = jnp.sum(head[:, :4], axis=0)
     whole, vectors, u = lax.optimization_barrier((whole, vectors, u))
 
     square, pair = (width, width), ((2, width, width), BF16)
     mults = 6 * width**3
 
     def stage(parts):
-        return [pltpu.VMEM((parts, peers, rows, width), F32), pltpu.SemaphoreType.DMA((parts,))]
+        return [pltpu.VMEM((parts, peers, rows, width), F32), pltpu.SemaphoreType.DMA((parts + 1,))]
 
     def pairs(count):
         return [pltpu.VMEM((count, 2, *square), BF16), pltpu.SemaphoreType.DMA((count,))]
@@ -347,16 +371,16 @@
         flops=6 * mults,
     )
     received = exchanged(packed)
-    drows, p2rows, p1, d = call(
+    drows, p2rows, p1, d, m2 = call(
         middle_kernel,
         rows,
-        (whole, place, bw, bp),
-        [flat(), flat()] + [pair] * 2,
-        {0, 2, 3},
-        range(2, 4),
-        stage(2) + pairs(2) + pairs(2),
+        (whole, head, place, bw, bp),
+        [flat(), flat()] + [pair] * 3,
+        {0, 1, 3, 4},
+        range(2, 5),
+        stage(2) + pairs(2) + pairs(3),
         flops=2 * mults,
-        small=(1,),
+        small=(2,),
     )
     later_p2 = passed_along(p2rows, -4)
     g1, g0, g0p = call(
@@ -366,21 +390,18 @@
     plus, minus, state = call(
         second_kernel,
         rows,
-        (received, jnp.concatenate([c0, j3]), vec, p0p, p0, g0, g0p, p1, g1, whole),
+        (received, jnp.concatenate([c0, j3]), vec, p0p, p0, g0, g0p, p1, g1, m2),
         [flat(8)] * 3,
         range(3, 10),
         (),
-        pairs(6) + stage(1),
+        pairs(7),
         flops=mults,
     )
-    d, state = lax.optimization_barrier((d, state))
-    (p2,) = call(carry_kernel, rows, (whole, d), [pair], {0, 1}, {0}, stage(1) + pairs(1) + pairs(1), flops=mults)
-
     prior, later = passed_along(plus, 4), passed_along(minus, -4)
     packed, later_a, row = call(
         third_kernel,
         rows,
-        (prior, later, later_p2, plus, state, p2, d),
+        (prior, later, later_p2, plus, state, m2, d),
         [((peers, rows, 4 * rows), F32), flat(), ((8, width), F32)],
         {5, 6},
         (),

time: 200 us -> 204 us (1.020)
  blocking collectives: 40.3 us -> 31.5 us
  waiting for transfers between devices: 40.3 us -> 45.5 us
  starting transfers between devices: 53.2 us -> 58.3 us
  local copies, waits for them, and re-layouts: 8.04 us -> 10.9 us
  Pallas kernels: 36.2 us -> 33.8 us
    all_gather x2 -> x1, blocking collectives: 40.3 us -> 31.5 us  [gathered(): return lax.all_gather(shard, 'panel', axis=0, tiled=False)]
    all_gather x1, waiting for transfers between devices: 0.01 us -> 3.62 us  [gathered(): return lax.all_gather(shard, 'panel', axis=0, tiled=False)]
    ppermute x11, waiting for transfers between devices: 30.6 us -> 33.8 us  [passed_along(): lax.ppermute(shard, 'tm', [(i, i + by) for i in range(peers) if 0 <= i +...]
    ppermute x11, starting transfers between devices: 41.6 us -> 44.7 us  [passed_along(): lax.ppermute(shard, 'tm', [(i, i + by) for i in range(peers) if 0 <= i +...]
    pallas_call x8 -> x7, Pallas kernels: 36.2 us -> 33.8 us  [call(): pl.pallas_call(functools.partial(kernel, rows), out_shape=[jax.ShapeDtype...]
    unnamed x27 -> x32, local copies, waits for them, and re-layouts: 3.86 us -> 6.14 us
  transfers between devices with their start and end apart: 14 -> 14, of which waited for: 8 -> 9; matrix products, arithmetic and copies ran while one was open for 4% -> 5% of each run, Pallas kernels for 9% -> 7%
where the time goes in v7:
time: 204 us; the launch traced here: 202 us
  starting transfers between devices  58.3 us (29%)
  waiting for transfers between devices  45.5 us (22%)
  Pallas kernels  33.8 us (17%)
  blocking collectives  31.5 us (15%)
  between operations  14.3 us (7%)
  local copies, waits for them, and re-layouts  10.9 us (5%)
  other arithmetic  7.59 us (4%)
    ppermute x11, starting transfers between devices, passed_along(): lax.ppermute(shard, 'tm', [(i, i + by) for i in range(peers) if 0 <= i +...  44.7 us
    pallas_call x7, Pallas kernels, call(): pl.pallas_call(functools.partial(kernel, rows), out_shape=[jax.ShapeDtype...  33.8 us
    ppermute x11, waiting for transfers between devices, passed_along(): lax.ppermute(shard, 'tm', [(i, i + by) for i in range(peers) if 0 <= i +...  33.8 us
    all_gather x1, blocking collectives, gathered(): return lax.all_gather(shard, 'panel', axis=0, tiled=False)  31.5 us
    all_to_all x2, starting transfers between devices, exchanged(): lax.all_to_all(packed, 'panel', split_axis=0, concat_axis=0, tiled=True)  13.5 us
    all_to_all x2, waiting for transfers between devices, exchanged(): lax.all_to_all(packed, 'panel', split_axis=0, concat_axis=0, tiled=True)  8.08 us
    unnamed x32, local copies, waits for them, and re-layouts  6.14 us
  transfers between devices with their start and end apart: 14, of which 9 were waited for; matrix products, arithmetic and copies ran while one was open for 5% of the time, Pallas kernels for 7%

profile of v7, /device:TPU:7, one launch (start us, length us, event | category | flops | bytes accessed | tf_op | source)
XLA Modules:
  0.0 201.9 jit_solution(10379659686390128631)
XLA Ops:
  7.2 0.8 slice_bitcast_fusion
  8.1 0.8 pad_maximum_fusion.1
  8.9 4.2 %collective-permute-start.1 = (f32[64,512]{1,0:T(8,128)S(1)}, f32[64,512]{1,0:T(8,128)S(1)}, u32[]{:S(2)}, u32[]{:S(2)}) collective-permute-start(f32[64,512]{1,0:T(8,128)S(1)} %pad_maximum_fusion.1), channel_id=1, source_target_pairs={{0,32},{16,48},{32,64},{48,80},{64,96},{80,112},{96,128},{112,144}... | collective-permute-start | bytes 393224 | tf_op jit(solution)/shard_map/ppermute | solution.py:300
  13.1 3.2 %collective-permute-start = (f32[32,512]{1,0:T(8,128)}, f32[32,512]{1,0:T(8,128)S(1)}, u32[]{:S(2)}, u32[]{:S(2)}) collective-permute-start(f32[32,512]{1,0:T(8,128)} %a0_ref.1), channel_id=1, source_target_pairs={{0,16},{16,32},{32,48},{48,64},{64,80},{80,96},{96,112},{112,128},... | collective-permute-start | bytes 196616 | tf_op jit(solution)/shard_map/ppermute | solution.py:300
  16.3 4.6 %collective-permute-start.2 = (f32[32,512]{1,0:T(8,128)}, f32[32,512]{1,0:T(8,128)S(1)}, u32[]{:S(2)}, u32[]{:S(2)}) collective-permute-start(f32[32,512]{1,0:T(8,128)} %a0_ref.1), channel_id=1, source_target_pairs={{0,48},{16,64},{32,80},{48,96},{64,112},{80,128},{96,144},{112,160... | collective-permute-start | bytes 196616 | tf_op jit(solution)/shard_map/ppermute | solution.py:300
  21.1 2.4 %collective-permute-done.a1_ref = f32[32,512]{1,0:T(8,128)S(1)} collective-permute-done((f32[32,512]{1,0:T(8,128)}, f32[32,512]{1,0:T(8,128)S(1)}, u32[]{:S(2)}, u32[]{:S(2)}) %collective-permute-start) | collective-permute-done | bytes 65568 | tf_op jit(solution)/shard_map/ppermute | solution.py:300
  23.4 2.8 %collective-permute-done.2.a3_ref = f32[32,512]{1,0:T(8,128)S(1)} collective-permute-done((f32[32,512]{1,0:T(8,128)}, f32[32,512]{1,0:T(8,128)S(1)}, u32[]{:S(2)}, u32[]{:S(2)}) %collective-permute-start.2) | collective-permute-done | bytes 65568 | tf_op jit(solution)/shard_map/ppermute | solution.py:300
  26.3 0.9 copy-done.1
  27.2 0.8 copy-done.2
  28.1 1.8 shard_map.101
  29.8 0.7 select_maximum_fusion
  30.5 0.9 pad_maximum_fusion
  31.4 1.9 collective-permute-start.5
  33.3 7.7 %collective-permute-start.4 = (f32[72,512]{1,0:T(8,128)S(1)}, f32[72,512]{1,0:T(8,128)S(1)}, u32[]{:S(2)}, u32[]{:S(2)}) collective-permute-start(f32[72,512]{1,0:T(8,128)S(1)} %pad_maximum_fusion), channel_id=1, source_target_pairs={{0,32},{16,48},{32,64},{48,80},{64,96},{80,112},{96,128},{112,144}... | collective-permute-start | bytes 442376 | tf_op jit(solution)/shard_map/ppermute | solution.py:300
  41.1 1.9 collective-permute-start.3
  43.0 9.8 %collective-permute-done.4 = f32[72,512]{1,0:T(8,128)S(1)} collective-permute-done((f32[72,512]{1,0:T(8,128)S(1)}, f32[72,512]{1,0:T(8,128)S(1)}, u32[]{:S(2)}, u32[]{:S(2)}) %collective-permute-start.4) | collective-permute-done | bytes 147488 | tf_op jit(solution)/shard_map/ppermute | solution.py:300
  52.9 4.1 %collective-permute-done.3 = f32[72,512]{1,0:T(8,128)S(1)} collective-permute-done((f32[72,512]{1,0:T(8,128)S(1)}, f32[72,512]{1,0:T(8,128)S(1)}, u32[]{:S(2)}, u32[]{:S(2)}) %collective-permute-start.3) | collective-permute-done | bytes 147488 | tf_op jit(solution)/shard_map/ppermute | solution.py:300
  57.0 0.7 concatenate.21
  57.9 0.9 constant_dynamic-update-slice_fusion
  58.8 0.7 slice_dynamic-update-slice_fusion
  59.7 31.5 %all-gather.1 = f32[384,512]{1,0:T(8,128)S(1)} all-gather(f32[24,512]{1,0:T(8,128)S(1)} %concatenate.22), channel_id=3, replica_groups=mesh['tm'=32,'panel'=16] {'panel'}, dimensions={0}, use_global_device_ids=true | all-gather | bytes 835584 | tf_op jit(solution)/shard_map/all_gather | solution.py:304
  91.4 0.7 reshape.51.vec_ref
  92.7 3.6 %all-gather.4.cloned.1.call-done = f32[3840,512]{1,0:T(8,128)} async-done(((f32[240,512]{1,0:T(8,128)}), f32[3840,512]{1,0:T(8,128)}) %all-gather.4.cloned.1.call-update) | async-done | bytes 7864336 | tf_op jit(solution)/shard_map/all_gather | solution.py:304
  96.3 10.7 %shard_map.102 = (f32[16,32,256]{2,1,0:T(8,128)}, f32[8,512]{1,0:T(8,128)}, bf16[2,512,512]{2,1,0:T(8,128)(2,1)}, bf16[2,512,512]{2,1,0:T(8,128)(2,1)}, bf16[2,5...) custom-call(f32[16,240,512]{2,1,0:T(8,128)} %bitcast.28, f32[192,512]{1,0:T(8,128)} %copy-done.14, ...), custom_call_target="tpu_custom_call" | custom-call | flops 4831838208 | bytes 8282112 | tf_op jit(solution)/shard_map/pallas_call | solution.py:287
  107.0 4.3 %all-to-all-start = ((f32[16,32,256]{2,1,0:T(8,128)}), f32[16,32,256]{2,1,0:T(8,128)S(1)}, u32[]{:S(2)}, u32[]{:S(2)}) async-start(f32[16,32,256]{2,1,0:T(8,128)} %get-tuple-element.58), calls=%async_computation | async-start | bytes 1048576 | tf_op jit(solution)/shard_map/all_to_all | solution.py:308
  111.3 0.7 pad_maximum_fusion.2.own_ref
  112.0 6.6 %shard_map.103 = (f32[32,512]{1,0:T(8,128)}, f32[32,512]{1,0:T(8,128)}, bf16[2,512,512]{2,1,0:T(8,128)(2,1)}, bf16[2,512,512]{2,1,0:T(8,128)(2,1)}, bf16[2,512,512]{2,1,0:T(8,128)(2,1)}) custom-call(f32[16,240,512]{2,1,0:T(8,128)} %bitcast.29, f32[16,24,512]{2,1,0:T(8,128)} %bitcast.33, s32[2]{0:T(128)} %copy-done.3, ...), custom_call_target="tpu_custom_call" | custom-call | flops 1610612736 | bytes 10747912 | tf_op jit(solution)/shard_map/pallas_call | solution.py:287
  118.6 7.7 %collective-permute-start.6 = (f32[32,512]{1,0:T(8,128)}, f32[32,512]{1,0:T(8,128)S(1)}, u32[]{:S(2)}, u32[]{:S(2)}) collective-permute-start(f32[32,512]{1,0:T(8,128)} %get-tuple-element.61.p2rows_ref), channel_id=1, source_target_pairs={{64,0},{80,16},{96,32},{112,48},{128,64},{144,80},{160,96},{176,11... | collective-permute-start | bytes 196616 | tf_op jit(solution)/shard_map/ppermute | solution.py:300
  126.3 6.0 %shard_map.104 = (bf16[2,512,512]{2,1,0:T(8,128)(2,1)}, bf16[2,512,512]{2,1,0:T(8,128)(2,1)}, bf16[2,512,512]{2,1,0:T(8,128)(2,1)}) custom-call(f32[16,240,512]{2,1,0:T(8,128)} %bitcast.30, bf16[2,512,512]{2,1,0:T(8,128)(2,1)} %get-tuple-element.60.bp_ref), custom_call_target="tpu_custom_call" | custom-call | flops 2415919104 | bytes 8912896 | tf_op jit(solution)/shard_map/pallas_call | solution.py:287
  132.4 0.8 copy-done.11
  133.1 5.3 %shard_map.105 = (f32[40,512]{1,0:T(8,128)}, f32[40,512]{1,0:T(8,128)}, f32[40,512]{1,0:T(8,128)}) custom-call(f32[512,256]{1,0:T(8,128)} %bitcast.34, f32[64,512]{1,0:T(8,128)} %pad_maximum_fusion.2.own_ref, f32[8,512]{1,0:T(8,128)} %get-tuple-element.63.vec_ref, bf16[2,512,512]{2,1,0:T(8,128)(2,1)} %get-tuple-element.64.p0p_ref, ...), custom_call_target="tpu_custom_call" | custom-call | flops 805306368 | bytes 8011776 | tf_op jit(solution)/shard_map/pallas_call | solution.py:287
  138.5 4.5 %collective-permute-start.8 = (f32[40,512]{1,0:T(8,128)}, f32[40,512]{1,0:T(8,128)S(1)}, u32[]{:S(2)}, u32[]{:S(2)}) collective-permute-start(f32[40,512]{1,0:T(8,128)} %get-tuple-element.72), channel_id=1, source_target_pairs={{64,0},{80,16},{96,32},{112,48},{128,64},{144,80},{160,96},{176,11... | collective-permute-start | bytes 245768 | tf_op jit(solution)/shard_map/ppermute | solution.py:300
  142.9 4.7 %collective-permute-start.7 = (f32[40,512]{1,0:T(8,128)}, f32[40,512]{1,0:T(8,128)S(1)}, u32[]{:S(2)}, u32[]{:S(2)}) collective-permute-start(f32[40,512]{1,0:T(8,128)} %get-tuple-element.71.plus_ref), channel_id=1, source_target_pairs={{0,64},{16,80},{32,96},{48,112},{64,128},{80,144},{96,160},{112,17... | collective-permute-start | bytes 245768 | tf_op jit(solution)/shard_map/ppermute | solution.py:300
  147.7 2.3 %collective-permute-done.8.later_ref = f32[40,512]{1,0:T(8,128)S(1)} collective-permute-done((f32[40,512]{1,0:T(8,128)}, f32[40,512]{1,0:T(8,128)S(1)}, u32[]{:S(2)}, u32[]{:S(2)}) %collective-permute-start.8) | collective-permute-done | bytes 81952 | tf_op jit(solution)/shard_map/ppermute | solution.py:300
  150.0 4.4 %collective-permute-done.7.prior_ref = f32[40,512]{1,0:T(8,128)S(1)} collective-permute-done((f32[40,512]{1,0:T(8,128)}, f32[40,512]{1,0:T(8,128)S(1)}, u32[]{:S(2)}, u32[]{:S(2)}) %collective-permute-start.7) | collective-permute-done | bytes 81952 | tf_op jit(solution)/shard_map/ppermute | solution.py:300
  154.4 0.9 copy-done.4
  155.3 0.9 copy-done.6
  156.2 2.0 %shard_map.106 = (f32[16,32,128]{2,1,0:T(8,128)}, f32[32,512]{1,0:T(8,128)S(1)}, f32[8,512]{1,0:T(8,128)S(1)}) custom-call(f32[40,512]{1,0:T(8,128)S(1)} %collective-permute-done.7.prior_ref, f32[40,512]{1,0:T(8,128)S(1)} %collective-permute-done.8.later_ref, f32[32,512]{1,0:T(8,128)S(1)} %collective-permute-done.6.later_p2_ref, f32[40,512]{1,0:T(8,128)S(1)} %copy-done.4, ...), custom_call_target="tpu_custom_call" | custom-call | flops 805306368 | bytes 2490368 | tf_op jit(solution)/shard_map/pallas_call | solution.py:287
  158.3 9.3 %all-to-all-start.1 = ((f32[16,32,128]{2,1,0:T(8,128)}), f32[16,32,128]{2,1,0:T(8,128)S(1)}, u32[]{:S(2)}, u32[]{:S(2)}) async-start(f32[16,32,128]{2,1,0:T(8,128)} %get-tuple-element.77), calls=%async_computation.1 | async-start | bytes 524288 | tf_op jit(solution)/shard_map/all_to_all | solution.py:308
  167.5 0.7 slice.83
  168.2 0.7 slice.81
  169.2 2.2 %collective-permute-start.9 = (f32[32,512]{1,0:T(8,128)S(1)}, f32[32,512]{1,0:T(8,128)S(1)}, u32[]{:S(2)}, u32[]{:S(2)}) collective-permute-start(f32[32,512]{1,0:T(8,128)S(1)} %get-tuple-element.76), channel_id=1, source_target_pairs={{0,64},{16,80},{32,96},{48,112},{64,128},{80,144},{96,160},{112,17... | collective-permute-start | bytes 196616 | tf_op jit(solution)/shard_map/ppermute | solution.py:300
  171.4 8.1 %all-to-all-done.1 = f32[16,32,128]{2,1,0:T(8,128)S(1)} async-done(((f32[16,32,128]{2,1,0:T(8,128)}), f32[16,32,128]{2,1,0:T(8,128)S(1)}, u32[]{:S(2)}, u32[]{:S(2)}) %all-to-all-start.1) | async-done | bytes 262176 | tf_op jit(solution)/shard_map/all_to_all | solution.py:308
  179.5 0.9 copy-done.5
  180.4 0.9 copy-done.7
  181.3 1.5 shard_map.107
  182.8 1.9 collective-permute-start.10
  186.0 7.9 %collective-permute-done.10 = f32[40,512]{1,0:T(8,128)S(1)} collective-permute-done((f32[40,512]{1,0:T(8,128)S(1)}, f32[40,512]{1,0:T(8,128)S(1)}, u32[]{:S(2)}, u32[]{:S(2)}) %collective-permute-start.10) | collective-permute-done | bytes 81952 | tf_op jit(solution)/shard_map/ppermute | solution.py:300
  (57 shorter events, 4.0 us)
Async XLA Ops:
  7.2 89.2 %all-gather.4.cloned.1.call-start = ((), (), s32[]{:S(2)}) async-start(), calls=%async_computation.2 | async-start | bytes 8355840 | tf_op jit(solution)/shard_map/all_gather | solution.py:304
  8.9 17.4 %collective-permute-start.1 = (f32[64,512]{1,0:T(8,128)S(1)}, f32[64,512]{1,0:T(8,128)S(1)}, u32[]{:S(2)}, u32[]{:S(2)}) collective-permute-start(f32[64,512]{1,0:T(8,128)S(1)} %pad_maximum_fusion.1), channel_id=1, source_target_pairs={{0,32},{16,48},{32,64},{48,80},{64,96},{80,112},{96,128},{112,144}... | collective-permute-start | bytes 393224 | tf_op jit(solution)/shard_map/ppermute | solution.py:300
  13.1 10.3 %collective-permute-start = (f32[32,512]{1,0:T(8,128)}, f32[32,512]{1,0:T(8,128)S(1)}, u32[]{:S(2)}, u32[]{:S(2)}) collective-permute-start(f32[32,512]{1,0:T(8,128)} %a0_ref.1), channel_id=1, source_target_pairs={{0,16},{16,32},{32,48},{48,64},{64,80},{80,96},{96,112},{112,128},... | collective-permute-start | bytes 196616 | tf_op jit(solution)/shard_map/ppermute | solution.py:300
  16.3 9.9 %collective-permute-start.2 = (f32[32,512]{1,0:T(8,128)}, f32[32,512]{1,0:T(8,128)S(1)}, u32[]{:S(2)}, u32[]{:S(2)}) collective-permute-start(f32[32,512]{1,0:T(8,128)} %a0_ref.1), channel_id=1, source_target_pairs={{0,48},{16,64},{32,80},{48,96},{64,112},{80,128},{96,144},{112,160... | collective-permute-start | bytes 196616 | tf_op jit(solution)/shard_map/ppermute | solution.py:300
  21.1 85.9 %copy-start.3 = (s32[2]{0:T(128)}, s32[2]{0:T(128)S(1)}, u32[]{:S(2)}) copy-start(s32[2]{0:T(128)S(1)} %pad_add_fusion.place_ref) | copy-start | bytes 28
  26.3 0.9 copy-start.1
  27.2 0.8 copy-start.2
  31.4 11.6 %collective-permute-start.5 = (f32[72,512]{1,0:T(8,128)S(1)}, f32[72,512]{1,0:T(8,128)S(1)}, u32[]{:S(2)}, u32[]{:S(2)}) collective-permute-start(f32[72,512]{1,0:T(8,128)S(1)} %pad_maximum_fusion), channel_id=1, source_target_pairs={{0,48},{16,64},{32,80},{48,96},{64,112},{80,128},{96,144},{112,160... | collective-permute-start | bytes 442376 | tf_op jit(solution)/shard_map/ppermute | solution.py:300
  33.3 19.5 %collective-permute-start.4 = (f32[72,512]{1,0:T(8,128)S(1)}, f32[72,512]{1,0:T(8,128)S(1)}, u32[]{:S(2)}, u32[]{:S(2)}) collective-permute-start(f32[72,512]{1,0:T(8,128)S(1)} %pad_maximum_fusion), channel_id=1, source_target_pairs={{0,32},{16,48},{32,64},{48,80},{64,96},{80,112},{96,128},{112,144}... | collective-permute-start | bytes 442376 | tf_op jit(solution)/shard_map/ppermute | solution.py:300
  41.1 15.9 %collective-permute-start.3 = (f32[72,512]{1,0:T(8,128)S(1)}, f32[72,512]{1,0:T(8,128)S(1)}, u32[]{:S(2)}, u32[]{:S(2)}) collective-permute-start(f32[72,512]{1,0:T(8,128)S(1)} %pad_maximum_fusion), channel_id=1, source_target_pairs={{0,16},{16,32},{32,48},{48,64},{64,80},{80,96},{96,112},{112,128},... | collective-permute-start | bytes 442376 | tf_op jit(solution)/shard_map/ppermute | solution.py:300
  59.7 36.7 %copy-start.14 = (f32[192,512]{1,0:T(8,128)}, f32[192,512]{1,0:T(8,128)S(1)}, u32[]{:S(2)}) copy-start(f32[192,512]{1,0:T(8,128)S(1)} %get-tuple-element.88.own_ref) | copy-start | bytes 1179652
  91.2 15.8 %copy-start.10 = (f32[384,512]{1,0:T(8,128)}, f32[384,512]{1,0:T(8,128)S(1)}, u32[]{:S(2)}) copy-start(f32[384,512]{1,0:T(8,128)S(1)} %all-gather.1) | copy-start | bytes 2359300
  96.3 15.0 %copy-start.12 = (f32[32,512]{1,0:T(8,128)S(1)}, f32[32,512]{1,0:T(8,128)}, u32[]{:S(2)}) copy-start(f32[32,512]{1,0:T(8,128)} %param.8) | copy-start | bytes 196612
  107.0 25.3 %all-to-all-start = ((f32[16,32,256]{2,1,0:T(8,128)}), f32[16,32,256]{2,1,0:T(8,128)S(1)}, u32[]{:S(2)}, u32[]{:S(2)}) async-start(f32[16,32,256]{2,1,0:T(8,128)} %get-tuple-element.58), calls=%async_computation | async-start | bytes 1048576 | tf_op jit(solution)/shard_map/all_to_all | solution.py:308
  118.6 35.9 %copy-start = (bf16[2,512,512]{2,1,0:T(8,128)(2,1)S(1)}, bf16[2,512,512]{2,1,0:T(8,128)(2,1)}, u32[]{:S(2)}) copy-start(bf16[2,512,512]{2,1,0:T(8,128)(2,1)} %get-tuple-element.70.m2_ref) | copy-start | bytes 3145732
  118.6 35.9 %copy-start.8 = (bf16[2,512,512]{2,1,0:T(8,128)(2,1)S(1)}, bf16[2,512,512]{2,1,0:T(8,128)(2,1)}, u32[]{:S(2)}) copy-start(bf16[2,512,512]{2,1,0:T(8,128)(2,1)} %get-tuple-element.75.d_ref) | copy-start | bytes 3145732
  118.6 13.7 %collective-permute-start.6 = (f32[32,512]{1,0:T(8,128)}, f32[32,512]{1,0:T(8,128)S(1)}, u32[]{:S(2)}, u32[]{:S(2)}) collective-permute-start(f32[32,512]{1,0:T(8,128)} %get-tuple-element.61.p2rows_ref), channel_id=1, source_target_pairs={{64,0},{80,16},{96,32},{112,48},{128,64},{144,80},{160,96},{176,11... | collective-permute-start | bytes 196616 | tf_op jit(solution)/shard_map/ppermute | solution.py:300
  132.3 47.2 %copy-start.9 = (f32[32,512]{1,0:T(8,128)S(1)}, f32[32,512]{1,0:T(8,128)}, u32[]{:S(2)}) copy-start(f32[32,512]{1,0:T(8,128)} %get-tuple-element.61.p2rows_ref) | copy-start | bytes 196612
  132.3 52.4 %copy-start.13 = (f32[32,512]{1,0:T(8,128)S(1)}, f32[32,512]{1,0:T(8,128)}, u32[]{:S(2)}) copy-start(f32[32,512]{1,0:T(8,128)} %get-tuple-element.81) | copy-start | bytes 196612
  132.3 0.8 copy-start.11
  138.5 11.5 %collective-permute-start.8 = (f32[40,512]{1,0:T(8,128)}, f32[40,512]{1,0:T(8,128)S(1)}, u32[]{:S(2)}, u32[]{:S(2)}) collective-permute-start(f32[40,512]{1,0:T(8,128)} %get-tuple-element.72), channel_id=1, source_target_pairs={{64,0},{80,16},{96,32},{112,48},{128,64},{144,80},{160,96},{176,11... | collective-permute-start | bytes 245768 | tf_op jit(solution)/shard_map/ppermute | solution.py:300
  142.9 11.5 %collective-permute-start.7 = (f32[40,512]{1,0:T(8,128)}, f32[40,512]{1,0:T(8,128)S(1)}, u32[]{:S(2)}, u32[]{:S(2)}) collective-permute-start(f32[40,512]{1,0:T(8,128)} %get-tuple-element.71.plus_ref), channel_id=1, source_target_pairs={{0,64},{16,80},{32,96},{48,112},{64,128},{80,144},{96,160},{112,17... | collective-permute-start | bytes 245768 | tf_op jit(solution)/shard_map/ppermute | solution.py:300
  154.4 0.9 copy-start.4
  155.3 0.9 copy-start.6
  158.3 21.3 %all-to-all-start.1 = ((f32[16,32,128]{2,1,0:T(8,128)}), f32[16,32,128]{2,1,0:T(8,128)S(1)}, u32[]{:S(2)}, u32[]{:S(2)}) async-start(f32[16,32,128]{2,1,0:T(8,128)} %get-tuple-element.77), calls=%async_computation.1 | async-start | bytes 524288 | tf_op jit(solution)/shard_map/all_to_all | solution.py:308
  169.2 15.5 %collective-permute-start.9 = (f32[32,512]{1,0:T(8,128)S(1)}, f32[32,512]{1,0:T(8,128)S(1)}, u32[]{:S(2)}, u32[]{:S(2)}) collective-permute-start(f32[32,512]{1,0:T(8,128)S(1)} %get-tuple-element.76), channel_id=1, source_target_pairs={{0,64},{16,80},{32,96},{48,112},{64,128},{80,144},{96,160},{112,17... | collective-permute-start | bytes 196616 | tf_op jit(solution)/shard_map/ppermute | solution.py:300
  179.5 0.9 copy-start.5
  180.4 0.9 copy-start.7
  182.8 11.1 %collective-permute-start.10 = (f32[40,512]{1,0:T(8,128)S(1)}, f32[40,512]{1,0:T(8,128)S(1)}, u32[]{:S(2)}, u32[]{:S(2)}) collective-permute-start(f32[40,512]{1,0:T(8,128)S(1)} %get-tuple-element.79), channel_id=1, source_target_pairs={{0,64},{16,80},{32,96},{48,112},{64,128},{80,144},{96,160},{112,17... | collective-permute-start | bytes 245768 | tf_op jit(solution)/shard_map/ppermute | solution.py:300
Sparse Core Ops, SparseCore 0:
  30.0 66.3 all-gather.3

commit v8 on v7

--- a/solution.py
+++ b/solution.py
@@ -39,6 +39,11 @@
 
 def stacked(*parts):
     return jnp.concatenate(parts)
+
+
+def joined(pair, *parts):
+    low = split(jnp.concatenate(parts))
+    return jnp.concatenate([pair[0], low[0]]), jnp.concatenate([pair[1], low[1]])
 
 
 def sixteen(*rows):
@@ -133,27 +138,34 @@
     return pair
 
 
-def ready_kernel(rows, place_ref, a1_ref, late_ref, a3_ref, a0_ref, inverses_ref, ready_ref, head_ref, own, mixers, sems):
-    fetch = Fetch((a0_ref, inverses_ref), (own, mixers), sems)
+def prepare_kernel(rows, place_ref, a0_ref, inverses_ref, pair_ref, fixed_ref, head_ref):
     time, mine = place_ref[0], place_ref[1]
-    shape, half = a1_ref.shape, rows // 2
+    shape, half = a0_ref.shape, rows // 2
     row = lax.broadcasted_iota(jnp.int32, shape, 0) + mine * rows
     eye = (row == lax.broadcasted_iota(jnp.int32, shape, 1)).astype(F32)
-
-    def put(i, value, since):
-        ready_ref[i * rows : (i + 1) * rows] = jnp.where(time >= since, value, eye)
-
-    put(1, a1_ref[...], 1)
-    put(2, late_ref[:rows], 2)
-    put(5, late_ref[rows:], 3)
-    put(3, a3_ref[...], 3)
-    ready_ref[:rows] = fetch(0)
-    inverses = fetch(1)
-    put(4, inverses[0], 1)
-    put(6, inverses[1], 2)
-    m2 = jnp.where(time >= 4, inverses[2], eye)
+    a0 = a0_ref[...]
+    pair_ref[:rows] = a0
+    pair_ref[rows:] = inverses_ref[0]
+    fixed_ref[:rows] = a0
+    fixed_ref[rows : 2 * rows] = jnp.where(time >= 1, inverses_ref[0], eye)
+    fixed_ref[2 * rows : 3 * rows] = jnp.where(time >= 2, inverses_ref[1], eye)
+    m2 = jnp.where(time >= 4, inverses_ref[2], eye)
     head_ref[...] = m2[:half]
-    ready_ref[7 * rows :] = m2[half:]
+    fixed_ref[3 * rows :] = m2[half:]
+
+
+def ready_kernel(rows, place_ref, a1_ref, late_ref, a3_ref, fixed_ref, ready_ref):
+    time, mine = place_ref[0], place_ref[1]
+    shape = a1_ref.shape
+    row = lax.broadcasted_iota(jnp.int32, shape, 0) + mine * rows
+    eye = (row == lax.broadcasted_iota(jnp.int32, shape, 1)).astype(F32)
+    ready_ref[:rows] = fixed_ref[:rows]
+    ready_ref[rows : 2 * rows] = jnp.where(time >= 1, a1_ref[...], eye)
+    ready_ref[2 * rows : 3 * rows] = jnp.where(time >= 2, late_ref[:rows], eye)
+    ready_ref[3 * rows : 4 * rows] = jnp.where(time >= 3, a3_ref[...], eye)
+    ready_ref[4 * rows : 5 * rows] = fixed_ref[rows : 2 * rows]
+    ready_ref[5 * rows : 6 * rows] = jnp.where(time >= 3, late_ref[rows:], eye)
+    ready_ref[6 * rows :] = fixed_ref[2 * rows :]
 
 
 def first_kernel(
@@ -167,20 +179,19 @@
     u1, u2, u3, u4 = (u_ref[i : i + 1] for i in range(4))
 
     a0, m0 = part(0), part(1)
-    p0 = store(split(dot(a0, m0)))
-    mixed = dot(split(sixteen(e0 - u2)), m0)
+    both = dot(joined(a0, sixteen(e0 - u2)), m0)
+    p0, mixed = store(split(both[:width])), both[width:]
     a1 = part(2)
-    bw = store(split(dot(p0, a1)))
-    both = dot(split(stacked(j0, mixed)), a1)
-    y0, e_t = both[:rows], both[rows : rows + 1] + e1
+    both = dot(joined(p0, j0, mixed), a1)
+    bw = store(split(both[:width]))
+    y0, e_t = both[width : width + rows], both[width + rows : width + rows + 1] + e1
     a2, m0p = part(3), part(4)
-    p0p = store(split(dot(a2, m0p)))
-    mixed = dot(split(sixteen(e2 - u4)), m0p)
+    both = dot(joined(a2, sixteen(e2 - u4)), m0p)
+    p0p, mixed = store(split(both[:width])), both[width:]
     a3 = part(5)
-    bp = store(split(dot(p0p, a3)))
-    both = dot(split(stacked(j2, mixed)), a3)
-    y2, e_p = both[:rows], both[rows : rows + 1] + e3
-    b_t = dot_nt(split(sixteen(b1 + u1)), p0)[:1] + b0
+    both = dot(joined(p0p, j2, mixed), a3)
+    bp = store(split(both[:width]))
+    y2, e_p = both[width : width + rows], both[width + rows : width + rows + 1] + e3
     b_p = dot_nt(split(sixteen(b3 + u3)), p0p)[:1] + b2
     w1 = rowwise(c3, dot(split(sixteen(e_t)), a2)[:1])
     w2 = rowwise(c2, e_t)
@@ -195,7 +206,7 @@
     extra = in_lanes((w1, w2, w3, w4), rows, 2 * rows)
     for peer in range(packed_ref.shape[0]):
         packed_ref[peer, :, 6 * rows :] = extra
-    vout_ref[...] = jnp.concatenate([b_t, e_t, b_p, e_p, jnp.zeros((4, width), F32)])
+    vout_ref[...] = jnp.concatenate([b1 + u1, e_t, b_p, e_p, b0, jnp.zeros((3, width), F32)])
     store.finish()
 
 
@@ -237,34 +248,36 @@
     columns = received_ref[...].T
     x1, x2, x3, y0, y1, y2 = (columns[i * rows : (i + 1) * rows] for i in range(6))
     w1, w2, w3, w4 = (columns[6 * rows + i : 6 * rows + i + 1] for i in range(4))
-    b_t, e_t, b_p, e_p = (vec_ref[i : i + 1] for i in range(4))
+    mixed, e_t, b_p, e_p, b0 = (vec_ref[i : i + 1] for i in range(5))
     c0, j3 = own_ref[:rows], own_ref[rows:]
     inner = dot_nt(split(stacked(x3, sixteen(w1))), pair(0)) + stacked(x2, sixteen(b_p + w2))
-    other = dot_nt(split(x1), pair(1)) + c0
+    other = dot_nt(split(stacked(x1, sixteen(mixed))), pair(1)) + stacked(c0, sixteen(b0))
     inner_j = dot(split(stacked(y0, sixteen(-w3))), pair(2)) + stacked(y1, sixteen(e_t - w4))
     other_j = dot(split(y2), pair(3)) + j3
-    outer = dot_nt(split(inner), pair(4)) + stacked(other, sixteen(b_t))
+    outer = dot_nt(split(inner), pair(4)) + other
     outer_j = dot(split(inner_j), pair(5)) + stacked(other_j, sixteen(e_p))
     plus_ref[...] = outer[: rows + 8]
-    state_ref[...] = outer_j[: rows + 8]
+    state_ref[:rows] = outer[:rows]
+    state_ref[rows : 2 * rows] = outer_j[:rows]
+    state_ref[2 * rows :] = sixteen(outer[rows : rows + 1], outer_j[rows : rows + 1])[:8]
     minus_ref[...] = dot(split(outer_j), pair(6))[: rows + 8]
 
 
 def third_kernel(
-    rows, prior_ref, later_ref, later_p2_ref, plus_ref, state_ref, m2_ref, d_ref, packed_ref, a_ref, row_ref, buf, sems
+    rows, prior_ref, later_ref, later_p2_ref, state_ref, m2_ref, d_ref, packed_ref, a_ref, row_ref, buf, sems
 ):
     pair = fetch_pairs((m2_ref, d_ref), buf, sems)
     v = dot_nt(split(prior_ref[:rows]), pair(0))
     d = pair(1)
     v = dot_nt(split(v), d)
     both = dot(split(stacked(later_ref[:rows], later_p2_ref[...], sixteen(later_ref[rows : rows + 1]))), d)
-    pack((v, plus_ref[:rows], both[:rows], state_ref[:rows]), packed_ref, rows)
+    pack((v, state_ref[:rows], both[:rows], state_ref[rows : 2 * rows]), packed_ref, rows)
     a_ref[...] = both[rows : 2 * rows]
     row_ref[...] = both[2 * rows : 2 * rows + 8]
 
 
 def last_kernel(
-    rows, received_ref, p2rows_ref, prior_ref, plus_ref, state_ref, part_ref, d_ref, new_c_ref, back_ref, j_ref, b_ref,
+    rows, received_ref, p2rows_ref, prior_ref, state_ref, part_ref, d_ref, new_c_ref, back_ref, j_ref, b_ref,
     buf, sems
 ):
     pair = fetch_pairs((d_ref,), buf, sems)
@@ -273,12 +286,12 @@
     d = pair(0)
     back_ref[:rows] = dot(split(z), d) + j_rows
     j_ref[...] = j_rows
-    later_e = part_ref[:, 1:2] - rowwise(z, plus_ref[rows : rows + 1])
+    later_e = part_ref[:, 1:2] - rowwise(z, state_ref[2 * rows : 2 * rows + 1])
     row = in_lanes((later_e,), rows, 128).T[:8]
     back_ref[rows:] = jnp.concatenate([row, jnp.zeros((8, back_ref.shape[1] - rows), F32)], axis=1)
     new_c_ref[...] = dot_nt(split(v), d) + c_rows
     new_b = part_ref[:, 0:1] + rowwise(p2rows_ref[...], prior_ref[rows : rows + 1])
-    b_ref[...] = in_lanes((new_b + rowwise(v, state_ref[rows : rows + 1]),), rows, 128)
+    b_ref[...] = in_lanes((new_b + rowwise(v, state_ref[2 * rows + 1 : 2 * rows + 2]),), rows, 128)
 
 
 def call(kernel, rows, operands, outs, placed=(), kept=(), scratch=(), flops=0, grant=58, small=()):
@@ -316,24 +329,29 @@
     place = jnp.stack([time, mine]).astype(jnp.int32)
     a0, c0, j0 = transition, covariance, information
 
-    sent = passed_along(a0, 1), passed_along(jnp.concatenate([a0, inverses[0]]), 2), passed_along(a0, 3)
-    a1, late, a3 = lax.optimization_barrier(sent)
-    ready, head = call(
-        ready_kernel,
-        rows,
-        (place, a1, late, a3, a0, inverses),
-        [((8 * rows - rows // 2, width), F32), ((rows // 2, width), F32)],
-        {4, 5},
-        (),
-        [pltpu.VMEM(a0.shape, F32), pltpu.VMEM(inverses.shape, F32), pltpu.SemaphoreType.DMA((2,))],
+    both, fixed, head = call(
+        prepare_kernel,
+        rows,
+        (place, a0, inverses),
+        [((2 * rows, width), F32), ((4 * rows - rows // 2, width), F32), ((rows // 2, width), F32)],
         small=(0,),
         grant=4,
     )
-    whole = gathered(ready)
+    sent = passed_along(both, 2), passed_along(a0, 1), passed_along(a0, 3)
+    late, a1, a3 = lax.optimization_barrier(sent)
+    (ready,) = call(
+        ready_kernel,
+        rows,
+        (place, a1, late, a3, fixed),
+        [((8 * rows - rows // 2, width), F32)],
+        small=(0,),
+        grant=4,
+    )
 
     v0 = jnp.stack([offset, info_vector])
     own = jnp.concatenate([c0, j0, jnp.pad(v0, ((0, 6), (0, width - rows)))])
-    own, head = lax.optimization_barrier((own, head))
+    own, ready = lax.optimization_barrier((own, ready))
+    whole = gathered(ready)
     got = lax.optimization_barrier(tuple(passed_along(own, by) for by in (1, 2, 3)))
     (c1, c2, c3), (j1, j2, j3) = ([g[i * rows : (i + 1) * rows] for g in got] for i in range(2))
     slices = jnp.concatenate([v0] + [g[2 * rows : 2 * rows + 2, :rows] for g in got])
@@ -391,7 +409,7 @@
         second_kernel,
         rows,
         (received, jnp.concatenate([c0, j3]), vec, p0p, p0, g0, g0p, p1, g1, m2),
-        [flat(8)] * 3,
+        [flat(8), flat(8), flat(rows + 8)],
         range(3, 10),
         (),
         pairs(7),
@@ -401,9 +419,9 @@
     packed, later_a, row = call(
         third_kernel,
         rows,
-        (prior, later, later_p2, plus, state, m2, d),
+        (prior, later, later_p2, state, m2, d),
         [((peers, rows, 4 * rows), F32), flat(), ((8, width), F32)],
-        {5, 6},
+        {4, 5},
         (),
         pairs(2),
         flops=mults,
@@ -415,15 +433,15 @@
     def own_part(vector):
         return lax.dynamic_slice_in_dim(vector, mine * rows, rows, 0)
 
-    own_e = own_part(state[rows])
-    parts = jnp.stack([own_part(plus[rows]), own_part(row[0]) + own_e], axis=1)
+    own_e = own_part(state[2 * rows + 1])
+    parts = jnp.stack([own_part(state[2 * rows]), own_part(row[0]) + own_e], axis=1)
     parts = jnp.pad(parts, ((0, 0), (0, 126)))
     new_c, later_j, own_j, new_b = call(
         last_kernel,
         rows,
-        (back, p2rows, prior, plus, state, parts, d),
+        (back, p2rows, prior, state, parts, d),
         [flat(), flat(8), flat(), ((rows, 128), F32)],
-        {6},
+        {5},
         (),
         pairs(1),
         flops=mults,

time: 204 us -> 199 us (0.975)
  the two profiles are of different devices: /device:TPU:7 before, /device:TPU:5 now
where the time goes in v8:
time: 199 us; the launch traced here: 198 us
  starting transfers between devices  61.2 us (31%)
  waiting for transfers between devices  43.9 us (22%)
  Pallas kernels  33.4 us (17%)
  blocking collectives  31 us (16%)
  between operations  14.4 us (7%)
  local copies, waits for them, and re-layouts  7.68 us (4%)
  other arithmetic  6.73 us (3%)
    ppermute x11, starting transfers between devices, passed_along(): lax.ppermute(shard, 'tm', [(i, i + by) for i in range(peers) if 0 <= i +...  45.6 us
    pallas_call x8, Pallas kernels, call(): pl.pallas_call(functools.partial(kernel, rows), out_shape=[jax.ShapeDtype...  33.4 us
    ppermute x11, waiting for transfers between devices, passed_along(): lax.ppermute(shard, 'tm', [(i, i + by) for i in range(peers) if 0 <= i +...  32.1 us
    all_gather x1, blocking collectives, gathered(): return lax.all_gather(shard, 'panel', axis=0, tiled=False)  31 us
    all_to_all x2, starting transfers between devices, exchanged(): lax.all_to_all(packed, 'panel', split_axis=0, concat_axis=0, tiled=True)  15.5 us
    all_to_all x2, waiting for transfers between devices, exchanged(): lax.all_to_all(packed, 'panel', split_axis=0, concat_axis=0, tiled=True)  6.27 us
    all_gather x1, waiting for transfers between devices, gathered(): return lax.all_gather(shard, 'panel', axis=0, tiled=False)  5.46 us
    unnamed x28, local copies, waits for them, and re-layouts  4.42 us
  transfers between devices with their start and end apart: 14, of which 9 were waited for; matrix products, arithmetic and copies ran while one was open for 4% of the time, Pallas kernels for 7%

profile of v8, /device:TPU:5, one launch (start us, length us, event | category | flops | bytes accessed | tf_op | source)
XLA Modules:
  0.0 198.2 jit_solution(15130659831455680253)
XLA Ops:
  7.2 5.2 %collective-permute-start.2 = (f32[32,512]{1,0:T(8,128)}, f32[32,512]{1,0:T(8,128)S(1)}, u32[]{:S(2)}, u32[]{:S(2)}) collective-permute-start(f32[32,512]{1,0:T(8,128)} %a0_ref.1), channel_id=1, source_target_pairs={{0,48},{16,64},{32,80},{48,96},{64,112},{80,128},{96,144},{112,160... | collective-permute-start | bytes 196616 | tf_op jit(solution)/shard_map/ppermute | solution.py:313
  12.4 4.4 %collective-permute-start.1 = (f32[32,512]{1,0:T(8,128)}, f32[32,512]{1,0:T(8,128)S(1)}, u32[]{:S(2)}, u32[]{:S(2)}) collective-permute-start(f32[32,512]{1,0:T(8,128)} %a0_ref.1), channel_id=1, source_target_pairs={{0,16},{16,32},{32,48},{48,64},{64,80},{80,96},{96,112},{112,128},... | collective-permute-start | bytes 196616 | tf_op jit(solution)/shard_map/ppermute | solution.py:313
  17.0 0.9 copy-done.1
  17.9 0.8 copy-done.2
  19.3 2.4 %collective-permute-start = (f32[64,512]{1,0:T(8,128)S(1)}, f32[64,512]{1,0:T(8,128)S(1)}, u32[]{:S(2)}, u32[]{:S(2)}) collective-permute-start(f32[64,512]{1,0:T(8,128)S(1)} %get-tuple-element.46), channel_id=1, source_target_pairs={{0,32},{16,48},{32,64},{48,80},{64,96},{80,112},{96,128},{112,144}... | collective-permute-start | bytes 393224 | tf_op jit(solution)/shard_map/ppermute | solution.py:313
  21.7 0.7 select_maximum_fusion
  22.4 0.9 pad_maximum_fusion
  23.3 8.5 %collective-permute-done.late_ref = f32[64,512]{1,0:T(8,128)S(1)} collective-permute-done((f32[64,512]{1,0:T(8,128)S(1)}, f32[64,512]{1,0:T(8,128)S(1)}, u32[]{:S(2)}, u32[]{:S(2)}) %collective-permute-start) | collective-permute-done | bytes 131104 | tf_op jit(solution)/shard_map/ppermute | solution.py:313
  31.8 1.4 shard_map.102
  33.2 1.9 collective-permute-start.5
  35.1 2.7 %collective-permute-start.4 = (f32[72,512]{1,0:T(8,128)S(1)}, f32[72,512]{1,0:T(8,128)S(1)}, u32[]{:S(2)}, u32[]{:S(2)}) collective-permute-start(f32[72,512]{1,0:T(8,128)S(1)} %pad_maximum_fusion), channel_id=1, source_target_pairs={{0,32},{16,48},{32,64},{48,80},{64,96},{80,112},{96,128},{112,144}... | collective-permute-start | bytes 442376 | tf_op jit(solution)/shard_map/ppermute | solution.py:313
  37.8 2.3 %collective-permute-start.3 = (f32[72,512]{1,0:T(8,128)S(1)}, f32[72,512]{1,0:T(8,128)S(1)}, u32[]{:S(2)}, u32[]{:S(2)}) collective-permute-start(f32[72,512]{1,0:T(8,128)S(1)} %pad_maximum_fusion), channel_id=1, source_target_pairs={{0,16},{16,32},{32,48},{48,64},{64,80},{80,96},{96,112},{112,128},... | collective-permute-start | bytes 442376 | tf_op jit(solution)/shard_map/ppermute | solution.py:313
  40.1 9.2 %collective-permute-done.5 = f32[72,512]{1,0:T(8,128)S(1)} collective-permute-done((f32[72,512]{1,0:T(8,128)S(1)}, f32[72,512]{1,0:T(8,128)S(1)}, u32[]{:S(2)}, u32[]{:S(2)}) %collective-permute-start.5) | collective-permute-done | bytes 147488 | tf_op jit(solution)/shard_map/ppermute | solution.py:313
  49.3 1.8 collective-permute-done.4
  51.1 2.9 %collective-permute-done.3 = f32[72,512]{1,0:T(8,128)S(1)} collective-permute-done((f32[72,512]{1,0:T(8,128)S(1)}, f32[72,512]{1,0:T(8,128)S(1)}, u32[]{:S(2)}, u32[]{:S(2)}) %collective-permute-start.3) | collective-permute-done | bytes 147488 | tf_op jit(solution)/shard_map/ppermute | solution.py:313
  53.9 0.7 concatenate.17
  54.9 0.9 constant_dynamic-update-slice_fusion
  55.8 0.7 slice_dynamic-update-slice_fusion
  56.7 31.0 %all-gather.1 = f32[384,512]{1,0:T(8,128)S(1)} all-gather(f32[24,512]{1,0:T(8,128)S(1)} %concatenate.18), channel_id=3, replica_groups=mesh['tm'=32,'panel'=16] {'panel'}, dimensions={0}, use_global_device_ids=true | all-gather | bytes 835584 | tf_op jit(solution)/shard_map/all_gather | solution.py:317
  87.8 0.7 reshape.51.vec_ref
  88.5 0.6 slice_reduce_fusion.u_ref
  89.1 5.5 %all-gather.4.cloned.1.call-done = f32[3840,512]{1,0:T(8,128)} async-done(((f32[240,512]{1,0:T(8,128)}), f32[3840,512]{1,0:T(8,128)}) %all-gather.4.cloned.1.call-update) | async-done | bytes 7864336 | tf_op jit(solution)/shard_map/all_gather | solution.py:317
  94.6 10.0 %shard_map.103 = (f32[16,32,256]{2,1,0:T(8,128)}, f32[8,512]{1,0:T(8,128)}, bf16[2,512,512]{2,1,0:T(8,128)(2,1)}, bf16[2,512,512]{2,1,0:T(8,128)(2,1)}, bf16[2,5...) custom-call(f32[16,240,512]{2,1,0:T(8,128)} %bitcast.26, f32[192,512]{1,0:T(8,128)} %copy-done.12, ...), custom_call_target="tpu_custom_call" | custom-call | flops 4831838208 | bytes 8282112 | tf_op jit(solution)/shard_map/pallas_call | solution.py:300
  104.6 4.3 %all-to-all-start = ((f32[16,32,256]{2,1,0:T(8,128)}), f32[16,32,256]{2,1,0:T(8,128)S(1)}, u32[]{:S(2)}, u32[]{:S(2)}) async-start(f32[16,32,256]{2,1,0:T(8,128)} %get-tuple-element.60), calls=%async_computation | async-start | bytes 1048576 | tf_op jit(solution)/shard_map/all_to_all | solution.py:321
  108.9 0.7 pad_maximum_fusion.1.own_ref
  109.6 6.6 %shard_map.104 = (f32[32,512]{1,0:T(8,128)}, f32[32,512]{1,0:T(8,128)}, bf16[2,512,512]{2,1,0:T(8,128)(2,1)}, bf16[2,512,512]{2,1,0:T(8,128)(2,1)}, bf16[2,512,512]{2,1,0:T(8,128)(2,1)}) custom-call(f32[16,240,512]{2,1,0:T(8,128)} %bitcast.27, f32[16,24,512]{2,1,0:T(8,128)} %bitcast.31, s32[2]{0:T(128)} %copy-done.3, ...), custom_call_target="tpu_custom_call" | custom-call | flops 1610612736 | bytes 10747912 | tf_op jit(solution)/shard_map/pallas_call | solution.py:300
  116.2 7.2 %collective-permute-start.6 = (f32[32,512]{1,0:T(8,128)}, f32[32,512]{1,0:T(8,128)S(1)}, u32[]{:S(2)}, u32[]{:S(2)}) collective-permute-start(f32[32,512]{1,0:T(8,128)} %get-tuple-element.63.p2rows_ref), channel_id=1, source_target_pairs={{64,0},{80,16},{96,32},{112,48},{128,64},{144,80},{160,96},{176,11... | collective-permute-start | bytes 196616 | tf_op jit(solution)/shard_map/ppermute | solution.py:313
  123.4 6.0 %shard_map.105 = (bf16[2,512,512]{2,1,0:T(8,128)(2,1)}, bf16[2,512,512]{2,1,0:T(8,128)(2,1)}, bf16[2,512,512]{2,1,0:T(8,128)(2,1)}) custom-call(f32[16,240,512]{2,1,0:T(8,128)} %bitcast.28, bf16[2,512,512]{2,1,0:T(8,128)(2,1)} %get-tuple-element.62.bp_ref), custom_call_target="tpu_custom_call" | custom-call | flops 2415919104 | bytes 8912896 | tf_op jit(solution)/shard_map/pallas_call | solution.py:300
  129.5 0.8 copy-done.9
  130.3 5.4 %shard_map.106 = (f32[40,512]{1,0:T(8,128)}, f32[40,512]{1,0:T(8,128)}, f32[72,512]{1,0:T(8,128)}) custom-call(f32[512,256]{1,0:T(8,128)} %bitcast.32, f32[64,512]{1,0:T(8,128)} %pad_maximum_fusion.1.own_ref, f32[8,512]{1,0:T(8,128)} %get-tuple-element.65.vec_ref, bf16[2,512,512]{2,1,0:T(8,128)(2,1)} %get-tuple-element.66.p0p_ref, ...), custom_call_target="tpu_custom_call" | custom-call | flops 805306368 | bytes 8011776 | tf_op jit(solution)/shard_map/pallas_call | solution.py:300
  135.6 4.6 %collective-permute-start.7 = (f32[40,512]{1,0:T(8,128)}, f32[40,512]{1,0:T(8,128)S(1)}, u32[]{:S(2)}, u32[]{:S(2)}) collective-permute-start(f32[40,512]{1,0:T(8,128)} %get-tuple-element.73), channel_id=1, source_target_pairs={{0,64},{16,80},{32,96},{48,112},{64,128},{80,144},{96,160},{112,17... | collective-permute-start | bytes 245768 | tf_op jit(solution)/shard_map/ppermute | solution.py:313
  140.3 5.5 %collective-permute-start.8 = (f32[40,512]{1,0:T(8,128)}, f32[40,512]{1,0:T(8,128)S(1)}, u32[]{:S(2)}, u32[]{:S(2)}) collective-permute-start(f32[40,512]{1,0:T(8,128)} %get-tuple-element.74), channel_id=1, source_target_pairs={{64,0},{80,16},{96,32},{112,48},{128,64},{144,80},{160,96},{176,11... | collective-permute-start | bytes 245768 | tf_op jit(solution)/shard_map/ppermute | solution.py:313
  145.8 2.4 %collective-permute-done.7.prior_ref = f32[40,512]{1,0:T(8,128)S(1)} collective-permute-done((f32[40,512]{1,0:T(8,128)}, f32[40,512]{1,0:T(8,128)S(1)}, u32[]{:S(2)}, u32[]{:S(2)}) %collective-permute-start.7) | collective-permute-done | bytes 81952 | tf_op jit(solution)/shard_map/ppermute | solution.py:313
  148.2 1.5 collective-permute-done.8.later_ref
  149.7 0.9 copy-done.4
  150.6 2.0 %shard_map.107 = (f32[16,32,128]{2,1,0:T(8,128)}, f32[32,512]{1,0:T(8,128)S(1)}, f32[8,512]{1,0:T(8,128)S(1)}) custom-call(f32[40,512]{1,0:T(8,128)S(1)} %collective-permute-done.7.prior_ref, f32[40,512]{1,0:T(8,128)S(1)} %collective-permute-done.8.later_ref, f32[32,512]{1,0:T(8,128)S(1)} %collective-permute-done.6.later_p2_ref, f32[72,512]{1,0:T(8,128)S(1)} %copy-done.4, ...), custom_call_target="tpu_custom_call" | custom-call | flops 805306368 | bytes 2473984 | tf_op jit(solution)/shard_map/pallas_call | solution.py:300
  152.6 11.3 %all-to-all-start.1 = ((f32[16,32,128]{2,1,0:T(8,128)}), f32[16,32,128]{2,1,0:T(8,128)S(1)}, u32[]{:S(2)}, u32[]{:S(2)}) async-start(f32[16,32,128]{2,1,0:T(8,128)} %get-tuple-element.79), calls=%async_computation.1 | async-start | bytes 524288 | tf_op jit(solution)/shard_map/all_to_all | solution.py:321
  163.9 0.8 fusion.4
  164.9 4.7 %collective-permute-start.9 = (f32[32,512]{1,0:T(8,128)S(1)}, f32[32,512]{1,0:T(8,128)S(1)}, u32[]{:S(2)}, u32[]{:S(2)}) collective-permute-start(f32[32,512]{1,0:T(8,128)S(1)} %get-tuple-element.78), channel_id=1, source_target_pairs={{0,64},{16,80},{32,96},{48,112},{64,128},{80,144},{96,160},{112,17... | collective-permute-start | bytes 196616 | tf_op jit(solution)/shard_map/ppermute | solution.py:313
  169.6 6.3 %all-to-all-done.1 = f32[16,32,128]{2,1,0:T(8,128)S(1)} async-done(((f32[16,32,128]{2,1,0:T(8,128)}), f32[16,32,128]{2,1,0:T(8,128)S(1)}, u32[]{:S(2)}, u32[]{:S(2)}) %all-to-all-start.1) | async-done | bytes 262176 | tf_op jit(solution)/shard_map/all_to_all | solution.py:321
  175.9 0.9 copy-done.5
  176.8 1.5 shard_map.108
  178.3 4.7 %collective-permute-start.10 = (f32[40,512]{1,0:T(8,128)S(1)}, f32[40,512]{1,0:T(8,128)S(1)}, u32[]{:S(2)}, u32[]{:S(2)}) collective-permute-start(f32[40,512]{1,0:T(8,128)S(1)} %get-tuple-element.81), channel_id=1, source_target_pairs={{0,64},{16,80},{32,96},{48,112},{64,128},{80,144},{96,160},{112,17... | collective-permute-start | bytes 245768 | tf_op jit(solution)/shard_map/ppermute | solution.py:313
  183.0 0.6 broadcast_select_fusion
  183.6 0.6 slice_reduce_fusion.2
  184.2 5.9 %collective-permute-done.10 = f32[40,512]{1,0:T(8,128)S(1)} collective-permute-done((f32[40,512]{1,0:T(8,128)S(1)}, f32[40,512]{1,0:T(8,128)S(1)}, u32[]{:S(2)}, u32[]{:S(2)}) %collective-permute-start.10) | collective-permute-done | bytes 81952 | tf_op jit(solution)/shard_map/ppermute | solution.py:313
  190.1 0.6 fusion.3
  190.7 0.6 slice_select_fusion
  (51 shorter events, 1.5 us)
Async XLA Ops:
  7.2 87.4 %all-gather.4.cloned.1.call-start = ((), (), s32[]{:S(2)}) async-start(), calls=%async_computation.2 | async-start | bytes 8355840 | tf_op jit(solution)/shard_map/all_gather | solution.py:317
  7.2 16.1 %collective-permute-start.2 = (f32[32,512]{1,0:T(8,128)}, f32[32,512]{1,0:T(8,128)S(1)}, u32[]{:S(2)}, u32[]{:S(2)}) collective-permute-start(f32[32,512]{1,0:T(8,128)} %a0_ref.1), channel_id=1, source_target_pairs={{0,48},{16,64},{32,80},{48,96},{64,112},{80,128},{96,144},{112,160... | collective-permute-start | bytes 196616 | tf_op jit(solution)/shard_map/ppermute | solution.py:313
  12.4 10.9 %collective-permute-start.1 = (f32[32,512]{1,0:T(8,128)}, f32[32,512]{1,0:T(8,128)S(1)}, u32[]{:S(2)}, u32[]{:S(2)}) collective-permute-start(f32[32,512]{1,0:T(8,128)} %a0_ref.1), channel_id=1, source_target_pairs={{0,16},{16,32},{32,48},{48,64},{64,80},{80,96},{96,112},{112,128},... | collective-permute-start | bytes 196616 | tf_op jit(solution)/shard_map/ppermute | solution.py:313
  17.0 0.9 copy-start.1
  17.9 0.8 copy-start.2
  18.7 85.9 %copy-start.3 = (s32[2]{0:T(128)}, s32[2]{0:T(128)S(1)}, u32[]{:S(2)}) copy-start(s32[2]{0:T(128)S(1)} %pad_add_fusion.place_ref) | copy-start | bytes 28
  19.3 12.5 %collective-permute-start = (f32[64,512]{1,0:T(8,128)S(1)}, f32[64,512]{1,0:T(8,128)S(1)}, u32[]{:S(2)}, u32[]{:S(2)}) collective-permute-start(f32[64,512]{1,0:T(8,128)S(1)} %get-tuple-element.46), channel_id=1, source_target_pairs={{0,32},{16,48},{32,64},{48,80},{64,96},{80,112},{96,128},{112,144}... | collective-permute-start | bytes 393224 | tf_op jit(solution)/shard_map/ppermute | solution.py:313
  33.2 16.0 %collective-permute-start.5 = (f32[72,512]{1,0:T(8,128)S(1)}, f32[72,512]{1,0:T(8,128)S(1)}, u32[]{:S(2)}, u32[]{:S(2)}) collective-permute-start(f32[72,512]{1,0:T(8,128)S(1)} %pad_maximum_fusion), channel_id=1, source_target_pairs={{0,48},{16,64},{32,80},{48,96},{64,112},{80,128},{96,144},{112,160... | collective-permute-start | bytes 442376 | tf_op jit(solution)/shard_map/ppermute | solution.py:313
  35.1 15.9 %collective-permute-start.4 = (f32[72,512]{1,0:T(8,128)S(1)}, f32[72,512]{1,0:T(8,128)S(1)}, u32[]{:S(2)}, u32[]{:S(2)}) collective-permute-start(f32[72,512]{1,0:T(8,128)S(1)} %pad_maximum_fusion), channel_id=1, source_target_pairs={{0,32},{16,48},{32,64},{48,80},{64,96},{80,112},{96,128},{112,144}... | collective-permute-start | bytes 442376 | tf_op jit(solution)/shard_map/ppermute | solution.py:313
  37.8 16.1 %collective-permute-start.3 = (f32[72,512]{1,0:T(8,128)S(1)}, f32[72,512]{1,0:T(8,128)S(1)}, u32[]{:S(2)}, u32[]{:S(2)}) collective-permute-start(f32[72,512]{1,0:T(8,128)S(1)} %pad_maximum_fusion), channel_id=1, source_target_pairs={{0,16},{16,32},{32,48},{48,64},{64,80},{80,96},{96,112},{112,128},... | collective-permute-start | bytes 442376 | tf_op jit(solution)/shard_map/ppermute | solution.py:313
  56.6 38.0 %copy-start.12 = (f32[192,512]{1,0:T(8,128)}, f32[192,512]{1,0:T(8,128)S(1)}, u32[]{:S(2)}) copy-start(f32[192,512]{1,0:T(8,128)S(1)} %get-tuple-element.92.own_ref) | copy-start | bytes 1179652
  87.6 17.0 %copy-start.8 = (f32[384,512]{1,0:T(8,128)}, f32[384,512]{1,0:T(8,128)S(1)}, u32[]{:S(2)}) copy-start(f32[384,512]{1,0:T(8,128)S(1)} %all-gather.1) | copy-start | bytes 2359300
  94.6 14.3 %copy-start.10 = (f32[32,512]{1,0:T(8,128)S(1)}, f32[32,512]{1,0:T(8,128)}, u32[]{:S(2)}) copy-start(f32[32,512]{1,0:T(8,128)} %param.8) | copy-start | bytes 196612
  104.6 24.8 %all-to-all-start = ((f32[16,32,256]{2,1,0:T(8,128)}), f32[16,32,256]{2,1,0:T(8,128)S(1)}, u32[]{:S(2)}, u32[]{:S(2)}) async-start(f32[16,32,256]{2,1,0:T(8,128)} %get-tuple-element.60), calls=%async_computation | async-start | bytes 1048576 | tf_op jit(solution)/shard_map/all_to_all | solution.py:321
  116.2 33.5 %copy-start = (bf16[2,512,512]{2,1,0:T(8,128)(2,1)S(1)}, bf16[2,512,512]{2,1,0:T(8,128)(2,1)}, u32[]{:S(2)}) copy-start(bf16[2,512,512]{2,1,0:T(8,128)(2,1)} %get-tuple-element.72.m2_ref) | copy-start | bytes 3145732
  116.2 33.5 %copy-start.6 = (bf16[2,512,512]{2,1,0:T(8,128)(2,1)S(1)}, bf16[2,512,512]{2,1,0:T(8,128)(2,1)}, u32[]{:S(2)}) copy-start(bf16[2,512,512]{2,1,0:T(8,128)(2,1)} %get-tuple-element.77.d_ref) | copy-start | bytes 3145732
  116.2 13.3 %collective-permute-start.6 = (f32[32,512]{1,0:T(8,128)}, f32[32,512]{1,0:T(8,128)S(1)}, u32[]{:S(2)}, u32[]{:S(2)}) collective-permute-start(f32[32,512]{1,0:T(8,128)} %get-tuple-element.63.p2rows_ref), channel_id=1, source_target_pairs={{64,0},{80,16},{96,32},{112,48},{128,64},{144,80},{160,96},{176,11... | collective-permute-start | bytes 196616 | tf_op jit(solution)/shard_map/ppermute | solution.py:313
  129.4 46.5 %copy-start.7 = (f32[32,512]{1,0:T(8,128)S(1)}, f32[32,512]{1,0:T(8,128)}, u32[]{:S(2)}) copy-start(f32[32,512]{1,0:T(8,128)} %get-tuple-element.63.p2rows_ref) | copy-start | bytes 196612
  129.4 53.5 %copy-start.11 = (f32[32,512]{1,0:T(8,128)S(1)}, f32[32,512]{1,0:T(8,128)}, u32[]{:S(2)}) copy-start(f32[32,512]{1,0:T(8,128)} %get-tuple-element.83) | copy-start | bytes 196612
  129.5 0.8 copy-start.9
  135.6 12.5 %collective-permute-start.7 = (f32[40,512]{1,0:T(8,128)}, f32[40,512]{1,0:T(8,128)S(1)}, u32[]{:S(2)}, u32[]{:S(2)}) collective-permute-start(f32[40,512]{1,0:T(8,128)} %get-tuple-element.73), channel_id=1, source_target_pairs={{0,64},{16,80},{32,96},{48,112},{64,128},{80,144},{96,160},{112,17... | collective-permute-start | bytes 245768 | tf_op jit(solution)/shard_map/ppermute | solution.py:313
  140.3 9.4 %collective-permute-start.8 = (f32[40,512]{1,0:T(8,128)}, f32[40,512]{1,0:T(8,128)S(1)}, u32[]{:S(2)}, u32[]{:S(2)}) collective-permute-start(f32[40,512]{1,0:T(8,128)} %get-tuple-element.74), channel_id=1, source_target_pairs={{64,0},{80,16},{96,32},{112,48},{128,64},{144,80},{160,96},{176,11... | collective-permute-start | bytes 245768 | tf_op jit(solution)/shard_map/ppermute | solution.py:313
  149.7 0.9 copy-start.4
  152.6 23.3 %all-to-all-start.1 = ((f32[16,32,128]{2,1,0:T(8,128)}), f32[16,32,128]{2,1,0:T(8,128)S(1)}, u32[]{:S(2)}, u32[]{:S(2)}) async-start(f32[16,32,128]{2,1,0:T(8,128)} %get-tuple-element.79), calls=%async_computation.1 | async-start | bytes 524288 | tf_op jit(solution)/shard_map/all_to_all | solution.py:321
  164.9 18.0 %collective-permute-start.9 = (f32[32,512]{1,0:T(8,128)S(1)}, f32[32,512]{1,0:T(8,128)S(1)}, u32[]{:S(2)}, u32[]{:S(2)}) collective-permute-start(f32[32,512]{1,0:T(8,128)S(1)} %get-tuple-element.78), channel_id=1, source_target_pairs={{0,64},{16,80},{32,96},{48,112},{64,128},{80,144},{96,160},{112,17... | collective-permute-start | bytes 196616 | tf_op jit(solution)/shard_map/ppermute | solution.py:313
  175.9 0.9 copy-start.5
  178.3 11.8 %collective-permute-start.10 = (f32[40,512]{1,0:T(8,128)S(1)}, f32[40,512]{1,0:T(8,128)S(1)}, u32[]{:S(2)}, u32[]{:S(2)}) collective-permute-start(f32[40,512]{1,0:T(8,128)S(1)} %get-tuple-element.81), channel_id=1, source_target_pairs={{0,64},{16,80},{32,96},{48,112},{64,128},{80,144},{96,160},{112,17... | collective-permute-start | bytes 245768 | tf_op jit(solution)/shard_map/ppermute | solution.py:313
Sparse Core Ops, SparseCore 0:
  33.3 61.2 all-gather.3

commit v9 on v8

--- a/solution.py
+++ b/solution.py
@@ -166,6 +166,16 @@
     ready_ref[4 * rows : 5 * rows] = fixed_ref[rows : 2 * rows]
     ready_ref[5 * rows : 6 * rows] = jnp.where(time >= 3, late_ref[rows:], eye)
     ready_ref[6 * rows :] = fixed_ref[2 * rows :]
+
+
+def drows_kernel(rows, whole_ref, a0_ref, drows_ref, buf, sems, start, start_sems):
+    first = Fetch([a0_ref], [start], start_sems)
+    order = (4, 1, 6, 2, 5, 3)
+    part = fetch_parts(whole_ref, order, rows, buf, sems)
+    total = first(0)
+    for k in range(len(order)):
+        total = dot(split(total), part(k))
+    drows_ref[...] = total
 
 
 def first_kernel(
@@ -211,8 +221,7 @@
 
 
 def middle_kernel(
-    rows, whole_ref, head_ref, place_ref, bw_ref, bp_ref, drows_ref, p2rows_ref, p1_ref, d_ref, m2_ref, buf, sems, pairs,
-    pair_sems, out, outs
+    rows, whole_ref, head_ref, bw_ref, bp_ref, p1_ref, d_ref, m2_ref, buf, sems, pairs, pair_sems, out, outs
 ):
     part = fetch_parts(whole_ref, (6, 7), rows, buf, sems, head_ref)
     pair = fetch_pairs((bw_ref, bp_ref), pairs, pair_sems)
@@ -220,13 +229,8 @@
     bw, m1 = pair(0), part(0)
     p1 = store(split(dot(bw, m1)))
     bp = pair(1)
-    d = store(split(dot(p1, bp)))
-    shape = drows_ref.shape
-    row = lax.broadcasted_iota(jnp.int32, shape, 0) + place_ref[1] * rows
-    eye = (row == lax.broadcasted_iota(jnp.int32, shape, 1)).astype(F32)
-    drows = dot(split(eye), d)
-    drows_ref[...] = drows
-    p2rows_ref[...] = dot(split(drows), store(part(1)))
+    store(split(dot(p1, bp)))
+    store(part(1))
     store.finish()
 
 
@@ -241,10 +245,9 @@
 
 
 def second_kernel(
-    rows, received_ref, own_ref, vec_ref, p0p_ref, p0_ref, g0_ref, g0p_ref, p1_ref, g1_ref, m2_ref, plus_ref, minus_ref,
-    state_ref, pairs, pair_sems
+    rows, received_ref, own_ref, vec_ref, p0p_ref, p0_ref, g0_ref, g0p_ref, p1_ref, g1_ref, state_ref, pairs, pair_sems
 ):
-    pair = fetch_pairs((p0p_ref, p0_ref, g0_ref, g0p_ref, p1_ref, g1_ref, m2_ref), pairs, pair_sems)
+    pair = fetch_pairs((p0p_ref, p0_ref, g0_ref, g0p_ref, p1_ref, g1_ref), pairs, pair_sems)
     columns = received_ref[...].T
     x1, x2, x3, y0, y1, y2 = (columns[i * rows : (i + 1) * rows] for i in range(6))
     w1, w2, w3, w4 = (columns[6 * rows + i : 6 * rows + i + 1] for i in range(4))
@@ -256,42 +259,47 @@
     other_j = dot(split(y2), pair(3)) + j3
     outer = dot_nt(split(inner), pair(4)) + other
     outer_j = dot(split(inner_j), pair(5)) + stacked(other_j, sixteen(e_p))
-    plus_ref[...] = outer[: rows + 8]
     state_ref[:rows] = outer[:rows]
     state_ref[rows : 2 * rows] = outer_j[:rows]
     state_ref[2 * rows :] = sixteen(outer[rows : rows + 1], outer_j[rows : rows + 1])[:8]
-    minus_ref[...] = dot(split(outer_j), pair(6))[: rows + 8]
 
 
 def third_kernel(
-    rows, prior_ref, later_ref, later_p2_ref, state_ref, m2_ref, d_ref, packed_ref, a_ref, row_ref, buf, sems
+    rows, state_ref, drows_ref, earlier_ref, m2_ref, z_ref, p2rows_ref, new_a_ref, buf, sems, pairs, pair_sems
 ):
+    part = fetch_parts(earlier_ref, (0,), rows, buf, sems)
+    pair = fetch_pairs((m2_ref,), pairs, pair_sems)
+    e_row = state_ref[2 * rows + 1 : 2 * rows + 2]
+    both = dot(split(stacked(state_ref[rows : 2 * rows], drows_ref[...], sixteen(e_row))), pair(0))
+    p2rows_ref[...] = both[rows : 2 * rows]
+    both = dot(split(both), part(0))
+    z_ref[:rows] = both[:rows]
+    z_ref[rows:] = both[2 * rows : 2 * rows + 8]
+    new_a_ref[...] = both[rows : 2 * rows]
+
+
+def fourth_kernel(rows, place_ref, prior_ref, state_ref, z_ref, m2_ref, d_ref, packed_ref, buf, sems):
     pair = fetch_pairs((m2_ref, d_ref), buf, sems)
     v = dot_nt(split(prior_ref[:rows]), pair(0))
-    d = pair(1)
-    v = dot_nt(split(v), d)
-    both = dot(split(stacked(later_ref[:rows], later_p2_ref[...], sixteen(later_ref[rows : rows + 1]))), d)
-    pack((v, state_ref[:rows], both[:rows], state_ref[rows : 2 * rows]), packed_ref, rows)
-    a_ref[...] = both[rows : 2 * rows]
-    row_ref[...] = both[2 * rows : 2 * rows + 8]
+    v = dot_nt(split(v), pair(1))
+    j = jnp.where(place_ref[0] >= 4, prior_ref[rows : 2 * rows], state_ref[rows : 2 * rows])
+    pack((v, state_ref[:rows], z_ref[:rows], j), packed_ref, rows)
 
 
 def last_kernel(
-    rows, received_ref, p2rows_ref, prior_ref, state_ref, part_ref, d_ref, new_c_ref, back_ref, j_ref, b_ref,
-    buf, sems
+    rows, received_ref, p2rows_ref, prior_ref, state_ref, part_ref, earlier_ref, d_ref, new_c_ref, new_j_ref, vectors_ref,
+    buf, sems, pairs, pair_sems
 ):
-    pair = fetch_pairs((d_ref,), buf, sems)
+    part = fetch_parts(earlier_ref, (0,), rows, buf, sems)
+    pair = fetch_pairs((d_ref,), pairs, pair_sems)
     back = received_ref[...].T
     v, c_rows, z, j_rows = (back[i * rows : (i + 1) * rows] for i in range(4))
-    d = pair(0)
-    back_ref[:rows] = dot(split(z), d) + j_rows
-    j_ref[...] = j_rows
-    later_e = part_ref[:, 1:2] - rowwise(z, state_ref[2 * rows : 2 * rows + 1])
-    row = in_lanes((later_e,), rows, 128).T[:8]
-    back_ref[rows:] = jnp.concatenate([row, jnp.zeros((8, back_ref.shape[1] - rows), F32)], axis=1)
-    new_c_ref[...] = dot_nt(split(v), d) + c_rows
-    new_b = part_ref[:, 0:1] + rowwise(p2rows_ref[...], prior_ref[rows : rows + 1])
-    b_ref[...] = in_lanes((new_b + rowwise(v, state_ref[2 * rows + 1 : 2 * rows + 2]),), rows, 128)
+    e_own, b_prior = state_ref[2 * rows + 1 : 2 * rows + 2], prior_ref[2 * rows : 2 * rows + 1]
+    new_b = rowwise(p2rows_ref[...], b_prior) + rowwise(v, e_own)
+    new_e = -rowwise(z, b_prior)
+    vectors_ref[...] = in_lanes((new_b, new_e), rows, 128) + part_ref[...]
+    new_j_ref[...] = dot(split(z), part(0)) + j_rows
+    new_c_ref[...] = dot_nt(split(v), pair(0)) + c_rows
 
 
 def call(kernel, rows, operands, outs, placed=(), kept=(), scratch=(), flops=0, grant=58, small=()):
@@ -378,6 +386,18 @@
     def flat(extra=0):
         return ((rows + extra, width), F32)
 
+    (drows,) = call(
+        drows_kernel,
+        rows,
+        (whole, a0),
+        [flat()],
+        {0, 1},
+        (),
+        stage(6) + [pltpu.VMEM((rows, width), F32), pltpu.SemaphoreType.DMA((1,))],
+        flops=mults,
+    )
+    earlier = gathered(passed_along(drows, 4))
+
     packed, vec, p0, bw, p0p, bp = call(
         first_kernel,
         rows,
@@ -389,74 +409,74 @@
         flops=6 * mults,
     )
     received = exchanged(packed)
-    drows, p2rows, p1, d, m2 = call(
+    p1, d, m2 = call(
         middle_kernel,
         rows,
-        (whole, head, place, bw, bp),
-        [flat(), flat()] + [pair] * 3,
-        {0, 1, 3, 4},
-        range(2, 5),
+        (whole, head, bw, bp),
+        [pair] * 3,
+        {0, 1, 2, 3},
+        range(3),
         stage(2) + pairs(2) + pairs(3),
         flops=2 * mults,
-        small=(2,),
-    )
-    later_p2 = passed_along(p2rows, -4)
+    )
     g1, g0, g0p = call(
         grams_kernel, rows, (whole, bp), [pair] * 3, {0, 1}, range(3), stage(5) + pairs(1) + pairs(3), flops=3 * mults
     )
-    received, later_p2 = lax.optimization_barrier((received, later_p2))
-    plus, minus, state = call(
+    (state,) = call(
         second_kernel,
         rows,
-        (received, jnp.concatenate([c0, j3]), vec, p0p, p0, g0, g0p, p1, g1, m2),
-        [flat(8), flat(8), flat(rows + 8)],
-        range(3, 10),
+        (received, jnp.concatenate([c0, j3]), vec, p0p, p0, g0, g0p, p1, g1),
+        [flat(rows + 8)],
+        range(3, 9),
         (),
-        pairs(7),
+        pairs(6),
         flops=mults,
     )
-    prior, later = passed_along(plus, 4), passed_along(minus, -4)
-    packed, later_a, row = call(
+
+    prior = passed_along(state, 4)
+    z, p2rows, new_a = call(
         third_kernel,
         rows,
-        (prior, later, later_p2, state, m2, d),
-        [((peers, rows, 4 * rows), F32), flat(), ((8, width), F32)],
+        (state, drows, earlier, m2),
+        [flat(8), flat(), flat()],
+        {2, 3},
+        (),
+        stage(1) + pairs(1),
+        flops=mults,
+        grant=16,
+    )
+    (packed,) = call(
+        fourth_kernel,
+        rows,
+        (place, prior, state, z, m2, d),
+        [((peers, rows, 4 * rows), F32)],
         {4, 5},
         (),
         pairs(2),
         flops=mults,
         grant=16,
+        small=(0,),
     )
     back = exchanged(packed)
-    new_a = passed_along(later_a, 4)
 
     def own_part(vector):
         return lax.dynamic_slice_in_dim(vector, mine * rows, rows, 0)
 
-    own_e = own_part(state[2 * rows + 1])
-    parts = jnp.stack([own_part(state[2 * rows]), own_part(row[0]) + own_e], axis=1)
+    e_before = jnp.where(time >= 4, z[rows] + prior[2 * rows + 1], state[2 * rows + 1])
+    parts = jnp.stack([own_part(state[2 * rows]), own_part(e_before)], axis=1)
     parts = jnp.pad(parts, ((0, 0), (0, 126)))
-    new_c, later_j, own_j, new_b = call(
+    new_c, new_j, both = call(
         last_kernel,
         rows,
-        (back, p2rows, prior, state, parts, d),
-        [flat(), flat(8), flat(), ((rows, 128), F32)],
-        {5},
+        (back, p2rows, prior, state, parts, earlier, d),
+        [flat(), flat(), ((rows, 128), F32)],
+        {5, 6},
         (),
-        pairs(1),
+        stage(1) + pairs(1),
         flops=mults,
         grant=16,
     )
-    new_j = passed_along(later_j, 4)
-    new_a, later_j = lax.optimization_barrier((new_a, later_j))
-    changed = time >= 4
-    return (
-        jnp.where(changed, new_a, drows),
-        new_b[:, 0],
-        new_c,
-        jnp.where(changed, new_j[rows, :rows], own_e),
-        jnp.where(changed, new_j[:rows], own_j),
-    )
+    return jnp.where(time >= 4, new_a, drows), both[:, 0], new_c, both[:, 1], new_j
 
 
 def solution(mesh):

time: 199 us -> 198 us (level)
  the two profiles are of different devices: /device:TPU:5 before, /device:TPU:7 now
where the time goes in v9:
time: 198 us; the launch traced here: 196 us
  waiting for transfers between devices  51.6 us (26%)
  starting transfers between devices  44.2 us (22%)
  Pallas kernels  38.2 us (19%)
  blocking collectives  30.7 us (16%)
  between operations  14.3 us (7%)
  local copies, waits for them, and re-layouts  11.7 us (6%)
  other arithmetic  5.51 us (3%)
    pallas_call x10, Pallas kernels, call(): pl.pallas_call(functools.partial(kernel, rows), out_shape=[jax.ShapeDtype...  38.2 us
    ppermute x8, starting transfers between devices, passed_along(): lax.ppermute(shard, 'tm', [(i, i + by) for i in range(peers) if 0 <= i +...  32.8 us
    ppermute x8, waiting for transfers between devices, passed_along(): lax.ppermute(shard, 'tm', [(i, i + by) for i in range(peers) if 0 <= i +...  32.6 us
    all_gather x1, blocking collectives, gathered(): return lax.all_gather(shard, 'panel', axis=0, tiled=False)  30.7 us
    all_to_all x2, waiting for transfers between devices, exchanged(): lax.all_to_all(packed, 'panel', split_axis=0, concat_axis=0, tiled=True)  16.6 us
    all_to_all x2, starting transfers between devices, exchanged(): lax.all_to_all(packed, 'panel', split_axis=0, concat_axis=0, tiled=True)  11.3 us
    unnamed x32, local copies, waits for them, and re-layouts  8.41 us
  transfers between devices with their start and end apart: 12, of which 9 were waited for; matrix products, arithmetic and copies ran while one was open for 4% of the time, Pallas kernels for 14%

profile of v9, /device:TPU:7, one launch (start us, length us, event | category | flops | bytes accessed | tf_op | source)
XLA Modules:
  0.0 196.2 jit_solution(9178836971882623898)
XLA Ops:
  7.2 3.2 %collective-permute-start.1 = (f32[32,512]{1,0:T(8,128)}, f32[32,512]{1,0:T(8,128)S(1)}, u32[]{:S(2)}, u32[]{:S(2)}) collective-permute-start(f32[32,512]{1,0:T(8,128)} %a0_ref.3), channel_id=1, source_target_pairs={{0,16},{16,32},{32,48},{48,64},{64,80},{80,96},{96,112},{112,128},... | collective-permute-start | bytes 196616 | tf_op jit(solution)/shard_map/ppermute | solution.py:321
  10.4 6.4 %collective-permute-start.2 = (f32[32,512]{1,0:T(8,128)}, f32[32,512]{1,0:T(8,128)S(1)}, u32[]{:S(2)}, u32[]{:S(2)}) collective-permute-start(f32[32,512]{1,0:T(8,128)} %a0_ref.3), channel_id=1, source_target_pairs={{0,48},{16,64},{32,80},{48,96},{64,112},{80,128},{96,144},{112,160... | collective-permute-start | bytes 196616 | tf_op jit(solution)/shard_map/ppermute | solution.py:321
  17.0 0.8 copy-done.1
  17.8 0.9 copy-done.2
  19.3 2.4 %collective-permute-start = (f32[64,512]{1,0:T(8,128)S(1)}, f32[64,512]{1,0:T(8,128)S(1)}, u32[]{:S(2)}, u32[]{:S(2)}) collective-permute-start(f32[64,512]{1,0:T(8,128)S(1)} %get-tuple-element.37), channel_id=1, source_target_pairs={{0,32},{16,48},{32,64},{48,80},{64,96},{80,112},{96,128},{112,144}... | collective-permute-start | bytes 393224 | tf_op jit(solution)/shard_map/ppermute | solution.py:321
  21.7 0.7 select_maximum_fusion
  22.4 0.9 pad_maximum_fusion
  23.3 8.1 %collective-permute-done.late_ref = f32[64,512]{1,0:T(8,128)S(1)} collective-permute-done((f32[64,512]{1,0:T(8,128)S(1)}, f32[64,512]{1,0:T(8,128)S(1)}, u32[]{:S(2)}, u32[]{:S(2)}) %collective-permute-start) | collective-permute-done | bytes 131104 | tf_op jit(solution)/shard_map/ppermute | solution.py:321
  31.4 1.4 shard_map.102
  32.9 1.9 collective-permute-start.3
  34.8 1.9 collective-permute-start.4
  36.8 3.0 %collective-permute-start.5 = (f32[72,512]{1,0:T(8,128)S(1)}, f32[72,512]{1,0:T(8,128)S(1)}, u32[]{:S(2)}, u32[]{:S(2)}) collective-permute-start(f32[72,512]{1,0:T(8,128)S(1)} %pad_maximum_fusion), channel_id=1, source_target_pairs={{0,48},{16,64},{32,80},{48,96},{64,112},{80,128},{96,144},{112,160... | collective-permute-start | bytes 442376 | tf_op jit(solution)/shard_map/ppermute | solution.py:321
  39.8 1.1 collective-permute-done.3
  40.9 3.1 %collective-permute-done.4 = f32[72,512]{1,0:T(8,128)S(1)} collective-permute-done((f32[72,512]{1,0:T(8,128)S(1)}, f32[72,512]{1,0:T(8,128)S(1)}, u32[]{:S(2)}, u32[]{:S(2)}) %collective-permute-start.4) | collective-permute-done | bytes 147488 | tf_op jit(solution)/shard_map/ppermute | solution.py:321
  44.0 13.4 %collective-permute-done.5 = f32[72,512]{1,0:T(8,128)S(1)} collective-permute-done((f32[72,512]{1,0:T(8,128)S(1)}, f32[72,512]{1,0:T(8,128)S(1)}, u32[]{:S(2)}, u32[]{:S(2)}) %collective-permute-start.5) | collective-permute-done | bytes 147488 | tf_op jit(solution)/shard_map/ppermute | solution.py:321
  57.4 0.7 concatenate.17
  58.3 0.9 constant_dynamic-update-slice_fusion
  59.3 0.7 slice_dynamic-update-slice_fusion
  60.1 30.7 %all-gather.1 = f32[384,512]{1,0:T(8,128)S(1)} all-gather(f32[24,512]{1,0:T(8,128)S(1)} %concatenate.18), channel_id=3, replica_groups=mesh['tm'=32,'panel'=16] {'panel'}, dimensions={0}, use_global_device_ids=true | all-gather | bytes 835584 | tf_op jit(solution)/shard_map/all_gather | solution.py:325
  91.0 0.7 reshape.34.vec_ref
  92.3 2.2 %all-gather.6.cloned.1.call-done = f32[3840,512]{1,0:T(8,128)} async-done(((f32[240,512]{1,0:T(8,128)}), f32[3840,512]{1,0:T(8,128)}) %all-gather.6.cloned.1.call-update) | async-done | bytes 7864336 | tf_op jit(solution)/shard_map/all_gather | solution.py:325
  94.6 4.9 %shard_map.107.drows_ref = f32[32,512]{1,0:T(8,128)} custom-call(f32[16,240,512]{2,1,0:T(8,128)} %bitcast.27, f32[32,512]{1,0:T(8,128)} %a0_ref.3), custom_call_target="tpu_custom_call" | custom-call | flops 805306368 | bytes 7929856 | tf_op jit(solution)/shard_map/pallas_call | solution.py:308
  99.5 7.1 %collective-permute-start.6 = (f32[32,512]{1,0:T(8,128)}, f32[32,512]{1,0:T(8,128)S(1)}, u32[]{:S(2)}, u32[]{:S(2)}) collective-permute-start(f32[32,512]{1,0:T(8,128)} %shard_map.107.drows_ref), channel_id=1, source_target_pairs={{0,64},{16,80},{32,96},{48,112},{64,128},{80,144},{96,160},{112,17... | collective-permute-start | bytes 196616 | tf_op jit(solution)/shard_map/ppermute | solution.py:321
  106.6 3.0 %collective-permute-done.6 = f32[32,512]{1,0:T(8,128)S(1)} collective-permute-done((f32[32,512]{1,0:T(8,128)}, f32[32,512]{1,0:T(8,128)S(1)}, u32[]{:S(2)}, u32[]{:S(2)}) %collective-permute-start.6) | collective-permute-done | bytes 65568 | tf_op jit(solution)/shard_map/ppermute | solution.py:321
  109.6 0.6 copy-done.13
  110.3 10.0 %shard_map.103 = (f32[16,32,256]{2,1,0:T(8,128)}, f32[8,512]{1,0:T(8,128)}, bf16[2,512,512]{2,1,0:T(8,128)(2,1)}, bf16[2,512,512]{2,1,0:T(8,128)(2,1)}, bf16[2,5...) custom-call(f32[16,240,512]{2,1,0:T(8,128)} %bitcast.28, f32[192,512]{1,0:T(8,128)} %copy-done.14, ...), custom_call_target="tpu_custom_call" | custom-call | flops 4831838208 | bytes 8282112 | tf_op jit(solution)/shard_map/pallas_call | solution.py:308
  120.3 5.4 %all-to-all-start = ((f32[16,32,256]{2,1,0:T(8,128)}), f32[16,32,256]{2,1,0:T(8,128)S(1)}, u32[]{:S(2)}, u32[]{:S(2)}) async-start(f32[16,32,256]{2,1,0:T(8,128)} %get-tuple-element.51), calls=%async_computation | async-start | bytes 1048576 | tf_op jit(solution)/shard_map/all_to_all | solution.py:329
  125.8 0.7 pad_maximum_fusion.1.own_ref
  126.4 5.2 %shard_map.105 = (bf16[2,512,512]{2,1,0:T(8,128)(2,1)}, bf16[2,512,512]{2,1,0:T(8,128)(2,1)}, bf16[2,512,512]{2,1,0:T(8,128)(2,1)}) custom-call(f32[16,240,512]{2,1,0:T(8,128)} %bitcast.29, f32[16,24,512]{2,1,0:T(8,128)} %bitcast.33, bf16[2,512,512]{2,1,0:T(8,128)(2,1)} %get-tuple-element.58.bw_ref, bf16[2,512,512]{2,1,0:T(8,128)(2,1)} %get-tuple-element.55.bp_ref), custom_call_target="tpu_custom_call" | custom-call | flops 1610612736 | bytes 10747904 | tf_op jit(solution)/shard_map/pallas_call | solution.py:308
  131.6 6.1 %shard_map.104 = (bf16[2,512,512]{2,1,0:T(8,128)(2,1)}, bf16[2,512,512]{2,1,0:T(8,128)(2,1)}, bf16[2,512,512]{2,1,0:T(8,128)(2,1)}) custom-call(f32[16,240,512]{2,1,0:T(8,128)} %bitcast.30, bf16[2,512,512]{2,1,0:T(8,128)(2,1)} %get-tuple-element.55.bp_ref), custom_call_target="tpu_custom_call" | custom-call | flops 2415919104 | bytes 8912896 | tf_op jit(solution)/shard_map/pallas_call | solution.py:308
  137.8 5.8 %all-to-all-done = f32[16,32,256]{2,1,0:T(8,128)S(1)} async-done(((f32[16,32,256]{2,1,0:T(8,128)}), f32[16,32,256]{2,1,0:T(8,128)S(1)}, u32[]{:S(2)}, u32[]{:S(2)}) %all-to-all-start) | async-done | bytes 524320 | tf_op jit(solution)/shard_map/all_to_all | solution.py:329
  143.6 0.8 copy-done.11
  144.4 5.1 %shard_map.106.state_ref = f32[72,512]{1,0:T(8,128)} custom-call(f32[512,256]{1,0:T(8,128)} %bitcast.34, f32[64,512]{1,0:T(8,128)} %pad_maximum_fusion.1.own_ref, f32[8,512]{1,0:T(8,128)} %get-tuple-element.52.vec_ref, bf16[2,512,512]{2,1,0:T(8,128)(2,1)} %get-tuple-element.53.p0p_ref, bf16[2,512,512]{2,1,0:T(8,128)(2,1)} %get-tuple-element.54.p0_ref, ...), custom_call_target="tpu_custom_call" | custom-call | flops 805306368 | bytes 6963200 | tf_op jit(solution)/shard_map/pallas_call | solution.py:308
  149.5 6.8 %collective-permute-start.7 = (f32[72,512]{1,0:T(8,128)}, f32[72,512]{1,0:T(8,128)S(1)}, u32[]{:S(2)}, u32[]{:S(2)}) collective-permute-start(f32[72,512]{1,0:T(8,128)} %shard_map.106.state_ref), channel_id=1, source_target_pairs={{0,64},{16,80},{32,96},{48,112},{64,128},{80,144},{96,160},{112,17... | collective-permute-start | bytes 442376 | tf_op jit(solution)/shard_map/ppermute | solution.py:321
  156.2 0.8 fusion.3
  157.0 0.9 copy-done.3
  157.9 1.2 copy-done.6
  159.2 0.8 shard_map.108
  160.0 3.9 %collective-permute-done.7.prior_ref = f32[72,512]{1,0:T(8,128)S(1)} collective-permute-done((f32[72,512]{1,0:T(8,128)}, f32[72,512]{1,0:T(8,128)S(1)}, u32[]{:S(2)}, u32[]{:S(2)}) %collective-permute-start.7) | collective-permute-done | bytes 147488 | tf_op jit(solution)/shard_map/ppermute | solution.py:321
  163.9 0.9 copy-done.4
  164.8 2.4 %shard_map.109 = f32[16,32,128]{2,1,0:T(8,128)} custom-call(s32[2]{0:T(128)S(1)} %pad_add_fusion.place_ref, f32[72,512]{1,0:T(8,128)S(1)} %collective-permute-done.7.prior_ref, f32[72,512]{1,0:T(8,128)S(1)} %copy-done.4, f32[40,512]{1,0:T(8,128)S(1)} %get-tuple-element.63.z_ref, bf16[2,512,512]{2,1,0:T(8,128)(2,1)S(1)} %copy-done.9, ...), custom_call_target="tpu_custom_call" | custom-call | flops 805306368 | bytes 2473992 | tf_op jit(solution)/shard_map/pallas_call | solution.py:308
  167.2 5.9 %all-to-all-start.1 = ((f32[16,32,128]{2,1,0:T(8,128)}), f32[16,32,128]{2,1,0:T(8,128)S(1)}, u32[]{:S(2)}, u32[]{:S(2)}) async-start(f32[16,32,128]{2,1,0:T(8,128)} %shard_map.109), calls=%async_computation.1 | async-start | bytes 524288 | tf_op jit(solution)/shard_map/all_to_all | solution.py:329
  173.3 0.6 broadcast_select_fusion
  174.0 10.8 %all-to-all-done.1 = f32[16,32,128]{2,1,0:T(8,128)S(1)} async-done(((f32[16,32,128]{2,1,0:T(8,128)}), f32[16,32,128]{2,1,0:T(8,128)S(1)}, u32[]{:S(2)}, u32[]{:S(2)}) %all-to-all-start.1) | async-done | bytes 262176 | tf_op jit(solution)/shard_map/all_to_all | solution.py:329
  184.8 0.9 copy-done.5
  185.7 1.2 copy-done.7
  186.9 1.7 shard_map.110
  188.6 0.7 slice_reduce_fusion.2
  (53 shorter events, 2.1 us)
Async XLA Ops:
  7.2 87.4 %all-gather.6.cloned.1.call-start = ((), (), s32[]{:S(2)}) async-start(), calls=%async_computation.2 | async-start | bytes 8355840 | tf_op jit(solution)/shard_map/all_gather | solution.py:325
  7.2 16.1 %collective-permute-start.1 = (f32[32,512]{1,0:T(8,128)}, f32[32,512]{1,0:T(8,128)S(1)}, u32[]{:S(2)}, u32[]{:S(2)}) collective-permute-start(f32[32,512]{1,0:T(8,128)} %a0_ref.3), channel_id=1, source_target_pairs={{0,16},{16,32},{32,48},{48,64},{64,80},{80,96},{96,112},{112,128},... | collective-permute-start | bytes 196616 | tf_op jit(solution)/shard_map/ppermute | solution.py:321
  10.4 12.9 %collective-permute-start.2 = (f32[32,512]{1,0:T(8,128)}, f32[32,512]{1,0:T(8,128)S(1)}, u32[]{:S(2)}, u32[]{:S(2)}) collective-permute-start(f32[32,512]{1,0:T(8,128)} %a0_ref.3), channel_id=1, source_target_pairs={{0,48},{16,64},{32,80},{48,96},{64,112},{80,128},{96,144},{112,160... | collective-permute-start | bytes 196616 | tf_op jit(solution)/shard_map/ppermute | solution.py:321
  17.0 0.8 copy-start.1
  17.8 0.9 copy-start.2
  19.3 12.1 %collective-permute-start = (f32[64,512]{1,0:T(8,128)S(1)}, f32[64,512]{1,0:T(8,128)S(1)}, u32[]{:S(2)}, u32[]{:S(2)}) collective-permute-start(f32[64,512]{1,0:T(8,128)S(1)} %get-tuple-element.37), channel_id=1, source_target_pairs={{0,32},{16,48},{32,64},{48,80},{64,96},{80,112},{96,128},{112,144}... | collective-permute-start | bytes 393224 | tf_op jit(solution)/shard_map/ppermute | solution.py:321
  32.8 124.2 %all-gather.8.cloned.1.call-start = ((), (), s32[]{:S(2)}) async-start(), calls=%async_computation.3 | async-start | bytes 1114112 | tf_op jit(solution)/shard_map/all_gather | solution.py:325
  32.9 8.0 %collective-permute-start.3 = (f32[72,512]{1,0:T(8,128)S(1)}, f32[72,512]{1,0:T(8,128)S(1)}, u32[]{:S(2)}, u32[]{:S(2)}) collective-permute-start(f32[72,512]{1,0:T(8,128)S(1)} %pad_maximum_fusion), channel_id=1, source_target_pairs={{0,16},{16,32},{32,48},{48,64},{64,80},{80,96},{96,112},{112,128},... | collective-permute-start | bytes 442376 | tf_op jit(solution)/shard_map/ppermute | solution.py:321
  34.8 9.1 %collective-permute-start.4 = (f32[72,512]{1,0:T(8,128)S(1)}, f32[72,512]{1,0:T(8,128)S(1)}, u32[]{:S(2)}, u32[]{:S(2)}) collective-permute-start(f32[72,512]{1,0:T(8,128)S(1)} %pad_maximum_fusion), channel_id=1, source_target_pairs={{0,32},{16,48},{32,64},{48,80},{64,96},{80,112},{96,128},{112,144}... | collective-permute-start | bytes 442376 | tf_op jit(solution)/shard_map/ppermute | solution.py:321
  36.8 20.7 %collective-permute-start.5 = (f32[72,512]{1,0:T(8,128)S(1)}, f32[72,512]{1,0:T(8,128)S(1)}, u32[]{:S(2)}, u32[]{:S(2)}) collective-permute-start(f32[72,512]{1,0:T(8,128)S(1)} %pad_maximum_fusion), channel_id=1, source_target_pairs={{0,48},{16,64},{32,80},{48,96},{64,112},{80,128},{96,144},{112,160... | collective-permute-start | bytes 442376 | tf_op jit(solution)/shard_map/ppermute | solution.py:321
  60.1 50.1 %copy-start.14 = (f32[192,512]{1,0:T(8,128)}, f32[192,512]{1,0:T(8,128)S(1)}, u32[]{:S(2)}) copy-start(f32[192,512]{1,0:T(8,128)S(1)} %get-tuple-element.76.own_ref) | copy-start | bytes 1179652
  90.8 29.5 %copy-start.10 = (f32[384,512]{1,0:T(8,128)}, f32[384,512]{1,0:T(8,128)S(1)}, u32[]{:S(2)}) copy-start(f32[384,512]{1,0:T(8,128)S(1)} %all-gather.1) | copy-start | bytes 2359300
  99.5 10.1 %collective-permute-start.6 = (f32[32,512]{1,0:T(8,128)}, f32[32,512]{1,0:T(8,128)S(1)}, u32[]{:S(2)}, u32[]{:S(2)}) collective-permute-start(f32[32,512]{1,0:T(8,128)} %shard_map.107.drows_ref), channel_id=1, source_target_pairs={{0,64},{16,80},{32,96},{48,112},{64,128},{80,144},{96,160},{112,17... | collective-permute-start | bytes 196616 | tf_op jit(solution)/shard_map/ppermute | solution.py:321
  109.6 0.6 copy-start.13
  110.2 15.5 %copy-start.12 = (f32[32,512]{1,0:T(8,128)S(1)}, f32[32,512]{1,0:T(8,128)}, u32[]{:S(2)}) copy-start(f32[32,512]{1,0:T(8,128)} %param.8) | copy-start | bytes 196612
  120.3 23.3 %all-to-all-start = ((f32[16,32,256]{2,1,0:T(8,128)}), f32[16,32,256]{2,1,0:T(8,128)S(1)}, u32[]{:S(2)}, u32[]{:S(2)}) async-start(f32[16,32,256]{2,1,0:T(8,128)} %get-tuple-element.51), calls=%async_computation | async-start | bytes 1048576 | tf_op jit(solution)/shard_map/all_to_all | solution.py:329
  131.6 25.4 %copy-start = (f32[32,512]{1,0:T(8,128)S(1)}, f32[32,512]{1,0:T(8,128)}, u32[]{:S(2)}) copy-start(f32[32,512]{1,0:T(8,128)} %shard_map.107.drows_ref) | copy-start | bytes 196612
  131.6 25.4 %copy-start.9 = (bf16[2,512,512]{2,1,0:T(8,128)(2,1)S(1)}, bf16[2,512,512]{2,1,0:T(8,128)(2,1)}, u32[]{:S(2)}) copy-start(bf16[2,512,512]{2,1,0:T(8,128)(2,1)} %get-tuple-element.61.m2_ref) | copy-start | bytes 3145732
  131.6 32.3 %copy-start.8 = (bf16[2,512,512]{2,1,0:T(8,128)(2,1)S(1)}, bf16[2,512,512]{2,1,0:T(8,128)(2,1)}, u32[]{:S(2)}) copy-start(bf16[2,512,512]{2,1,0:T(8,128)(2,1)} %get-tuple-element.64.d_ref) | copy-start | bytes 3145732
  143.6 0.8 copy-start.11
  149.5 14.4 %collective-permute-start.7 = (f32[72,512]{1,0:T(8,128)}, f32[72,512]{1,0:T(8,128)S(1)}, u32[]{:S(2)}, u32[]{:S(2)}) collective-permute-start(f32[72,512]{1,0:T(8,128)} %shard_map.106.state_ref), channel_id=1, source_target_pairs={{0,64},{16,80},{32,96},{48,112},{64,128},{80,144},{96,160},{112,17... | collective-permute-start | bytes 442376 | tf_op jit(solution)/shard_map/ppermute | solution.py:321
  157.0 0.9 copy-start.3
  157.9 1.2 copy-start.6
  163.9 0.9 copy-start.4
  167.2 17.6 %all-to-all-start.1 = ((f32[16,32,128]{2,1,0:T(8,128)}), f32[16,32,128]{2,1,0:T(8,128)S(1)}, u32[]{:S(2)}, u32[]{:S(2)}) async-start(f32[16,32,128]{2,1,0:T(8,128)} %shard_map.109), calls=%async_computation.1 | async-start | bytes 524288 | tf_op jit(solution)/shard_map/all_to_all | solution.py:329
  184.8 0.9 copy-start.5
  185.7 1.2 copy-start.7
Sparse Core Ops, SparseCore 0:
  33.0 61.5 all-gather.5
  110.4 43.9 all-gather.7

commit v10 on v9

--- a/solution.py
+++ b/solution.py
@@ -138,15 +138,12 @@
     return pair
 
 
-def prepare_kernel(rows, place_ref, a0_ref, inverses_ref, pair_ref, fixed_ref, head_ref):
+def prepare_kernel(rows, place_ref, a0_ref, inverses_ref, fixed_ref, head_ref):
     time, mine = place_ref[0], place_ref[1]
     shape, half = a0_ref.shape, rows // 2
     row = lax.broadcasted_iota(jnp.int32, shape, 0) + mine * rows
     eye = (row == lax.broadcasted_iota(jnp.int32, shape, 1)).astype(F32)
-    a0 = a0_ref[...]
-    pair_ref[:rows] = a0
-    pair_ref[rows:] = inverses_ref[0]
-    fixed_ref[:rows] = a0
+    fixed_ref[:rows] = a0_ref[...]
     fixed_ref[rows : 2 * rows] = jnp.where(time >= 1, inverses_ref[0], eye)
     fixed_ref[2 * rows : 3 * rows] = jnp.where(time >= 2, inverses_ref[1], eye)
     m2 = jnp.where(time >= 4, inverses_ref[2], eye)
@@ -265,36 +262,36 @@
 
 
 def third_kernel(
-    rows, state_ref, drows_ref, earlier_ref, m2_ref, z_ref, p2rows_ref, new_a_ref, buf, sems, pairs, pair_sems
+    rows, place_ref, prior_ref, state_ref, drows_ref, earlier_ref, m2_ref, d_ref, packed_ref, p2rows_ref, new_a_ref,
+    row_ref, buf, sems, pairs, pair_sems
 ):
     part = fetch_parts(earlier_ref, (0,), rows, buf, sems)
-    pair = fetch_pairs((m2_ref,), pairs, pair_sems)
+    pair = fetch_pairs((m2_ref, d_ref), pairs, pair_sems)
     e_row = state_ref[2 * rows + 1 : 2 * rows + 2]
-    both = dot(split(stacked(state_ref[rows : 2 * rows], drows_ref[...], sixteen(e_row))), pair(0))
+    m2 = pair(0)
+    v = dot_nt(split(prior_ref[:rows]), m2)
+    both = dot(split(stacked(state_ref[rows : 2 * rows], drows_ref[...], sixteen(e_row))), m2)
     p2rows_ref[...] = both[rows : 2 * rows]
+    v = dot_nt(split(v), pair(1))
     both = dot(split(both), part(0))
-    z_ref[:rows] = both[:rows]
-    z_ref[rows:] = both[2 * rows : 2 * rows + 8]
     new_a_ref[...] = both[rows : 2 * rows]
-
-
-def fourth_kernel(rows, place_ref, prior_ref, state_ref, z_ref, m2_ref, d_ref, packed_ref, buf, sems):
-    pair = fetch_pairs((m2_ref, d_ref), buf, sems)
-    v = dot_nt(split(prior_ref[:rows]), pair(0))
-    v = dot_nt(split(v), pair(1))
-    j = jnp.where(place_ref[0] >= 4, prior_ref[rows : 2 * rows], state_ref[rows : 2 * rows])
-    pack((v, state_ref[:rows], z_ref[:rows], j), packed_ref, rows)
+    active = place_ref[0] >= 4
+    j = jnp.where(active, prior_ref[rows : 2 * rows], state_ref[rows : 2 * rows])
+    pack((v, state_ref[:rows], both[:rows], j), packed_ref, rows)
+    prior_b, prior_e = prior_ref[2 * rows : 2 * rows + 1], prior_ref[2 * rows + 1 : 2 * rows + 2]
+    e_before = jnp.where(active, both[2 * rows : 2 * rows + 1] + prior_e, e_row)
+    row_ref[...] = sixteen(e_row, prior_b, state_ref[2 * rows : 2 * rows + 1], e_before)[:8]
 
 
 def last_kernel(
-    rows, received_ref, p2rows_ref, prior_ref, state_ref, part_ref, earlier_ref, d_ref, new_c_ref, new_j_ref, vectors_ref,
+    rows, received_ref, p2rows_ref, row_ref, part_ref, earlier_ref, d_ref, new_c_ref, new_j_ref, vectors_ref,
     buf, sems, pairs, pair_sems
 ):
     part = fetch_parts(earlier_ref, (0,), rows, buf, sems)
     pair = fetch_pairs((d_ref,), pairs, pair_sems)
     back = received_ref[...].T
     v, c_rows, z, j_rows = (back[i * rows : (i + 1) * rows] for i in range(4))
-    e_own, b_prior = state_ref[2 * rows + 1 : 2 * rows + 2], prior_ref[2 * rows : 2 * rows + 1]
+    e_own, b_prior = row_ref[0:1], row_ref[1:2]
     new_b = rowwise(p2rows_ref[...], b_prior) + rowwise(v, e_own)
     new_e = -rowwise(z, b_prior)
     vectors_ref[...] = in_lanes((new_b, new_e), rows, 128) + part_ref[...]
@@ -337,15 +334,15 @@
     place = jnp.stack([time, mine]).astype(jnp.int32)
     a0, c0, j0 = transition, covariance, information
 
-    both, fixed, head = call(
+    sent = passed_along(jnp.concatenate([a0, inverses[0]]), 2), passed_along(a0, 1), passed_along(a0, 3)
+    fixed, head = call(
         prepare_kernel,
         rows,
         (place, a0, inverses),
-        [((2 * rows, width), F32), ((4 * rows - rows // 2, width), F32), ((rows // 2, width), F32)],
+        [((4 * rows - rows // 2, width), F32), ((rows // 2, width), F32)],
         small=(0,),
         grant=4,
     )
-    sent = passed_along(both, 2), passed_along(a0, 1), passed_along(a0, 3)
     late, a1, a3 = lax.optimization_barrier(sent)
     (ready,) = call(
         ready_kernel,
@@ -434,43 +431,27 @@
     )
 
     prior = passed_along(state, 4)
-    z, p2rows, new_a = call(
+    packed, p2rows, new_a, lines = call(
         third_kernel,
         rows,
-        (state, drows, earlier, m2),
-        [flat(8), flat(), flat()],
-        {2, 3},
+        (place, prior, state, drows, earlier, m2, d),
+        [((peers, rows, 4 * rows), F32), flat(), flat(), ((8, width), F32)],
+        {4, 5, 6},
         (),
-        stage(1) + pairs(1),
-        flops=mults,
-        grant=16,
-    )
-    (packed,) = call(
-        fourth_kernel,
-        rows,
-        (place, prior, state, z, m2, d),
-        [((peers, rows, 4 * rows), F32)],
-        {4, 5},
-        (),
-        pairs(2),
+        stage(1) + pairs(2),
         flops=mults,
         grant=16,
         small=(0,),
     )
     back = exchanged(packed)
-
-    def own_part(vector):
-        return lax.dynamic_slice_in_dim(vector, mine * rows, rows, 0)
-
-    e_before = jnp.where(time >= 4, z[rows] + prior[2 * rows + 1], state[2 * rows + 1])
-    parts = jnp.stack([own_part(state[2 * rows]), own_part(e_before)], axis=1)
+    parts = lax.dynamic_slice_in_dim(lines[2:4], mine * rows, rows, 1).T
     parts = jnp.pad(parts, ((0, 0), (0, 126)))
     new_c, new_j, both = call(
         last_kernel,
         rows,
-        (back, p2rows, prior, state, parts, earlier, d),
+        (back, p2rows, lines, parts, earlier, d),
         [flat(), flat(), ((rows, 128), F32)],
-        {5, 6},
+        {4, 5},
         (),
         stage(1) + pairs(1),
         flops=mults,

time: 198 us -> 198 us (level)
  starting transfers between devices: 44.2 us -> 46.8 us
    all_to_all x2, starting transfers between devices: 11.3 us -> 13.5 us  [exchanged(): lax.all_to_all(packed, 'panel', split_axis=0, concat_axis=0, tiled=True)]
    unnamed x32 -> x29, local copies, waits for them, and re-layouts: 8.41 us -> 6.68 us
    pallas_call x10 -> x9, Pallas kernels: 38.2 us -> 38 us  [call(): pl.pallas_call(functools.partial(kernel, rows), out_shape=[jax.ShapeDtype...]
  transfers between devices with their start and end apart: 12 -> 12, of which waited for: 9 -> 9; matrix products, arithmetic and copies ran while one was open for 4% -> 5% of each run, Pallas kernels for 14% -> 14%
where the time goes in v10:
time: 198 us; the launch traced here: 196 us
  waiting for transfers between devices  50.2 us (25%)
  starting transfers between devices  46.8 us (24%)
  Pallas kernels  38 us (19%)
  blocking collectives  30.8 us (16%)
  between operations  14.3 us (7%)
  local copies, waits for them, and re-layouts  9.99 us (5%)
  other arithmetic  6.26 us (3%)
    pallas_call x9, Pallas kernels, call(): pl.pallas_call(functools.partial(kernel, rows), out_shape=[jax.ShapeDtype...  38 us
    ppermute x8, starting transfers between devices, passed_along(): lax.ppermute(shard, 'tm', [(i, i + by) for i in range(peers) if 0 <= i +...  33.3 us
    all_gather x1, blocking collectives, gathered(): return lax.all_gather(shard, 'panel', axis=0, tiled=False)  30.8 us
    ppermute x8, waiting for transfers between devices, passed_along(): lax.ppermute(shard, 'tm', [(i, i + by) for i in range(peers) if 0 <= i +...  30.8 us
    all_to_all x2, waiting for transfers between devices, exchanged(): lax.all_to_all(packed, 'panel', split_axis=0, concat_axis=0, tiled=True)  16.8 us
    all_to_all x2, starting transfers between devices, exchanged(): lax.all_to_all(packed, 'panel', split_axis=0, concat_axis=0, tiled=True)  13.5 us
    unnamed x29, local copies, waits for them, and re-layouts  6.68 us
  transfers between devices with their start and end apart: 12, of which 9 were waited for; matrix products, arithmetic and copies ran while one was open for 5% of the time, Pallas kernels for 14%

profile of v10, /device:TPU:7, one launch (start us, length us, event | category | flops | bytes accessed | tf_op | source)
XLA Modules:
  0.0 196.4 jit_solution(13164927588099815468)
XLA Ops:
  7.2 3.2 %collective-permute-start.1 = (f32[32,512]{1,0:T(8,128)}, f32[32,512]{1,0:T(8,128)S(1)}, u32[]{:S(2)}, u32[]{:S(2)}) collective-permute-start(f32[32,512]{1,0:T(8,128)} %a0_ref.3), channel_id=1, source_target_pairs={{0,16},{16,32},{32,48},{48,64},{64,80},{80,96},{96,112},{112,128},... | collective-permute-start | bytes 196616 | tf_op jit(solution)/shard_map/ppermute | solution.py:318
  10.4 6.4 %collective-permute-start.2 = (f32[32,512]{1,0:T(8,128)}, f32[32,512]{1,0:T(8,128)S(1)}, u32[]{:S(2)}, u32[]{:S(2)}) collective-permute-start(f32[32,512]{1,0:T(8,128)} %a0_ref.3), channel_id=1, source_target_pairs={{0,48},{16,64},{32,80},{48,96},{64,112},{80,128},{96,144},{112,160... | collective-permute-start | bytes 196616 | tf_op jit(solution)/shard_map/ppermute | solution.py:318
  16.9 0.8 slice_bitcast_fusion
  17.7 0.8 pad_maximum_fusion.1
  18.6 2.4 %collective-permute-start = (f32[64,512]{1,0:T(8,128)S(1)}, f32[64,512]{1,0:T(8,128)S(1)}, u32[]{:S(2)}, u32[]{:S(2)}) collective-permute-start(f32[64,512]{1,0:T(8,128)S(1)} %pad_maximum_fusion.1), channel_id=1, source_target_pairs={{0,32},{16,48},{32,64},{48,80},{64,96},{80,112},{96,128},{112,144}... | collective-permute-start | bytes 393224 | tf_op jit(solution)/shard_map/ppermute | solution.py:318
  21.0 0.7 select_maximum_fusion
  21.8 0.8 copy-done.6
  22.6 0.9 copy-done.7
  23.5 0.6 shard_map.101
  24.1 0.9 pad_maximum_fusion
  25.0 5.8 %collective-permute-done.late_ref = f32[64,512]{1,0:T(8,128)S(1)} collective-permute-done((f32[64,512]{1,0:T(8,128)S(1)}, f32[64,512]{1,0:T(8,128)S(1)}, u32[]{:S(2)}, u32[]{:S(2)}) %collective-permute-start) | collective-permute-done | bytes 131104 | tf_op jit(solution)/shard_map/ppermute | solution.py:318
  30.8 1.4 shard_map.102
  32.3 1.9 collective-permute-start.3
  34.2 1.9 collective-permute-start.4
  36.2 2.8 %collective-permute-start.5 = (f32[72,512]{1,0:T(8,128)S(1)}, f32[72,512]{1,0:T(8,128)S(1)}, u32[]{:S(2)}, u32[]{:S(2)}) collective-permute-start(f32[72,512]{1,0:T(8,128)S(1)} %pad_maximum_fusion), channel_id=1, source_target_pairs={{0,48},{16,64},{32,80},{48,96},{64,112},{80,128},{96,144},{112,160... | collective-permute-start | bytes 442376 | tf_op jit(solution)/shard_map/ppermute | solution.py:318
  39.0 1.3 collective-permute-done.3
  40.3 4.3 %collective-permute-done.4 = f32[72,512]{1,0:T(8,128)S(1)} collective-permute-done((f32[72,512]{1,0:T(8,128)S(1)}, f32[72,512]{1,0:T(8,128)S(1)}, u32[]{:S(2)}, u32[]{:S(2)}) %collective-permute-start.4) | collective-permute-done | bytes 147488 | tf_op jit(solution)/shard_map/ppermute | solution.py:318
  44.6 11.5 %collective-permute-done.5 = f32[72,512]{1,0:T(8,128)S(1)} collective-permute-done((f32[72,512]{1,0:T(8,128)S(1)}, f32[72,512]{1,0:T(8,128)S(1)}, u32[]{:S(2)}, u32[]{:S(2)}) %collective-permute-start.5) | collective-permute-done | bytes 147488 | tf_op jit(solution)/shard_map/ppermute | solution.py:318
  56.2 0.7 concatenate.21
  57.1 0.9 constant_dynamic-update-slice_fusion
  58.0 0.7 slice_dynamic-update-slice_fusion
  58.9 30.8 %all-gather.1 = f32[384,512]{1,0:T(8,128)S(1)} all-gather(f32[24,512]{1,0:T(8,128)S(1)} %concatenate.22), channel_id=3, replica_groups=mesh['tm'=32,'panel'=16] {'panel'}, dimensions={0}, use_global_device_ids=true | all-gather | bytes 835584 | tf_op jit(solution)/shard_map/all_gather | solution.py:322
  89.9 0.7 reshape.27.vec_ref
  90.6 0.6 slice_reduce_fusion.u_ref
  91.2 2.6 %all-gather.6.cloned.1.call-done = f32[3840,512]{1,0:T(8,128)} async-done(((f32[240,512]{1,0:T(8,128)}), f32[3840,512]{1,0:T(8,128)}) %all-gather.6.cloned.1.call-update) | async-done | bytes 7864336 | tf_op jit(solution)/shard_map/all_gather | solution.py:322
  93.8 4.9 %shard_map.107.drows_ref = f32[32,512]{1,0:T(8,128)} custom-call(f32[16,240,512]{2,1,0:T(8,128)} %bitcast.26, f32[32,512]{1,0:T(8,128)} %a0_ref.3), custom_call_target="tpu_custom_call" | custom-call | flops 805306368 | bytes 7929856 | tf_op jit(solution)/shard_map/pallas_call | solution.py:305
  98.7 7.1 %collective-permute-start.7 = (f32[32,512]{1,0:T(8,128)}, f32[32,512]{1,0:T(8,128)S(1)}, u32[]{:S(2)}, u32[]{:S(2)}) collective-permute-start(f32[32,512]{1,0:T(8,128)} %shard_map.107.drows_ref), channel_id=1, source_target_pairs={{0,64},{16,80},{32,96},{48,112},{64,128},{80,144},{96,160},{112,17... | collective-permute-start | bytes 196616 | tf_op jit(solution)/shard_map/ppermute | solution.py:318
  105.8 3.0 %collective-permute-done.7 = f32[32,512]{1,0:T(8,128)S(1)} collective-permute-done((f32[32,512]{1,0:T(8,128)}, f32[32,512]{1,0:T(8,128)S(1)}, u32[]{:S(2)}, u32[]{:S(2)}) %collective-permute-start.7) | collective-permute-done | bytes 65568 | tf_op jit(solution)/shard_map/ppermute | solution.py:318
  108.8 0.6 copy-done.11
  109.5 10.0 %shard_map.103 = (f32[16,32,256]{2,1,0:T(8,128)}, f32[8,512]{1,0:T(8,128)}, bf16[2,512,512]{2,1,0:T(8,128)(2,1)}, bf16[2,512,512]{2,1,0:T(8,128)(2,1)}, bf16[2,5...) custom-call(f32[16,240,512]{2,1,0:T(8,128)} %bitcast.27, f32[192,512]{1,0:T(8,128)} %copy-done.12, ...), custom_call_target="tpu_custom_call" | custom-call | flops 4831838208 | bytes 8282112 | tf_op jit(solution)/shard_map/pallas_call | solution.py:305
  119.6 5.4 %all-to-all-start = ((f32[16,32,256]{2,1,0:T(8,128)}), f32[16,32,256]{2,1,0:T(8,128)S(1)}, u32[]{:S(2)}, u32[]{:S(2)}) async-start(f32[16,32,256]{2,1,0:T(8,128)} %get-tuple-element.50), calls=%async_computation | async-start | bytes 1048576 | tf_op jit(solution)/shard_map/all_to_all | solution.py:326
  125.0 0.7 pad_maximum_fusion.2.own_ref
  125.7 5.1 %shard_map.105 = (bf16[2,512,512]{2,1,0:T(8,128)(2,1)}, bf16[2,512,512]{2,1,0:T(8,128)(2,1)}, bf16[2,512,512]{2,1,0:T(8,128)(2,1)}) custom-call(f32[16,240,512]{2,1,0:T(8,128)} %bitcast.28, f32[16,24,512]{2,1,0:T(8,128)} %bitcast.32, bf16[2,512,512]{2,1,0:T(8,128)(2,1)} %get-tuple-element.57.bw_ref, bf16[2,512,512]{2,1,0:T(8,128)(2,1)} %get-tuple-element.54.bp_ref), custom_call_target="tpu_custom_call" | custom-call | flops 1610612736 | bytes 10747904 | tf_op jit(solution)/shard_map/pallas_call | solution.py:305
  130.9 6.2 %shard_map.104 = (bf16[2,512,512]{2,1,0:T(8,128)(2,1)}, bf16[2,512,512]{2,1,0:T(8,128)(2,1)}, bf16[2,512,512]{2,1,0:T(8,128)(2,1)}) custom-call(f32[16,240,512]{2,1,0:T(8,128)} %bitcast.29, bf16[2,512,512]{2,1,0:T(8,128)(2,1)} %get-tuple-element.54.bp_ref), custom_call_target="tpu_custom_call" | custom-call | flops 2415919104 | bytes 8912896 | tf_op jit(solution)/shard_map/pallas_call | solution.py:305
  137.0 5.9 %all-to-all-done = f32[16,32,256]{2,1,0:T(8,128)S(1)} async-done(((f32[16,32,256]{2,1,0:T(8,128)}), f32[16,32,256]{2,1,0:T(8,128)S(1)}, u32[]{:S(2)}, u32[]{:S(2)}) %all-to-all-start) | async-done | bytes 524320 | tf_op jit(solution)/shard_map/all_to_all | solution.py:326
  142.9 0.8 copy-done.9
  143.7 5.1 %shard_map.106.state_ref = f32[72,512]{1,0:T(8,128)} custom-call(f32[512,256]{1,0:T(8,128)} %bitcast.33, f32[64,512]{1,0:T(8,128)} %pad_maximum_fusion.2.own_ref, f32[8,512]{1,0:T(8,128)} %get-tuple-element.51.vec_ref, bf16[2,512,512]{2,1,0:T(8,128)(2,1)} %get-tuple-element.52.p0p_ref, bf16[2,512,512]{2,1,0:T(8,128)(2,1)} %get-tuple-element.53.p0_ref, ...), custom_call_target="tpu_custom_call" | custom-call | flops 805306368 | bytes 6963200 | tf_op jit(solution)/shard_map/pallas_call | solution.py:305
  148.8 7.5 %collective-permute-start.6 = (f32[72,512]{1,0:T(8,128)}, f32[72,512]{1,0:T(8,128)S(1)}, u32[]{:S(2)}, u32[]{:S(2)}) collective-permute-start(f32[72,512]{1,0:T(8,128)} %shard_map.106.state_ref), channel_id=1, source_target_pairs={{0,64},{16,80},{32,96},{48,112},{64,128},{80,144},{96,160},{112,17... | collective-permute-start | bytes 442376 | tf_op jit(solution)/shard_map/ppermute | solution.py:318
  156.3 4.8 %collective-permute-done.6.prior_ref = f32[72,512]{1,0:T(8,128)S(1)} collective-permute-done((f32[72,512]{1,0:T(8,128)}, f32[72,512]{1,0:T(8,128)S(1)}, u32[]{:S(2)}, u32[]{:S(2)}) %collective-permute-start.6) | collective-permute-done | bytes 147488 | tf_op jit(solution)/shard_map/ppermute | solution.py:318
  161.1 1.2 copy-done
  162.3 0.9 copy-done.4
  163.3 2.9 %shard_map.108 = (f32[16,32,128]{2,1,0:T(8,128)}, f32[32,512]{1,0:T(8,128)S(1)}, f32[32,512]{1,0:T(8,128)S(1)}, f32[8,512]{1,0:T(8,128)S(1)}) custom-call(s32[2]{0:T(128)S(1)} %pad_add_fusion.place_ref, f32[72,512]{1,0:T(8,128)S(1)} %collective-permute-done.6.prior_ref, f32[72,512]{1,0:T(8,128)S(1)} %copy-done.4, f32[32,512]{1,0:T(8,128)S(1)} %copy-done.5, ...), custom_call_target="tpu_custom_call" | custom-call | flops 805306368 | bytes 3506184 | tf_op jit(solution)/shard_map/pallas_call | solution.py:305
  166.2 8.0 %all-to-all-start.1 = ((f32[16,32,128]{2,1,0:T(8,128)}), f32[16,32,128]{2,1,0:T(8,128)S(1)}, u32[]{:S(2)}, u32[]{:S(2)}) async-start(f32[16,32,128]{2,1,0:T(8,128)} %get-tuple-element.63), calls=%async_computation.1 | async-start | bytes 524288 | tf_op jit(solution)/shard_map/all_to_all | solution.py:326
  174.4 0.6 broadcast_select_fusion
  175.1 10.9 %all-to-all-done.1 = f32[16,32,128]{2,1,0:T(8,128)S(1)} async-done(((f32[16,32,128]{2,1,0:T(8,128)}), f32[16,32,128]{2,1,0:T(8,128)S(1)}, u32[]{:S(2)}, u32[]{:S(2)}) %all-to-all-start.1) | async-done | bytes 262176 | tf_op jit(solution)/shard_map/all_to_all | solution.py:326
  185.9 1.2 copy-done.1
  187.2 1.7 shard_map.109
  188.9 0.7 slice_reduce_fusion.2
  (46 shorter events, 0.9 us)
Async XLA Ops:
  7.2 86.7 %all-gather.6.cloned.1.call-start = ((), (), s32[]{:S(2)}) async-start(), calls=%async_computation.2 | async-start | bytes 8355840 | tf_op jit(solution)/shard_map/all_gather | solution.py:322
  7.2 17.8 %collective-permute-start.1 = (f32[32,512]{1,0:T(8,128)}, f32[32,512]{1,0:T(8,128)S(1)}, u32[]{:S(2)}, u32[]{:S(2)}) collective-permute-start(f32[32,512]{1,0:T(8,128)} %a0_ref.3), channel_id=1, source_target_pairs={{0,16},{16,32},{32,48},{48,64},{64,80},{80,96},{96,112},{112,128},... | collective-permute-start | bytes 196616 | tf_op jit(solution)/shard_map/ppermute | solution.py:318
  10.4 14.6 %collective-permute-start.2 = (f32[32,512]{1,0:T(8,128)}, f32[32,512]{1,0:T(8,128)S(1)}, u32[]{:S(2)}, u32[]{:S(2)}) collective-permute-start(f32[32,512]{1,0:T(8,128)} %a0_ref.3), channel_id=1, source_target_pairs={{0,48},{16,64},{32,80},{48,96},{64,112},{80,128},{96,144},{112,160... | collective-permute-start | bytes 196616 | tf_op jit(solution)/shard_map/ppermute | solution.py:318
  18.6 12.2 %collective-permute-start = (f32[64,512]{1,0:T(8,128)S(1)}, f32[64,512]{1,0:T(8,128)S(1)}, u32[]{:S(2)}, u32[]{:S(2)}) collective-permute-start(f32[64,512]{1,0:T(8,128)S(1)} %pad_maximum_fusion.1), channel_id=1, source_target_pairs={{0,32},{16,48},{32,64},{48,80},{64,96},{80,112},{96,128},{112,144}... | collective-permute-start | bytes 393224 | tf_op jit(solution)/shard_map/ppermute | solution.py:318
  21.8 0.8 copy-start.6
  22.6 0.9 copy-start.7
  32.2 128.9 %all-gather.8.cloned.1.call-start = ((), (), s32[]{:S(2)}) async-start(), calls=%async_computation.3 | async-start | bytes 1114112 | tf_op jit(solution)/shard_map/all_gather | solution.py:322
  32.3 8.0 %collective-permute-start.3 = (f32[72,512]{1,0:T(8,128)S(1)}, f32[72,512]{1,0:T(8,128)S(1)}, u32[]{:S(2)}, u32[]{:S(2)}) collective-permute-start(f32[72,512]{1,0:T(8,128)S(1)} %pad_maximum_fusion), channel_id=1, source_target_pairs={{0,16},{16,32},{32,48},{48,64},{64,80},{80,96},{96,112},{112,128},... | collective-permute-start | bytes 442376 | tf_op jit(solution)/shard_map/ppermute | solution.py:318
  34.2 10.4 %collective-permute-start.4 = (f32[72,512]{1,0:T(8,128)S(1)}, f32[72,512]{1,0:T(8,128)S(1)}, u32[]{:S(2)}, u32[]{:S(2)}) collective-permute-start(f32[72,512]{1,0:T(8,128)S(1)} %pad_maximum_fusion), channel_id=1, source_target_pairs={{0,32},{16,48},{32,64},{48,80},{64,96},{80,112},{96,128},{112,144}... | collective-permute-start | bytes 442376 | tf_op jit(solution)/shard_map/ppermute | solution.py:318
  36.2 20.0 %collective-permute-start.5 = (f32[72,512]{1,0:T(8,128)S(1)}, f32[72,512]{1,0:T(8,128)S(1)}, u32[]{:S(2)}, u32[]{:S(2)}) collective-permute-start(f32[72,512]{1,0:T(8,128)S(1)} %pad_maximum_fusion), channel_id=1, source_target_pairs={{0,48},{16,64},{32,80},{48,96},{64,112},{80,128},{96,144},{112,160... | collective-permute-start | bytes 442376 | tf_op jit(solution)/shard_map/ppermute | solution.py:318
  58.8 50.7 %copy-start.12 = (f32[192,512]{1,0:T(8,128)}, f32[192,512]{1,0:T(8,128)S(1)}, u32[]{:S(2)}) copy-start(f32[192,512]{1,0:T(8,128)S(1)} %get-tuple-element.74.own_ref) | copy-start | bytes 1179652
  89.7 29.8 %copy-start.8 = (f32[384,512]{1,0:T(8,128)}, f32[384,512]{1,0:T(8,128)S(1)}, u32[]{:S(2)}) copy-start(f32[384,512]{1,0:T(8,128)S(1)} %all-gather.1) | copy-start | bytes 2359300
  98.7 10.1 %collective-permute-start.7 = (f32[32,512]{1,0:T(8,128)}, f32[32,512]{1,0:T(8,128)S(1)}, u32[]{:S(2)}, u32[]{:S(2)}) collective-permute-start(f32[32,512]{1,0:T(8,128)} %shard_map.107.drows_ref), channel_id=1, source_target_pairs={{0,64},{16,80},{32,96},{48,112},{64,128},{80,144},{96,160},{112,17... | collective-permute-start | bytes 196616 | tf_op jit(solution)/shard_map/ppermute | solution.py:318
  108.8 0.6 copy-start.11
  109.5 15.5 %copy-start.10 = (f32[32,512]{1,0:T(8,128)S(1)}, f32[32,512]{1,0:T(8,128)}, u32[]{:S(2)}) copy-start(f32[32,512]{1,0:T(8,128)} %param.8) | copy-start | bytes 196612
  119.6 23.3 %all-to-all-start = ((f32[16,32,256]{2,1,0:T(8,128)}), f32[16,32,256]{2,1,0:T(8,128)S(1)}, u32[]{:S(2)}, u32[]{:S(2)}) async-start(f32[16,32,256]{2,1,0:T(8,128)} %get-tuple-element.50), calls=%async_computation | async-start | bytes 1048576 | tf_op jit(solution)/shard_map/all_to_all | solution.py:326
  130.8 30.3 %copy-start.2 = (bf16[2,512,512]{2,1,0:T(8,128)(2,1)S(1)}, bf16[2,512,512]{2,1,0:T(8,128)(2,1)}, u32[]{:S(2)}) copy-start(bf16[2,512,512]{2,1,0:T(8,128)(2,1)} %get-tuple-element.61.d_ref) | copy-start | bytes 3145732
  130.9 30.3 %copy-start.3 = (bf16[2,512,512]{2,1,0:T(8,128)(2,1)S(1)}, bf16[2,512,512]{2,1,0:T(8,128)(2,1)}, u32[]{:S(2)}) copy-start(bf16[2,512,512]{2,1,0:T(8,128)(2,1)} %get-tuple-element.60.m2_ref) | copy-start | bytes 3145732
  130.9 30.2 %copy-start.5 = (f32[32,512]{1,0:T(8,128)S(1)}, f32[32,512]{1,0:T(8,128)}, u32[]{:S(2)}) copy-start(f32[32,512]{1,0:T(8,128)} %shard_map.107.drows_ref) | copy-start | bytes 196612
  142.9 0.8 copy-start.9
  148.8 12.3 %collective-permute-start.6 = (f32[72,512]{1,0:T(8,128)}, f32[72,512]{1,0:T(8,128)S(1)}, u32[]{:S(2)}, u32[]{:S(2)}) collective-permute-start(f32[72,512]{1,0:T(8,128)} %shard_map.106.state_ref), channel_id=1, source_target_pairs={{0,64},{16,80},{32,96},{48,112},{64,128},{80,144},{96,160},{112,17... | collective-permute-start | bytes 442376 | tf_op jit(solution)/shard_map/ppermute | solution.py:318
  161.1 1.2 copy-start
  162.3 0.9 copy-start.4
  166.2 19.7 %all-to-all-start.1 = ((f32[16,32,128]{2,1,0:T(8,128)}), f32[16,32,128]{2,1,0:T(8,128)S(1)}, u32[]{:S(2)}, u32[]{:S(2)}) async-start(f32[16,32,128]{2,1,0:T(8,128)} %get-tuple-element.63), calls=%async_computation.1 | async-start | bytes 524288 | tf_op jit(solution)/shard_map/all_to_all | solution.py:326
  185.9 1.2 copy-start.1
Sparse Core Ops, SparseCore 0:
  32.4 61.4 all-gather.5
  109.6 43.9 all-gather.7

commit v11 on v10

--- a/solution.py
+++ b/solution.py
@@ -82,32 +82,11 @@
         return value
 
 
-def fetch_parts(stack_ref, order, rows, buf, sems, head_ref=None):
-    width, half = stack_ref.shape[2], rows // 2
-    copies = []
-    for k, i in enumerate(order):
-        if head_ref is not None and i == 7:
-            low, high = pl.ds(0, half), pl.ds(half, half)
-            copies.append(
-                [
-                    pltpu.make_async_copy(head_ref.at[:, pl.ds(8, half), :], buf.at[k, :, low, :], sems.at[k]),
-                    pltpu.make_async_copy(
-                        stack_ref.at[:, pl.ds(i * rows, half), :], buf.at[k, :, high, :], sems.at[len(order)]
-                    ),
-                ]
-            )
-        else:
-            copies.append([pltpu.make_async_copy(stack_ref.at[:, pl.ds(i * rows, rows), :], buf.at[k], sems.at[k])])
-    for group in copies:
-        for copy in group:
-            copy.start()
-
-    def part(k):
-        for copy in copies[k]:
-            copy.wait()
-        return split(buf[k].reshape(width, width))
-
-    return part
+def fetch_parts(stack_ref, order, rows, buf, sems):
+    sources = [stack_ref.at[:, pl.ds(i * rows, rows), :] for i in order]
+    fetch = Fetch(sources, [buf.at[k] for k in range(len(order))], sems)
+    width = stack_ref.shape[2]
+    return lambda k: split(fetch(k).reshape(width, width))
 
 
 class Store:
@@ -138,40 +117,40 @@
     return pair
 
 
-def prepare_kernel(rows, place_ref, a0_ref, inverses_ref, fixed_ref, head_ref):
+def prepare_kernel(rows, place_ref, a0_ref, inverses_ref, own_ref, fixed_ref, m2_ref):
     time, mine = place_ref[0], place_ref[1]
-    shape, half = a0_ref.shape, rows // 2
+    shape = a0_ref.shape
     row = lax.broadcasted_iota(jnp.int32, shape, 0) + mine * rows
     eye = (row == lax.broadcasted_iota(jnp.int32, shape, 1)).astype(F32)
-    fixed_ref[:rows] = a0_ref[...]
-    fixed_ref[rows : 2 * rows] = jnp.where(time >= 1, inverses_ref[0], eye)
-    fixed_ref[2 * rows : 3 * rows] = jnp.where(time >= 2, inverses_ref[1], eye)
-    m2 = jnp.where(time >= 4, inverses_ref[2], eye)
-    head_ref[...] = m2[:half]
-    fixed_ref[3 * rows :] = m2[half:]
-
-
-def ready_kernel(rows, place_ref, a1_ref, late_ref, a3_ref, fixed_ref, ready_ref):
+    own_ref[...] = a0_ref[...]
+    fixed_ref[:rows] = jnp.where(time >= 1, inverses_ref[0], eye)
+    fixed_ref[rows:] = jnp.where(time >= 2, inverses_ref[1], eye)
+    m2_ref[...] = jnp.where(time >= 4, inverses_ref[2], eye)
+
+
+def ready_kernel(rows, place_ref, own_ref, a1_ref, late_ref, a3_ref, fixed_ref, ready_ref):
     time, mine = place_ref[0], place_ref[1]
     shape = a1_ref.shape
     row = lax.broadcasted_iota(jnp.int32, shape, 0) + mine * rows
     eye = (row == lax.broadcasted_iota(jnp.int32, shape, 1)).astype(F32)
-    ready_ref[:rows] = fixed_ref[:rows]
+    ready_ref[:rows] = own_ref[...]
     ready_ref[rows : 2 * rows] = jnp.where(time >= 1, a1_ref[...], eye)
     ready_ref[2 * rows : 3 * rows] = jnp.where(time >= 2, late_ref[:rows], eye)
     ready_ref[3 * rows : 4 * rows] = jnp.where(time >= 3, a3_ref[...], eye)
-    ready_ref[4 * rows : 5 * rows] = fixed_ref[rows : 2 * rows]
+    ready_ref[4 * rows : 5 * rows] = fixed_ref[:rows]
     ready_ref[5 * rows : 6 * rows] = jnp.where(time >= 3, late_ref[rows:], eye)
-    ready_ref[6 * rows :] = fixed_ref[2 * rows :]
+    ready_ref[6 * rows :] = fixed_ref[rows:]
 
 
 def drows_kernel(rows, whole_ref, a0_ref, drows_ref, buf, sems, start, start_sems):
     first = Fetch([a0_ref], [start], start_sems)
     order = (4, 1, 6, 2, 5, 3)
     part = fetch_parts(whole_ref, order, rows, buf, sems)
-    total = first(0)
+    total, factor = first(0), part(0)
     for k in range(len(order)):
-        total = dot(split(total), part(k))
+        after = part(k + 1) if k + 1 < len(order) else None
+        total = dot(split(total), factor)
+        factor = after
     drows_ref[...] = total
 
 
@@ -185,17 +164,16 @@
     b0, e0, b1, e1, b2, e2, b3, e3 = (vec_ref[i : i + 1] for i in range(8))
     u1, u2, u3, u4 = (u_ref[i : i + 1] for i in range(4))
 
-    a0, m0 = part(0), part(1)
+    a0, m0, a1 = part(0), part(1), part(2)
     both = dot(joined(a0, sixteen(e0 - u2)), m0)
+    a2, m0p = part(3), part(4)
     p0, mixed = store(split(both[:width])), both[width:]
-    a1 = part(2)
     both = dot(joined(p0, j0, mixed), a1)
+    a3 = part(5)
     bw = store(split(both[:width]))
     y0, e_t = both[width : width + rows], both[width + rows : width + rows + 1] + e1
-    a2, m0p = part(3), part(4)
     both = dot(joined(a2, sixteen(e2 - u4)), m0p)
     p0p, mixed = store(split(both[:width])), both[width:]
-    a3 = part(5)
     both = dot(joined(p0p, j2, mixed), a3)
     bp = store(split(both[:width]))
     y2, e_p = both[width : width + rows], both[width + rows : width + rows + 1] + e3
@@ -217,17 +195,14 @@
     store.finish()
 
 
-def middle_kernel(
-    rows, whole_ref, head_ref, bw_ref, bp_ref, p1_ref, d_ref, m2_ref, buf, sems, pairs, pair_sems, out, outs
-):
-    part = fetch_parts(whole_ref, (6, 7), rows, buf, sems, head_ref)
+def middle_kernel(rows, whole_ref, bw_ref, bp_ref, p1_ref, d_ref, buf, sems, pairs, pair_sems, out, outs):
+    part = fetch_parts(whole_ref, (6,), rows, buf, sems)
     pair = fetch_pairs((bw_ref, bp_ref), pairs, pair_sems)
-    store = Store((p1_ref, d_ref, m2_ref), out, outs)
+    store = Store((p1_ref, d_ref), out, outs)
     bw, m1 = pair(0), part(0)
+    bp = pair(1)
     p1 = store(split(dot(bw, m1)))
-    bp = pair(1)
     store(split(dot(p1, bp)))
-    store(part(1))
     store.finish()
 
 
@@ -262,18 +237,19 @@
 
 
 def third_kernel(
-    rows, place_ref, prior_ref, state_ref, drows_ref, earlier_ref, m2_ref, d_ref, packed_ref, p2rows_ref, new_a_ref,
-    row_ref, buf, sems, pairs, pair_sems
+    rows, place_ref, prior_ref, state_ref, drows_ref, second_ref, d_ref, packed_ref, p2rows_ref, new_a_ref,
+    row_ref, earlier_ref, buf, sems, pairs, pair_sems, out, outs
 ):
-    part = fetch_parts(earlier_ref, (0,), rows, buf, sems)
-    pair = fetch_pairs((m2_ref, d_ref), pairs, pair_sems)
+    part = fetch_parts(second_ref, (1, 0), rows, buf, sems)
+    store = Store((earlier_ref,), out, outs)
+    pair = fetch_pairs((d_ref,), pairs, pair_sems)
     e_row = state_ref[2 * rows + 1 : 2 * rows + 2]
-    m2 = pair(0)
+    m2, d, earlier = part(0), pair(0), store(part(1))
     v = dot_nt(split(prior_ref[:rows]), m2)
     both = dot(split(stacked(state_ref[rows : 2 * rows], drows_ref[...], sixteen(e_row))), m2)
     p2rows_ref[...] = both[rows : 2 * rows]
-    v = dot_nt(split(v), pair(1))
-    both = dot(split(both), part(0))
+    v = dot_nt(split(v), d)
+    both = dot(split(both), earlier)
     new_a_ref[...] = both[rows : 2 * rows]
     active = place_ref[0] >= 4
     j = jnp.where(active, prior_ref[rows : 2 * rows], state_ref[rows : 2 * rows])
@@ -281,22 +257,22 @@
     prior_b, prior_e = prior_ref[2 * rows : 2 * rows + 1], prior_ref[2 * rows + 1 : 2 * rows + 2]
     e_before = jnp.where(active, both[2 * rows : 2 * rows + 1] + prior_e, e_row)
     row_ref[...] = sixteen(e_row, prior_b, state_ref[2 * rows : 2 * rows + 1], e_before)[:8]
+    store.finish()
 
 
 def last_kernel(
-    rows, received_ref, p2rows_ref, row_ref, part_ref, earlier_ref, d_ref, new_c_ref, new_j_ref, vectors_ref,
-    buf, sems, pairs, pair_sems
+    rows, received_ref, p2rows_ref, row_ref, part_ref, earlier_ref, d_ref, new_c_ref, new_j_ref, vectors_ref, pairs,
+    pair_sems
 ):
-    part = fetch_parts(earlier_ref, (0,), rows, buf, sems)
-    pair = fetch_pairs((d_ref,), pairs, pair_sems)
+    pair = fetch_pairs((earlier_ref, d_ref), pairs, pair_sems)
     back = received_ref[...].T
     v, c_rows, z, j_rows = (back[i * rows : (i + 1) * rows] for i in range(4))
     e_own, b_prior = row_ref[0:1], row_ref[1:2]
     new_b = rowwise(p2rows_ref[...], b_prior) + rowwise(v, e_own)
     new_e = -rowwise(z, b_prior)
     vectors_ref[...] = in_lanes((new_b, new_e), rows, 128) + part_ref[...]
-    new_j_ref[...] = dot(split(z), part(0)) + j_rows
-    new_c_ref[...] = dot_nt(split(v), pair(0)) + c_rows
+    new_j_ref[...] = dot(split(z), pair(0)) + j_rows
+    new_c_ref[...] = dot_nt(split(v), pair(1)) + c_rows
 
 
 def call(kernel, rows, operands, outs, placed=(), kept=(), scratch=(), flops=0, grant=58, small=()):
@@ -334,21 +310,21 @@
     place = jnp.stack([time, mine]).astype(jnp.int32)
     a0, c0, j0 = transition, covariance, information
 
-    sent = passed_along(jnp.concatenate([a0, inverses[0]]), 2), passed_along(a0, 1), passed_along(a0, 3)
-    fixed, head = call(
+    sent = passed_along(a0, 1), passed_along(jnp.concatenate([a0, inverses[0]]), 2), passed_along(a0, 3)
+    a1, late, a3 = lax.optimization_barrier(sent)
+    own, fixed, m2 = call(
         prepare_kernel,
         rows,
         (place, a0, inverses),
-        [((4 * rows - rows // 2, width), F32), ((rows // 2, width), F32)],
+        [((rows, width), F32), ((2 * rows, width), F32), ((rows, width), F32)],
         small=(0,),
         grant=4,
     )
-    late, a1, a3 = lax.optimization_barrier(sent)
     (ready,) = call(
         ready_kernel,
         rows,
-        (place, a1, late, a3, fixed),
-        [((8 * rows - rows // 2, width), F32)],
+        (place, own, a1, late, a3, fixed),
+        [((7 * rows, width), F32)],
         small=(0,),
         grant=4,
     )
@@ -366,7 +342,7 @@
 
     shares = jnp.stack([share(slices[1], c1), share(slices[2], j0), share(slices[5], c3), share(slices[6], j2)])
     line = jnp.pad(slices.reshape(1, -1), ((0, 3), (0, width - 8 * rows)))
-    head = gathered(jnp.concatenate([shares, line, head]))
+    head = gathered(jnp.concatenate([shares, line]))
     vectors = head[:, 4, : 8 * rows].reshape(peers, 8, rows).transpose(1, 0, 2).reshape(8, width)
     u = jnp.sum(head[:, :4], axis=0)
     whole, vectors, u = lax.optimization_barrier((whole, vectors, u))
@@ -375,7 +351,7 @@
     mults = 6 * width**3
 
     def stage(parts):
-        return [pltpu.VMEM((parts, peers, rows, width), F32), pltpu.SemaphoreType.DMA((parts + 1,))]
+        return [pltpu.VMEM((parts, peers, rows, width), F32), pltpu.SemaphoreType.DMA((parts,))]
 
     def pairs(count):
         return [pltpu.VMEM((count, 2, *square), BF16), pltpu.SemaphoreType.DMA((count,))]
@@ -393,7 +369,7 @@
         stage(6) + [pltpu.VMEM((rows, width), F32), pltpu.SemaphoreType.DMA((1,))],
         flops=mults,
     )
-    earlier = gathered(passed_along(drows, 4))
+    second = gathered(jnp.concatenate([passed_along(drows, 4), m2]))
 
     packed, vec, p0, bw, p0p, bp = call(
         first_kernel,
@@ -406,14 +382,14 @@
         flops=6 * mults,
     )
     received = exchanged(packed)
-    p1, d, m2 = call(
+    p1, d = call(
         middle_kernel,
         rows,
-        (whole, head, bw, bp),
-        [pair] * 3,
-        {0, 1, 2, 3},
-        range(3),
-        stage(2) + pairs(2) + pairs(3),
+        (whole, bw, bp),
+        [pair] * 2,
+        {0, 1, 2},
+        range(2),
+        stage(1) + pairs(2) + pairs(2),
         flops=2 * mults,
     )
     g1, g0, g0p = call(
@@ -428,19 +404,20 @@
         (),
         pairs(6),
         flops=mults,
+        grant=58,
     )
 
     prior = passed_along(state, 4)
-    packed, p2rows, new_a, lines = call(
+    packed, p2rows, new_a, lines, earlier = call(
         third_kernel,
         rows,
-        (place, prior, state, drows, earlier, m2, d),
-        [((peers, rows, 4 * rows), F32), flat(), flat(), ((8, width), F32)],
-        {4, 5, 6},
-        (),
-        stage(1) + pairs(2),
+        (place, prior, state, drows, second, d),
+        [((peers, rows, 4 * rows), F32), flat(), flat(), ((8, width), F32), pair],
+        {4, 5},
+        {4},
+        stage(2) + pairs(1) + pairs(1),
         flops=mults,
-        grant=16,
+        grant=40,
         small=(0,),
     )
     back = exchanged(packed)
@@ -453,9 +430,9 @@
         [flat(), flat(), ((rows, 128), F32)],
         {4, 5},
         (),
-        stage(1) + pairs(1),
+        pairs(2),
         flops=mults,
-        grant=16,
+        grant=36,
     )
     return jnp.where(time >= 4, new_a, drows), both[:, 0], new_c, both[:, 1], new_j
 

time: 198 us -> 195 us (0.985)
  blocking collectives: 30.8 us -> 26.3 us
  waiting for transfers between devices: 50.2 us -> 54.2 us
  starting transfers between devices: 46.8 us -> 43.6 us
    all_gather x1, blocking collectives: 30.8 us -> 26.3 us  [gathered(): return lax.all_gather(shard, 'panel', axis=0, tiled=False)]
    all_to_all x2, waiting for transfers between devices: 16.8 us -> 19.1 us  [exchanged(): lax.all_to_all(packed, 'panel', split_axis=0, concat_axis=0, tiled=True)]
    ppermute x8, waiting for transfers between devices: 30.8 us -> 33.2 us  [passed_along(): lax.ppermute(shard, 'tm', [(i, i + by) for i in range(peers) if 0 <= i +...]
    unnamed x29 -> x21, local copies, waits for them, and re-layouts: 6.68 us -> 5.22 us
where the time goes in v11:
time: 195 us; the launch traced here: 193 us
  waiting for transfers between devices  54.2 us (28%)
  starting transfers between devices  43.6 us (22%)
  Pallas kernels  39.5 us (20%)
  blocking collectives  26.3 us (13%)
  between operations  14.3 us (7%)
  local copies, waits for them, and re-layouts  8.5 us (4%)
  other arithmetic  6.91 us (4%)
    pallas_call x9, Pallas kernels, call(): pl.pallas_call(functools.partial(kernel, rows), out_shape=[jax.ShapeDtype...  39.5 us
    ppermute x8, waiting for transfers between devices, passed_along(): lax.ppermute(shard, 'tm', [(i, i + by) for i in range(peers) if 0 <= i +...  33.2 us
    ppermute x8, starting transfers between devices, passed_along(): lax.ppermute(shard, 'tm', [(i, i + by) for i in range(peers) if 0 <= i +...  31.3 us
    all_gather x1, blocking collectives, gathered(): return lax.all_gather(shard, 'panel', axis=0, tiled=False)  26.3 us
    all_to_all x2, waiting for transfers between devices, exchanged(): lax.all_to_all(packed, 'panel', split_axis=0, concat_axis=0, tiled=True)  19.1 us
    all_to_all x2, starting transfers between devices, exchanged(): lax.all_to_all(packed, 'panel', split_axis=0, concat_axis=0, tiled=True)  12.2 us
    unnamed x21, local copies, waits for them, and re-layouts  5.22 us
  transfers between devices with their start and end apart: 12, of which 9 were waited for; matrix products, arithmetic and copies ran while one was open for 5% of the time, Pallas kernels for 14%

profile of v11, /device:TPU:7, one launch (start us, length us, event | category | flops | bytes accessed | tf_op | source)
XLA Modules:
  0.0 193.3 jit_solution(3613227359287259192)
XLA Ops:
  7.2 3.2 %collective-permute-start = (f32[32,512]{1,0:T(8,128)}, f32[32,512]{1,0:T(8,128)S(1)}, u32[]{:S(2)}, u32[]{:S(2)}) collective-permute-start(f32[32,512]{1,0:T(8,128)} %a0_ref.3), channel_id=1, source_target_pairs={{0,16},{16,32},{32,48},{48,64},{64,80},{80,96},{96,112},{112,128},... | collective-permute-start | bytes 196616 | tf_op jit(solution)/shard_map/ppermute | solution.py:294
  10.4 6.4 %collective-permute-start.2 = (f32[32,512]{1,0:T(8,128)}, f32[32,512]{1,0:T(8,128)S(1)}, u32[]{:S(2)}, u32[]{:S(2)}) collective-permute-start(f32[32,512]{1,0:T(8,128)} %a0_ref.3), channel_id=1, source_target_pairs={{0,48},{16,64},{32,80},{48,96},{64,112},{80,128},{96,144},{112,160... | collective-permute-start | bytes 196616 | tf_op jit(solution)/shard_map/ppermute | solution.py:294
  16.9 0.8 slice_bitcast_fusion
  17.7 0.8 pad_maximum_fusion.1
  18.6 2.4 %collective-permute-start.1 = (f32[64,512]{1,0:T(8,128)S(1)}, f32[64,512]{1,0:T(8,128)S(1)}, u32[]{:S(2)}, u32[]{:S(2)}) collective-permute-start(f32[64,512]{1,0:T(8,128)S(1)} %pad_maximum_fusion.1), channel_id=1, source_target_pairs={{0,32},{16,48},{32,64},{48,80},{64,96},{80,112},{96,128},{112,144}... | collective-permute-start | bytes 393224 | tf_op jit(solution)/shard_map/ppermute | solution.py:294
  21.0 0.7 select_maximum_fusion
  21.8 0.8 copy-done.4
  22.6 0.9 copy-done.5
  23.5 0.6 shard_map.101
  24.1 0.9 pad_maximum_fusion
  25.0 5.8 %collective-permute-done.1.late_ref = f32[64,512]{1,0:T(8,128)S(1)} collective-permute-done((f32[64,512]{1,0:T(8,128)S(1)}, f32[64,512]{1,0:T(8,128)S(1)}, u32[]{:S(2)}, u32[]{:S(2)}) %collective-permute-start.1) | collective-permute-done | bytes 131104 | tf_op jit(solution)/shard_map/ppermute | solution.py:294
  30.8 1.3 shard_map.102
  32.2 1.9 collective-permute-start.3
  34.2 1.9 collective-permute-start.4
  36.1 2.8 %collective-permute-start.5 = (f32[72,512]{1,0:T(8,128)S(1)}, f32[72,512]{1,0:T(8,128)S(1)}, u32[]{:S(2)}, u32[]{:S(2)}) collective-permute-start(f32[72,512]{1,0:T(8,128)S(1)} %pad_maximum_fusion), channel_id=1, source_target_pairs={{0,48},{16,64},{32,80},{48,96},{64,112},{80,128},{96,144},{112,160... | collective-permute-start | bytes 442376 | tf_op jit(solution)/shard_map/ppermute | solution.py:294
  38.9 1.3 collective-permute-done.3
  40.2 4.3 %collective-permute-done.4 = f32[72,512]{1,0:T(8,128)S(1)} collective-permute-done((f32[72,512]{1,0:T(8,128)S(1)}, f32[72,512]{1,0:T(8,128)S(1)}, u32[]{:S(2)}, u32[]{:S(2)}) %collective-permute-start.4) | collective-permute-done | bytes 147488 | tf_op jit(solution)/shard_map/ppermute | solution.py:294
  44.6 11.5 %collective-permute-done.5 = f32[72,512]{1,0:T(8,128)S(1)} collective-permute-done((f32[72,512]{1,0:T(8,128)S(1)}, f32[72,512]{1,0:T(8,128)S(1)}, u32[]{:S(2)}, u32[]{:S(2)}) %collective-permute-start.5) | collective-permute-done | bytes 147488 | tf_op jit(solution)/shard_map/ppermute | solution.py:294
  56.1 0.7 concatenate.24
  56.9 0.1 fusion
  57.0 0.9 constant_dynamic-update-slice_fusion
  57.9 0.7 slice_dynamic-update-slice_fusion
  58.8 26.3 %all-gather.1 = f32[128,512]{1,0:T(8,128)S(1)} all-gather(f32[8,512]{1,0:T(8,128)S(1)} %concatenate.25), channel_id=3, replica_groups=mesh['tm'=32,'panel'=16] {'panel'}, dimensions={0}, use_global_device_ids=true | all-gather | bytes 278528 | tf_op jit(solution)/shard_map/all_gather | solution.py:298
  85.3 0.7 reshape.27.vec_ref
  86.0 0.6 slice_reduce_fusion.u_ref
  86.6 1.9 all-gather.6.cloned.1.call-done
  88.5 5.2 %shard_map.107.drows_ref = f32[32,512]{1,0:T(8,128)} custom-call(f32[16,224,512]{2,1,0:T(8,128)} %bitcast.25, f32[32,512]{1,0:T(8,128)} %a0_ref.3), custom_call_target="tpu_custom_call" | custom-call | flops 805306368 | bytes 7405568 | tf_op jit(solution)/shard_map/pallas_call | solution.py:281
  93.7 7.1 %collective-permute-start.7 = (f32[32,512]{1,0:T(8,128)}, f32[32,512]{1,0:T(8,128)S(1)}, u32[]{:S(2)}, u32[]{:S(2)}) collective-permute-start(f32[32,512]{1,0:T(8,128)} %shard_map.107.drows_ref), channel_id=1, source_target_pairs={{0,64},{16,80},{32,96},{48,112},{64,128},{80,144},{96,160},{112,17... | collective-permute-start | bytes 196616 | tf_op jit(solution)/shard_map/ppermute | solution.py:294
  100.8 3.0 %collective-permute-done.7 = f32[32,512]{1,0:T(8,128)S(1)} collective-permute-done((f32[32,512]{1,0:T(8,128)}, f32[32,512]{1,0:T(8,128)S(1)}, u32[]{:S(2)}, u32[]{:S(2)}) %collective-permute-start.7) | collective-permute-done | bytes 65568 | tf_op jit(solution)/shard_map/ppermute | solution.py:294
  103.8 0.7 pad_maximum_fusion.3
  104.5 11.5 %shard_map.103 = (f32[16,32,256]{2,1,0:T(8,128)}, f32[8,512]{1,0:T(8,128)}, bf16[2,512,512]{2,1,0:T(8,128)(2,1)}, bf16[2,512,512]{2,1,0:T(8,128)(2,1)}, bf16[2,5...) custom-call(f32[16,224,512]{2,1,0:T(8,128)} %bitcast.26, f32[192,512]{1,0:T(8,128)} %copy-done.8, ...), custom_call_target="tpu_custom_call" | custom-call | flops 4831838208 | bytes 7757824 | tf_op jit(solution)/shard_map/pallas_call | solution.py:281
  116.0 5.4 %all-to-all-start = ((f32[16,32,256]{2,1,0:T(8,128)}), f32[16,32,256]{2,1,0:T(8,128)S(1)}, u32[]{:S(2)}, u32[]{:S(2)}) async-start(f32[16,32,256]{2,1,0:T(8,128)} %get-tuple-element.51), calls=%async_computation | async-start | bytes 1048576 | tf_op jit(solution)/shard_map/all_to_all | solution.py:302
  121.4 0.7 pad_maximum_fusion.2.own_ref
  122.1 4.7 %shard_map.105 = (bf16[2,512,512]{2,1,0:T(8,128)(2,1)}, bf16[2,512,512]{2,1,0:T(8,128)(2,1)}) custom-call(f32[16,224,512]{2,1,0:T(8,128)} %bitcast.27, bf16[2,512,512]{2,1,0:T(8,128)(2,1)} %get-tuple-element.58.bw_ref, bf16[2,512,512]{2,1,0:T(8,128)(2,1)} %get-tuple-element.55.bp_ref), custom_call_target="tpu_custom_call" | custom-call | flops 1610612736 | bytes 9437184 | tf_op jit(solution)/shard_map/pallas_call | solution.py:281
  126.8 6.1 %shard_map.104 = (bf16[2,512,512]{2,1,0:T(8,128)(2,1)}, bf16[2,512,512]{2,1,0:T(8,128)(2,1)}, bf16[2,512,512]{2,1,0:T(8,128)(2,1)}) custom-call(f32[16,224,512]{2,1,0:T(8,128)} %bitcast.28, bf16[2,512,512]{2,1,0:T(8,128)(2,1)} %get-tuple-element.55.bp_ref), custom_call_target="tpu_custom_call" | custom-call | flops 2415919104 | bytes 8388608 | tf_op jit(solution)/shard_map/pallas_call | solution.py:281
  132.9 8.3 %all-to-all-done = f32[16,32,256]{2,1,0:T(8,128)S(1)} async-done(((f32[16,32,256]{2,1,0:T(8,128)}), f32[16,32,256]{2,1,0:T(8,128)S(1)}, u32[]{:S(2)}, u32[]{:S(2)}) %all-to-all-start) | async-done | bytes 524320 | tf_op jit(solution)/shard_map/all_to_all | solution.py:302
  141.2 0.8 copy-done.6
  142.0 5.1 %shard_map.106.state_ref = f32[72,512]{1,0:T(8,128)} custom-call(f32[512,256]{1,0:T(8,128)} %bitcast.29, f32[64,512]{1,0:T(8,128)} %pad_maximum_fusion.2.own_ref, f32[8,512]{1,0:T(8,128)} %get-tuple-element.52.vec_ref, bf16[2,512,512]{2,1,0:T(8,128)(2,1)} %get-tuple-element.53.p0p_ref, bf16[2,512,512]{2,1,0:T(8,128)(2,1)} %get-tuple-element.54.p0_ref, ...), custom_call_target="tpu_custom_call" | custom-call | flops 805306368 | bytes 6963200 | tf_op jit(solution)/shard_map/pallas_call | solution.py:281
  147.1 5.5 %collective-permute-start.6 = (f32[72,512]{1,0:T(8,128)}, f32[72,512]{1,0:T(8,128)S(1)}, u32[]{:S(2)}, u32[]{:S(2)}) collective-permute-start(f32[72,512]{1,0:T(8,128)} %shard_map.106.state_ref), channel_id=1, source_target_pairs={{0,64},{16,80},{32,96},{48,112},{64,128},{80,144},{96,160},{112,17... | collective-permute-start | bytes 442376 | tf_op jit(solution)/shard_map/ppermute | solution.py:294
  152.7 7.2 %collective-permute-done.6.prior_ref = f32[72,512]{1,0:T(8,128)S(1)} collective-permute-done((f32[72,512]{1,0:T(8,128)}, f32[72,512]{1,0:T(8,128)S(1)}, u32[]{:S(2)}, u32[]{:S(2)}) %collective-permute-start.6) | collective-permute-done | bytes 147488 | tf_op jit(solution)/shard_map/ppermute | solution.py:294
  159.8 1.6 copy-done
  161.4 0.9 copy-done.2
  162.3 3.2 %shard_map.108 = (f32[16,32,128]{2,1,0:T(8,128)}, f32[32,512]{1,0:T(8,128)S(1)}, f32[32,512]{1,0:T(8,128)S(1)}, f32[8,512]{1,0:T(8,128)S(1)}, bf16[2,512,512]{2,1,0:T(8,128)(2,1)S(1)}) custom-call(s32[2]{0:T(128)S(1)} %pad_add_fusion.place_ref, f32[72,512]{1,0:T(8,128)S(1)} %collective-permute-done.6.prior_ref, f32[72,512]{1,0:T(8,128)S(1)} %copy-done.2, ...), custom_call_target="tpu_custom_call" | custom-call | flops 805306368 | bytes 3506184 | tf_op jit(solution)/shard_map/pallas_call | solution.py:281
  165.6 6.8 %all-to-all-start.1 = ((f32[16,32,128]{2,1,0:T(8,128)}), f32[16,32,128]{2,1,0:T(8,128)S(1)}, u32[]{:S(2)}, u32[]{:S(2)}) async-start(f32[16,32,128]{2,1,0:T(8,128)} %get-tuple-element.64), calls=%async_computation.1 | async-start | bytes 524288 | tf_op jit(solution)/shard_map/all_to_all | solution.py:302
  172.6 0.6 broadcast_select_fusion
  173.2 10.9 %all-to-all-done.1 = f32[16,32,128]{2,1,0:T(8,128)S(1)} async-done(((f32[16,32,128]{2,1,0:T(8,128)}), f32[16,32,128]{2,1,0:T(8,128)S(1)}, u32[]{:S(2)}, u32[]{:S(2)}) %all-to-all-start.1) | async-done | bytes 262176 | tf_op jit(solution)/shard_map/all_to_all | solution.py:302
  184.1 1.7 shard_map.109
  185.8 0.7 slice_reduce_fusion.2
  (39 shorter events, 0.8 us)
Async XLA Ops:
  7.2 81.3 %all-gather.6.cloned.1.call-start = ((), (), s32[]{:S(2)}) async-start(), calls=%async_computation.2 | async-start | bytes 7798784 | tf_op jit(solution)/shard_map/all_gather | solution.py:298
  7.2 17.8 %collective-permute-start = (f32[32,512]{1,0:T(8,128)}, f32[32,512]{1,0:T(8,128)S(1)}, u32[]{:S(2)}, u32[]{:S(2)}) collective-permute-start(f32[32,512]{1,0:T(8,128)} %a0_ref.3), channel_id=1, source_target_pairs={{0,16},{16,32},{32,48},{48,64},{64,80},{80,96},{96,112},{112,128},... | collective-permute-start | bytes 196616 | tf_op jit(solution)/shard_map/ppermute | solution.py:294
  10.4 14.6 %collective-permute-start.2 = (f32[32,512]{1,0:T(8,128)}, f32[32,512]{1,0:T(8,128)S(1)}, u32[]{:S(2)}, u32[]{:S(2)}) collective-permute-start(f32[32,512]{1,0:T(8,128)} %a0_ref.3), channel_id=1, source_target_pairs={{0,48},{16,64},{32,80},{48,96},{64,112},{80,128},{96,144},{112,160... | collective-permute-start | bytes 196616 | tf_op jit(solution)/shard_map/ppermute | solution.py:294
  18.6 12.2 %collective-permute-start.1 = (f32[64,512]{1,0:T(8,128)S(1)}, f32[64,512]{1,0:T(8,128)S(1)}, u32[]{:S(2)}, u32[]{:S(2)}) collective-permute-start(f32[64,512]{1,0:T(8,128)S(1)} %pad_maximum_fusion.1), channel_id=1, source_target_pairs={{0,32},{16,48},{32,64},{48,80},{64,96},{80,112},{96,128},{112,144}... | collective-permute-start | bytes 393224 | tf_op jit(solution)/shard_map/ppermute | solution.py:294
  21.8 0.8 copy-start.4
  22.6 0.9 copy-start.5
  32.2 127.7 %all-gather.8.cloned.1.call-start = ((), (), s32[]{:S(2)}) async-start(), calls=%async_computation.3 | async-start | bytes 2228224 | tf_op jit(solution)/shard_map/all_gather | solution.py:298
  32.2 8.0 %collective-permute-start.3 = (f32[72,512]{1,0:T(8,128)S(1)}, f32[72,512]{1,0:T(8,128)S(1)}, u32[]{:S(2)}, u32[]{:S(2)}) collective-permute-start(f32[72,512]{1,0:T(8,128)S(1)} %pad_maximum_fusion), channel_id=1, source_target_pairs={{0,16},{16,32},{32,48},{48,64},{64,80},{80,96},{96,112},{112,128},... | collective-permute-start | bytes 442376 | tf_op jit(solution)/shard_map/ppermute | solution.py:294
  34.2 10.4 %collective-permute-start.4 = (f32[72,512]{1,0:T(8,128)S(1)}, f32[72,512]{1,0:T(8,128)S(1)}, u32[]{:S(2)}, u32[]{:S(2)}) collective-permute-start(f32[72,512]{1,0:T(8,128)S(1)} %pad_maximum_fusion), channel_id=1, source_target_pairs={{0,32},{16,48},{32,64},{48,80},{64,96},{80,112},{96,128},{112,144}... | collective-permute-start | bytes 442376 | tf_op jit(solution)/shard_map/ppermute | solution.py:294
  36.1 20.0 %collective-permute-start.5 = (f32[72,512]{1,0:T(8,128)S(1)}, f32[72,512]{1,0:T(8,128)S(1)}, u32[]{:S(2)}, u32[]{:S(2)}) collective-permute-start(f32[72,512]{1,0:T(8,128)S(1)} %pad_maximum_fusion), channel_id=1, source_target_pairs={{0,48},{16,64},{32,80},{48,96},{64,112},{80,128},{96,144},{112,160... | collective-permute-start | bytes 442376 | tf_op jit(solution)/shard_map/ppermute | solution.py:294
  58.8 45.7 %copy-start.8 = (f32[192,512]{1,0:T(8,128)}, f32[192,512]{1,0:T(8,128)S(1)}, u32[]{:S(2)}) copy-start(f32[192,512]{1,0:T(8,128)S(1)} %get-tuple-element.76.own_ref) | copy-start | bytes 1179652
  93.7 10.1 %collective-permute-start.7 = (f32[32,512]{1,0:T(8,128)}, f32[32,512]{1,0:T(8,128)S(1)}, u32[]{:S(2)}, u32[]{:S(2)}) collective-permute-start(f32[32,512]{1,0:T(8,128)} %shard_map.107.drows_ref), channel_id=1, source_target_pairs={{0,64},{16,80},{32,96},{48,112},{64,128},{80,144},{96,160},{112,17... | collective-permute-start | bytes 196616 | tf_op jit(solution)/shard_map/ppermute | solution.py:294
  104.5 16.9 %copy-start.7 = (f32[32,512]{1,0:T(8,128)S(1)}, f32[32,512]{1,0:T(8,128)}, u32[]{:S(2)}) copy-start(f32[32,512]{1,0:T(8,128)} %param.8) | copy-start | bytes 196612
  116.0 25.2 %all-to-all-start = ((f32[16,32,256]{2,1,0:T(8,128)}), f32[16,32,256]{2,1,0:T(8,128)S(1)}, u32[]{:S(2)}, u32[]{:S(2)}) async-start(f32[16,32,256]{2,1,0:T(8,128)} %get-tuple-element.51), calls=%async_computation | async-start | bytes 1048576 | tf_op jit(solution)/shard_map/all_to_all | solution.py:302
  126.8 33.0 %copy-start.1 = (bf16[2,512,512]{2,1,0:T(8,128)(2,1)S(1)}, bf16[2,512,512]{2,1,0:T(8,128)(2,1)}, u32[]{:S(2)}) copy-start(bf16[2,512,512]{2,1,0:T(8,128)(2,1)} %get-tuple-element.62.d_ref) | copy-start | bytes 3145732
  126.8 33.0 %copy-start.3 = (f32[32,512]{1,0:T(8,128)S(1)}, f32[32,512]{1,0:T(8,128)}, u32[]{:S(2)}) copy-start(f32[32,512]{1,0:T(8,128)} %shard_map.107.drows_ref) | copy-start | bytes 196612
  141.2 0.8 copy-start.6
  147.1 12.7 %collective-permute-start.6 = (f32[72,512]{1,0:T(8,128)}, f32[72,512]{1,0:T(8,128)S(1)}, u32[]{:S(2)}, u32[]{:S(2)}) collective-permute-start(f32[72,512]{1,0:T(8,128)} %shard_map.106.state_ref), channel_id=1, source_target_pairs={{0,64},{16,80},{32,96},{48,112},{64,128},{80,144},{96,160},{112,17... | collective-permute-start | bytes 442376 | tf_op jit(solution)/shard_map/ppermute | solution.py:294
  159.8 1.6 copy-start
  161.4 0.9 copy-start.2
  165.6 18.5 %all-to-all-start.1 = ((f32[16,32,128]{2,1,0:T(8,128)}), f32[16,32,128]{2,1,0:T(8,128)S(1)}, u32[]{:S(2)}, u32[]{:S(2)}) async-start(f32[16,32,128]{2,1,0:T(8,128)} %get-tuple-element.64), calls=%async_computation.1 | async-start | bytes 524288 | tf_op jit(solution)/shard_map/all_to_all | solution.py:302
Sparse Core Ops, SparseCore 0:
  32.3 56.1 all-gather.5
  104.6 47.5 all-gather.7

commit v12 on v11

--- a/solution.py
+++ b/solution.py
@@ -146,11 +146,9 @@
     first = Fetch([a0_ref], [start], start_sems)
     order = (4, 1, 6, 2, 5, 3)
     part = fetch_parts(whole_ref, order, rows, buf, sems)
-    total, factor = first(0), part(0)
+    total = first(0)
     for k in range(len(order)):
-        after = part(k + 1) if k + 1 < len(order) else None
-        total = dot(split(total), factor)
-        factor = after
+        total = dot(split(total), part(k))
     drows_ref[...] = total
 
 
@@ -164,16 +162,17 @@
     b0, e0, b1, e1, b2, e2, b3, e3 = (vec_ref[i : i + 1] for i in range(8))
     u1, u2, u3, u4 = (u_ref[i : i + 1] for i in range(4))
 
-    a0, m0, a1 = part(0), part(1), part(2)
+    a0, m0 = part(0), part(1)
     both = dot(joined(a0, sixteen(e0 - u2)), m0)
-    a2, m0p = part(3), part(4)
     p0, mixed = store(split(both[:width])), both[width:]
+    a1 = part(2)
     both = dot(joined(p0, j0, mixed), a1)
-    a3 = part(5)
     bw = store(split(both[:width]))
     y0, e_t = both[width : width + rows], both[width + rows : width + rows + 1] + e1
+    a2, m0p = part(3), part(4)
     both = dot(joined(a2, sixteen(e2 - u4)), m0p)
     p0p, mixed = store(split(both[:width])), both[width:]
+    a3 = part(5)
     both = dot(joined(p0p, j2, mixed), a3)
     bp = store(split(both[:width]))
     y2, e_p = both[width : width + rows], both[width + rows : width + rows + 1] + e3
@@ -237,27 +236,34 @@
 
 
 def third_kernel(
-    rows, place_ref, prior_ref, state_ref, drows_ref, second_ref, d_ref, packed_ref, p2rows_ref, new_a_ref,
-    row_ref, earlier_ref, buf, sems, pairs, pair_sems, out, outs
+    rows, state_ref, drows_ref, second_ref, z_ref, own_ref, p2rows_ref, new_a_ref, m2_ref, earlier_ref, buf, sems
 ):
     part = fetch_parts(second_ref, (1, 0), rows, buf, sems)
-    store = Store((earlier_ref,), out, outs)
-    pair = fetch_pairs((d_ref,), pairs, pair_sems)
+    own_ref[...] = state_ref[...]
     e_row = state_ref[2 * rows + 1 : 2 * rows + 2]
-    m2, d, earlier = part(0), pair(0), store(part(1))
-    v = dot_nt(split(prior_ref[:rows]), m2)
+    m2 = part(0)
+    m2_ref[0], m2_ref[1] = m2
     both = dot(split(stacked(state_ref[rows : 2 * rows], drows_ref[...], sixteen(e_row))), m2)
     p2rows_ref[...] = both[rows : 2 * rows]
-    v = dot_nt(split(v), d)
+    earlier = part(1)
+    earlier_ref[0], earlier_ref[1] = earlier
     both = dot(split(both), earlier)
     new_a_ref[...] = both[rows : 2 * rows]
+    z_ref[:rows] = both[:rows]
+    z_ref[rows:] = both[2 * rows : 2 * rows + 8]
+
+
+def fourth_kernel(rows, place_ref, prior_ref, own_ref, z_ref, m2_ref, d_ref, packed_ref, row_ref, pairs, pair_sems):
+    pair = fetch_pairs((d_ref,), pairs, pair_sems)
+    v = dot_nt(split(prior_ref[:rows]), (m2_ref[0], m2_ref[1]))
     active = place_ref[0] >= 4
-    j = jnp.where(active, prior_ref[rows : 2 * rows], state_ref[rows : 2 * rows])
-    pack((v, state_ref[:rows], both[:rows], j), packed_ref, rows)
+    j = jnp.where(active, prior_ref[rows : 2 * rows], own_ref[rows : 2 * rows])
     prior_b, prior_e = prior_ref[2 * rows : 2 * rows + 1], prior_ref[2 * rows + 1 : 2 * rows + 2]
-    e_before = jnp.where(active, both[2 * rows : 2 * rows + 1] + prior_e, e_row)
-    row_ref[...] = sixteen(e_row, prior_b, state_ref[2 * rows : 2 * rows + 1], e_before)[:8]
-    store.finish()
+    own_b, own_e = own_ref[2 * rows : 2 * rows + 1], own_ref[2 * rows + 1 : 2 * rows + 2]
+    e_before = jnp.where(active, z_ref[rows : rows + 1] + prior_e, own_e)
+    row_ref[...] = sixteen(own_e, prior_b, own_b, e_before)[:8]
+    v = dot_nt(split(v), pair(0))
+    pack((v, own_ref[:rows], z_ref[:rows], j), packed_ref, rows)
 
 
 def last_kernel(
@@ -408,16 +414,27 @@
     )
 
     prior = passed_along(state, 4)
-    packed, p2rows, new_a, lines, earlier = call(
+    z, own, p2rows, new_a, m2, earlier = call(
         third_kernel,
         rows,
-        (place, prior, state, drows, second, d),
-        [((peers, rows, 4 * rows), F32), flat(), flat(), ((8, width), F32), pair],
-        {4, 5},
-        {4},
-        stage(2) + pairs(1) + pairs(1),
+        (state, drows, second),
+        [flat(8), flat(rows + 8), flat(), flat(), pair, pair],
+        {2},
+        (),
+        stage(2),
         flops=mults,
         grant=40,
+    )
+    packed, lines = call(
+        fourth_kernel,
+        rows,
+        (place, prior, own, z, m2, d),
+        [((peers, rows, 4 * rows), F32), ((8, width), F32)],
+        {5},
+        (),
+        pairs(1),
+        flops=mults,
+        grant=36,
         small=(0,),
     )
     back = exchanged(packed)

time: 195 us -> 191 us (0.979)
  waiting for transfers between devices: 54.2 us -> 47.7 us
  starting transfers between devices: 43.6 us -> 47.1 us
    ppermute x8, waiting for transfers between devices: 33.2 us -> 27 us  [passed_along(): lax.ppermute(shard, 'tm', [(i, i + by) for i in range(peers) if 0 <= i +...]
    ppermute x8, starting transfers between devices: 31.3 us -> 33.6 us  [passed_along(): lax.ppermute(shard, 'tm', [(i, i + by) for i in range(peers) if 0 <= i +...]
    pallas_call x9 -> x10, Pallas kernels: 39.5 us -> 37.6 us  [call(): pl.pallas_call(functools.partial(kernel, rows), out_shape=[jax.ShapeDtype...]
where the time goes in v12:
time: 191 us; the launch traced here: 189 us
  waiting for transfers between devices  47.7 us (25%)
  starting transfers between devices  47.1 us (25%)
  Pallas kernels  37.6 us (20%)
  blocking collectives  26.3 us (14%)
  between operations  14.3 us (7%)
  local copies, waits for them, and re-layouts  8.52 us (4%)
  other arithmetic  6.93 us (4%)
    pallas_call x10, Pallas kernels, call(): pl.pallas_call(functools.partial(kernel, rows), out_shape=[jax.ShapeDtype...  37.6 us
    ppermute x8, starting transfers between devices, passed_along(): lax.ppermute(shard, 'tm', [(i, i + by) for i in range(peers) if 0 <= i +...  33.6 us
    ppermute x8, waiting for transfers between devices, passed_along(): lax.ppermute(shard, 'tm', [(i, i + by) for i in range(peers) if 0 <= i +...  27 us
    all_gather x1, blocking collectives, gathered(): return lax.all_gather(shard, 'panel', axis=0, tiled=False)  26.3 us
    all_to_all x2, waiting for transfers between devices, exchanged(): lax.all_to_all(packed, 'panel', split_axis=0, concat_axis=0, tiled=True)  18.9 us
    all_to_all x2, starting transfers between devices, exchanged(): lax.all_to_all(packed, 'panel', split_axis=0, concat_axis=0, tiled=True)  13.4 us
    unnamed x21, local copies, waits for them, and re-layouts  5.23 us
  transfers between devices with their start and end apart: 12, of which 9 were waited for; matrix products, arithmetic and copies ran while one was open for 5% of the time, Pallas kernels for 14%

profile of v12, /device:TPU:7, one launch (start us, length us, event | category | flops | bytes accessed | tf_op | source)
XLA Modules:
  0.0 188.5 jit_solution(3463158191774707977)
XLA Ops:
  7.2 3.2 %collective-permute-start = (f32[32,512]{1,0:T(8,128)}, f32[32,512]{1,0:T(8,128)S(1)}, u32[]{:S(2)}, u32[]{:S(2)}) collective-permute-start(f32[32,512]{1,0:T(8,128)} %a0_ref.3), channel_id=1, source_target_pairs={{0,16},{16,32},{32,48},{48,64},{64,80},{80,96},{96,112},{112,128},... | collective-permute-start | bytes 196616 | tf_op jit(solution)/shard_map/ppermute | solution.py:300
  10.4 6.4 %collective-permute-start.2 = (f32[32,512]{1,0:T(8,128)}, f32[32,512]{1,0:T(8,128)S(1)}, u32[]{:S(2)}, u32[]{:S(2)}) collective-permute-start(f32[32,512]{1,0:T(8,128)} %a0_ref.3), channel_id=1, source_target_pairs={{0,48},{16,64},{32,80},{48,96},{64,112},{80,128},{96,144},{112,160... | collective-permute-start | bytes 196616 | tf_op jit(solution)/shard_map/ppermute | solution.py:300
  16.9 0.8 slice_bitcast_fusion
  17.7 0.8 pad_maximum_fusion.1
  18.6 2.4 %collective-permute-start.1 = (f32[64,512]{1,0:T(8,128)S(1)}, f32[64,512]{1,0:T(8,128)S(1)}, u32[]{:S(2)}, u32[]{:S(2)}) collective-permute-start(f32[64,512]{1,0:T(8,128)S(1)} %pad_maximum_fusion.1), channel_id=1, source_target_pairs={{0,32},{16,48},{32,64},{48,80},{64,96},{80,112},{96,128},{112,144}... | collective-permute-start | bytes 393224 | tf_op jit(solution)/shard_map/ppermute | solution.py:300
  21.0 0.7 select_maximum_fusion
  21.8 0.8 copy-done
  22.6 0.9 copy-done.1
  23.5 0.6 shard_map.101
  24.1 0.9 pad_maximum_fusion
  25.0 5.8 %collective-permute-done.1.late_ref = f32[64,512]{1,0:T(8,128)S(1)} collective-permute-done((f32[64,512]{1,0:T(8,128)S(1)}, f32[64,512]{1,0:T(8,128)S(1)}, u32[]{:S(2)}, u32[]{:S(2)}) %collective-permute-start.1) | collective-permute-done | bytes 131104 | tf_op jit(solution)/shard_map/ppermute | solution.py:300
  30.8 1.4 shard_map.102
  32.2 1.9 %collective-permute-start.3 = (f32[72,512]{1,0:T(8,128)S(1)}, f32[72,512]{1,0:T(8,128)S(1)}, u32[]{:S(2)}, u32[]{:S(2)}) collective-permute-start(f32[72,512]{1,0:T(8,128)S(1)} %pad_maximum_fusion), channel_id=1, source_target_pairs={{0,16},{16,32},{32,48},{48,64},{64,80},{80,96},{96,112},{112,128},... | collective-permute-start | bytes 442376 | tf_op jit(solution)/shard_map/ppermute | solution.py:300
  34.2 1.9 %collective-permute-start.4 = (f32[72,512]{1,0:T(8,128)S(1)}, f32[72,512]{1,0:T(8,128)S(1)}, u32[]{:S(2)}, u32[]{:S(2)}) collective-permute-start(f32[72,512]{1,0:T(8,128)S(1)} %pad_maximum_fusion), channel_id=1, source_target_pairs={{0,32},{16,48},{32,64},{48,80},{64,96},{80,112},{96,128},{112,144}... | collective-permute-start | bytes 442376 | tf_op jit(solution)/shard_map/ppermute | solution.py:300
  36.1 2.8 %collective-permute-start.5 = (f32[72,512]{1,0:T(8,128)S(1)}, f32[72,512]{1,0:T(8,128)S(1)}, u32[]{:S(2)}, u32[]{:S(2)}) collective-permute-start(f32[72,512]{1,0:T(8,128)S(1)} %pad_maximum_fusion), channel_id=1, source_target_pairs={{0,48},{16,64},{32,80},{48,96},{64,112},{80,128},{96,144},{112,160... | collective-permute-start | bytes 442376 | tf_op jit(solution)/shard_map/ppermute | solution.py:300
  38.9 1.3 collective-permute-done.3
  40.2 4.3 %collective-permute-done.4 = f32[72,512]{1,0:T(8,128)S(1)} collective-permute-done((f32[72,512]{1,0:T(8,128)S(1)}, f32[72,512]{1,0:T(8,128)S(1)}, u32[]{:S(2)}, u32[]{:S(2)}) %collective-permute-start.4) | collective-permute-done | bytes 147488 | tf_op jit(solution)/shard_map/ppermute | solution.py:300
  44.6 11.5 %collective-permute-done.5 = f32[72,512]{1,0:T(8,128)S(1)} collective-permute-done((f32[72,512]{1,0:T(8,128)S(1)}, f32[72,512]{1,0:T(8,128)S(1)}, u32[]{:S(2)}, u32[]{:S(2)}) %collective-permute-start.5) | collective-permute-done | bytes 147488 | tf_op jit(solution)/shard_map/ppermute | solution.py:300
  56.1 0.7 concatenate.24
  57.0 0.9 constant_dynamic-update-slice_fusion
  58.0 0.7 slice_dynamic-update-slice_fusion
  58.8 26.3 %all-gather.1 = f32[128,512]{1,0:T(8,128)S(1)} all-gather(f32[8,512]{1,0:T(8,128)S(1)} %concatenate.25), channel_id=3, replica_groups=mesh['tm'=32,'panel'=16] {'panel'}, dimensions={0}, use_global_device_ids=true | all-gather | bytes 278528 | tf_op jit(solution)/shard_map/all_gather | solution.py:304
  85.3 0.7 reshape.27.vec_ref
  86.0 0.6 slice_reduce_fusion.u_ref
  86.6 1.9 all-gather.6.cloned.1.call-done
  88.5 4.9 %shard_map.107.drows_ref = f32[32,512]{1,0:T(8,128)} custom-call(f32[16,224,512]{2,1,0:T(8,128)} %bitcast.25, f32[32,512]{1,0:T(8,128)} %a0_ref.3), custom_call_target="tpu_custom_call" | custom-call | flops 805306368 | bytes 7405568 | tf_op jit(solution)/shard_map/pallas_call | solution.py:287
  93.4 7.1 %collective-permute-start.6 = (f32[32,512]{1,0:T(8,128)}, f32[32,512]{1,0:T(8,128)S(1)}, u32[]{:S(2)}, u32[]{:S(2)}) collective-permute-start(f32[32,512]{1,0:T(8,128)} %shard_map.107.drows_ref), channel_id=1, source_target_pairs={{0,64},{16,80},{32,96},{48,112},{64,128},{80,144},{96,160},{112,17... | collective-permute-start | bytes 196616 | tf_op jit(solution)/shard_map/ppermute | solution.py:300
  100.5 3.0 %collective-permute-done.6 = f32[32,512]{1,0:T(8,128)S(1)} collective-permute-done((f32[32,512]{1,0:T(8,128)}, f32[32,512]{1,0:T(8,128)S(1)}, u32[]{:S(2)}, u32[]{:S(2)}) %collective-permute-start.6) | collective-permute-done | bytes 65568 | tf_op jit(solution)/shard_map/ppermute | solution.py:300
  103.5 0.7 pad_maximum_fusion.3
  104.2 10.1 %shard_map.103 = (f32[16,32,256]{2,1,0:T(8,128)}, f32[8,512]{1,0:T(8,128)}, bf16[2,512,512]{2,1,0:T(8,128)(2,1)}, bf16[2,512,512]{2,1,0:T(8,128)(2,1)}, bf16[2,5...) custom-call(f32[16,224,512]{2,1,0:T(8,128)} %bitcast.26, f32[192,512]{1,0:T(8,128)} %copy-done.8, ...), custom_call_target="tpu_custom_call" | custom-call | flops 4831838208 | bytes 7757824 | tf_op jit(solution)/shard_map/pallas_call | solution.py:287
  114.3 5.4 %all-to-all-start = ((f32[16,32,256]{2,1,0:T(8,128)}), f32[16,32,256]{2,1,0:T(8,128)S(1)}, u32[]{:S(2)}, u32[]{:S(2)}) async-start(f32[16,32,256]{2,1,0:T(8,128)} %get-tuple-element.54), calls=%async_computation | async-start | bytes 1048576 | tf_op jit(solution)/shard_map/all_to_all | solution.py:308
  119.7 0.7 pad_maximum_fusion.2.own_ref
  120.4 4.7 %shard_map.105 = (bf16[2,512,512]{2,1,0:T(8,128)(2,1)}, bf16[2,512,512]{2,1,0:T(8,128)(2,1)}) custom-call(f32[16,224,512]{2,1,0:T(8,128)} %bitcast.27, bf16[2,512,512]{2,1,0:T(8,128)(2,1)} %get-tuple-element.61.bw_ref, bf16[2,512,512]{2,1,0:T(8,128)(2,1)} %get-tuple-element.58.bp_ref), custom_call_target="tpu_custom_call" | custom-call | flops 1610612736 | bytes 9437184 | tf_op jit(solution)/shard_map/pallas_call | solution.py:287
  125.1 6.1 %shard_map.104 = (bf16[2,512,512]{2,1,0:T(8,128)(2,1)}, bf16[2,512,512]{2,1,0:T(8,128)(2,1)}, bf16[2,512,512]{2,1,0:T(8,128)(2,1)}) custom-call(f32[16,224,512]{2,1,0:T(8,128)} %bitcast.28, bf16[2,512,512]{2,1,0:T(8,128)(2,1)} %get-tuple-element.58.bp_ref), custom_call_target="tpu_custom_call" | custom-call | flops 2415919104 | bytes 8388608 | tf_op jit(solution)/shard_map/pallas_call | solution.py:287
  131.2 8.0 %all-to-all-done = f32[16,32,256]{2,1,0:T(8,128)S(1)} async-done(((f32[16,32,256]{2,1,0:T(8,128)}), f32[16,32,256]{2,1,0:T(8,128)S(1)}, u32[]{:S(2)}, u32[]{:S(2)}) %all-to-all-start) | async-done | bytes 524320 | tf_op jit(solution)/shard_map/all_to_all | solution.py:308
  139.2 0.8 copy-done.6
  140.0 5.1 %shard_map.106.state_ref = f32[72,512]{1,0:T(8,128)} custom-call(f32[512,256]{1,0:T(8,128)} %bitcast.29, f32[64,512]{1,0:T(8,128)} %pad_maximum_fusion.2.own_ref, f32[8,512]{1,0:T(8,128)} %get-tuple-element.55.vec_ref, bf16[2,512,512]{2,1,0:T(8,128)(2,1)} %get-tuple-element.56.p0p_ref, bf16[2,512,512]{2,1,0:T(8,128)(2,1)} %get-tuple-element.57.p0_ref, ...), custom_call_target="tpu_custom_call" | custom-call | flops 805306368 | bytes 6963200 | tf_op jit(solution)/shard_map/pallas_call | solution.py:287
  145.1 7.8 %collective-permute-start.7 = (f32[72,512]{1,0:T(8,128)}, f32[72,512]{1,0:T(8,128)S(1)}, u32[]{:S(2)}, u32[]{:S(2)}) collective-permute-start(f32[72,512]{1,0:T(8,128)} %shard_map.106.state_ref), channel_id=1, source_target_pairs={{0,64},{16,80},{32,96},{48,112},{64,128},{80,144},{96,160},{112,17... | collective-permute-start | bytes 442376 | tf_op jit(solution)/shard_map/ppermute | solution.py:300
  152.9 0.9 copy-done.3
  153.9 1.6 copy-done.4
  155.4 0.8 shard_map.108
  156.3 1.0 collective-permute-done.7.prior_ref
  157.3 2.3 %shard_map.109 = (f32[16,32,128]{2,1,0:T(8,128)}, f32[8,512]{1,0:T(8,128)S(1)}) custom-call(s32[2]{0:T(128)S(1)} %pad_add_fusion.place_ref, f32[72,512]{1,0:T(8,128)S(1)} %collective-permute-done.7.prior_ref, f32[72,512]{1,0:T(8,128)S(1)} %get-tuple-element.66.own_ref, f32[40,512]{1,0:T(8,128)S(1)} %get-tuple-element.67.z_ref, ...), custom_call_target="tpu_custom_call" | custom-call | flops 805306368 | bytes 2473992 | tf_op jit(solution)/shard_map/pallas_call | solution.py:287
  159.6 8.0 %all-to-all-start.1 = ((f32[16,32,128]{2,1,0:T(8,128)}), f32[16,32,128]{2,1,0:T(8,128)S(1)}, u32[]{:S(2)}, u32[]{:S(2)}) async-start(f32[16,32,128]{2,1,0:T(8,128)} %get-tuple-element.70), calls=%async_computation.1 | async-start | bytes 524288 | tf_op jit(solution)/shard_map/all_to_all | solution.py:308
  167.7 0.6 broadcast_select_fusion
  168.4 10.9 %all-to-all-done.1 = f32[16,32,128]{2,1,0:T(8,128)S(1)} async-done(((f32[16,32,128]{2,1,0:T(8,128)}), f32[16,32,128]{2,1,0:T(8,128)S(1)}, u32[]{:S(2)}, u32[]{:S(2)}) %all-to-all-start.1) | async-done | bytes 262176 | tf_op jit(solution)/shard_map/all_to_all | solution.py:308
  179.3 1.7 shard_map.110
  181.0 0.7 slice_reduce_fusion.2
  (40 shorter events, 0.9 us)
Async XLA Ops:
  7.2 81.3 %all-gather.6.cloned.1.call-start = ((), (), s32[]{:S(2)}) async-start(), calls=%async_computation.2 | async-start | bytes 7798784 | tf_op jit(solution)/shard_map/all_gather | solution.py:304
  7.2 17.8 %collective-permute-start = (f32[32,512]{1,0:T(8,128)}, f32[32,512]{1,0:T(8,128)S(1)}, u32[]{:S(2)}, u32[]{:S(2)}) collective-permute-start(f32[32,512]{1,0:T(8,128)} %a0_ref.3), channel_id=1, source_target_pairs={{0,16},{16,32},{32,48},{48,64},{64,80},{80,96},{96,112},{112,128},... | collective-permute-start | bytes 196616 | tf_op jit(solution)/shard_map/ppermute | solution.py:300
  10.4 14.6 %collective-permute-start.2 = (f32[32,512]{1,0:T(8,128)}, f32[32,512]{1,0:T(8,128)S(1)}, u32[]{:S(2)}, u32[]{:S(2)}) collective-permute-start(f32[32,512]{1,0:T(8,128)} %a0_ref.3), channel_id=1, source_target_pairs={{0,48},{16,64},{32,80},{48,96},{64,112},{80,128},{96,144},{112,160... | collective-permute-start | bytes 196616 | tf_op jit(solution)/shard_map/ppermute | solution.py:300
  18.6 12.2 %collective-permute-start.1 = (f32[64,512]{1,0:T(8,128)S(1)}, f32[64,512]{1,0:T(8,128)S(1)}, u32[]{:S(2)}, u32[]{:S(2)}) collective-permute-start(f32[64,512]{1,0:T(8,128)S(1)} %pad_maximum_fusion.1), channel_id=1, source_target_pairs={{0,32},{16,48},{32,64},{48,80},{64,96},{80,112},{96,128},{112,144}... | collective-permute-start | bytes 393224 | tf_op jit(solution)/shard_map/ppermute | solution.py:300
  21.8 0.8 copy-start
  22.6 0.9 copy-start.1
  32.2 120.7 %all-gather.8.cloned.1.call-start = ((), (), s32[]{:S(2)}) async-start(), calls=%async_computation.3 | async-start | bytes 2228224 | tf_op jit(solution)/shard_map/all_gather | solution.py:304
  32.2 8.0 %collective-permute-start.3 = (f32[72,512]{1,0:T(8,128)S(1)}, f32[72,512]{1,0:T(8,128)S(1)}, u32[]{:S(2)}, u32[]{:S(2)}) collective-permute-start(f32[72,512]{1,0:T(8,128)S(1)} %pad_maximum_fusion), channel_id=1, source_target_pairs={{0,16},{16,32},{32,48},{48,64},{64,80},{80,96},{96,112},{112,128},... | collective-permute-start | bytes 442376 | tf_op jit(solution)/shard_map/ppermute | solution.py:300
  34.2 10.4 %collective-permute-start.4 = (f32[72,512]{1,0:T(8,128)S(1)}, f32[72,512]{1,0:T(8,128)S(1)}, u32[]{:S(2)}, u32[]{:S(2)}) collective-permute-start(f32[72,512]{1,0:T(8,128)S(1)} %pad_maximum_fusion), channel_id=1, source_target_pairs={{0,32},{16,48},{32,64},{48,80},{64,96},{80,112},{96,128},{112,144}... | collective-permute-start | bytes 442376 | tf_op jit(solution)/shard_map/ppermute | solution.py:300
  36.1 20.0 %collective-permute-start.5 = (f32[72,512]{1,0:T(8,128)S(1)}, f32[72,512]{1,0:T(8,128)S(1)}, u32[]{:S(2)}, u32[]{:S(2)}) collective-permute-start(f32[72,512]{1,0:T(8,128)S(1)} %pad_maximum_fusion), channel_id=1, source_target_pairs={{0,48},{16,64},{32,80},{48,96},{64,112},{80,128},{96,144},{112,160... | collective-permute-start | bytes 442376 | tf_op jit(solution)/shard_map/ppermute | solution.py:300
  58.8 45.4 %copy-start.8 = (f32[192,512]{1,0:T(8,128)}, f32[192,512]{1,0:T(8,128)S(1)}, u32[]{:S(2)}) copy-start(f32[192,512]{1,0:T(8,128)S(1)} %get-tuple-element.82.own_ref) | copy-start | bytes 1179652
  93.4 10.1 %collective-permute-start.6 = (f32[32,512]{1,0:T(8,128)}, f32[32,512]{1,0:T(8,128)S(1)}, u32[]{:S(2)}, u32[]{:S(2)}) collective-permute-start(f32[32,512]{1,0:T(8,128)} %shard_map.107.drows_ref), channel_id=1, source_target_pairs={{0,64},{16,80},{32,96},{48,112},{64,128},{80,144},{96,160},{112,17... | collective-permute-start | bytes 196616 | tf_op jit(solution)/shard_map/ppermute | solution.py:300
  104.2 15.5 %copy-start.7 = (f32[32,512]{1,0:T(8,128)S(1)}, f32[32,512]{1,0:T(8,128)}, u32[]{:S(2)}) copy-start(f32[32,512]{1,0:T(8,128)} %param.8) | copy-start | bytes 196612
  114.3 24.9 %all-to-all-start = ((f32[16,32,256]{2,1,0:T(8,128)}), f32[16,32,256]{2,1,0:T(8,128)S(1)}, u32[]{:S(2)}, u32[]{:S(2)}) async-start(f32[16,32,256]{2,1,0:T(8,128)} %get-tuple-element.54), calls=%async_computation | async-start | bytes 1048576 | tf_op jit(solution)/shard_map/all_to_all | solution.py:308
  125.1 27.9 %copy-start.2 = (f32[32,512]{1,0:T(8,128)S(1)}, f32[32,512]{1,0:T(8,128)}, u32[]{:S(2)}) copy-start(f32[32,512]{1,0:T(8,128)} %shard_map.107.drows_ref) | copy-start | bytes 196612
  125.1 32.2 %copy-start.5 = (bf16[2,512,512]{2,1,0:T(8,128)(2,1)S(1)}, bf16[2,512,512]{2,1,0:T(8,128)(2,1)}, u32[]{:S(2)}) copy-start(bf16[2,512,512]{2,1,0:T(8,128)(2,1)} %get-tuple-element.69.d_ref) | copy-start | bytes 3145732
  139.1 0.8 copy-start.6
  145.1 12.2 %collective-permute-start.7 = (f32[72,512]{1,0:T(8,128)}, f32[72,512]{1,0:T(8,128)S(1)}, u32[]{:S(2)}, u32[]{:S(2)}) collective-permute-start(f32[72,512]{1,0:T(8,128)} %shard_map.106.state_ref), channel_id=1, source_target_pairs={{0,64},{16,80},{32,96},{48,112},{64,128},{80,144},{96,160},{112,17... | collective-permute-start | bytes 442376 | tf_op jit(solution)/shard_map/ppermute | solution.py:300
  152.9 0.9 copy-start.3
  153.9 1.6 copy-start.4
  159.6 19.7 %all-to-all-start.1 = ((f32[16,32,128]{2,1,0:T(8,128)}), f32[16,32,128]{2,1,0:T(8,128)S(1)}, u32[]{:S(2)}, u32[]{:S(2)}) async-start(f32[16,32,128]{2,1,0:T(8,128)} %get-tuple-element.70), calls=%async_computation.1 | async-start | bytes 524288 | tf_op jit(solution)/shard_map/all_to_all | solution.py:308
Sparse Core Ops, SparseCore 0:
  32.3 56.1 all-gather.5
  104.3 47.0 all-gather.7

commit v13 on v12

--- a/solution.py
+++ b/solution.py
@@ -177,12 +177,11 @@
     bp = store(split(both[:width]))
     y2, e_p = both[width : width + rows], both[width + rows : width + rows + 1] + e3
     b_p = dot_nt(split(sixteen(b3 + u3)), p0p)[:1] + b2
-    w1 = rowwise(c3, dot(split(sixteen(e_t)), a2)[:1])
-    w2 = rowwise(c2, e_t)
-    w3 = rowwise(j0, dot_nt(split(sixteen(b_p)), a1)[:1])
-    w4 = rowwise(j1, b_p)
+    x3 = dot_nt(split(c3), a2)
+    w1, w2 = rowwise(x3, e_t), rowwise(c2, e_t)
+    w3, w4 = rowwise(y0, b_p), rowwise(j1, b_p)
     x1 = dot_nt(split(c1), a0)
-    right = dot_nt(split(stacked(dot_nt(split(c3), a2), c2)), bw)
+    right = dot_nt(split(stacked(x3, c2)), bw)
     x3, x2 = right[:rows], right[rows:]
     right = dot(split(stacked(y0, j1)), bp)
     y0, y1 = right[:rows], right[rows:]

time: 191 us -> 190 us (level)
  waiting for transfers between devices: 47.7 us -> 51.3 us
  starting transfers between devices: 47.1 us -> 43.9 us
    ppermute x8, waiting for transfers between devices: 27 us -> 29.4 us  [passed_along(): lax.ppermute(shard, 'tm', [(i, i + by) for i in range(peers) if 0 <= i +...]
    all_to_all x2, starting transfers between devices: 13.4 us -> 11.1 us  [exchanged(): lax.all_to_all(packed, 'panel', split_axis=0, concat_axis=0, tiled=True)]
where the time goes in v13:
time: 190 us; the launch traced here: 188 us
  waiting for transfers between devices  51.3 us (27%)
  starting transfers between devices  43.9 us (23%)
  Pallas kernels  37.1 us (20%)
  blocking collectives  26.3 us (14%)
  between operations  14.3 us (8%)
  local copies, waits for them, and re-layouts  8.52 us (4%)
  other arithmetic  6.93 us (4%)
    pallas_call x10, Pallas kernels, call(): pl.pallas_call(functools.partial(kernel, rows), out_shape=[jax.ShapeDtype...  37.1 us
    ppermute x8, starting transfers between devices, passed_along(): lax.ppermute(shard, 'tm', [(i, i + by) for i in range(peers) if 0 <= i +...  32.7 us
    ppermute x8, waiting for transfers between devices, passed_along(): lax.ppermute(shard, 'tm', [(i, i + by) for i in range(peers) if 0 <= i +...  29.4 us
    all_gather x1, blocking collectives, gathered(): return lax.all_gather(shard, 'panel', axis=0, tiled=False)  26.3 us
    all_to_all x2, waiting for transfers between devices, exchanged(): lax.all_to_all(packed, 'panel', split_axis=0, concat_axis=0, tiled=True)  20 us
    all_to_all x2, starting transfers between devices, exchanged(): lax.all_to_all(packed, 'panel', split_axis=0, concat_axis=0, tiled=True)  11.1 us
    unnamed x21, local copies, waits for them, and re-layouts  5.23 us
  transfers between devices with their start and end apart: 12, of which 9 were waited for; matrix products, arithmetic and copies ran while one was open for 5% of the time, Pallas kernels for 14%

profile of v13, /device:TPU:7, one launch (start us, length us, event | category | flops | bytes accessed | tf_op | source)
XLA Modules:
  0.0 188.3 jit_solution(15307494170547162058)
XLA Ops:
  7.2 3.2 %collective-permute-start = (f32[32,512]{1,0:T(8,128)}, f32[32,512]{1,0:T(8,128)S(1)}, u32[]{:S(2)}, u32[]{:S(2)}) collective-permute-start(f32[32,512]{1,0:T(8,128)} %a0_ref.3), channel_id=1, source_target_pairs={{0,16},{16,32},{32,48},{48,64},{64,80},{80,96},{96,112},{112,128},... | collective-permute-start | bytes 196616 | tf_op jit(solution)/shard_map/ppermute | solution.py:299
  10.4 6.4 %collective-permute-start.2 = (f32[32,512]{1,0:T(8,128)}, f32[32,512]{1,0:T(8,128)S(1)}, u32[]{:S(2)}, u32[]{:S(2)}) collective-permute-start(f32[32,512]{1,0:T(8,128)} %a0_ref.3), channel_id=1, source_target_pairs={{0,48},{16,64},{32,80},{48,96},{64,112},{80,128},{96,144},{112,160... | collective-permute-start | bytes 196616 | tf_op jit(solution)/shard_map/ppermute | solution.py:299
  16.9 0.8 slice_bitcast_fusion
  17.7 0.8 pad_maximum_fusion.1
  18.6 2.4 %collective-permute-start.1 = (f32[64,512]{1,0:T(8,128)S(1)}, f32[64,512]{1,0:T(8,128)S(1)}, u32[]{:S(2)}, u32[]{:S(2)}) collective-permute-start(f32[64,512]{1,0:T(8,128)S(1)} %pad_maximum_fusion.1), channel_id=1, source_target_pairs={{0,32},{16,48},{32,64},{48,80},{64,96},{80,112},{96,128},{112,144}... | collective-permute-start | bytes 393224 | tf_op jit(solution)/shard_map/ppermute | solution.py:299
  21.0 0.7 select_maximum_fusion
  21.8 0.8 copy-done
  22.6 0.9 copy-done.1
  23.5 0.6 shard_map.101
  24.1 0.9 pad_maximum_fusion
  25.0 5.8 %collective-permute-done.1.late_ref = f32[64,512]{1,0:T(8,128)S(1)} collective-permute-done((f32[64,512]{1,0:T(8,128)S(1)}, f32[64,512]{1,0:T(8,128)S(1)}, u32[]{:S(2)}, u32[]{:S(2)}) %collective-permute-start.1) | collective-permute-done | bytes 131104 | tf_op jit(solution)/shard_map/ppermute | solution.py:299
  30.8 1.4 shard_map.102
  32.2 1.9 %collective-permute-start.3 = (f32[72,512]{1,0:T(8,128)S(1)}, f32[72,512]{1,0:T(8,128)S(1)}, u32[]{:S(2)}, u32[]{:S(2)}) collective-permute-start(f32[72,512]{1,0:T(8,128)S(1)} %pad_maximum_fusion), channel_id=1, source_target_pairs={{0,16},{16,32},{32,48},{48,64},{64,80},{80,96},{96,112},{112,128},... | collective-permute-start | bytes 442376 | tf_op jit(solution)/shard_map/ppermute | solution.py:299
  34.2 1.9 %collective-permute-start.4 = (f32[72,512]{1,0:T(8,128)S(1)}, f32[72,512]{1,0:T(8,128)S(1)}, u32[]{:S(2)}, u32[]{:S(2)}) collective-permute-start(f32[72,512]{1,0:T(8,128)S(1)} %pad_maximum_fusion), channel_id=1, source_target_pairs={{0,32},{16,48},{32,64},{48,80},{64,96},{80,112},{96,128},{112,144}... | collective-permute-start | bytes 442376 | tf_op jit(solution)/shard_map/ppermute | solution.py:299
  36.1 2.8 %collective-permute-start.5 = (f32[72,512]{1,0:T(8,128)S(1)}, f32[72,512]{1,0:T(8,128)S(1)}, u32[]{:S(2)}, u32[]{:S(2)}) collective-permute-start(f32[72,512]{1,0:T(8,128)S(1)} %pad_maximum_fusion), channel_id=1, source_target_pairs={{0,48},{16,64},{32,80},{48,96},{64,112},{80,128},{96,144},{112,160... | collective-permute-start | bytes 442376 | tf_op jit(solution)/shard_map/ppermute | solution.py:299
  38.9 1.3 collective-permute-done.3
  40.2 4.3 %collective-permute-done.4 = f32[72,512]{1,0:T(8,128)S(1)} collective-permute-done((f32[72,512]{1,0:T(8,128)S(1)}, f32[72,512]{1,0:T(8,128)S(1)}, u32[]{:S(2)}, u32[]{:S(2)}) %collective-permute-start.4) | collective-permute-done | bytes 147488 | tf_op jit(solution)/shard_map/ppermute | solution.py:299
  44.6 11.5 %collective-permute-done.5 = f32[72,512]{1,0:T(8,128)S(1)} collective-permute-done((f32[72,512]{1,0:T(8,128)S(1)}, f32[72,512]{1,0:T(8,128)S(1)}, u32[]{:S(2)}, u32[]{:S(2)}) %collective-permute-start.5) | collective-permute-done | bytes 147488 | tf_op jit(solution)/shard_map/ppermute | solution.py:299
  56.1 0.7 concatenate.24
  57.0 0.9 constant_dynamic-update-slice_fusion
  58.0 0.7 slice_dynamic-update-slice_fusion
  58.8 26.3 %all-gather.1 = f32[128,512]{1,0:T(8,128)S(1)} all-gather(f32[8,512]{1,0:T(8,128)S(1)} %concatenate.25), channel_id=3, replica_groups=mesh['tm'=32,'panel'=16] {'panel'}, dimensions={0}, use_global_device_ids=true | all-gather | bytes 278528 | tf_op jit(solution)/shard_map/all_gather | solution.py:303
  85.3 0.7 reshape.27.vec_ref
  86.0 0.6 slice_reduce_fusion.u_ref
  86.6 1.9 all-gather.6.cloned.1.call-done
  88.5 4.9 %shard_map.107.drows_ref = f32[32,512]{1,0:T(8,128)} custom-call(f32[16,224,512]{2,1,0:T(8,128)} %bitcast.25, f32[32,512]{1,0:T(8,128)} %a0_ref.3), custom_call_target="tpu_custom_call" | custom-call | flops 805306368 | bytes 7405568 | tf_op jit(solution)/shard_map/pallas_call | solution.py:286
  93.4 7.1 %collective-permute-start.6 = (f32[32,512]{1,0:T(8,128)}, f32[32,512]{1,0:T(8,128)S(1)}, u32[]{:S(2)}, u32[]{:S(2)}) collective-permute-start(f32[32,512]{1,0:T(8,128)} %shard_map.107.drows_ref), channel_id=1, source_target_pairs={{0,64},{16,80},{32,96},{48,112},{64,128},{80,144},{96,160},{112,17... | collective-permute-start | bytes 196616 | tf_op jit(solution)/shard_map/ppermute | solution.py:299
  100.5 3.0 %collective-permute-done.6 = f32[32,512]{1,0:T(8,128)S(1)} collective-permute-done((f32[32,512]{1,0:T(8,128)}, f32[32,512]{1,0:T(8,128)S(1)}, u32[]{:S(2)}, u32[]{:S(2)}) %collective-permute-start.6) | collective-permute-done | bytes 65568 | tf_op jit(solution)/shard_map/ppermute | solution.py:299
  103.5 0.7 pad_maximum_fusion.3
  104.2 9.6 %shard_map.103 = (f32[16,32,256]{2,1,0:T(8,128)}, f32[8,512]{1,0:T(8,128)}, bf16[2,512,512]{2,1,0:T(8,128)(2,1)}, bf16[2,512,512]{2,1,0:T(8,128)(2,1)}, bf16[2,5...) custom-call(f32[16,224,512]{2,1,0:T(8,128)} %bitcast.26, f32[192,512]{1,0:T(8,128)} %copy-done.8, ...), custom_call_target="tpu_custom_call" | custom-call | flops 4831838208 | bytes 7757824 | tf_op jit(solution)/shard_map/pallas_call | solution.py:286
  113.8 5.4 %all-to-all-start = ((f32[16,32,256]{2,1,0:T(8,128)}), f32[16,32,256]{2,1,0:T(8,128)S(1)}, u32[]{:S(2)}, u32[]{:S(2)}) async-start(f32[16,32,256]{2,1,0:T(8,128)} %get-tuple-element.54), calls=%async_computation | async-start | bytes 1048576 | tf_op jit(solution)/shard_map/all_to_all | solution.py:307
  119.2 0.7 pad_maximum_fusion.2.own_ref
  119.9 4.7 %shard_map.105 = (bf16[2,512,512]{2,1,0:T(8,128)(2,1)}, bf16[2,512,512]{2,1,0:T(8,128)(2,1)}) custom-call(f32[16,224,512]{2,1,0:T(8,128)} %bitcast.27, bf16[2,512,512]{2,1,0:T(8,128)(2,1)} %get-tuple-element.61.bw_ref, bf16[2,512,512]{2,1,0:T(8,128)(2,1)} %get-tuple-element.58.bp_ref), custom_call_target="tpu_custom_call" | custom-call | flops 1610612736 | bytes 9437184 | tf_op jit(solution)/shard_map/pallas_call | solution.py:286
  124.6 6.1 %shard_map.104 = (bf16[2,512,512]{2,1,0:T(8,128)(2,1)}, bf16[2,512,512]{2,1,0:T(8,128)(2,1)}, bf16[2,512,512]{2,1,0:T(8,128)(2,1)}) custom-call(f32[16,224,512]{2,1,0:T(8,128)} %bitcast.28, bf16[2,512,512]{2,1,0:T(8,128)(2,1)} %get-tuple-element.58.bp_ref), custom_call_target="tpu_custom_call" | custom-call | flops 2415919104 | bytes 8388608 | tf_op jit(solution)/shard_map/pallas_call | solution.py:286
  130.7 9.1 %all-to-all-done = f32[16,32,256]{2,1,0:T(8,128)S(1)} async-done(((f32[16,32,256]{2,1,0:T(8,128)}), f32[16,32,256]{2,1,0:T(8,128)S(1)}, u32[]{:S(2)}, u32[]{:S(2)}) %all-to-all-start) | async-done | bytes 524320 | tf_op jit(solution)/shard_map/all_to_all | solution.py:307
  139.8 0.8 copy-done.6
  140.6 5.1 %shard_map.106.state_ref = f32[72,512]{1,0:T(8,128)} custom-call(f32[512,256]{1,0:T(8,128)} %bitcast.29, f32[64,512]{1,0:T(8,128)} %pad_maximum_fusion.2.own_ref, f32[8,512]{1,0:T(8,128)} %get-tuple-element.55.vec_ref, bf16[2,512,512]{2,1,0:T(8,128)(2,1)} %get-tuple-element.56.p0p_ref, bf16[2,512,512]{2,1,0:T(8,128)(2,1)} %get-tuple-element.57.p0_ref, ...), custom_call_target="tpu_custom_call" | custom-call | flops 805306368 | bytes 6963200 | tf_op jit(solution)/shard_map/pallas_call | solution.py:286
  145.7 6.9 %collective-permute-start.7 = (f32[72,512]{1,0:T(8,128)}, f32[72,512]{1,0:T(8,128)S(1)}, u32[]{:S(2)}, u32[]{:S(2)}) collective-permute-start(f32[72,512]{1,0:T(8,128)} %shard_map.106.state_ref), channel_id=1, source_target_pairs={{0,64},{16,80},{32,96},{48,112},{64,128},{80,144},{96,160},{112,17... | collective-permute-start | bytes 442376 | tf_op jit(solution)/shard_map/ppermute | solution.py:299
  152.7 0.9 copy-done.3
  153.6 1.6 copy-done.4
  155.2 0.8 shard_map.108
  156.1 3.4 %collective-permute-done.7.prior_ref = f32[72,512]{1,0:T(8,128)S(1)} collective-permute-done((f32[72,512]{1,0:T(8,128)}, f32[72,512]{1,0:T(8,128)S(1)}, u32[]{:S(2)}, u32[]{:S(2)}) %collective-permute-start.7) | collective-permute-done | bytes 147488 | tf_op jit(solution)/shard_map/ppermute | solution.py:299
  159.5 2.3 %shard_map.109 = (f32[16,32,128]{2,1,0:T(8,128)}, f32[8,512]{1,0:T(8,128)S(1)}) custom-call(s32[2]{0:T(128)S(1)} %pad_add_fusion.place_ref, f32[72,512]{1,0:T(8,128)S(1)} %collective-permute-done.7.prior_ref, f32[72,512]{1,0:T(8,128)S(1)} %get-tuple-element.66.own_ref, f32[40,512]{1,0:T(8,128)S(1)} %get-tuple-element.67.z_ref, ...), custom_call_target="tpu_custom_call" | custom-call | flops 805306368 | bytes 2473992 | tf_op jit(solution)/shard_map/pallas_call | solution.py:286
  161.8 5.6 %all-to-all-start.1 = ((f32[16,32,128]{2,1,0:T(8,128)}), f32[16,32,128]{2,1,0:T(8,128)S(1)}, u32[]{:S(2)}, u32[]{:S(2)}) async-start(f32[16,32,128]{2,1,0:T(8,128)} %get-tuple-element.70), calls=%async_computation.1 | async-start | bytes 524288 | tf_op jit(solution)/shard_map/all_to_all | solution.py:307
  167.6 0.6 broadcast_select_fusion
  168.2 10.9 %all-to-all-done.1 = f32[16,32,128]{2,1,0:T(8,128)S(1)} async-done(((f32[16,32,128]{2,1,0:T(8,128)}), f32[16,32,128]{2,1,0:T(8,128)S(1)}, u32[]{:S(2)}, u32[]{:S(2)}) %all-to-all-start.1) | async-done | bytes 262176 | tf_op jit(solution)/shard_map/all_to_all | solution.py:307
  179.1 1.7 shard_map.110
  180.8 0.7 slice_reduce_fusion.2
  (40 shorter events, 0.9 us)
Async XLA Ops:
  7.2 81.3 %all-gather.6.cloned.1.call-start = ((), (), s32[]{:S(2)}) async-start(), calls=%async_computation.2 | async-start | bytes 7798784 | tf_op jit(solution)/shard_map/all_gather | solution.py:303
  7.2 17.8 %collective-permute-start = (f32[32,512]{1,0:T(8,128)}, f32[32,512]{1,0:T(8,128)S(1)}, u32[]{:S(2)}, u32[]{:S(2)}) collective-permute-start(f32[32,512]{1,0:T(8,128)} %a0_ref.3), channel_id=1, source_target_pairs={{0,16},{16,32},{32,48},{48,64},{64,80},{80,96},{96,112},{112,128},... | collective-permute-start | bytes 196616 | tf_op jit(solution)/shard_map/ppermute | solution.py:299
  10.4 14.6 %collective-permute-start.2 = (f32[32,512]{1,0:T(8,128)}, f32[32,512]{1,0:T(8,128)S(1)}, u32[]{:S(2)}, u32[]{:S(2)}) collective-permute-start(f32[32,512]{1,0:T(8,128)} %a0_ref.3), channel_id=1, source_target_pairs={{0,48},{16,64},{32,80},{48,96},{64,112},{80,128},{96,144},{112,160... | collective-permute-start | bytes 196616 | tf_op jit(solution)/shard_map/ppermute | solution.py:299
  18.6 12.2 %collective-permute-start.1 = (f32[64,512]{1,0:T(8,128)S(1)}, f32[64,512]{1,0:T(8,128)S(1)}, u32[]{:S(2)}, u32[]{:S(2)}) collective-permute-start(f32[64,512]{1,0:T(8,128)S(1)} %pad_maximum_fusion.1), channel_id=1, source_target_pairs={{0,32},{16,48},{32,64},{48,80},{64,96},{80,112},{96,128},{112,144}... | collective-permute-start | bytes 393224 | tf_op jit(solution)/shard_map/ppermute | solution.py:299
  21.8 0.8 copy-start
  22.6 0.9 copy-start.1
  32.2 120.5 %all-gather.8.cloned.1.call-start = ((), (), s32[]{:S(2)}) async-start(), calls=%async_computation.3 | async-start | bytes 2228224 | tf_op jit(solution)/shard_map/all_gather | solution.py:303
  32.2 8.0 %collective-permute-start.3 = (f32[72,512]{1,0:T(8,128)S(1)}, f32[72,512]{1,0:T(8,128)S(1)}, u32[]{:S(2)}, u32[]{:S(2)}) collective-permute-start(f32[72,512]{1,0:T(8,128)S(1)} %pad_maximum_fusion), channel_id=1, source_target_pairs={{0,16},{16,32},{32,48},{48,64},{64,80},{80,96},{96,112},{112,128},... | collective-permute-start | bytes 442376 | tf_op jit(solution)/shard_map/ppermute | solution.py:299
  34.2 10.4 %collective-permute-start.4 = (f32[72,512]{1,0:T(8,128)S(1)}, f32[72,512]{1,0:T(8,128)S(1)}, u32[]{:S(2)}, u32[]{:S(2)}) collective-permute-start(f32[72,512]{1,0:T(8,128)S(1)} %pad_maximum_fusion), channel_id=1, source_target_pairs={{0,32},{16,48},{32,64},{48,80},{64,96},{80,112},{96,128},{112,144}... | collective-permute-start | bytes 442376 | tf_op jit(solution)/shard_map/ppermute | solution.py:299
  36.1 20.0 %collective-permute-start.5 = (f32[72,512]{1,0:T(8,128)S(1)}, f32[72,512]{1,0:T(8,128)S(1)}, u32[]{:S(2)}, u32[]{:S(2)}) collective-permute-start(f32[72,512]{1,0:T(8,128)S(1)} %pad_maximum_fusion), channel_id=1, source_target_pairs={{0,48},{16,64},{32,80},{48,96},{64,112},{80,128},{96,144},{112,160... | collective-permute-start | bytes 442376 | tf_op jit(solution)/shard_map/ppermute | solution.py:299
  58.8 45.4 %copy-start.8 = (f32[192,512]{1,0:T(8,128)}, f32[192,512]{1,0:T(8,128)S(1)}, u32[]{:S(2)}) copy-start(f32[192,512]{1,0:T(8,128)S(1)} %get-tuple-element.82.own_ref) | copy-start | bytes 1179652
  93.4 10.1 %collective-permute-start.6 = (f32[32,512]{1,0:T(8,128)}, f32[32,512]{1,0:T(8,128)S(1)}, u32[]{:S(2)}, u32[]{:S(2)}) collective-permute-start(f32[32,512]{1,0:T(8,128)} %shard_map.107.drows_ref), channel_id=1, source_target_pairs={{0,64},{16,80},{32,96},{48,112},{64,128},{80,144},{96,160},{112,17... | collective-permute-start | bytes 196616 | tf_op jit(solution)/shard_map/ppermute | solution.py:299
  104.2 15.0 %copy-start.7 = (f32[32,512]{1,0:T(8,128)S(1)}, f32[32,512]{1,0:T(8,128)}, u32[]{:S(2)}) copy-start(f32[32,512]{1,0:T(8,128)} %param.8) | copy-start | bytes 196612
  113.8 26.0 %all-to-all-start = ((f32[16,32,256]{2,1,0:T(8,128)}), f32[16,32,256]{2,1,0:T(8,128)S(1)}, u32[]{:S(2)}, u32[]{:S(2)}) async-start(f32[16,32,256]{2,1,0:T(8,128)} %get-tuple-element.54), calls=%async_computation | async-start | bytes 1048576 | tf_op jit(solution)/shard_map/all_to_all | solution.py:307
  124.6 28.1 %copy-start.2 = (f32[32,512]{1,0:T(8,128)S(1)}, f32[32,512]{1,0:T(8,128)}, u32[]{:S(2)}) copy-start(f32[32,512]{1,0:T(8,128)} %shard_map.107.drows_ref) | copy-start | bytes 196612
  124.6 34.9 %copy-start.5 = (bf16[2,512,512]{2,1,0:T(8,128)(2,1)S(1)}, bf16[2,512,512]{2,1,0:T(8,128)(2,1)}, u32[]{:S(2)}) copy-start(bf16[2,512,512]{2,1,0:T(8,128)(2,1)} %get-tuple-element.69.d_ref) | copy-start | bytes 3145732
  139.8 0.8 copy-start.6
  145.7 13.7 %collective-permute-start.7 = (f32[72,512]{1,0:T(8,128)}, f32[72,512]{1,0:T(8,128)S(1)}, u32[]{:S(2)}, u32[]{:S(2)}) collective-permute-start(f32[72,512]{1,0:T(8,128)} %shard_map.106.state_ref), channel_id=1, source_target_pairs={{0,64},{16,80},{32,96},{48,112},{64,128},{80,144},{96,160},{112,17... | collective-permute-start | bytes 442376 | tf_op jit(solution)/shard_map/ppermute | solution.py:299
  152.7 0.9 copy-start.3
  153.6 1.6 copy-start.4
  161.8 17.3 %all-to-all-start.1 = ((f32[16,32,128]{2,1,0:T(8,128)}), f32[16,32,128]{2,1,0:T(8,128)S(1)}, u32[]{:S(2)}, u32[]{:S(2)}) async-start(f32[16,32,128]{2,1,0:T(8,128)} %get-tuple-element.70), calls=%async_computation.1 | async-start | bytes 524288 | tf_op jit(solution)/shard_map/all_to_all | solution.py:307
Sparse Core Ops, SparseCore 0:
  32.3 56.1 all-gather.5
  104.3 46.5 all-gather.7

commit v14 on v13

--- a/solution.py
+++ b/solution.py
@@ -422,7 +422,7 @@
         (),
         stage(2),
         flops=mults,
-        grant=40,
+        grant=53,
     )
     packed, lines = call(
         fourth_kernel,

time: 190 us -> 193 us (1.016)
  Pallas kernels: 37.1 us -> 39.2 us
    pallas_call x10, Pallas kernels: 37.1 us -> 39.2 us  [call(): pl.pallas_call(functools.partial(kernel, rows), out_shape=[jax.ShapeDtype...]
    unnamed x21 -> x23, local copies, waits for them, and re-layouts: 5.23 us -> 6.09 us
  transfers between devices with their start and end apart: 12 -> 12, of which waited for: 9 -> 9; matrix products, arithmetic and copies ran while one was open for 5% -> 5% of each run, Pallas kernels for 14% -> 15%
where the time goes in v14:
time: 193 us; the launch traced here: 191 us
  waiting for transfers between devices  50.8 us (26%)
  starting transfers between devices  43.9 us (23%)
  Pallas kernels  39.2 us (20%)
  blocking collectives  26.3 us (14%)
  between operations  14.3 us (7%)
  local copies, waits for them, and re-layouts  9.38 us (5%)
  other arithmetic  6.92 us (4%)
    pallas_call x10, Pallas kernels, call(): pl.pallas_call(functools.partial(kernel, rows), out_shape=[jax.ShapeDtype...  39.2 us
    ppermute x8, starting transfers between devices, passed_along(): lax.ppermute(shard, 'tm', [(i, i + by) for i in range(peers) if 0 <= i +...  32.7 us
    ppermute x8, waiting for transfers between devices, passed_along(): lax.ppermute(shard, 'tm', [(i, i + by) for i in range(peers) if 0 <= i +...  28.8 us
    all_gather x1, blocking collectives, gathered(): return lax.all_gather(shard, 'panel', axis=0, tiled=False)  26.3 us
    all_to_all x2, waiting for transfers between devices, exchanged(): lax.all_to_all(packed, 'panel', split_axis=0, concat_axis=0, tiled=True)  20 us
    all_to_all x2, starting transfers between devices, exchanged(): lax.all_to_all(packed, 'panel', split_axis=0, concat_axis=0, tiled=True)  11.2 us
    unnamed x23, local copies, waits for them, and re-layouts  6.09 us
  transfers between devices with their start and end apart: 12, of which 9 were waited for; matrix products, arithmetic and copies ran while one was open for 5% of the time, Pallas kernels for 15%

profile of v14, /device:TPU:7, one launch (start us, length us, event | category | flops | bytes accessed | tf_op | source)
XLA Modules:
  0.0 190.8 jit_solution(11841246466840175457)
XLA Ops:
  7.2 3.2 %collective-permute-start = (f32[32,512]{1,0:T(8,128)}, f32[32,512]{1,0:T(8,128)S(1)}, u32[]{:S(2)}, u32[]{:S(2)}) collective-permute-start(f32[32,512]{1,0:T(8,128)} %a0_ref.3), channel_id=1, source_target_pairs={{0,16},{16,32},{32,48},{48,64},{64,80},{80,96},{96,112},{112,128},... | collective-permute-start | bytes 196616 | tf_op jit(solution)/shard_map/ppermute | solution.py:299
  10.4 6.4 %collective-permute-start.2 = (f32[32,512]{1,0:T(8,128)}, f32[32,512]{1,0:T(8,128)S(1)}, u32[]{:S(2)}, u32[]{:S(2)}) collective-permute-start(f32[32,512]{1,0:T(8,128)} %a0_ref.3), channel_id=1, source_target_pairs={{0,48},{16,64},{32,80},{48,96},{64,112},{80,128},{96,144},{112,160... | collective-permute-start | bytes 196616 | tf_op jit(solution)/shard_map/ppermute | solution.py:299
  16.9 0.8 slice_bitcast_fusion
  17.7 0.8 pad_maximum_fusion.1
  18.6 2.4 %collective-permute-start.1 = (f32[64,512]{1,0:T(8,128)S(1)}, f32[64,512]{1,0:T(8,128)S(1)}, u32[]{:S(2)}, u32[]{:S(2)}) collective-permute-start(f32[64,512]{1,0:T(8,128)S(1)} %pad_maximum_fusion.1), channel_id=1, source_target_pairs={{0,32},{16,48},{32,64},{48,80},{64,96},{80,112},{96,128},{112,144}... | collective-permute-start | bytes 393224 | tf_op jit(solution)/shard_map/ppermute | solution.py:299
  21.0 0.7 select_maximum_fusion
  21.8 0.8 copy-done
  22.6 0.9 copy-done.1
  24.1 0.9 pad_maximum_fusion
  25.0 5.8 %collective-permute-done.1.late_ref = f32[64,512]{1,0:T(8,128)S(1)} collective-permute-done((f32[64,512]{1,0:T(8,128)S(1)}, f32[64,512]{1,0:T(8,128)S(1)}, u32[]{:S(2)}, u32[]{:S(2)}) %collective-permute-start.1) | collective-permute-done | bytes 131104 | tf_op jit(solution)/shard_map/ppermute | solution.py:299
  30.8 1.3 shard_map.102
  32.2 1.9 %collective-permute-start.3 = (f32[72,512]{1,0:T(8,128)S(1)}, f32[72,512]{1,0:T(8,128)S(1)}, u32[]{:S(2)}, u32[]{:S(2)}) collective-permute-start(f32[72,512]{1,0:T(8,128)S(1)} %pad_maximum_fusion), channel_id=1, source_target_pairs={{0,16},{16,32},{32,48},{48,64},{64,80},{80,96},{96,112},{112,128},... | collective-permute-start | bytes 442376 | tf_op jit(solution)/shard_map/ppermute | solution.py:299
  34.2 1.9 %collective-permute-start.4 = (f32[72,512]{1,0:T(8,128)S(1)}, f32[72,512]{1,0:T(8,128)S(1)}, u32[]{:S(2)}, u32[]{:S(2)}) collective-permute-start(f32[72,512]{1,0:T(8,128)S(1)} %pad_maximum_fusion), channel_id=1, source_target_pairs={{0,32},{16,48},{32,64},{48,80},{64,96},{80,112},{96,128},{112,144}... | collective-permute-start | bytes 442376 | tf_op jit(solution)/shard_map/ppermute | solution.py:299
  36.1 2.8 %collective-permute-start.5 = (f32[72,512]{1,0:T(8,128)S(1)}, f32[72,512]{1,0:T(8,128)S(1)}, u32[]{:S(2)}, u32[]{:S(2)}) collective-permute-start(f32[72,512]{1,0:T(8,128)S(1)} %pad_maximum_fusion), channel_id=1, source_target_pairs={{0,48},{16,64},{32,80},{48,96},{64,112},{80,128},{96,144},{112,160... | collective-permute-start | bytes 442376 | tf_op jit(solution)/shard_map/ppermute | solution.py:299
  38.9 1.3 collective-permute-done.3
  40.2 4.3 %collective-permute-done.4 = f32[72,512]{1,0:T(8,128)S(1)} collective-permute-done((f32[72,512]{1,0:T(8,128)S(1)}, f32[72,512]{1,0:T(8,128)S(1)}, u32[]{:S(2)}, u32[]{:S(2)}) %collective-permute-start.4) | collective-permute-done | bytes 147488 | tf_op jit(solution)/shard_map/ppermute | solution.py:299
  44.6 11.5 %collective-permute-done.5 = f32[72,512]{1,0:T(8,128)S(1)} collective-permute-done((f32[72,512]{1,0:T(8,128)S(1)}, f32[72,512]{1,0:T(8,128)S(1)}, u32[]{:S(2)}, u32[]{:S(2)}) %collective-permute-start.5) | collective-permute-done | bytes 147488 | tf_op jit(solution)/shard_map/ppermute | solution.py:299
  56.1 0.7 concatenate.24
  57.0 0.9 constant_dynamic-update-slice_fusion
  57.9 0.7 slice_dynamic-update-slice_fusion
  58.8 26.3 %all-gather.1 = f32[128,512]{1,0:T(8,128)S(1)} all-gather(f32[8,512]{1,0:T(8,128)S(1)} %concatenate.25), channel_id=3, replica_groups=mesh['tm'=32,'panel'=16] {'panel'}, dimensions={0}, use_global_device_ids=true | all-gather | bytes 278528 | tf_op jit(solution)/shard_map/all_gather | solution.py:303
  85.3 0.7 reshape.27.vec_ref
  86.0 0.6 slice_reduce_fusion.u_ref
  86.6 1.9 all-gather.6.cloned.1.call-done
  88.5 4.9 %shard_map.107.drows_ref = f32[32,512]{1,0:T(8,128)} custom-call(f32[16,224,512]{2,1,0:T(8,128)} %bitcast.24, f32[32,512]{1,0:T(8,128)} %a0_ref.3), custom_call_target="tpu_custom_call" | custom-call | flops 805306368 | bytes 7405568 | tf_op jit(solution)/shard_map/pallas_call | solution.py:286
  93.4 7.1 %collective-permute-start.6 = (f32[32,512]{1,0:T(8,128)}, f32[32,512]{1,0:T(8,128)S(1)}, u32[]{:S(2)}, u32[]{:S(2)}) collective-permute-start(f32[32,512]{1,0:T(8,128)} %shard_map.107.drows_ref), channel_id=1, source_target_pairs={{0,64},{16,80},{32,96},{48,112},{64,128},{80,144},{96,160},{112,17... | collective-permute-start | bytes 196616 | tf_op jit(solution)/shard_map/ppermute | solution.py:299
  100.5 3.0 %collective-permute-done.6 = f32[32,512]{1,0:T(8,128)S(1)} collective-permute-done((f32[32,512]{1,0:T(8,128)}, f32[32,512]{1,0:T(8,128)S(1)}, u32[]{:S(2)}, u32[]{:S(2)}) %collective-permute-start.6) | collective-permute-done | bytes 65568 | tf_op jit(solution)/shard_map/ppermute | solution.py:299
  103.5 0.7 pad_maximum_fusion.3
  104.2 9.6 %shard_map.103 = (f32[16,32,256]{2,1,0:T(8,128)}, f32[8,512]{1,0:T(8,128)}, bf16[2,512,512]{2,1,0:T(8,128)(2,1)}, bf16[2,512,512]{2,1,0:T(8,128)(2,1)}, bf16[2,5...) custom-call(f32[16,224,512]{2,1,0:T(8,128)} %bitcast.25, f32[192,512]{1,0:T(8,128)} %copy-done.9, ...), custom_call_target="tpu_custom_call" | custom-call | flops 4831838208 | bytes 7757824 | tf_op jit(solution)/shard_map/pallas_call | solution.py:286
  113.8 5.4 %all-to-all-start = ((f32[16,32,256]{2,1,0:T(8,128)}), f32[16,32,256]{2,1,0:T(8,128)S(1)}, u32[]{:S(2)}, u32[]{:S(2)}) async-start(f32[16,32,256]{2,1,0:T(8,128)} %get-tuple-element.54), calls=%async_computation | async-start | bytes 1048576 | tf_op jit(solution)/shard_map/all_to_all | solution.py:307
  119.2 0.7 pad_maximum_fusion.2.own_ref
  119.9 4.7 %shard_map.105 = (bf16[2,512,512]{2,1,0:T(8,128)(2,1)}, bf16[2,512,512]{2,1,0:T(8,128)(2,1)}) custom-call(f32[16,224,512]{2,1,0:T(8,128)} %bitcast.26, bf16[2,512,512]{2,1,0:T(8,128)(2,1)} %get-tuple-element.61.bw_ref, bf16[2,512,512]{2,1,0:T(8,128)(2,1)} %get-tuple-element.58.bp_ref), custom_call_target="tpu_custom_call" | custom-call | flops 1610612736 | bytes 9437184 | tf_op jit(solution)/shard_map/pallas_call | solution.py:286
  124.6 6.1 %shard_map.104 = (bf16[2,512,512]{2,1,0:T(8,128)(2,1)}, bf16[2,512,512]{2,1,0:T(8,128)(2,1)}, bf16[2,512,512]{2,1,0:T(8,128)(2,1)}) custom-call(f32[16,224,512]{2,1,0:T(8,128)} %bitcast.27, bf16[2,512,512]{2,1,0:T(8,128)(2,1)} %get-tuple-element.58.bp_ref), custom_call_target="tpu_custom_call" | custom-call | flops 2415919104 | bytes 8388608 | tf_op jit(solution)/shard_map/pallas_call | solution.py:286
  130.7 9.2 %all-to-all-done = f32[16,32,256]{2,1,0:T(8,128)S(1)} async-done(((f32[16,32,256]{2,1,0:T(8,128)}), f32[16,32,256]{2,1,0:T(8,128)S(1)}, u32[]{:S(2)}, u32[]{:S(2)}) %all-to-all-start) | async-done | bytes 524320 | tf_op jit(solution)/shard_map/all_to_all | solution.py:307
  139.8 0.8 copy-done.7
  140.6 5.1 %shard_map.106.state_ref = f32[72,512]{1,0:T(8,128)} custom-call(f32[512,256]{1,0:T(8,128)} %bitcast.28, f32[64,512]{1,0:T(8,128)} %pad_maximum_fusion.2.own_ref, f32[8,512]{1,0:T(8,128)} %get-tuple-element.55.vec_ref, bf16[2,512,512]{2,1,0:T(8,128)(2,1)} %get-tuple-element.56.p0p_ref, bf16[2,512,512]{2,1,0:T(8,128)(2,1)} %get-tuple-element.57.p0_ref, ...), custom_call_target="tpu_custom_call" | custom-call | flops 805306368 | bytes 6963200 | tf_op jit(solution)/shard_map/pallas_call | solution.py:286
  145.8 6.9 %collective-permute-start.7 = (f32[72,512]{1,0:T(8,128)}, f32[72,512]{1,0:T(8,128)S(1)}, u32[]{:S(2)}, u32[]{:S(2)}) collective-permute-start(f32[72,512]{1,0:T(8,128)} %shard_map.106.state_ref), channel_id=1, source_target_pairs={{0,64},{16,80},{32,96},{48,112},{64,128},{80,144},{96,160},{112,17... | collective-permute-start | bytes 442376 | tf_op jit(solution)/shard_map/ppermute | solution.py:299
  152.7 0.9 copy-done.3
  153.6 2.9 %shard_map.108 = (f32[40,512]{1,0:T(8,128)S(1)}, f32[72,512]{1,0:T(8,128)S(1)}, f32[32,512]{1,0:T(8,128)S(1)}, f32[32,512]{1,0:T(8,128)S(1)}, bf16[2,512,512]{2,...) custom-call(f32[72,512]{1,0:T(8,128)S(1)} %copy-done.3, f32[32,512]{1,0:T(8,128)S(1)} %copy-done.2, f32[16,64,512]{2,1,0:T(8,128)} %bitcast.41), custom_call_target="tpu_custom_call" | custom-call | flops 805306368 | bytes 2310144 | tf_op jit(solution)/shard_map/pallas_call | solution.py:286
  156.5 2.8 %collective-permute-done.7.prior_ref = f32[72,512]{1,0:T(8,128)S(1)} collective-permute-done((f32[72,512]{1,0:T(8,128)}, f32[72,512]{1,0:T(8,128)S(1)}, u32[]{:S(2)}, u32[]{:S(2)}) %collective-permute-start.7) | collective-permute-done | bytes 147488 | tf_op jit(solution)/shard_map/ppermute | solution.py:299
  159.4 1.2 copy-done.5
  160.6 2.3 %shard_map.109 = (f32[16,32,128]{2,1,0:T(8,128)}, f32[8,512]{1,0:T(8,128)S(1)}) custom-call(s32[2]{0:T(128)S(1)} %pad_add_fusion.place_ref, f32[72,512]{1,0:T(8,128)S(1)} %collective-permute-done.7.prior_ref, f32[72,512]{1,0:T(8,128)S(1)} %get-tuple-element.66.own_ref, f32[40,512]{1,0:T(8,128)S(1)} %get-tuple-element.67.z_ref, ...), custom_call_target="tpu_custom_call" | custom-call | flops 805306368 | bytes 2473992 | tf_op jit(solution)/shard_map/pallas_call | solution.py:286
  162.9 5.7 %all-to-all-start.1 = ((f32[16,32,128]{2,1,0:T(8,128)}), f32[16,32,128]{2,1,0:T(8,128)S(1)}, u32[]{:S(2)}, u32[]{:S(2)}) async-start(f32[16,32,128]{2,1,0:T(8,128)} %get-tuple-element.70), calls=%async_computation.1 | async-start | bytes 524288 | tf_op jit(solution)/shard_map/all_to_all | solution.py:307
  168.8 0.6 broadcast_select_fusion
  169.4 10.9 %all-to-all-done.1 = f32[16,32,128]{2,1,0:T(8,128)S(1)} async-done(((f32[16,32,128]{2,1,0:T(8,128)}), f32[16,32,128]{2,1,0:T(8,128)S(1)}, u32[]{:S(2)}, u32[]{:S(2)}) %all-to-all-start.1) | async-done | bytes 262176 | tf_op jit(solution)/shard_map/all_to_all | solution.py:307
  180.3 1.2 copy-done.6
  181.5 1.7 shard_map.110
  183.3 0.7 slice_reduce_fusion.2
  (42 shorter events, 1.4 us)
Async XLA Ops:
  7.2 81.3 %all-gather.6.cloned.1.call-start = ((), (), s32[]{:S(2)}) async-start(), calls=%async_computation.2 | async-start | bytes 7798784 | tf_op jit(solution)/shard_map/all_gather | solution.py:303
  7.2 17.8 %collective-permute-start = (f32[32,512]{1,0:T(8,128)}, f32[32,512]{1,0:T(8,128)S(1)}, u32[]{:S(2)}, u32[]{:S(2)}) collective-permute-start(f32[32,512]{1,0:T(8,128)} %a0_ref.3), channel_id=1, source_target_pairs={{0,16},{16,32},{32,48},{48,64},{64,80},{80,96},{96,112},{112,128},... | collective-permute-start | bytes 196616 | tf_op jit(solution)/shard_map/ppermute | solution.py:299
  10.4 14.6 %collective-permute-start.2 = (f32[32,512]{1,0:T(8,128)}, f32[32,512]{1,0:T(8,128)S(1)}, u32[]{:S(2)}, u32[]{:S(2)}) collective-permute-start(f32[32,512]{1,0:T(8,128)} %a0_ref.3), channel_id=1, source_target_pairs={{0,48},{16,64},{32,80},{48,96},{64,112},{80,128},{96,144},{112,160... | collective-permute-start | bytes 196616 | tf_op jit(solution)/shard_map/ppermute | solution.py:299
  18.6 12.2 %collective-permute-start.1 = (f32[64,512]{1,0:T(8,128)S(1)}, f32[64,512]{1,0:T(8,128)S(1)}, u32[]{:S(2)}, u32[]{:S(2)}) collective-permute-start(f32[64,512]{1,0:T(8,128)S(1)} %pad_maximum_fusion.1), channel_id=1, source_target_pairs={{0,32},{16,48},{32,64},{48,80},{64,96},{80,112},{96,128},{112,144}... | collective-permute-start | bytes 393224 | tf_op jit(solution)/shard_map/ppermute | solution.py:299
  21.8 0.8 copy-start
  22.6 0.9 copy-start.1
  32.2 120.5 %all-gather.8.cloned.1.call-start = ((), (), s32[]{:S(2)}) async-start(), calls=%async_computation.3 | async-start | bytes 2228224 | tf_op jit(solution)/shard_map/all_gather | solution.py:303
  32.2 8.0 %collective-permute-start.3 = (f32[72,512]{1,0:T(8,128)S(1)}, f32[72,512]{1,0:T(8,128)S(1)}, u32[]{:S(2)}, u32[]{:S(2)}) collective-permute-start(f32[72,512]{1,0:T(8,128)S(1)} %pad_maximum_fusion), channel_id=1, source_target_pairs={{0,16},{16,32},{32,48},{48,64},{64,80},{80,96},{96,112},{112,128},... | collective-permute-start | bytes 442376 | tf_op jit(solution)/shard_map/ppermute | solution.py:299
  34.2 10.4 %collective-permute-start.4 = (f32[72,512]{1,0:T(8,128)S(1)}, f32[72,512]{1,0:T(8,128)S(1)}, u32[]{:S(2)}, u32[]{:S(2)}) collective-permute-start(f32[72,512]{1,0:T(8,128)S(1)} %pad_maximum_fusion), channel_id=1, source_target_pairs={{0,32},{16,48},{32,64},{48,80},{64,96},{80,112},{96,128},{112,144}... | collective-permute-start | bytes 442376 | tf_op jit(solution)/shard_map/ppermute | solution.py:299
  36.1 20.0 %collective-permute-start.5 = (f32[72,512]{1,0:T(8,128)S(1)}, f32[72,512]{1,0:T(8,128)S(1)}, u32[]{:S(2)}, u32[]{:S(2)}) collective-permute-start(f32[72,512]{1,0:T(8,128)S(1)} %pad_maximum_fusion), channel_id=1, source_target_pairs={{0,48},{16,64},{32,80},{48,96},{64,112},{80,128},{96,144},{112,160... | collective-permute-start | bytes 442376 | tf_op jit(solution)/shard_map/ppermute | solution.py:299
  58.8 45.4 %copy-start.9 = (f32[192,512]{1,0:T(8,128)}, f32[192,512]{1,0:T(8,128)S(1)}, u32[]{:S(2)}) copy-start(f32[192,512]{1,0:T(8,128)S(1)} %get-tuple-element.82.own_ref) | copy-start | bytes 1179652
  93.4 10.1 %collective-permute-start.6 = (f32[32,512]{1,0:T(8,128)}, f32[32,512]{1,0:T(8,128)S(1)}, u32[]{:S(2)}, u32[]{:S(2)}) collective-permute-start(f32[32,512]{1,0:T(8,128)} %shard_map.107.drows_ref), channel_id=1, source_target_pairs={{0,64},{16,80},{32,96},{48,112},{64,128},{80,144},{96,160},{112,17... | collective-permute-start | bytes 196616 | tf_op jit(solution)/shard_map/ppermute | solution.py:299
  104.2 15.0 %copy-start.8 = (f32[32,512]{1,0:T(8,128)S(1)}, f32[32,512]{1,0:T(8,128)}, u32[]{:S(2)}) copy-start(f32[32,512]{1,0:T(8,128)} %param.8) | copy-start | bytes 196612
  113.8 26.0 %all-to-all-start = ((f32[16,32,256]{2,1,0:T(8,128)}), f32[16,32,256]{2,1,0:T(8,128)S(1)}, u32[]{:S(2)}, u32[]{:S(2)}) async-start(f32[16,32,256]{2,1,0:T(8,128)} %get-tuple-element.54), calls=%async_computation | async-start | bytes 1048576 | tf_op jit(solution)/shard_map/all_to_all | solution.py:307
  124.5 28.1 %copy-start.2 = (f32[32,512]{1,0:T(8,128)S(1)}, f32[32,512]{1,0:T(8,128)}, u32[]{:S(2)}) copy-start(f32[32,512]{1,0:T(8,128)} %shard_map.107.drows_ref) | copy-start | bytes 196612
  124.6 34.8 %copy-start.4 = (bf16[2,512,512]{2,1,0:T(8,128)(2,1)S(1)}, bf16[2,512,512]{2,1,0:T(8,128)(2,1)}, u32[]{:S(2)}) copy-start(bf16[2,512,512]{2,1,0:T(8,128)(2,1)} %get-tuple-element.69.d_ref) | copy-start | bytes 3145732
  139.8 0.8 copy-start.7
  145.8 13.6 %collective-permute-start.7 = (f32[72,512]{1,0:T(8,128)}, f32[72,512]{1,0:T(8,128)S(1)}, u32[]{:S(2)}, u32[]{:S(2)}) collective-permute-start(f32[72,512]{1,0:T(8,128)} %shard_map.106.state_ref), channel_id=1, source_target_pairs={{0,64},{16,80},{32,96},{48,112},{64,128},{80,144},{96,160},{112,17... | collective-permute-start | bytes 442376 | tf_op jit(solution)/shard_map/ppermute | solution.py:299
  152.7 0.9 copy-start.3
  159.4 1.2 copy-start.5
  162.9 17.4 %all-to-all-start.1 = ((f32[16,32,128]{2,1,0:T(8,128)}), f32[16,32,128]{2,1,0:T(8,128)S(1)}, u32[]{:S(2)}, u32[]{:S(2)}) async-start(f32[16,32,128]{2,1,0:T(8,128)} %get-tuple-element.70), calls=%async_computation.1 | async-start | bytes 524288 | tf_op jit(solution)/shard_map/all_to_all | solution.py:307
  180.3 1.2 copy-start.6
Sparse Core Ops, SparseCore 0:
  32.3 56.1 all-gather.5
  104.3 46.5 all-gather.7
